TPU v7x, 32 devices: a whole 2x2x4 slice. The times are simulated.
32 devices in a mesh: ia: 4 (over y, x), ja: 4 (over z), ka: 2 (over core).
Axes of the slice: x: 2, y: 2, z: 4, core: 2. Of those that a mesh axis runs over, the one named last changes fastest.
Arguments:
- state: float32 [8, 7, 64, 2048], P('ia', None, 'ja', 'ka'), may hold values from -6 to 6
- inverse: bfloat16 [8, 7, 7, 64, 2048], P('ia', None, None, 'ja', 'ka'), may hold values from -1 to 1
- coupling: float32 [8, 2, 64, 2048], P('ia', None, 'ja', 'ka'), may hold values from 0.49 to 1
- wall: int32 [8, 64, 2048], P('ia', 'ja', 'ka'), may hold values 0 or 1
Outputs:
- correction: float32 [8, 7, 64, 2048], P('ia', None, 'ja', 'ka')
All inputs are finite; a program needn't handle non-finite values. No bound on the sum of `wall` on one device may be relied on, other than what follows from the above.
Results may differ from a plain program's by a relative error of at most 0.0003.
Values may be sent and summed in bfloat16 or wider, within the bound.
No kernel may reach another device: no remote copies, remote signals or barrier semaphores. Data moves between devices by JAX's collectives and lax.ppermute only.
A program may use at most 128 MiB of HBM per device.

v0:
```python
import jax
import jax.numpy as jnp
from jax import lax
from jax.sharding import PartitionSpec as P

advection = 0.012
viscosity = 0.006
damping = 0.003


def padded_2(cells, sides, width):
    for axis, dim in sides:
        count = lax.axis_size(axis)
        ends = count - 1
        head = lax.slice_in_dim(cells, 0, width, axis=dim)
        tail = lax.slice_in_dim(cells, cells.shape[dim] - width, cells.shape[dim], axis=dim)
        cells = jnp.concatenate(
            [
                lax.ppermute(tail, axis, [(i, (i + 1) % count) for i in range(ends)]),
                cells,
                lax.ppermute(head, axis, [((i + 1) % count, i) for i in range(ends)]),
            ],
            axis=dim,
        )
    return cells


def from_behind(value, axis, by):
    peers = lax.axis_size(axis)
    pairs = [(i, i + by) for i in range(peers) if 0 <= i + by < peers]
    return lax.ppermute(value, axis, pairs)


def sliced(padded, shift_i, shift_j, shift_k):
    rows_i = padded.shape[0] - 4
    rows_j = padded.shape[2] - 4
    rows_k = padded.shape[3] - 4
    return padded[
        2 + shift_i : 2 + shift_i + rows_i,
        :,
        2 + shift_j : 2 + shift_j + rows_j,
        2 + shift_k : 2 + shift_k + rows_k,
    ]


def fourth_along(padded, centre, shift_i, shift_j, shift_k):
    return (
        sliced(padded, 2 * shift_i, 2 * shift_j, 2 * shift_k)
        - 4.0 * sliced(padded, shift_i, shift_j, shift_k)
        + 6.0 * centre
        - 4.0 * sliced(padded, -shift_i, -shift_j, -shift_k)
        + sliced(padded, -2 * shift_i, -2 * shift_j, -2 * shift_k)
    )


def stencil(padded, wall):
    centre = sliced(padded, 0, 0, 0)
    convect = (
        -advection
        * 0.5
        * (3.0 * centre - 4.0 * sliced(padded, -1, 0, 0) + sliced(padded, -2, 0, 0))
    )
    laplace = (
        sliced(padded, 1, 0, 0)
        + sliced(padded, -1, 0, 0)
        + sliced(padded, 0, 1, 0)
        + sliced(padded, 0, -1, 0)
        + sliced(padded, 0, 0, 1)
        + sliced(padded, 0, 0, -1)
        - 6.0 * centre
    )
    fourth = (
        fourth_along(padded, centre, 1, 0, 0)
        + fourth_along(padded, centre, 0, 1, 0)
        + fourth_along(padded, centre, 0, 0, 1)
    )
    open_cells = (1 - wall).astype(jnp.float32)[:, None]
    return open_cells * (convect + viscosity * laplace - damping * fourth)


def apply_inverse(inverse_plane, vector):
    return jnp.sum(inverse_plane.astype(jnp.float32) * vector[None], axis=1)


def forward_local(inverse, residual, factors, entry_face):

    def forward_advance(running, inputs):
        inverse_plane, residual_plane, relaxation_factor = inputs
        result = apply_inverse(inverse_plane, residual_plane + relaxation_factor[None] * running)
        return (result, result)

    last_plane, planes = lax.scan(forward_advance, entry_face, (inverse, residual, factors))
    return (planes, last_plane)


def backward_local(inverse, base_planes, factors, entry_face):

    def backward_advance(running, inputs):
        inverse_plane, base_plane, relaxation_factor = inputs
        result = base_plane + apply_inverse(inverse_plane, relaxation_factor[None] * running)
        return (result, result)

    first_plane, planes = lax.scan(
        backward_advance, entry_face, (inverse, base_planes, factors), reverse=True
    )
    return (planes, first_plane)


def shards(state, inverse, coupling, wall):
    padded = padded_2(state, (("ia", 0), ("ja", 2), ("ka", 3)), 2)
    residual = stencil(padded, wall)
    lower = coupling[:, 0]
    upper = coupling[:, 1]
    count_vars = state.shape[1]
    zero_face = jnp.zeros((count_vars, state.shape[2], state.shape[3]), jnp.float32)
    planes, last_plane = forward_local(inverse, residual, lower, zero_face)

    def forward_round(round_index, running):
        entry_face = from_behind(running[1], "ia", 1)
        return forward_local(inverse, residual, lower, entry_face)

    planes, last_plane = lax.fori_loop(1, lax.axis_size("ia"), forward_round, (planes, last_plane))
    correction, first_plane = backward_local(inverse, planes, upper, zero_face)

    def backward_round(round_index, running):
        entry_face = from_behind(running[1], "ia", -1)
        return backward_local(inverse, planes, upper, entry_face)

    correction, first_plane = lax.fori_loop(
        1, lax.axis_size("ia"), backward_round, (correction, first_plane)
    )
    return correction


def solution(mesh):
    return jax.shard_map(
        shards,
        mesh=mesh,
        in_specs=(
            P("ia", None, "ja", "ka"),
            P("ia", None, None, "ja", "ka"),
            P("ia", None, "ja", "ka"),
            P("ia", "ja", "ka"),
        ),
        out_specs=P("ia", None, "ja", "ka"),
        check_vma=False,
    )
```

profile of v0, /device:TPU:0, one launch (start us, length us, event | category | flops | bytes accessed | tf_op | source)
XLA Modules:
  0.0 247.7 jit_solution(2809628675011330879)
XLA Ops:
  0.0 5.0 %collective-permute-start.2 = (f32[2,7,16,1024]{3,2,1,0:T(8,128)}, f32[2,7,16,1024]{3,2,1,0:T(8,128)S(1)}, u32[]{:S(2)}, u32[]{:S(2)}) collective-permute-start(f32[2,7,16,1024]{3,2,1,0:T(8,128)} %param.16), channel_id=1, source_target_pairs={{0,8},{8,16},{16,24},{1,9},{9,17},{17,25},{2,10},{10,18},{18,26},{... | collective-permute-start | bytes 2752520 | tf_op jit(solution)/shard_map/ppermute | solution.py:19
  6.3 18.5 %collective-permute-done.2 = f32[2,7,16,1024]{3,2,1,0:T(8,128)S(1)} collective-permute-done((f32[2,7,16,1024]{3,2,1,0:T(8,128)}, f32[2,7,16,1024]{3,2,1,0:T(8,128)S(1)}, u32[]{:S(2)}, u32[]{:S(2)}) %collective-permute-start.2) | collective-permute-done | bytes 917536 | tf_op jit(solution)/shard_map/ppermute | solution.py:19
  26.5 19.9 %collective-permute-done.3 = f32[2,7,16,1024]{3,2,1,0:T(8,128)S(1)} collective-permute-done((f32[2,7,16,1024]{3,2,1,0:T(8,128)}, f32[2,7,16,1024]{3,2,1,0:T(8,128)S(1)}, u32[]{:S(2)}, u32[]{:S(2)}) %collective-permute-start.3) | collective-permute-done | bytes 917536 | tf_op jit(solution)/shard_map/ppermute | solution.py:21
  49.1 4.6 %collective-permute-start.5 = (f32[6,7,2,1024]{3,2,1,0:T(2,128)S(1)}, f32[6,7,2,1024]{3,2,1,0:T(2,128)S(1)}, u32[]{:S(2)}, u32[]{:S(2)}) collective-permute-start(f32[6,7,2,1024]{3,2,1,0:T(2,128)S(1)} %get-tuple-element.591), channel_id=1, source_target_pairs={{0,2},{2,4},{4,6},{1,3},{3,5},{5,7},{8,10},{10,12},{12,14},{9,11},... | collective-permute-start | bytes 1032200 | tf_op jit(solution)/shard_map/ppermute | solution.py:19
  53.7 4.9 %collective-permute-done.4 = f32[6,7,2,1024]{3,2,1,0:T(2,128)S(1)} collective-permute-done((f32[6,7,2,1024]{3,2,1,0:T(2,128)S(1)}, f32[6,7,2,1024]{3,2,1,0:T(2,128)S(1)}, u32[]{:S(2)}, u32[]{:S(2)}) %collective-permute-start.4) | collective-permute-done | bytes 344096 | tf_op jit(solution)/shard_map/ppermute | solution.py:21
  63.1 4.6 %collective-permute-start.7 = (f32[6,7,20,2]{3,2,1,0:T(8,128)}, f32[6,7,20,2]{3,2,1,0:T(8,128)}, u32[]{:S(2)}, u32[]{:S(2)}) collective-permute-start(f32[6,7,20,2]{3,2,1,0:T(8,128)} %get-tuple-element.590), channel_id=1, source_target_pairs={{0,1},{2,3},{4,5},{6,7},{8,9},{10,11},{12,13},{14,15},{16,17},{18,... | collective-permute-start | bytes 20168 | tf_op jit(solution)/shard_map/ppermute | solution.py:19
  68.7 10.0 %fusion.10 = f32[2,7,16,1024]{3,2,1,0:T(8,128)} fusion(f32[6,7,20,2]{3,2,1,0:T(8,128)} %collective-permute-done.7, f32[6,7,2,1024]{3,2,1,0:T(2,128)} %copy-done.5, f32[6,7,16,1024]{3,2,1,0:T(8,128)} %copy-done.2, f32[6,7,2,1024]{3,2,1,0:T(2,128)} %copy-done.6, f32[6,7,20,2]{3,2,1,0:T(8,128)} %collective-permute-done.6, f32[2,7,16,1024]{3,2,1,0:T(8,128)} %copy-done.3, ...), kind=kLoop, calls=%fused_computation.29 | loop fusion | flops 12386304 | bytes 7255168 | tf_op jit(solution)/shard_map/mul | solution.py:78
  80.6 6.3 %while.93 = (s32[]{:T(128)}, f32[7,16,1024]{2,1,0:T(8,128)}, f32[2,7,16,1024]{3,2,1,0:T(8,128)}, bf16[2,7,7,16,1024]{4,3,2,1,0:T(8,128)(2,1)S(1)}, f32[2,7,16,10...) while((s32[]{:T(128)}, f32[7,16,1024]{2,1,0:T(8,128)}, f32[2,7,16,1024]{3,2,1,0:T(8,128)}, ...), condition=%wide.region_2.3_spmd, body=%wide.region_0.2_spmd.sunk | while | flops 2523138 | bytes 6849141 | solution.py:92
  86.9 72.0 %while.95 = (s32[]{:T(128)}, f32[2,7,16,1024]{3,2,1,0:T(8,128)}, f32[7,16,1024]{2,1,0:T(8,128)}, bf16[2,7,7,16,1024]{4,3,2,1,0:T(8,128)(2,1)S(1)}, f32[2,7,16,10...) while((s32[]{:T(128)}, f32[2,7,16,1024]{3,2,1,0:T(8,128)}, ...), condition=%wide.region_7.8_spmd, body=%wide.region_3.7_spmd.sunk | while | flops 2523140 | bytes 7766814 | solution.py:122
  86.9 4.2 %collective-permute-start.1 = (f32[7,16,1024]{2,1,0:T(8,128)}, f32[7,16,1024]{2,1,0:T(8,128)}, u32[]{:S(2)}, u32[]{:S(2)}) collective-permute-start(f32[7,16,1024]{2,1,0:T(8,128)} %get-tuple-element.921), channel_id=1, source_target_pairs={{0,8},{8,16},{16,24},{1,9},{9,17},{17,25},{2,10},{10,18},{18,26},{... | collective-permute-start | bytes 1376264 | tf_op jit(solution)/shard_map/while/body/eval_jaxpr/ppermute | solution.py:31
  91.1 9.8 %collective-permute-done.1 = f32[7,16,1024]{2,1,0:T(8,128)} collective-permute-done((f32[7,16,1024]{2,1,0:T(8,128)}, f32[7,16,1024]{2,1,0:T(8,128)}, u32[]{:S(2)}, u32[]{:S(2)}) %collective-permute-start.1) | collective-permute-done | bytes 458784 | tf_op jit(solution)/shard_map/while/body/eval_jaxpr/ppermute | solution.py:31
  100.9 8.4 %while.99 = (s32[]{:T(128)}, f32[7,16,1024]{2,1,0:T(8,128)}, f32[2,7,16,1024]{3,2,1,0:T(8,128)}, bf16[2,7,7,16,1024]{4,3,2,1,0:T(8,128)(2,1)S(1)}, f32[2,7,16,10...) while((s32[]{:T(128)}, f32[7,16,1024]{2,1,0:T(8,128)}, f32[2,7,16,1024]{3,2,1,0:T(8,128)}, ...), condition=%wide.region_6.6_spmd, body=%wide.region_4.5_spmd.sunk | while | flops 2523138 | bytes 5014105 | solution.py:92
  103.2 1.8 bitcast_dynamic-update-slice_fusion.5
  111.1 5.2 %collective-permute-start.1 = (f32[7,16,1024]{2,1,0:T(8,128)}, f32[7,16,1024]{2,1,0:T(8,128)}, u32[]{:S(2)}, u32[]{:S(2)}) collective-permute-start(f32[7,16,1024]{2,1,0:T(8,128)} %get-tuple-element.921), channel_id=1, source_target_pairs={{0,8},{8,16},{16,24},{1,9},{9,17},{17,25},{2,10},{10,18},{18,26},{... | collective-permute-start | bytes 1376264 | tf_op jit(solution)/shard_map/while/body/eval_jaxpr/ppermute | solution.py:31
  116.2 9.0 %collective-permute-done.1 = f32[7,16,1024]{2,1,0:T(8,128)} collective-permute-done((f32[7,16,1024]{2,1,0:T(8,128)}, f32[7,16,1024]{2,1,0:T(8,128)}, u32[]{:S(2)}, u32[]{:S(2)}) %collective-permute-start.1) | collective-permute-done | bytes 458784 | tf_op jit(solution)/shard_map/while/body/eval_jaxpr/ppermute | solution.py:31
  125.3 8.4 %while.99 = (s32[]{:T(128)}, f32[7,16,1024]{2,1,0:T(8,128)}, f32[2,7,16,1024]{3,2,1,0:T(8,128)}, bf16[2,7,7,16,1024]{4,3,2,1,0:T(8,128)(2,1)S(1)}, f32[2,7,16,10...) while((s32[]{:T(128)}, f32[7,16,1024]{2,1,0:T(8,128)}, f32[2,7,16,1024]{3,2,1,0:T(8,128)}, ...), condition=%wide.region_6.6_spmd, body=%wide.region_4.5_spmd.sunk | while | flops 2523138 | bytes 5014105 | solution.py:92
  127.6 1.8 bitcast_dynamic-update-slice_fusion.5
  135.4 5.2 %collective-permute-start.1 = (f32[7,16,1024]{2,1,0:T(8,128)}, f32[7,16,1024]{2,1,0:T(8,128)}, u32[]{:S(2)}, u32[]{:S(2)}) collective-permute-start(f32[7,16,1024]{2,1,0:T(8,128)} %get-tuple-element.921), channel_id=1, source_target_pairs={{0,8},{8,16},{16,24},{1,9},{9,17},{17,25},{2,10},{10,18},{18,26},{... | collective-permute-start | bytes 1376264 | tf_op jit(solution)/shard_map/while/body/eval_jaxpr/ppermute | solution.py:31
  140.6 8.1 %collective-permute-done.1 = f32[7,16,1024]{2,1,0:T(8,128)} collective-permute-done((f32[7,16,1024]{2,1,0:T(8,128)}, f32[7,16,1024]{2,1,0:T(8,128)}, u32[]{:S(2)}, u32[]{:S(2)}) %collective-permute-start.1) | collective-permute-done | bytes 458784 | tf_op jit(solution)/shard_map/while/body/eval_jaxpr/ppermute | solution.py:31
  148.7 8.4 %while.99 = (s32[]{:T(128)}, f32[7,16,1024]{2,1,0:T(8,128)}, f32[2,7,16,1024]{3,2,1,0:T(8,128)}, bf16[2,7,7,16,1024]{4,3,2,1,0:T(8,128)(2,1)S(1)}, f32[2,7,16,10...) while((s32[]{:T(128)}, f32[7,16,1024]{2,1,0:T(8,128)}, f32[2,7,16,1024]{3,2,1,0:T(8,128)}, ...), condition=%wide.region_6.6_spmd, body=%wide.region_4.5_spmd.sunk | while | flops 2523138 | bytes 5014105 | solution.py:92
  151.1 1.8 bitcast_dynamic-update-slice_fusion.5
  159.9 9.3 %while.98 = (s32[]{:T(128)}, f32[7,16,1024]{2,1,0:T(8,128)}, f32[2,7,16,1024]{3,2,1,0:T(8,128)}, f32[2,7,16,1024]{3,2,1,0:T(8,128)}, bf16[2,7,7,16,1024]{4,3,2,1...) while((s32[]{:T(128)}, f32[7,16,1024]{2,1,0:T(8,128)}, ...), condition=%wide.region_10.11_spmd.clone, body=%wide.region_8.10_spmd.clone.sunk | while | flops 2752516 | bytes 6389883 | solution.py:103
  160.3 1.9 fusion.28
  162.2 1.9 bitcast_add_fusion.11
  165.5 1.9 fusion.28
  167.3 1.9 bitcast_add_fusion.11
  169.2 78.4 %while.97 = (s32[]{:T(128)}, f32[2,7,16,1024]{3,2,1,0:T(8,128)}, f32[7,16,1024]{2,1,0:T(8,128)}, f32[2,7,16,1024]{3,2,1,0:T(8,128)}, bf16[2,7,7,16,1024]{4,3,2,1...) while((s32[]{:T(128)}, f32[2,7,16,1024]{3,2,1,0:T(8,128)}, ...), condition=%wide.region_15.16_spmd, body=%wide.region_11.15_spmd.sunk | while | flops 2637829 | bytes 10060090 | solution.py:129
  170.5 12.2 %collective-permute-done = f32[7,16,1024]{2,1,0:T(8,128)} collective-permute-done((f32[7,16,1024]{2,1,0:T(8,128)}, f32[7,16,1024]{2,1,0:T(8,128)}, u32[]{:S(2)}, u32[]{:S(2)}) %collective-permute-start) | collective-permute-done | bytes 458784 | tf_op jit(solution)/shard_map/while/body/eval_jaxpr/ppermute | solution.py:31
  183.7 10.3 %while.100 = (s32[]{:T(128)}, f32[7,16,1024]{2,1,0:T(8,128)}, f32[2,7,16,1024]{3,2,1,0:T(8,128)}, f32[2,7,16,1024]{3,2,1,0:T(8,128)}, bf16[2,7,7,16,1024]{4,3,2,...) while((s32[]{:T(128)}, f32[7,16,1024]{2,1,0:T(8,128)}, f32[2,7,16,1024]{3,2,1,0:T(8,128)}, ...), condition=%wide.region_14.14_spmd, body=%wide.region_12.13_spmd.sunk | while | flops 2637827 | bytes 6389865 | solution.py:103
  185.1 1.9 fusion.30
  187.0 1.9 bitcast_add_fusion.12
  190.3 1.9 fusion.30
  192.1 1.9 bitcast_add_fusion.12
  194.0 1.8 copy.68
  197.1 12.3 %collective-permute-done = f32[7,16,1024]{2,1,0:T(8,128)} collective-permute-done((f32[7,16,1024]{2,1,0:T(8,128)}, f32[7,16,1024]{2,1,0:T(8,128)}, u32[]{:S(2)}, u32[]{:S(2)}) %collective-permute-start) | collective-permute-done | bytes 458784 | tf_op jit(solution)/shard_map/while/body/eval_jaxpr/ppermute | solution.py:31
  210.5 10.3 %while.100 = (s32[]{:T(128)}, f32[7,16,1024]{2,1,0:T(8,128)}, f32[2,7,16,1024]{3,2,1,0:T(8,128)}, f32[2,7,16,1024]{3,2,1,0:T(8,128)}, bf16[2,7,7,16,1024]{4,3,2,...) while((s32[]{:T(128)}, f32[7,16,1024]{2,1,0:T(8,128)}, f32[2,7,16,1024]{3,2,1,0:T(8,128)}, ...), condition=%wide.region_14.14_spmd, body=%wide.region_12.13_spmd.sunk | while | flops 2637827 | bytes 6389865 | solution.py:103
  211.9 1.9 fusion.30
  213.7 1.9 bitcast_add_fusion.12
  217.0 1.9 fusion.30
  218.9 1.9 bitcast_add_fusion.12
  220.7 1.8 copy.68
  223.9 10.7 %collective-permute-done = f32[7,16,1024]{2,1,0:T(8,128)} collective-permute-done((f32[7,16,1024]{2,1,0:T(8,128)}, f32[7,16,1024]{2,1,0:T(8,128)}, u32[]{:S(2)}, u32[]{:S(2)}) %collective-permute-start) | collective-permute-done | bytes 458784 | tf_op jit(solution)/shard_map/while/body/eval_jaxpr/ppermute | solution.py:31
  235.5 10.3 %while.100 = (s32[]{:T(128)}, f32[7,16,1024]{2,1,0:T(8,128)}, f32[2,7,16,1024]{3,2,1,0:T(8,128)}, f32[2,7,16,1024]{3,2,1,0:T(8,128)}, bf16[2,7,7,16,1024]{4,3,2,...) while((s32[]{:T(128)}, f32[7,16,1024]{2,1,0:T(8,128)}, f32[2,7,16,1024]{3,2,1,0:T(8,128)}, ...), condition=%wide.region_14.14_spmd, body=%wide.region_12.13_spmd.sunk | while | flops 2637827 | bytes 6389865 | solution.py:103
  237.0 1.9 fusion.30
  238.8 1.9 bitcast_add_fusion.12
  242.1 1.9 fusion.30
  244.0 1.9 bitcast_add_fusion.12
  245.8 1.8 copy.68
  (102 shorter events, 62.5 us)
Async XLA Ops:
  0.0 53.6 %copy-start.7 = (f32[2,2,16,1024]{3,2,1,0:T(8,128)S(1)}, f32[2,2,16,1024]{3,2,1,0:T(8,128)}, u32[]{:S(2)}) copy-start(f32[2,2,16,1024]{3,2,1,0:T(8,128)} %param.18) | copy-start | bytes 786436
  0.0 24.9 %collective-permute-start.2 = (f32[2,7,16,1024]{3,2,1,0:T(8,128)}, f32[2,7,16,1024]{3,2,1,0:T(8,128)S(1)}, u32[]{:S(2)}, u32[]{:S(2)}) collective-permute-start(f32[2,7,16,1024]{3,2,1,0:T(8,128)} %param.16), channel_id=1, source_target_pairs={{0,8},{8,16},{16,24},{1,9},{9,17},{17,25},{2,10},{10,18},{18,26},{... | collective-permute-start | bytes 2752520 | tf_op jit(solution)/shard_map/ppermute | solution.py:19
  5.0 41.4 %collective-permute-start.3 = (f32[2,7,16,1024]{3,2,1,0:T(8,128)}, f32[2,7,16,1024]{3,2,1,0:T(8,128)S(1)}, u32[]{:S(2)}, u32[]{:S(2)}) collective-permute-start(f32[2,7,16,1024]{3,2,1,0:T(8,128)} %param.16), channel_id=1, source_target_pairs={{8,0},{16,8},{24,16},{9,1},{17,9},{25,17},{10,2},{18,10},{26,18},{... | collective-permute-start | bytes 2752520 | tf_op jit(solution)/shard_map/ppermute | solution.py:21
  24.9 1.6 copy-start.3
  46.4 0.9 copy-start.4
  47.4 21.0 %copy-start.2 = (f32[6,7,16,1024]{3,2,1,0:T(8,128)}, f32[6,7,16,1024]{3,2,1,0:T(8,128)S(1)}, u32[]{:S(2)}) copy-start(f32[6,7,16,1024]{3,2,1,0:T(8,128)S(1)} %constant_dynamic-update-slice_fusion) | copy-start | bytes 8257540
  47.4 20.3 %copy-start.8 = (s32[2,16,1024]{2,1,0:T(8,128)S(1)}, s32[2,16,1024]{2,1,0:T(8,128)}, u32[]{:S(2)}) copy-start(s32[2,16,1024]{2,1,0:T(8,128)} %param.19) | copy-start | bytes 393220
  47.8 10.8 %collective-permute-start.4 = (f32[6,7,2,1024]{3,2,1,0:T(2,128)S(1)}, f32[6,7,2,1024]{3,2,1,0:T(2,128)S(1)}, u32[]{:S(2)}, u32[]{:S(2)}) collective-permute-start(f32[6,7,2,1024]{3,2,1,0:T(2,128)S(1)} %get-tuple-element.592), channel_id=1, source_target_pairs={{2,0},{4,2},{6,4},{3,1},{5,3},{7,5},{10,8},{12,10},{14,12},{11,9},... | collective-permute-start | bytes 1032200 | tf_op jit(solution)/shard_map/ppermute | solution.py:21
  49.1 10.7 %collective-permute-start.5 = (f32[6,7,2,1024]{3,2,1,0:T(2,128)S(1)}, f32[6,7,2,1024]{3,2,1,0:T(2,128)S(1)}, u32[]{:S(2)}, u32[]{:S(2)}) collective-permute-start(f32[6,7,2,1024]{3,2,1,0:T(2,128)S(1)} %get-tuple-element.591), channel_id=1, source_target_pairs={{0,2},{2,4},{4,6},{1,3},{3,5},{5,7},{8,10},{10,12},{12,14},{9,11},... | collective-permute-start | bytes 1032200 | tf_op jit(solution)/shard_map/ppermute | solution.py:19
  58.6 9.8 %copy-start.5 = (f32[6,7,2,1024]{3,2,1,0:T(2,128)}, f32[6,7,2,1024]{3,2,1,0:T(2,128)S(1)}, u32[]{:S(2)}) copy-start(f32[6,7,2,1024]{3,2,1,0:T(2,128)S(1)} %collective-permute-done.4) | copy-start | bytes 1032196
  59.8 0.7 copy-start.6
  61.8 6.6 %collective-permute-start.6 = (f32[6,7,20,2]{3,2,1,0:T(8,128)}, f32[6,7,20,2]{3,2,1,0:T(8,128)}, u32[]{:S(2)}, u32[]{:S(2)}) collective-permute-start(f32[6,7,20,2]{3,2,1,0:T(8,128)} %get-tuple-element.589), channel_id=1, source_target_pairs={{1,0},{3,2},{5,4},{7,6},{9,8},{11,10},{13,12},{15,14},{17,16},{19,... | collective-permute-start | bytes 20168 | tf_op jit(solution)/shard_map/ppermute | solution.py:21
  63.1 5.7 %collective-permute-start.7 = (f32[6,7,20,2]{3,2,1,0:T(8,128)}, f32[6,7,20,2]{3,2,1,0:T(8,128)}, u32[]{:S(2)}, u32[]{:S(2)}) collective-permute-start(f32[6,7,20,2]{3,2,1,0:T(8,128)} %get-tuple-element.590), channel_id=1, source_target_pairs={{0,1},{2,3},{4,5},{6,7},{8,9},{10,11},{12,13},{14,15},{16,17},{18,... | collective-permute-start | bytes 20168 | tf_op jit(solution)/shard_map/ppermute | solution.py:19
  68.4 12.2 %copy-start = (bf16[2,7,7,16,1024]{4,3,2,1,0:T(8,128)(2,1)S(1)}, bf16[2,7,7,16,1024]{4,3,2,1,0:T(8,128)(2,1)}, u32[]{:S(2)}) copy-start(bf16[2,7,7,16,1024]{4,3,2,1,0:T(8,128)(2,1)} %param.17) | copy-start | bytes 9633796
  82.2 0.8 copy-start.1
  85.3 0.8 copy-start.1
  86.9 14.0 %collective-permute-start.1 = (f32[7,16,1024]{2,1,0:T(8,128)}, f32[7,16,1024]{2,1,0:T(8,128)}, u32[]{:S(2)}, u32[]{:S(2)}) collective-permute-start(f32[7,16,1024]{2,1,0:T(8,128)} %get-tuple-element.921), channel_id=1, source_target_pairs={{0,8},{8,16},{16,24},{1,9},{9,17},{17,25},{2,10},{10,18},{18,26},{... | collective-permute-start | bytes 1376264 | tf_op jit(solution)/shard_map/while/body/eval_jaxpr/ppermute | solution.py:31
  111.1 14.2 %collective-permute-start.1 = (f32[7,16,1024]{2,1,0:T(8,128)}, f32[7,16,1024]{2,1,0:T(8,128)}, u32[]{:S(2)}, u32[]{:S(2)}) collective-permute-start(f32[7,16,1024]{2,1,0:T(8,128)} %get-tuple-element.921), channel_id=1, source_target_pairs={{0,8},{8,16},{16,24},{1,9},{9,17},{17,25},{2,10},{10,18},{18,26},{... | collective-permute-start | bytes 1376264 | tf_op jit(solution)/shard_map/while/body/eval_jaxpr/ppermute | solution.py:31
  135.4 13.3 %collective-permute-start.1 = (f32[7,16,1024]{2,1,0:T(8,128)}, f32[7,16,1024]{2,1,0:T(8,128)}, u32[]{:S(2)}, u32[]{:S(2)}) collective-permute-start(f32[7,16,1024]{2,1,0:T(8,128)} %get-tuple-element.921), channel_id=1, source_target_pairs={{0,8},{8,16},{16,24},{1,9},{9,17},{17,25},{2,10},{10,18},{18,26},{... | collective-permute-start | bytes 1376264 | tf_op jit(solution)/shard_map/while/body/eval_jaxpr/ppermute | solution.py:31
  169.2 13.5 %collective-permute-start = (f32[7,16,1024]{2,1,0:T(8,128)}, f32[7,16,1024]{2,1,0:T(8,128)}, u32[]{:S(2)}, u32[]{:S(2)}) collective-permute-start(f32[7,16,1024]{2,1,0:T(8,128)} %get-tuple-element.973), channel_id=1, source_target_pairs={{8,0},{16,8},{24,16},{9,1},{17,9},{25,17},{10,2},{18,10},{26,18},{... | collective-permute-start | bytes 1376264 | tf_op jit(solution)/shard_map/while/body/eval_jaxpr/ppermute | solution.py:31
  195.8 13.6 %collective-permute-start = (f32[7,16,1024]{2,1,0:T(8,128)}, f32[7,16,1024]{2,1,0:T(8,128)}, u32[]{:S(2)}, u32[]{:S(2)}) collective-permute-start(f32[7,16,1024]{2,1,0:T(8,128)} %get-tuple-element.973), channel_id=1, source_target_pairs={{8,0},{16,8},{24,16},{9,1},{17,9},{25,17},{10,2},{18,10},{26,18},{... | collective-permute-start | bytes 1376264 | tf_op jit(solution)/shard_map/while/body/eval_jaxpr/ppermute | solution.py:31
  222.6 12.0 %collective-permute-start = (f32[7,16,1024]{2,1,0:T(8,128)}, f32[7,16,1024]{2,1,0:T(8,128)}, u32[]{:S(2)}, u32[]{:S(2)}) collective-permute-start(f32[7,16,1024]{2,1,0:T(8,128)} %get-tuple-element.973), channel_id=1, source_target_pairs={{8,0},{16,8},{24,16},{9,1},{17,9},{25,17},{10,2},{18,10},{26,18},{... | collective-permute-start | bytes 1376264 | tf_op jit(solution)/shard_map/while/body/eval_jaxpr/ppermute | solution.py:31
where the time goes:
time: 250 us; the launch traced here: 248 us
  waiting for transfers between devices  107 us (43%)
  other arithmetic  69.1 us (28%)
  starting transfers between devices  36.4 us (15%)
  local copies, waits for them, and re-layouts  34.8 us (14%)
    ppermute x6, waiting for transfers between devices, from_behind(): return lax.ppermute(value, axis, pairs)  62.1 us
    ppermute x3, waiting for transfers between devices, padded_2(): lax.ppermute(head, axis, [((i + 1) % count, i) for i in range(ends)])  24.8 us
    ppermute x3, waiting for transfers between devices, padded_2(): lax.ppermute(tail, axis, [(i, (i + 1) % count) for i in range(ends)])  20.1 us
    ppermute x6, starting transfers between devices, from_behind(): return lax.ppermute(value, axis, pairs)  18.4 us
    add x8, other arithmetic, backward_advance(): base_plane + apply_inverse(inverse_plane, relaxation_factor[None] * running)  14.9 us
    dynamic_update_slice x8, other arithmetic, forward_local(): lax.scan(forward_advance, entry_face, (inverse, residual, factors))  14.8 us
    ppermute x3, starting transfers between devices, padded_2(): lax.ppermute(tail, axis, [(i, (i + 1) % count) for i in range(ends)])  14.2 us
    dynamic_update_slice x8, local copies, waits for them, and re-layouts, forward_local(): lax.scan(forward_advance, entry_face, (inverse, residual, factors))  12.5 us
  transfers between devices with their start and end apart: 12, of which 11 were waited for; matrix products, arithmetic and copies ran while one was open for 1% of the time, Pallas kernels for 0%

commit v1 on v0

v1 whole, which is shorter than its diff:
```python
import functools

import jax
import jax.numpy as jnp
from jax import lax
from jax.experimental import pallas as pl
from jax.experimental.pallas import tpu as pltpu
from jax.sharding import PartitionSpec as P

advection = 0.012
viscosity = 0.006
damping = 0.003

CENTRE = -1.5 * advection - 6.0 * viscosity - 18.0 * damping
BEHIND_1 = 2.0 * advection + viscosity + 4.0 * damping
BEHIND_2 = -0.5 * advection - damping
NEAR = viscosity + 4.0 * damping
FAR = -damping

LANES = 128
TOP = 32767.0
VMEM = pltpu.VMEM
CHUNKS = 2


def scale_of(code):
    return jnp.exp2(code.astype(jnp.float32) * (1.0 / 256.0))


def put_coded(blocks, most, out_ref, rows):
    code = jnp.ceil(256.0 * jnp.log2(jnp.maximum(most, 1e-30))).astype(jnp.int32)
    factor = TOP / scale_of(code)
    for index, block in enumerate(blocks):
        coded = jnp.floor(block() * factor + 0.5)
        coded = jnp.minimum(jnp.maximum(coded, -TOP), TOP).astype(jnp.int32)
        out_ref[index * rows : (index + 1) * rows, :] = coded.astype(jnp.int16)
    count = len(blocks)
    out_ref[count * rows : (count + 1) * rows, :] = code.astype(jnp.int16)


def get_scale(coded_ref, count, rows):
    code = coded_ref[count * rows : (count + 1) * rows, :].astype(jnp.int32)
    return scale_of(code) * (1.0 / TOP)


def get_coded(coded_ref, index, rows, scale):
    return coded_ref[index * rows : (index + 1) * rows, :].astype(jnp.int32).astype(jnp.float32) * scale


def encode_kernel(state_ref, *out_refs):
    planes, nv, rows, columns = state_ref.shape
    width = columns // len(out_refs)
    for chunk, out_ref in enumerate(out_refs):
        places = [
            (p, v, chunk * width + b * LANES)
            for p in range(planes)
            for v in range(nv)
            for b in range(width // LANES)
        ]
        most = None
        for p, v, at in places:
            size = jnp.abs(state_ref[p, v, :, at : at + LANES])
            most = size if most is None else jnp.maximum(most, size)
        blocks = [
            (lambda p=p, v=v, at=at: state_ref[p, v, :, at : at + LANES]) for p, v, at in places
        ]
        put_coded(blocks, most, out_ref, rows)


def residual_kernel(
    chunk, chunks, count_k, state_ref, low_j, high_j, low_k, high_k, ahead, wall_ref, x_out, rows_pad
):
    planes, nv, rows, columns = state_ref.shape
    width = columns // chunks
    start = chunk * width
    stop = start + width
    per = width // LANES
    scale = get_scale(ahead, planes * nv * per, rows)
    place_k = lax.axis_index("ka")
    open_cells = [1.0 - wall_ref[p, :, start:stop].astype(jnp.float32) for p in range(planes)]

    def next_plane(p, v):
        parts = [get_coded(ahead, (p * nv + v) * per + b, rows, scale) for b in range(per)]
        return jnp.concatenate(parts, axis=1)

    for v in range(nv):
        here = [state_ref[p, v, :, start:stop] for p in range(planes)]
        after = [next_plane(p, v) for p in range(planes)]
        for p in range(planes):
            line = here + after
            total = CENTRE * here[p] + NEAR * line[p + 1] + FAR * line[p + 2]
            if p >= 1:
                total += BEHIND_1 * here[p - 1]
            if p >= 2:
                total += BEHIND_2 * here[p - 2]
            rows_pad[6:8, :] = low_j[p, v, :, start:stop]
            rows_pad[8 : 8 + rows, :] = here[p]
            rows_pad[8 + rows : 10 + rows, :] = high_j[p, v, :, start:stop]
            total += NEAR * (rows_pad[7 : 7 + rows, :] + rows_pad[9 : 9 + rows, :])
            total += FAR * (rows_pad[6 : 6 + rows, :] + rows_pad[10 : 10 + rows, :])
            if start == 0:
                left = jnp.where(place_k > 0, low_k[p, v], 0.0)
            else:
                left = state_ref[p, v, :, start - LANES : start]
            if stop == columns:
                right = jnp.where(place_k < count_k - 1, high_k[p, v], 0.0)
            else:
                right = state_ref[p, v, :, stop : stop + LANES]
            wide = jnp.concatenate([left, here[p], right], axis=1)
            span = wide.shape[1]
            one = pltpu.roll(wide, 1, 1) + pltpu.roll(wide, span - 1, 1)
            two = pltpu.roll(wide, 2, 1) + pltpu.roll(wide, span - 2, 1)
            total += (NEAR * one + FAR * two)[:, LANES : LANES + width]
            x_out[p, v] = open_cells[p] * total


def apply_block(inverse_ref, p, at, vector):
    result = []
    for a in range(len(vector)):
        total = None
        for b in range(len(vector)):
            term = inverse_ref[p, a, b, :, at : at + LANES].astype(jnp.float32) * vector[b]
            total = term if total is None else total + term
        result.append(total)
    return result


def forward_part(chunk, first, inverse_ref, coupling_ref, wall_ref, behind, face, x_in, x_out, send):
    planes, nv, rows, width = x_out.shape
    per = width // LANES
    if not first:
        face_scale = get_scale(face, nv * per, rows)
        behind_scale = get_scale(behind, planes * nv * per, rows)
    most = None
    for block in range(per):
        own = slice(block * LANES, (block + 1) * LANES)
        at = chunk * width + block * LANES
        running = None
        if not first:
            running = [get_coded(face, v * per + block, rows, face_scale) for v in range(nv)]

            def old(p, v):
                return get_coded(behind, (p * nv + v) * per + block, rows, behind_scale)

        for p in range(planes):
            factor = coupling_ref[p, 0, :, at : at + LANES]
            if not first and p < 2:
                open_cells = 1.0 - wall_ref[p, :, at : at + LANES].astype(jnp.float32)
            right = []
            for v in range(nv):
                entry = x_in[p, v, :, own]
                if running is not None:
                    entry = entry + factor * running[v]
                if not first and p == 0:
                    entry += open_cells * (BEHIND_1 * old(planes - 1, v) + BEHIND_2 * old(planes - 2, v))
                if not first and p == 1:
                    entry += open_cells * (BEHIND_2 * old(planes - 1, v))
                right.append(entry)
            running = apply_block(inverse_ref, p, at, right)
            for v in range(nv):
                x_out[p, v, :, own] = running[v]
        for v in range(nv):
            size = jnp.abs(running[v])
            most = size if most is None else jnp.maximum(most, size)
    if send is not None:
        put_face(planes - 1, most, x_out, send)


def put_face(plane, most, x_out, send):
    nv, rows, width = x_out.shape[1:]
    blocks = [
        (lambda v=v, at=b * LANES: x_out[plane, v, :, at : at + LANES])
        for v in range(nv)
        for b in range(width // LANES)
    ]
    put_coded(blocks, most, send, rows)


def backward_part(chunk, last, inverse_ref, coupling_ref, face, x_in, x_out, send):
    planes, nv, rows, width = x_out.shape
    per = width // LANES
    if not last:
        scale = get_scale(face, nv * per, rows)
    most = None
    for block in range(per):
        own = slice(block * LANES, (block + 1) * LANES)
        at = chunk * width + block * LANES
        running = None
        if not last:
            running = [get_coded(face, v * per + block, rows, scale) for v in range(nv)]
        for p in reversed(range(planes)):
            base = [x_in[p, v, :, own] for v in range(nv)]
            if running is None:
                running = base
            else:
                factor = coupling_ref[p, 1, :, at : at + LANES]
                change = apply_block(inverse_ref, p, at, [factor * running[v] for v in range(nv)])
                running = [base[v] + change[v] for v in range(nv)]
            for v in range(nv):
                x_out[p, v, :, own] = running[v]
        for v in range(nv):
            size = jnp.abs(running[v])
            most = size if most is None else jnp.maximum(most, size)
    if send is not None:
        put_face(0, most, x_out, send)


def forward_kernel(chunk, hop, count, inverse_ref, coupling_ref, wall_ref, behind, face, x_in, x_out, send):
    active = lax.axis_index("ia") == hop
    last = hop == count - 1

    @pl.when(active)
    def _():
        forward_part(
            chunk, hop == 0, inverse_ref, coupling_ref, wall_ref, behind, face, x_in, x_out,
            None if last else send,
        )
        if last:
            backward_part(chunk, True, inverse_ref, coupling_ref, None, x_out, x_out, send)

    @pl.when(jnp.logical_not(active))
    def _():
        x_out[...] = x_in[...]


def backward_kernel(chunk, hop, inverse_ref, coupling_ref, face, x_in, x_out, send):
    active = lax.axis_index("ia") == hop

    @pl.when(active)
    def _():
        backward_part(chunk, False, inverse_ref, coupling_ref, face, x_in, x_out, send)

    @pl.when(jnp.logical_not(active))
    def _():
        x_out[...] = x_in[...]


def final_kernel(chunk, inverse_ref, coupling_ref, face, *refs):
    parts, out = refs[:-1], refs[-1]
    width = parts[0].shape[3]
    mine = out.at[:, :, :, chunk * width : (chunk + 1) * width]
    active = lax.axis_index("ia") == 0

    @pl.when(active)
    def _():
        backward_part(chunk, False, inverse_ref, coupling_ref, face, parts[chunk], mine, None)

    @pl.when(jnp.logical_not(active))
    def _():
        mine[...] = parts[chunk][...]

    for other, part in enumerate(parts):
        if other != chunk:
            out[:, :, :, other * width : (other + 1) * width] = part[...]


def whole():
    return pl.BlockSpec(memory_space=VMEM)


def call(kernel, operands, outs, name, alias=None, scratch=()):
    return pl.pallas_call(
        kernel,
        in_specs=[whole()] * len(operands),
        out_specs=[whole()] * len(outs),
        out_shape=outs,
        scratch_shapes=list(scratch),
        input_output_aliases=alias or {},
        compiler_params=pltpu.CompilerParams(vmem_limit_bytes=24 * 2**20),
        name=name,
    )(*operands)


def shards(state, inverse, coupling, wall):
    planes, nv, rows, columns = state.shape
    chunks = CHUNKS
    width = columns // chunks
    per = width // LANES
    count = lax.axis_size("ia")
    count_j = lax.axis_size("ja")
    count_k = lax.axis_size("ka")
    up = lambda n: [(i, i + 1) for i in range(n - 1)]
    down = lambda n: [(i + 1, i) for i in range(n - 1)]

    halo_code = jax.ShapeDtypeStruct(((planes * nv * per + 1) * rows, LANES), jnp.int16)
    face_code = jax.ShapeDtypeStruct(((nv * per + 1) * rows, LANES), jnp.int16)
    full = jax.ShapeDtypeStruct(state.shape, jnp.float32)
    part = jax.ShapeDtypeStruct((planes, nv, rows, width), jnp.float32)

    coded = call(encode_kernel, [state], [halo_code] * chunks, "encode")
    ahead = [lax.ppermute(coded[c], "ia", down(count)) for c in range(chunks)]

    head_k = state[:, :, :, :LANES]
    tail_k = state[:, :, :, columns - LANES :]
    if count_k == 2:
        mine = jnp.where(lax.axis_index("ka") == 0, tail_k, head_k)
        low_k = lax.ppermute(mine, "ka", [(0, 1), (1, 0)])
        high_k = low_k
    else:
        low_k = lax.ppermute(tail_k, "ka", up(count_k))
        high_k = lax.ppermute(head_k, "ka", down(count_k))
    low_j = lax.ppermute(state[:, :, rows - 2 :, :], "ja", up(count_j))
    high_j = lax.ppermute(state[:, :, :2, :], "ja", down(count_j))
    behind = [lax.ppermute(coded[c], "ia", up(count)) for c in range(chunks)]

    x = []
    for c in range(chunks):
        kernel = functools.partial(residual_kernel, c, chunks, count_k)
        operands = [state, low_j, high_j, low_k, high_k, ahead[c], wall]
        x += call(kernel, operands, [part], "residual", None, [VMEM((rows + 16, width), jnp.float32)])

    face = [None] * chunks
    for hop in range(count):
        for c in range(chunks):
            if hop == 0:
                def kernel(inverse_ref, coupling_ref, wall_ref, *refs, c=c):
                    forward_kernel(c, 0, count, inverse_ref, coupling_ref, wall_ref, None, None, *refs)
                operands = [inverse, coupling, wall, x[c]]
            else:
                kernel = functools.partial(forward_kernel, c, hop, count)
                operands = [inverse, coupling, wall, behind[c], face[c], x[c]]
            x[c], send = call(kernel, operands, [part, face_code], "forward", {len(operands) - 1: 0})
            pair = (hop, hop + 1) if hop < count - 1 else (hop, hop - 1)
            face[c] = lax.ppermute(send, "ia", [pair])
    for hop in reversed(range(count - 1)):
        for c in range(chunks):
            if hop == 0 and c == chunks - 1:
                operands = [inverse, coupling, face[c], *x]
                return call(functools.partial(final_kernel, c), operands, [full], "last")[0]
            if hop == 0:
                def kernel(*refs, c=c):
                    backward_kernel(c, 0, *refs, None)
                (x[c],) = call(kernel, [inverse, coupling, face[c], x[c]], [part], "backward", {3: 0})
                continue
            kernel = functools.partial(backward_kernel, c, hop)
            x[c], send = call(kernel, [inverse, coupling, face[c], x[c]], [part, face_code], "backward", {3: 0})
            face[c] = lax.ppermute(send, "ia", [(hop, hop - 1)])


def solution(mesh):
    return jax.shard_map(
        shards,
        mesh=mesh,
        in_specs=(
            P("ia", None, "ja", "ka"),
            P("ia", None, None, "ja", "ka"),
            P("ia", None, "ja", "ka"),
            P("ia", "ja", "ka"),
        ),
        out_specs=P("ia", None, "ja", "ka"),
        check_vma=False,
    )
```

time: 250 us -> 68.7 us (0.27)
  waiting for transfers between devices: 107 us -> 25.6 us
  other arithmetic: 69.1 us -> 1.12 us
  local copies, waits for them, and re-layouts: 34.8 us -> 3.35 us
  Pallas kernels: 0 us -> 5.52 us
  starting transfers between devices: 36.4 us -> 32.2 us
    ppermute x12 -> x19, waiting for transfers between devices: 107 us -> 25.6 us  [the longest x4 23.9 us: shards(): face[c] = lax.ppermute(send, 'ia', [(hop, hop - 1)])]
    add x16 -> x0, other arithmetic: 24.6 us -> none  [the longest x8 14.9 us: backward_advance(): base_plane + apply_inverse(inverse_plane, relaxation_factor[None] * running)]
    mul x9 -> x0, other arithmetic: 17.4 us -> none  [the longest x1 9.97 us: stencil(): return open_cells * (convect + viscosity * laplace - damping * fourth)]
    dynamic_update_slice x8 -> x0, other arithmetic: 14.8 us -> none  [forward_local(): lax.scan(forward_advance, entry_face, (inverse, residual, factors))]
    dynamic_update_slice x8 -> x0, local copies, waits for them, and re-layouts: 12.5 us -> none  [forward_local(): lax.scan(forward_advance, entry_face, (inverse, residual, factors))]
    while x10 -> x0, local copies, waits for them, and re-layouts: 12.5 us -> none
    reduce_sum x16 -> x0, other arithmetic: 10.3 us -> none  [apply_inverse(): return jnp.sum(inverse_plane.astype(jnp.float32) * vector[None], axis=1)]
    pallas_call x0 -> x17, Pallas kernels: none -> 5.52 us  [call(): pl.pallas_call(kernel, in_specs=[whole()] * len(operands), out_specs=[who...]
  transfers between devices with their start and end apart: 12 -> 19, of which waited for: 11 -> 4; matrix products, arithmetic and copies ran while one was open for 1% -> 0% of each run, Pallas kernels for 0% -> 6%
where the time goes in v1:
time: 68.7 us; the launch traced here: 68.2 us
  starting transfers between devices  32.2 us (47%)
  waiting for transfers between devices  25.6 us (37%)
  Pallas kernels  5.52 us (8%)
  local copies, waits for them, and re-layouts  3.35 us (5%)
  other arithmetic  1.12 us (2%)
    ppermute x4, waiting for transfers between devices, shards(): face[c] = lax.ppermute(send, 'ia', [(hop, hop - 1)])  23.9 us
    ppermute x2, starting transfers between devices, shards(): behind = [lax.ppermute(coded[c], 'ia', up(count)) for c in range(chunks)]  10 us
    ppermute x8, starting transfers between devices, shards(): face[c] = lax.ppermute(send, 'ia', [pair])  8.71 us
    pallas_call x17, Pallas kernels, call(): pl.pallas_call(kernel, in_specs=[whole()] * len(operands), out_specs=[who...  5.52 us
    ppermute x1, starting transfers between devices, shards(): low_j = lax.ppermute(state[:, :, rows - 2:, :], 'ja', up(count_j))  5.13 us
    ppermute x4, starting transfers between devices, shards(): face[c] = lax.ppermute(send, 'ia', [(hop, hop - 1)])  3.92 us
    unnamed x12, local copies, waits for them, and re-layouts  3.27 us
    ppermute x2, starting transfers between devices, shards(): ahead = [lax.ppermute(coded[c], 'ia', down(count)) for c in range(chunks)]  2.58 us
  transfers between devices with their start and end apart: 19, of which 4 were waited for; matrix products, arithmetic and copies ran while one was open for 0% of the time, Pallas kernels for 6%

profile of v1, /device:TPU:0, one launch (start us, length us, event | category | flops | bytes accessed | tf_op | source)
XLA Modules:
  0.0 68.2 jit_solution(14206029290619435949)
XLA Ops:
  0.0 1.1 %slice_select_fusion = f32[2,7,16,128]{3,2,1,0:T(8,128)S(1)} fusion(f32[2,7,16,1024]{3,2,1,0:T(8,128)} %state_ref.5, pred[]{:T(512)S(6)} %eq.3), kind=kLoop, calls=%fused_computation | loop fusion | flops 28672 | bytes 344065 | tf_op jit(solution)/shard_map/jit(_where)/select_n | solution.py:296
  1.1 0.5 collective-permute-start.3
  1.6 1.2 %copy-done.4 = f32[2,7,16,1024]{3,2,1,0:T(8,128)S(1)} copy-done((f32[2,7,16,1024]{3,2,1,0:T(8,128)S(1)}, f32[2,7,16,1024]{3,2,1,0:T(8,128)}, u32[]{:S(2)}) %copy-start.4) | copy-done | bytes 917528
  2.8 0.3 encode.1
  3.1 1.3 %collective-permute-start.4 = (s16[912,128]{1,0:T(8,128)(2,1)S(1)}, s16[912,128]{1,0:T(8,128)(2,1)S(1)}, u32[]{:S(2)}, u32[]{:S(2)}) collective-permute-start(s16[912,128]{1,0:T(8,128)(2,1)S(1)} %get-tuple-element.31), channel_id=1, source_target_pairs={{8,0},{16,8},{24,16},{9,1},{17,9},{25,17},{10,2},{18,10},{26,18},{... | collective-permute-start | bytes 700424 | tf_op jit(solution)/shard_map/ppermute | solution.py:291
  4.4 1.3 %collective-permute-start.12 = (s16[912,128]{1,0:T(8,128)(2,1)S(1)}, s16[912,128]{1,0:T(8,128)(2,1)S(1)}, u32[]{:S(2)}, u32[]{:S(2)}) collective-permute-start(s16[912,128]{1,0:T(8,128)(2,1)S(1)} %get-tuple-element.43), channel_id=1, source_target_pairs={{8,0},{16,8},{24,16},{9,1},{17,9},{25,17},{10,2},{18,10},{26,18},{... | collective-permute-start | bytes 700424 | tf_op jit(solution)/shard_map/ppermute | solution.py:291
  5.7 0.1 fusion
  5.8 1.3 %collective-permute-start.2 = (f32[2,7,2,1024]{3,2,1,0:T(2,128)S(1)}, f32[2,7,2,1024]{3,2,1,0:T(2,128)S(1)}, u32[]{:S(2)}, u32[]{:S(2)}) collective-permute-start(f32[2,7,2,1024]{3,2,1,0:T(2,128)S(1)} %get-tuple-element.57), channel_id=1, source_target_pairs={{2,0},{4,2},{6,4},{3,1},{5,3},{7,5},{10,8},{12,10},{14,12},{11,9},... | collective-permute-start | bytes 344072 | tf_op jit(solution)/shard_map/ppermute | solution.py:303
  7.1 5.1 %collective-permute-start.1 = (f32[2,7,2,1024]{3,2,1,0:T(2,128)S(1)}, f32[2,7,2,1024]{3,2,1,0:T(2,128)S(1)}, u32[]{:S(2)}, u32[]{:S(2)}) collective-permute-start(f32[2,7,2,1024]{3,2,1,0:T(2,128)S(1)} %get-tuple-element.58), channel_id=1, source_target_pairs={{0,2},{2,4},{4,6},{1,3},{3,5},{5,7},{8,10},{10,12},{12,14},{9,11},... | collective-permute-start | bytes 344072 | tf_op jit(solution)/shard_map/ppermute | solution.py:302
  12.3 0.0 collective-permute-done.3.low_k.high_k
  12.3 5.2 %collective-permute-start.11 = (s16[912,128]{1,0:T(8,128)(2,1)S(1)}, s16[912,128]{1,0:T(8,128)(2,1)S(1)}, u32[]{:S(2)}, u32[]{:S(2)}) collective-permute-start(s16[912,128]{1,0:T(8,128)(2,1)S(1)} %get-tuple-element.43), channel_id=1, source_target_pairs={{0,8},{8,16},{16,24},{1,9},{9,17},{17,25},{2,10},{10,18},{18,26},{... | collective-permute-start | bytes 700424 | tf_op jit(solution)/shard_map/ppermute | solution.py:304
  17.5 4.8 %collective-permute-start = (s16[912,128]{1,0:T(8,128)(2,1)S(1)}, s16[912,128]{1,0:T(8,128)(2,1)S(1)}, u32[]{:S(2)}, u32[]{:S(2)}) collective-permute-start(s16[912,128]{1,0:T(8,128)(2,1)S(1)} %get-tuple-element.31), channel_id=1, source_target_pairs={{0,8},{8,16},{16,24},{1,9},{9,17},{17,25},{2,10},{10,18},{18,26},{... | collective-permute-start | bytes 700424 | tf_op jit(solution)/shard_map/ppermute | solution.py:304
  22.3 0.0 copy-start.2
  22.3 0.9 %copy-done.2 = s32[2,16,1024]{2,1,0:T(8,128)S(1)} copy-done((s32[2,16,1024]{2,1,0:T(8,128)S(1)}, s32[2,16,1024]{2,1,0:T(8,128)}, u32[]{:S(2)}) %copy-start.2) | copy-done | bytes 131096
  23.2 1.2 %copy-done.5 = f32[2,7,16,1024]{3,2,1,0:T(8,128)S(1)} copy-done((f32[2,7,16,1024]{3,2,1,0:T(8,128)S(1)}, f32[2,7,16,1024]{3,2,1,0:T(8,128)}, u32[]{:S(2)}) %copy-start.5) | copy-done | bytes 917528
  24.4 0.8 %residual.3.refs_0_ = f32[2,7,16,512]{3,2,1,0:T(8,128)S(1)} custom-call(f32[2,7,16,1024]{3,2,1,0:T(8,128)S(1)} %copy-done.5, f32[2,7,2,1024]{3,2,1,0:T(2,128)S(1)} %collective-permute-done.1.low_j, f32[2,7,2,1024]{3,2,1,0:T(2,128)S(1)} %collective-permute-done.2.high_j, f32[2,7,16,128]{3,2,1,0:T(8,128)S(1)} %collective-permute-done.3.low_k.high_k, ...), custom_call_target="tpu_custom_call" | custom-call | tf_op jit(solution)/shard_map/residual/pallas_call | solution.py:262
  25.2 0.5 forward.12
  25.7 3.4 %collective-permute-start.13 = (s16[464,128]{1,0:T(8,128)(2,1)S(1)}, s16[464,128]{1,0:T(8,128)(2,1)S(1)}, u32[]{:S(2)}, u32[]{:S(2)}) collective-permute-start(s16[464,128]{1,0:T(8,128)(2,1)S(1)} %get-tuple-element.44), channel_id=1, source_target_pairs={{0,8},{1,9},{2,10},{3,11},{4,12},{5,13},{6,14},{7,15}} | collective-permute-start | bytes 356360 | tf_op jit(solution)/shard_map/ppermute | solution.py:324
  29.1 0.0 collective-permute-done.4.ahead
  29.2 0.7 %residual.2.refs_0_ = f32[2,7,16,512]{3,2,1,0:T(8,128)S(1)} custom-call(f32[2,7,16,1024]{3,2,1,0:T(8,128)S(1)} %copy-done.5, f32[2,7,2,1024]{3,2,1,0:T(2,128)S(1)} %collective-permute-done.1.low_j, f32[2,7,2,1024]{3,2,1,0:T(2,128)S(1)} %collective-permute-done.2.high_j, f32[2,7,16,128]{3,2,1,0:T(8,128)S(1)} %collective-permute-done.3.low_k.high_k, ...), custom_call_target="tpu_custom_call" | custom-call | tf_op jit(solution)/shard_map/residual/pallas_call | solution.py:262
  29.9 0.5 forward.8
  30.4 1.3 %collective-permute-start.5 = (s16[464,128]{1,0:T(8,128)(2,1)S(1)}, s16[464,128]{1,0:T(8,128)(2,1)S(1)}, u32[]{:S(2)}, u32[]{:S(2)}) collective-permute-start(s16[464,128]{1,0:T(8,128)(2,1)S(1)} %get-tuple-element.32), channel_id=1, source_target_pairs={{0,8},{1,9},{2,10},{3,11},{4,12},{5,13},{6,14},{7,15}} | collective-permute-start | bytes 356360 | tf_op jit(solution)/shard_map/ppermute | solution.py:324
  31.7 0.7 collective-permute-done.13.face
  32.4 0.1 forward.13
  32.5 0.7 collective-permute-start.14
  33.1 1.0 %collective-permute-done.5.face = s16[464,128]{1,0:T(8,128)(2,1)S(1)} collective-permute-done((s16[464,128]{1,0:T(8,128)(2,1)S(1)}, s16[464,128]{1,0:T(8,128)(2,1)S(1)}, u32[]{:S(2)}, u32[]{:S(2)}) %collective-permute-start.5) | collective-permute-done | bytes 118816 | tf_op jit(solution)/shard_map/ppermute | solution.py:324
  34.1 0.1 forward.9
  34.2 0.7 collective-permute-start.6
  34.9 0.1 forward.14
  34.9 0.7 collective-permute-start.15
  35.6 0.1 forward.10
  35.7 0.7 collective-permute-start.7
  36.4 0.1 forward.15
  36.5 0.7 collective-permute-start.16
  37.2 0.1 forward.11
  37.3 0.7 collective-permute-start.8
  37.9 0.1 backward.7
  38.0 0.7 collective-permute-start.17
  38.7 0.1 backward.5
  38.8 0.7 collective-permute-start.9
  39.5 0.1 backward.8
  39.6 1.3 %collective-permute-start.18 = (s16[464,128]{1,0:T(8,128)(2,1)S(1)}, s16[464,128]{1,0:T(8,128)(2,1)S(1)}, u32[]{:S(2)}, u32[]{:S(2)}) collective-permute-start(s16[464,128]{1,0:T(8,128)(2,1)S(1)} %get-tuple-element.54), channel_id=1, source_target_pairs={{8,0},{9,1},{10,2},{11,3},{12,4},{13,5},{14,6},{15,7}} | collective-permute-start | bytes 356360 | tf_op jit(solution)/shard_map/ppermute | solution.py:337
  40.9 0.1 backward.6
  41.0 1.3 %collective-permute-start.10 = (s16[464,128]{1,0:T(8,128)(2,1)S(1)}, s16[464,128]{1,0:T(8,128)(2,1)S(1)}, u32[]{:S(2)}, u32[]{:S(2)}) collective-permute-start(s16[464,128]{1,0:T(8,128)(2,1)S(1)} %get-tuple-element.42), channel_id=1, source_target_pairs={{8,0},{9,1},{10,2},{11,3},{12,4},{13,5},{14,6},{15,7}} | collective-permute-start | bytes 356360 | tf_op jit(solution)/shard_map/ppermute | solution.py:337
  42.3 22.3 %collective-permute-done.18.refs_2_ = s16[464,128]{1,0:T(8,128)(2,1)S(1)} collective-permute-done((s16[464,128]{1,0:T(8,128)(2,1)S(1)}, s16[464,128]{1,0:T(8,128)(2,1)S(1)}, u32[]{:S(2)}, u32[]{:S(2)}) %collective-permute-start.18) | collective-permute-done | bytes 118816 | tf_op jit(solution)/shard_map/ppermute | solution.py:337
  64.6 0.6 backward.9.refs_0_
  65.1 1.6 %collective-permute-done.10.face = s16[464,128]{1,0:T(8,128)(2,1)S(1)} collective-permute-done((s16[464,128]{1,0:T(8,128)(2,1)S(1)}, s16[464,128]{1,0:T(8,128)(2,1)S(1)}, u32[]{:S(2)}, u32[]{:S(2)}) %collective-permute-start.10) | collective-permute-done | bytes 118816 | tf_op jit(solution)/shard_map/ppermute | solution.py:337
  66.8 1.4 %last.1 = f32[2,7,16,1024]{3,2,1,0:T(8,128)} custom-call(bf16[2,7,7,16,1024]{4,3,2,1,0:T(8,128)(2,1)S(1)} %copy-done, f32[2,2,16,1024]{3,2,1,0:T(8,128)S(1)} %copy-done.1, s16[464,128]{1,0:T(8,128)(2,1)S(1)} %collective-permute-done.10.face, f32[2,7,16,512]{3,2,1,0:T(8,128)S(1)} %backward.9.refs_0_, f32[2,7,16,512]{3,2,1,0:T(8,128)S(1)} %get-tuple-element.56.refs_1_), custom_call_target="tpu_custom_call" | custom-call | tf_op jit(solution)/shard_map/last/pallas_call | solution.py:262
  (21 shorter events, 0.0 us)
Async XLA Ops:
  0.0 25.2 %copy-start.1 = (f32[2,2,16,1024]{3,2,1,0:T(8,128)S(1)}, f32[2,2,16,1024]{3,2,1,0:T(8,128)}, u32[]{:S(2)}) copy-start(f32[2,2,16,1024]{3,2,1,0:T(8,128)} %coupling_ref.25) | copy-start | bytes 786436
  0.0 25.2 %copy-start = (bf16[2,7,7,16,1024]{4,3,2,1,0:T(8,128)(2,1)S(1)}, bf16[2,7,7,16,1024]{4,3,2,1,0:T(8,128)(2,1)}, u32[]{:S(2)}) copy-start(bf16[2,7,7,16,1024]{4,3,2,1,0:T(8,128)(2,1)} %inverse_ref.25) | copy-start | bytes 9633796
  1.1 11.1 %collective-permute-start.3 = (f32[2,7,16,128]{3,2,1,0:T(8,128)S(1)}, f32[2,7,16,128]{3,2,1,0:T(8,128)S(1)}, u32[]{:S(2)}, u32[]{:S(2)}) collective-permute-start(f32[2,7,16,128]{3,2,1,0:T(8,128)S(1)} %slice_select_fusion), channel_id=1, source_target_pairs={{0,1},{1,0},{2,3},{3,2},{4,5},{5,4},{6,7},{7,6},{8,9},{9,8},{10,11... | collective-permute-start | bytes 344072 | tf_op jit(solution)/shard_map/ppermute | solution.py:297
  1.6 1.2 %copy-start.4 = (f32[2,7,16,1024]{3,2,1,0:T(8,128)S(1)}, f32[2,7,16,1024]{3,2,1,0:T(8,128)}, u32[]{:S(2)}) copy-start(f32[2,7,16,1024]{3,2,1,0:T(8,128)} %state_ref.5) | copy-start | bytes 2752516
  3.1 26.0 %collective-permute-start.4 = (s16[912,128]{1,0:T(8,128)(2,1)S(1)}, s16[912,128]{1,0:T(8,128)(2,1)S(1)}, u32[]{:S(2)}, u32[]{:S(2)}) collective-permute-start(s16[912,128]{1,0:T(8,128)(2,1)S(1)} %get-tuple-element.31), channel_id=1, source_target_pairs={{8,0},{16,8},{24,16},{9,1},{17,9},{25,17},{10,2},{18,10},{26,18},{... | collective-permute-start | bytes 700424 | tf_op jit(solution)/shard_map/ppermute | solution.py:291
  4.4 17.9 %collective-permute-start.12 = (s16[912,128]{1,0:T(8,128)(2,1)S(1)}, s16[912,128]{1,0:T(8,128)(2,1)S(1)}, u32[]{:S(2)}, u32[]{:S(2)}) collective-permute-start(s16[912,128]{1,0:T(8,128)(2,1)S(1)} %get-tuple-element.43), channel_id=1, source_target_pairs={{8,0},{16,8},{24,16},{9,1},{17,9},{25,17},{10,2},{18,10},{26,18},{... | collective-permute-start | bytes 700424 | tf_op jit(solution)/shard_map/ppermute | solution.py:291
  5.8 11.6 %collective-permute-start.2 = (f32[2,7,2,1024]{3,2,1,0:T(2,128)S(1)}, f32[2,7,2,1024]{3,2,1,0:T(2,128)S(1)}, u32[]{:S(2)}, u32[]{:S(2)}) collective-permute-start(f32[2,7,2,1024]{3,2,1,0:T(2,128)S(1)} %get-tuple-element.57), channel_id=1, source_target_pairs={{2,0},{4,2},{6,4},{3,1},{5,3},{7,5},{10,8},{12,10},{14,12},{11,9},... | collective-permute-start | bytes 344072 | tf_op jit(solution)/shard_map/ppermute | solution.py:303
  7.1 15.2 %collective-permute-start.1 = (f32[2,7,2,1024]{3,2,1,0:T(2,128)S(1)}, f32[2,7,2,1024]{3,2,1,0:T(2,128)S(1)}, u32[]{:S(2)}, u32[]{:S(2)}) collective-permute-start(f32[2,7,2,1024]{3,2,1,0:T(2,128)S(1)} %get-tuple-element.58), channel_id=1, source_target_pairs={{0,2},{2,4},{4,6},{1,3},{3,5},{5,7},{8,10},{10,12},{12,14},{9,11},... | collective-permute-start | bytes 344072 | tf_op jit(solution)/shard_map/ppermute | solution.py:302
  12.3 19.5 %collective-permute-start.11 = (s16[912,128]{1,0:T(8,128)(2,1)S(1)}, s16[912,128]{1,0:T(8,128)(2,1)S(1)}, u32[]{:S(2)}, u32[]{:S(2)}) collective-permute-start(s16[912,128]{1,0:T(8,128)(2,1)S(1)} %get-tuple-element.43), channel_id=1, source_target_pairs={{0,8},{8,16},{16,24},{1,9},{9,17},{17,25},{2,10},{10,18},{18,26},{... | collective-permute-start | bytes 700424 | tf_op jit(solution)/shard_map/ppermute | solution.py:304
  17.5 15.7 %collective-permute-start = (s16[912,128]{1,0:T(8,128)(2,1)S(1)}, s16[912,128]{1,0:T(8,128)(2,1)S(1)}, u32[]{:S(2)}, u32[]{:S(2)}) collective-permute-start(s16[912,128]{1,0:T(8,128)(2,1)S(1)} %get-tuple-element.31), channel_id=1, source_target_pairs={{0,8},{8,16},{16,24},{1,9},{9,17},{17,25},{2,10},{10,18},{18,26},{... | collective-permute-start | bytes 700424 | tf_op jit(solution)/shard_map/ppermute | solution.py:304
  22.3 0.9 %copy-start.2 = (s32[2,16,1024]{2,1,0:T(8,128)S(1)}, s32[2,16,1024]{2,1,0:T(8,128)}, u32[]{:S(2)}) copy-start(s32[2,16,1024]{2,1,0:T(8,128)} %wall_ref.19) | copy-start | bytes 393220
  23.2 1.2 %copy-start.5 = (f32[2,7,16,1024]{3,2,1,0:T(8,128)S(1)}, f32[2,7,16,1024]{3,2,1,0:T(8,128)}, u32[]{:S(2)}) copy-start(f32[2,7,16,1024]{3,2,1,0:T(8,128)} %state_ref.5) | copy-start | bytes 2752516
  24.4 4.7 %copy-start.3 = (s32[2,16,1024]{2,1,0:T(8,128)S(1)}, s32[2,16,1024]{2,1,0:T(8,128)}, u32[]{:S(2)}) copy-start(s32[2,16,1024]{2,1,0:T(8,128)} %wall_ref.19) | copy-start | bytes 393220
  25.7 6.7 %collective-permute-start.13 = (s16[464,128]{1,0:T(8,128)(2,1)S(1)}, s16[464,128]{1,0:T(8,128)(2,1)S(1)}, u32[]{:S(2)}, u32[]{:S(2)}) collective-permute-start(s16[464,128]{1,0:T(8,128)(2,1)S(1)} %get-tuple-element.44), channel_id=1, source_target_pairs={{0,8},{1,9},{2,10},{3,11},{4,12},{5,13},{6,14},{7,15}} | collective-permute-start | bytes 356360 | tf_op jit(solution)/shard_map/ppermute | solution.py:324
  30.4 3.7 %collective-permute-start.5 = (s16[464,128]{1,0:T(8,128)(2,1)S(1)}, s16[464,128]{1,0:T(8,128)(2,1)S(1)}, u32[]{:S(2)}, u32[]{:S(2)}) collective-permute-start(s16[464,128]{1,0:T(8,128)(2,1)S(1)} %get-tuple-element.32), channel_id=1, source_target_pairs={{0,8},{1,9},{2,10},{3,11},{4,12},{5,13},{6,14},{7,15}} | collective-permute-start | bytes 356360 | tf_op jit(solution)/shard_map/ppermute | solution.py:324
  32.5 2.4 %collective-permute-start.14 = (s16[464,128]{1,0:T(8,128)(2,1)S(1)}, s16[464,128]{1,0:T(8,128)(2,1)S(1)}, u32[]{:S(2)}, u32[]{:S(2)}) collective-permute-start(s16[464,128]{1,0:T(8,128)(2,1)S(1)} %get-tuple-element.46), channel_id=1, source_target_pairs={{8,16},{9,17},{10,18},{11,19},{12,20},{13,21},{14,22},{15,23}} | collective-permute-start | bytes 356360 | tf_op jit(solution)/shard_map/ppermute | solution.py:324
  34.2 1.5 %collective-permute-start.6 = (s16[464,128]{1,0:T(8,128)(2,1)S(1)}, s16[464,128]{1,0:T(8,128)(2,1)S(1)}, u32[]{:S(2)}, u32[]{:S(2)}) collective-permute-start(s16[464,128]{1,0:T(8,128)(2,1)S(1)} %get-tuple-element.34), channel_id=1, source_target_pairs={{8,16},{9,17},{10,18},{11,19},{12,20},{13,21},{14,22},{15,23}} | collective-permute-start | bytes 356360 | tf_op jit(solution)/shard_map/ppermute | solution.py:324
  34.9 1.5 %collective-permute-start.15 = (s16[464,128]{1,0:T(8,128)(2,1)S(1)}, s16[464,128]{1,0:T(8,128)(2,1)S(1)}, u32[]{:S(2)}, u32[]{:S(2)}) collective-permute-start(s16[464,128]{1,0:T(8,128)(2,1)S(1)} %get-tuple-element.48), channel_id=1, source_target_pairs={{16,24},{17,25},{18,26},{19,27},{20,28},{21,29},{22,30},{23,31}} | collective-permute-start | bytes 356360 | tf_op jit(solution)/shard_map/ppermute | solution.py:324
  35.7 1.5 %collective-permute-start.7 = (s16[464,128]{1,0:T(8,128)(2,1)S(1)}, s16[464,128]{1,0:T(8,128)(2,1)S(1)}, u32[]{:S(2)}, u32[]{:S(2)}) collective-permute-start(s16[464,128]{1,0:T(8,128)(2,1)S(1)} %get-tuple-element.36), channel_id=1, source_target_pairs={{16,24},{17,25},{18,26},{19,27},{20,28},{21,29},{22,30},{23,31}} | collective-permute-start | bytes 356360 | tf_op jit(solution)/shard_map/ppermute | solution.py:324
  36.5 1.5 %collective-permute-start.16 = (s16[464,128]{1,0:T(8,128)(2,1)S(1)}, s16[464,128]{1,0:T(8,128)(2,1)S(1)}, u32[]{:S(2)}, u32[]{:S(2)}) collective-permute-start(s16[464,128]{1,0:T(8,128)(2,1)S(1)} %get-tuple-element.50), channel_id=1, source_target_pairs={{24,16},{25,17},{26,18},{27,19},{28,20},{29,21},{30,22},{31,23}} | collective-permute-start | bytes 356360 | tf_op jit(solution)/shard_map/ppermute | solution.py:324
  37.3 1.5 %collective-permute-start.8 = (s16[464,128]{1,0:T(8,128)(2,1)S(1)}, s16[464,128]{1,0:T(8,128)(2,1)S(1)}, u32[]{:S(2)}, u32[]{:S(2)}) collective-permute-start(s16[464,128]{1,0:T(8,128)(2,1)S(1)} %get-tuple-element.38), channel_id=1, source_target_pairs={{24,16},{25,17},{26,18},{27,19},{28,20},{29,21},{30,22},{31,23}} | collective-permute-start | bytes 356360 | tf_op jit(solution)/shard_map/ppermute | solution.py:324
  38.0 1.5 %collective-permute-start.17 = (s16[464,128]{1,0:T(8,128)(2,1)S(1)}, s16[464,128]{1,0:T(8,128)(2,1)S(1)}, u32[]{:S(2)}, u32[]{:S(2)}) collective-permute-start(s16[464,128]{1,0:T(8,128)(2,1)S(1)} %get-tuple-element.52), channel_id=1, source_target_pairs={{16,8},{17,9},{18,10},{19,11},{20,12},{21,13},{22,14},{23,15}} | collective-permute-start | bytes 356360 | tf_op jit(solution)/shard_map/ppermute | solution.py:337
  38.8 2.1 %collective-permute-start.9 = (s16[464,128]{1,0:T(8,128)(2,1)S(1)}, s16[464,128]{1,0:T(8,128)(2,1)S(1)}, u32[]{:S(2)}, u32[]{:S(2)}) collective-permute-start(s16[464,128]{1,0:T(8,128)(2,1)S(1)} %get-tuple-element.40), channel_id=1, source_target_pairs={{16,8},{17,9},{18,10},{19,11},{20,12},{21,13},{22,14},{23,15}} | collective-permute-start | bytes 356360 | tf_op jit(solution)/shard_map/ppermute | solution.py:337
  39.6 25.0 %collective-permute-start.18 = (s16[464,128]{1,0:T(8,128)(2,1)S(1)}, s16[464,128]{1,0:T(8,128)(2,1)S(1)}, u32[]{:S(2)}, u32[]{:S(2)}) collective-permute-start(s16[464,128]{1,0:T(8,128)(2,1)S(1)} %get-tuple-element.54), channel_id=1, source_target_pairs={{8,0},{9,1},{10,2},{11,3},{12,4},{13,5},{14,6},{15,7}} | collective-permute-start | bytes 356360 | tf_op jit(solution)/shard_map/ppermute | solution.py:337
  41.0 25.8 %collective-permute-start.10 = (s16[464,128]{1,0:T(8,128)(2,1)S(1)}, s16[464,128]{1,0:T(8,128)(2,1)S(1)}, u32[]{:S(2)}, u32[]{:S(2)}) collective-permute-start(s16[464,128]{1,0:T(8,128)(2,1)S(1)} %get-tuple-element.42), channel_id=1, source_target_pairs={{8,0},{9,1},{10,2},{11,3},{12,4},{13,5},{14,6},{15,7}} | collective-permute-start | bytes 356360 | tf_op jit(solution)/shard_map/ppermute | solution.py:337

commit v2 on v1

--- a/solution.py
+++ b/solution.py
@@ -47,10 +47,11 @@
     return coded_ref[index * rows : (index + 1) * rows, :].astype(jnp.int32).astype(jnp.float32) * scale
 
 
-def encode_kernel(state_ref, *out_refs):
+def encode_kernel(chunks, both_k, state_ref, wall_ref, *outs):
     planes, nv, rows, columns = state_ref.shape
-    width = columns // len(out_refs)
-    for chunk, out_ref in enumerate(out_refs):
+    coded, (j_first, j_second), edges_k, open_ref = outs[:chunks], outs[chunks : chunks + 2], outs[chunks + 2 : -1], outs[-1]
+    width = columns // chunks
+    for chunk, out_ref in enumerate(coded):
         places = [
             (p, v, chunk * width + b * LANES)
             for p in range(planes)
@@ -65,53 +66,161 @@
             (lambda p=p, v=v, at=at: state_ref[p, v, :, at : at + LANES]) for p, v, at in places
         ]
         put_coded(blocks, most, out_ref, rows)
-
-
-def residual_kernel(
-    chunk, chunks, count_k, state_ref, low_j, high_j, low_k, high_k, ahead, wall_ref, x_out, rows_pad
-):
+    open_ref[...] = 1.0 - wall_ref[...].astype(jnp.float32)
+
+    def rows_for(next_ref, previous_ref):
+        for p in range(planes):
+            for v in range(nv):
+                end = rows - 1
+                next_ref[p, v, 0:1, :] = NEAR * state_ref[p, v, end:rows, :] + FAR * state_ref[p, v, end - 1 : end, :]
+                next_ref[p, v, 1:2, :] = FAR * state_ref[p, v, end:rows, :]
+                previous_ref[p, v, 0:1, :] = FAR * state_ref[p, v, 0:1, :]
+                previous_ref[p, v, 1:2, :] = NEAR * state_ref[p, v, 0:1, :] + FAR * state_ref[p, v, 1:2, :]
+
+    even_j = lax.axis_index("ja") % 2 == 0
+    pl.when(even_j)(lambda: rows_for(j_first, j_second))
+    pl.when(jnp.logical_not(even_j))(lambda: rows_for(j_second, j_first))
+
+    lane = lax.broadcasted_iota(jnp.int32, (rows, LANES), 1)
+
+    def columns_for_next(out_ref):
+        for p in range(planes):
+            for v in range(nv):
+                block = state_ref[p, v, :, columns - LANES :]
+                one, two = pltpu.roll(block, 1, 1), pltpu.roll(block, 2, 1)
+                out_ref[p, v] = jnp.where(lane < 1, NEAR * one, 0.0) + jnp.where(lane < 2, FAR * two, 0.0)
+
+    def columns_for_previous(out_ref):
+        for p in range(planes):
+            for v in range(nv):
+                block = state_ref[p, v, :, :LANES]
+                one, two = pltpu.roll(block, LANES - 1, 1), pltpu.roll(block, LANES - 2, 1)
+                out_ref[p, v] = jnp.where(lane > LANES - 2, NEAR * one, 0.0) + jnp.where(lane > LANES - 3, FAR * two, 0.0)
+
+    even_k = lax.axis_index("ka") % 2 == 0
+
+    @pl.when(even_k)
+    def _():
+        columns_for_next(edges_k[0])
+        if both_k:
+            columns_for_previous(edges_k[1])
+
+    @pl.when(jnp.logical_not(even_k))
+    def _():
+        columns_for_previous(edges_k[0])
+        if both_k:
+            columns_for_next(edges_k[1])
+
+
+def local_kernel(state_ref, *refs):
+    x_outs, rows_pad = refs[:-1], refs[-1]
     planes, nv, rows, columns = state_ref.shape
-    width = columns // chunks
+    width = columns // len(x_outs)
+    nothing = jnp.zeros((rows, LANES), jnp.float32)
+    rows_pad[0:8, :] = jnp.zeros((8, width), jnp.float32)
+    rows_pad[8 + rows :, :] = jnp.zeros((8, width), jnp.float32)
+    for chunk, x_out in enumerate(x_outs):
+        start, stop = chunk * width, (chunk + 1) * width
+        for v in range(nv):
+            here = [state_ref[p, v, :, start:stop] for p in range(planes)]
+            for p in range(planes):
+                total = CENTRE * here[p]
+                for shift, factor in ((-2, BEHIND_2), (-1, BEHIND_1), (1, NEAR), (2, FAR)):
+                    if 0 <= p + shift < planes:
+                        total += factor * here[p + shift]
+                rows_pad[8 : 8 + rows, :] = here[p]
+                total += NEAR * (rows_pad[7 : 7 + rows, :] + rows_pad[9 : 9 + rows, :])
+                total += FAR * (rows_pad[6 : 6 + rows, :] + rows_pad[10 : 10 + rows, :])
+                left = nothing if start == 0 else state_ref[p, v, :, start - LANES : start]
+                right = nothing if stop == columns else state_ref[p, v, :, stop : stop + LANES]
+                wide = jnp.concatenate([left, here[p], right], axis=1)
+                span = wide.shape[1]
+                one = pltpu.roll(wide, 1, 1) + pltpu.roll(wide, span - 1, 1)
+                two = pltpu.roll(wide, 2, 1) + pltpu.roll(wide, span - 2, 1)
+                total += (NEAR * one + FAR * two)[:, LANES : LANES + width]
+                x_out[p, v] = total
+
+
+def add_plane_terms(coded, x_ref, p, v, block, terms, scale, per):
+    nv, rows = x_ref.shape[1:3]
+    own = slice(block * LANES, (block + 1) * LANES)
+    total = x_ref[p, v, :, own]
+    for q, factor in terms:
+        total += factor * get_coded(coded, (q * nv + v) * per + block, rows, scale)
+    return total
+
+
+def terms_ahead(planes, p):
+    found = [(p + shift - planes, factor) for shift, factor in ((1, NEAR), (2, FAR))]
+    return [(q, factor) for q, factor in found if q >= 0]
+
+
+def terms_behind(planes, p):
+    found = [(planes + p - shift, factor) for shift, factor in ((1, BEHIND_1), (2, BEHIND_2))]
+    return [(q, factor) for q, factor in found if q < planes]
+
+
+def halo_kernel(chunk, chunks, counts, j_first, j_second, edges_k, neighbour, open_ref, x_in, x_out):
+    planes, nv, rows, width = x_out.shape
+    per = width // LANES
     start = chunk * width
-    stop = start + width
-    per = width // LANES
-    scale = get_scale(ahead, planes * nv * per, rows)
-    place_k = lax.axis_index("ka")
-    open_cells = [1.0 - wall_ref[p, :, start:stop].astype(jnp.float32) for p in range(planes)]
-
-    def next_plane(p, v):
-        parts = [get_coded(ahead, (p * nv + v) * per + b, rows, scale) for b in range(per)]
-        return jnp.concatenate(parts, axis=1)
-
-    for v in range(nv):
-        here = [state_ref[p, v, :, start:stop] for p in range(planes)]
-        after = [next_plane(p, v) for p in range(planes)]
-        for p in range(planes):
-            line = here + after
-            total = CENTRE * here[p] + NEAR * line[p + 1] + FAR * line[p + 2]
-            if p >= 1:
-                total += BEHIND_1 * here[p - 1]
-            if p >= 2:
-                total += BEHIND_2 * here[p - 2]
-            rows_pad[6:8, :] = low_j[p, v, :, start:stop]
-            rows_pad[8 : 8 + rows, :] = here[p]
-            rows_pad[8 + rows : 10 + rows, :] = high_j[p, v, :, start:stop]
-            total += NEAR * (rows_pad[7 : 7 + rows, :] + rows_pad[9 : 9 + rows, :])
-            total += FAR * (rows_pad[6 : 6 + rows, :] + rows_pad[10 : 10 + rows, :])
-            if start == 0:
-                left = jnp.where(place_k > 0, low_k[p, v], 0.0)
-            else:
-                left = state_ref[p, v, :, start - LANES : start]
-            if stop == columns:
-                right = jnp.where(place_k < count_k - 1, high_k[p, v], 0.0)
-            else:
-                right = state_ref[p, v, :, stop : stop + LANES]
-            wide = jnp.concatenate([left, here[p], right], axis=1)
-            span = wide.shape[1]
-            one = pltpu.roll(wide, 1, 1) + pltpu.roll(wide, span - 1, 1)
-            two = pltpu.roll(wide, 2, 1) + pltpu.roll(wide, span - 2, 1)
-            total += (NEAR * one + FAR * two)[:, LANES : LANES + width]
-            x_out[p, v] = open_cells[p] * total
+    place_i, place_j, place_k = (lax.axis_index(name) for name in ("ia", "ja", "ka"))
+    count_i, count_j, count_k = counts
+    scale = get_scale(neighbour, planes * nv * per, rows)
+    even_i = place_i % 2 == 0
+
+    def with_planes(terms_of):
+        for p in range(planes):
+            for v in range(nv):
+                for block in range(per):
+                    own = slice(block * LANES, (block + 1) * LANES)
+                    x_out[p, v, :, own] = add_plane_terms(neighbour, x_in, p, v, block, terms_of(planes, p), scale, per)
+
+    takes_ahead = jnp.logical_and(even_i, place_i + 1 < count_i)
+    takes_behind = jnp.logical_not(even_i)
+    pl.when(takes_ahead)(lambda: with_planes(terms_ahead))
+    pl.when(takes_behind)(lambda: with_planes(terms_behind))
+    if count_i % 2:
+        pl.when(place_i == count_i - 1)(lambda: with_planes(lambda planes, p: []))
+
+    even_j = place_j % 2 == 0
+    from_next = place_j + 1 < count_j
+    from_previous = place_j > 0
+
+    def add_rows(ref, low):
+        at = 0 if low else rows - 2
+        for p in range(planes):
+            for v in range(nv):
+                x_out[p, v, at : at + 2, :] += ref[p, v, :, start : start + width]
+
+    pl.when(jnp.logical_and(even_j, from_next))(lambda: add_rows(j_first, False))
+    pl.when(jnp.logical_and(even_j, from_previous))(lambda: add_rows(j_second, True))
+    odd_j = jnp.logical_not(even_j)
+    pl.when(odd_j)(lambda: add_rows(j_first, True))
+    pl.when(jnp.logical_and(odd_j, from_next))(lambda: add_rows(j_second, False))
+
+    even_k = place_k % 2 == 0
+    odd_k = jnp.logical_not(even_k)
+
+    def add_columns(ref, low):
+        at = 0 if low else width - LANES
+        for p in range(planes):
+            for v in range(nv):
+                x_out[p, v, :, at : at + LANES] += ref[p, v]
+
+    if chunk == 0:
+        pl.when(odd_k)(lambda: add_columns(edges_k[0], True))
+        if len(edges_k) > 1:
+            pl.when(jnp.logical_and(even_k, place_k > 0))(lambda: add_columns(edges_k[1], True))
+    if chunk == chunks - 1:
+        pl.when(jnp.logical_and(even_k, place_k + 1 < count_k))(lambda: add_columns(edges_k[0], False))
+        if len(edges_k) > 1:
+            pl.when(jnp.logical_and(odd_k, place_k + 1 < count_k))(lambda: add_columns(edges_k[1], False))
+
+    for p in range(planes):
+        open_cells = open_ref[p, :, start : start + width]
+        for v in range(nv):
+            x_out[p, v] = open_cells * x_out[p, v]
 
 
 def apply_block(inverse_ref, p, at, vector):
@@ -125,12 +234,19 @@
     return result
 
 
-def forward_part(chunk, first, inverse_ref, coupling_ref, wall_ref, behind, face, x_in, x_out, send):
+def forward_part(chunk, hop, count, inverse_ref, coupling_ref, open_ref, neighbour, face, x_in, x_out, send):
     planes, nv, rows, width = x_out.shape
     per = width // LANES
+    first = hop == 0
+    terms_of = None
     if not first:
         face_scale = get_scale(face, nv * per, rows)
-        behind_scale = get_scale(behind, planes * nv * per, rows)
+        if hop % 2 == 0:
+            terms_of = terms_behind
+        elif hop < count - 1:
+            terms_of = terms_ahead
+    if terms_of is not None:
+        scale = get_scale(neighbour, planes * nv * per, rows)
     most = None
     for block in range(per):
         own = slice(block * LANES, (block + 1) * LANES)
@@ -138,23 +254,22 @@
         running = None
         if not first:
             running = [get_coded(face, v * per + block, rows, face_scale) for v in range(nv)]
-
-            def old(p, v):
-                return get_coded(behind, (p * nv + v) * per + block, rows, behind_scale)
-
         for p in range(planes):
             factor = coupling_ref[p, 0, :, at : at + LANES]
-            if not first and p < 2:
-                open_cells = 1.0 - wall_ref[p, :, at : at + LANES].astype(jnp.float32)
+            if terms_of is not None:
+                open_cells = open_ref[p, :, at : at + LANES]
             right = []
             for v in range(nv):
                 entry = x_in[p, v, :, own]
+                if terms_of is not None:
+                    extra = None
+                    for q, weight in terms_of(planes, p):
+                        term = weight * get_coded(neighbour, (q * nv + v) * per + block, rows, scale)
+                        extra = term if extra is None else extra + term
+                    if extra is not None:
+                        entry += open_cells * extra
                 if running is not None:
-                    entry = entry + factor * running[v]
-                if not first and p == 0:
-                    entry += open_cells * (BEHIND_1 * old(planes - 1, v) + BEHIND_2 * old(planes - 2, v))
-                if not first and p == 1:
-                    entry += open_cells * (BEHIND_2 * old(planes - 1, v))
+                    entry += factor * running[v]
                 right.append(entry)
             running = apply_block(inverse_ref, p, at, right)
             for v in range(nv):
@@ -205,15 +320,14 @@
         put_face(0, most, x_out, send)
 
 
-def forward_kernel(chunk, hop, count, inverse_ref, coupling_ref, wall_ref, behind, face, x_in, x_out, send):
+def forward_kernel(chunk, hop, count, inverse_ref, coupling_ref, open_ref, neighbour, face, x_in, x_out, send):
     active = lax.axis_index("ia") == hop
     last = hop == count - 1
 
     @pl.when(active)
     def _():
         forward_part(
-            chunk, hop == 0, inverse_ref, coupling_ref, wall_ref, behind, face, x_in, x_out,
-            None if last else send,
+            chunk, hop, count, inverse_ref, coupling_ref, open_ref, neighbour, face, x_in, x_out, None if last else send
         )
         if last:
             backward_part(chunk, True, inverse_ref, coupling_ref, None, x_out, x_out, send)
@@ -271,57 +385,71 @@
     )(*operands)
 
 
+def swaps(count, first):
+    partner = list(range(count))
+    for i in range(first, count - 1, 2):
+        partner[i], partner[i + 1] = i + 1, i
+    return list(enumerate(partner))
+
+
+def swap_of(count, low):
+    partner = list(range(count))
+    partner[low], partner[low + 1] = low + 1, low
+    return list(enumerate(partner))
+
+
 def shards(state, inverse, coupling, wall):
     planes, nv, rows, columns = state.shape
     chunks = CHUNKS
     width = columns // chunks
     per = width // LANES
-    count = lax.axis_size("ia")
-    count_j = lax.axis_size("ja")
-    count_k = lax.axis_size("ka")
-    up = lambda n: [(i, i + 1) for i in range(n - 1)]
-    down = lambda n: [(i + 1, i) for i in range(n - 1)]
+    counts = count, count_j, count_k = [lax.axis_size(name) for name in ("ia", "ja", "ka")]
+    sets_k = 1 if count_k == 2 else 2
 
     halo_code = jax.ShapeDtypeStruct(((planes * nv * per + 1) * rows, LANES), jnp.int16)
     face_code = jax.ShapeDtypeStruct(((nv * per + 1) * rows, LANES), jnp.int16)
     full = jax.ShapeDtypeStruct(state.shape, jnp.float32)
     part = jax.ShapeDtypeStruct((planes, nv, rows, width), jnp.float32)
-
-    coded = call(encode_kernel, [state], [halo_code] * chunks, "encode")
-    ahead = [lax.ppermute(coded[c], "ia", down(count)) for c in range(chunks)]
-
-    head_k = state[:, :, :, :LANES]
-    tail_k = state[:, :, :, columns - LANES :]
-    if count_k == 2:
-        mine = jnp.where(lax.axis_index("ka") == 0, tail_k, head_k)
-        low_k = lax.ppermute(mine, "ka", [(0, 1), (1, 0)])
-        high_k = low_k
-    else:
-        low_k = lax.ppermute(tail_k, "ka", up(count_k))
-        high_k = lax.ppermute(head_k, "ka", down(count_k))
-    low_j = lax.ppermute(state[:, :, rows - 2 :, :], "ja", up(count_j))
-    high_j = lax.ppermute(state[:, :, :2, :], "ja", down(count_j))
-    behind = [lax.ppermute(coded[c], "ia", up(count)) for c in range(chunks)]
-
-    x = []
+    edge_j = jax.ShapeDtypeStruct((planes, nv, 2, columns), jnp.float32)
+    edge_k = jax.ShapeDtypeStruct((planes, nv, rows, LANES), jnp.float32)
+    cells = jax.ShapeDtypeStruct((planes, rows, columns), jnp.float32)
+
+    made = call(
+        functools.partial(encode_kernel, chunks, sets_k == 2),
+        [state, wall],
+        [halo_code] * chunks + [edge_j] * 2 + [edge_k] * sets_k + [cells],
+        "encode",
+    )
+    coded, edges_j, edges_k, open_cells = made[:chunks], made[chunks : chunks + 2], made[chunks + 2 : -1], made[-1]
+    near = [lax.ppermute(coded[c], "ia", swaps(count, 0)) for c in range(chunks)]
+    edges_k = [lax.ppermute(edge, "ka", swaps(count_k, s)) for s, edge in enumerate(edges_k)]
+    edges_j = [lax.ppermute(edge, "ja", swaps(count_j, s)) for s, edge in enumerate(edges_j)]
+    local = call(local_kernel, [state], [part] * chunks, "local", None, [VMEM((rows + 16, width), jnp.float32)])
+
+    x, far = [], []
     for c in range(chunks):
-        kernel = functools.partial(residual_kernel, c, chunks, count_k)
-        operands = [state, low_j, high_j, low_k, high_k, ahead[c], wall]
-        x += call(kernel, operands, [part], "residual", None, [VMEM((rows + 16, width), jnp.float32)])
+        later, _ = lax.optimization_barrier((coded[c], near[c]))
+        far.append(lax.ppermute(later, "ia", swaps(count, 1)))
+
+        def kernel(*refs, c=c):
+            rest = refs[2 + sets_k :]
+            halo_kernel(c, chunks, counts, *refs[:2], refs[2 : 2 + sets_k], *rest)
+
+        operands = [*edges_j, *edges_k, near[c], open_cells, local[c]]
+        x += call(kernel, operands, [part], "halo", {len(operands) - 1: 0})
 
     face = [None] * chunks
     for hop in range(count):
         for c in range(chunks):
             if hop == 0:
-                def kernel(inverse_ref, coupling_ref, wall_ref, *refs, c=c):
-                    forward_kernel(c, 0, count, inverse_ref, coupling_ref, wall_ref, None, None, *refs)
-                operands = [inverse, coupling, wall, x[c]]
+                def kernel(inverse_ref, coupling_ref, *refs, c=c):
+                    forward_kernel(c, 0, count, inverse_ref, coupling_ref, None, None, None, *refs)
+                operands = [inverse, coupling, x[c]]
             else:
                 kernel = functools.partial(forward_kernel, c, hop, count)
-                operands = [inverse, coupling, wall, behind[c], face[c], x[c]]
+                operands = [inverse, coupling, open_cells, far[c], face[c], x[c]]
             x[c], send = call(kernel, operands, [part, face_code], "forward", {len(operands) - 1: 0})
-            pair = (hop, hop + 1) if hop < count - 1 else (hop, hop - 1)
-            face[c] = lax.ppermute(send, "ia", [pair])
+            face[c] = lax.ppermute(send, "ia", swap_of(count, min(hop, count - 2)))
     for hop in reversed(range(count - 1)):
         for c in range(chunks):
             if hop == 0 and c == chunks - 1:
@@ -334,7 +462,7 @@
                 continue
             kernel = functools.partial(backward_kernel, c, hop)
             x[c], send = call(kernel, [inverse, coupling, face[c], x[c]], [part, face_code], "backward", {3: 0})
-            face[c] = lax.ppermute(send, "ia", [(hop, hop - 1)])
+            face[c] = lax.ppermute(send, "ia", swap_of(count, hop - 1))
 
 
 def solution(mesh):

time: 68.7 us -> 72.7 us (1.058)
  starting transfers between devices: 32.2 us -> 48.4 us
  waiting for transfers between devices: 25.6 us -> 14.9 us
  local copies, waits for them, and re-layouts: 3.35 us -> 2.13 us
  other arithmetic: 1.12 us -> 0 us
  Pallas kernels: 5.52 us -> 6.37 us
    ppermute x19, starting transfers between devices: 32.2 us -> 48.4 us  [the longest x4 29.5 us: shards(): face[c] = lax.ppermute(send, 'ia', swap_of(count, hop - 1))]
    ppermute x19, waiting for transfers between devices: 25.6 us -> 14.9 us  [the longest x2 7.46 us: shards(): lax.ppermute(coded[c], 'ia', swaps(count, 0))]
    unnamed x12 -> x8, local copies, waits for them, and re-layouts: 3.27 us -> 2.13 us
    select_n x1 -> x0, other arithmetic: 1.12 us -> none  [shards(): mine = jnp.where(lax.axis_index('ka') == 0, tail_k, head_k)]
    pallas_call x17 -> x18, Pallas kernels: 5.52 us -> 6.37 us  [call(): pl.pallas_call(kernel, in_specs=[whole()] * len(operands), out_specs=[who...]
  transfers between devices with their start and end apart: 19 -> 19, of which waited for: 4 -> 5; matrix products, arithmetic and copies ran while one was open for 0% -> 0% of each run, Pallas kernels for 6% -> 6%
where the time goes in v2:
time: 72.7 us; the launch traced here: 72.2 us
  starting transfers between devices  48.4 us (67%)
  waiting for transfers between devices  14.9 us (20%)
  Pallas kernels  6.37 us (9%)
  local copies, waits for them, and re-layouts  2.13 us (3%)
    ppermute x4, starting transfers between devices, shards(): face[c] = lax.ppermute(send, 'ia', swap_of(count, hop - 1))  29.5 us
    ppermute x8, starting transfers between devices, shards(): face[c] = lax.ppermute(send, 'ia', swap_of(count, min(hop, count - 2)))  11.7 us
    ppermute x2, waiting for transfers between devices, shards(): lax.ppermute(coded[c], 'ia', swaps(count, 0))  7.46 us
    pallas_call x18, Pallas kernels, call(): pl.pallas_call(kernel, in_specs=[whole()] * len(operands), out_specs=[who...  6.37 us
    ppermute x8, waiting for transfers between devices, shards(): face[c] = lax.ppermute(send, 'ia', swap_of(count, min(hop, count - 2)))  5.26 us
    ppermute x2, starting transfers between devices, shards(): lax.ppermute(coded[c], 'ia', swaps(count, 0))  3.08 us
    ppermute x2, starting transfers between devices, shards(): lax.ppermute(edge, 'ja', swaps(count_j, s))  2.69 us
    ppermute x4, waiting for transfers between devices, shards(): face[c] = lax.ppermute(send, 'ia', swap_of(count, hop - 1))  2.21 us
  transfers between devices with their start and end apart: 19, of which 5 were waited for; matrix products, arithmetic and copies ran while one was open for 0% of the time, Pallas kernels for 6%

profile of v2, /device:TPU:0, one launch (start us, length us, event | category | flops | bytes accessed | tf_op | source)
XLA Modules:
  0.0 72.2 jit_solution(13033024802468153464)
XLA Ops:
  0.0 1.2 %copy-done.2 = f32[2,7,16,1024]{3,2,1,0:T(8,128)S(1)} copy-done((f32[2,7,16,1024]{3,2,1,0:T(8,128)S(1)}, f32[2,7,16,1024]{3,2,1,0:T(8,128)}, u32[]{:S(2)}) %copy-start.2) | copy-done | bytes 917528
  1.2 0.9 %copy-done.3 = s32[2,16,1024]{2,1,0:T(8,128)S(1)} copy-done((s32[2,16,1024]{2,1,0:T(8,128)S(1)}, s32[2,16,1024]{2,1,0:T(8,128)}, u32[]{:S(2)}) %copy-start.3) | copy-done | bytes 131096
  2.1 0.5 encode.1
  2.7 3.0 %collective-permute-start.11 = (s16[912,128]{1,0:T(8,128)(2,1)S(1)}, s16[912,128]{1,0:T(8,128)(2,1)S(1)}, u32[]{:S(2)}, u32[]{:S(2)}) collective-permute-start(s16[912,128]{1,0:T(8,128)(2,1)S(1)} %get-tuple-element.58), channel_id=1, source_target_pairs={{0,8},{8,0},{16,24},{24,16},{1,9},{9,1},{17,25},{25,17},{2,10},{10... | collective-permute-start | bytes 700424 | tf_op jit(solution)/shard_map/ppermute | solution.py:424
  5.7 0.1 collective-permute-start
  5.7 2.0 %collective-permute-start.2 = (f32[2,7,2,1024]{3,2,1,0:T(2,128)S(1)}, f32[2,7,2,1024]{3,2,1,0:T(2,128)S(1)}, u32[]{:S(2)}, u32[]{:S(2)}) collective-permute-start(f32[2,7,2,1024]{3,2,1,0:T(2,128)S(1)} %get-tuple-element.42), channel_id=1, source_target_pairs={{0,2},{2,0},{4,6},{6,4},{1,3},{3,1},{5,7},{7,5},{8,10},{10,8},{12,... | collective-permute-start | bytes 344072 | tf_op jit(solution)/shard_map/ppermute | solution.py:426
  7.8 0.7 collective-permute-start.3
  8.4 0.1 collective-permute-start.4
  8.5 3.7 %collective-permute-done.11.refs_3_ = s16[912,128]{1,0:T(8,128)(2,1)S(1)} collective-permute-done((s16[912,128]{1,0:T(8,128)(2,1)S(1)}, s16[912,128]{1,0:T(8,128)(2,1)S(1)}, u32[]{:S(2)}, u32[]{:S(2)}) %collective-permute-start.11) | collective-permute-done | bytes 233504 | tf_op jit(solution)/shard_map/ppermute | solution.py:424
  12.2 0.7 collective-permute-start.12
  12.9 3.8 %collective-permute-done.refs_3_ = s16[912,128]{1,0:T(8,128)(2,1)S(1)} collective-permute-done((s16[912,128]{1,0:T(8,128)(2,1)S(1)}, s16[912,128]{1,0:T(8,128)(2,1)S(1)}, u32[]{:S(2)}, u32[]{:S(2)}) %collective-permute-start) | collective-permute-done | bytes 233504 | tf_op jit(solution)/shard_map/ppermute | solution.py:424
  16.6 0.7 collective-permute-start.1
  17.3 1.2 %local.1 = (f32[2,7,16,512]{3,2,1,0:T(8,128)S(1)}, f32[2,7,16,512]{3,2,1,0:T(8,128)S(1)}) custom-call(f32[2,7,16,1024]{3,2,1,0:T(8,128)S(1)} %copy-done.2), custom_call_target="tpu_custom_call" | custom-call | tf_op jit(solution)/shard_map/local/pallas_call | solution.py:376
  18.5 0.0 collective-permute-done.3.refs_1_
  18.5 0.0 collective-permute-done.4.refs_2_
  18.5 0.3 halo.3.refs_0_
  18.9 0.5 forward.12
  19.4 5.8 %collective-permute-start.13 = (s16[464,128]{1,0:T(8,128)(2,1)S(1)}, s16[464,128]{1,0:T(8,128)(2,1)S(1)}, u32[]{:S(2)}, u32[]{:S(2)}) collective-permute-start(s16[464,128]{1,0:T(8,128)(2,1)S(1)} %get-tuple-element.60), channel_id=1, source_target_pairs={{0,8},{8,0},{16,16},{24,24},{1,9},{9,1},{17,17},{25,25},{2,10},{10... | collective-permute-start | bytes 356360 | tf_op jit(solution)/shard_map/ppermute | solution.py:452
  25.2 0.4 halo.2.refs_0_
  25.6 0.5 forward.8
  26.1 1.9 %collective-permute-start.5 = (s16[464,128]{1,0:T(8,128)(2,1)S(1)}, s16[464,128]{1,0:T(8,128)(2,1)S(1)}, u32[]{:S(2)}, u32[]{:S(2)}) collective-permute-start(s16[464,128]{1,0:T(8,128)(2,1)S(1)} %get-tuple-element.46), channel_id=1, source_target_pairs={{0,8},{8,0},{16,16},{24,24},{1,9},{9,1},{17,17},{25,25},{2,10},{10... | collective-permute-start | bytes 356360 | tf_op jit(solution)/shard_map/ppermute | solution.py:452
  28.0 1.4 %collective-permute-done.13.face = s16[464,128]{1,0:T(8,128)(2,1)S(1)} collective-permute-done((s16[464,128]{1,0:T(8,128)(2,1)S(1)}, s16[464,128]{1,0:T(8,128)(2,1)S(1)}, u32[]{:S(2)}, u32[]{:S(2)}) %collective-permute-start.13) | collective-permute-done | bytes 118816 | tf_op jit(solution)/shard_map/ppermute | solution.py:452
  29.5 0.0 collective-permute-done.12.neighbour
  29.5 0.1 forward.13
  29.5 0.7 collective-permute-start.14
  30.2 3.8 %collective-permute-done.5.face = s16[464,128]{1,0:T(8,128)(2,1)S(1)} collective-permute-done((s16[464,128]{1,0:T(8,128)(2,1)S(1)}, s16[464,128]{1,0:T(8,128)(2,1)S(1)}, u32[]{:S(2)}, u32[]{:S(2)}) %collective-permute-start.5) | collective-permute-done | bytes 118816 | tf_op jit(solution)/shard_map/ppermute | solution.py:452
  34.0 0.1 forward.9
  34.1 0.7 collective-permute-start.6
  34.8 0.1 forward.14
  34.9 0.7 collective-permute-start.15
  35.6 0.0 collective-permute-done.6.face
  35.6 0.1 forward.10
  35.6 0.7 collective-permute-start.7
  36.3 0.1 forward.15
  36.4 0.7 collective-permute-start.16
  37.1 0.1 forward.11
  37.2 0.7 collective-permute-start.8
  37.9 0.1 backward.7
  38.0 0.7 collective-permute-start.17
  38.7 0.1 backward.5
  38.7 0.7 collective-permute-start.9
  39.4 0.3 backward.8
  39.7 24.1 %collective-permute-start.18 = (s16[464,128]{1,0:T(8,128)(2,1)S(1)}, s16[464,128]{1,0:T(8,128)(2,1)S(1)}, u32[]{:S(2)}, u32[]{:S(2)}) collective-permute-start(s16[464,128]{1,0:T(8,128)(2,1)S(1)} %get-tuple-element.70), channel_id=1, source_target_pairs={{0,8},{8,0},{16,16},{24,24},{1,9},{9,1},{17,17},{25,25},{2,10},{10... | collective-permute-start | bytes 356360 | tf_op jit(solution)/shard_map/ppermute | solution.py:465
  63.9 0.1 backward.6
  63.9 4.0 %collective-permute-start.10 = (s16[464,128]{1,0:T(8,128)(2,1)S(1)}, s16[464,128]{1,0:T(8,128)(2,1)S(1)}, u32[]{:S(2)}, u32[]{:S(2)}) collective-permute-start(s16[464,128]{1,0:T(8,128)(2,1)S(1)} %get-tuple-element.56), channel_id=1, source_target_pairs={{0,8},{8,0},{16,16},{24,24},{1,9},{9,1},{17,17},{25,25},{2,10},{10... | collective-permute-start | bytes 356360 | tf_op jit(solution)/shard_map/ppermute | solution.py:465
  68.0 0.6 backward.9.refs_0_
  68.6 2.2 %collective-permute-done.10.face = s16[464,128]{1,0:T(8,128)(2,1)S(1)} collective-permute-done((s16[464,128]{1,0:T(8,128)(2,1)S(1)}, s16[464,128]{1,0:T(8,128)(2,1)S(1)}, u32[]{:S(2)}, u32[]{:S(2)}) %collective-permute-start.10) | collective-permute-done | bytes 118816 | tf_op jit(solution)/shard_map/ppermute | solution.py:465
  70.8 1.4 %last.1 = f32[2,7,16,1024]{3,2,1,0:T(8,128)} custom-call(bf16[2,7,7,16,1024]{4,3,2,1,0:T(8,128)(2,1)S(1)} %copy-done, f32[2,2,16,1024]{3,2,1,0:T(8,128)S(1)} %copy-done.1, s16[464,128]{1,0:T(8,128)(2,1)S(1)} %collective-permute-done.10.face, f32[2,7,16,512]{3,2,1,0:T(8,128)S(1)} %backward.9.refs_0_, f32[2,7,16,512]{3,2,1,0:T(8,128)S(1)} %get-tuple-element.72.refs_1_), custom_call_target="tpu_custom_call" | custom-call | tf_op jit(solution)/shard_map/last/pallas_call | solution.py:376
  (16 shorter events, 0.0 us)
Async XLA Ops:
  0.0 18.9 %copy-start.1 = (f32[2,2,16,1024]{3,2,1,0:T(8,128)S(1)}, f32[2,2,16,1024]{3,2,1,0:T(8,128)}, u32[]{:S(2)}) copy-start(f32[2,2,16,1024]{3,2,1,0:T(8,128)} %coupling_ref.25) | copy-start | bytes 786436
  0.0 1.2 %copy-start.2 = (f32[2,7,16,1024]{3,2,1,0:T(8,128)S(1)}, f32[2,7,16,1024]{3,2,1,0:T(8,128)}, u32[]{:S(2)}) copy-start(f32[2,7,16,1024]{3,2,1,0:T(8,128)} %state_ref.3) | copy-start | bytes 2752516
  1.2 0.9 %copy-start.3 = (s32[2,16,1024]{2,1,0:T(8,128)S(1)}, s32[2,16,1024]{2,1,0:T(8,128)}, u32[]{:S(2)}) copy-start(s32[2,16,1024]{2,1,0:T(8,128)} %wall_ref.1) | copy-start | bytes 393220
  2.1 16.7 %copy-start = (bf16[2,7,7,16,1024]{4,3,2,1,0:T(8,128)(2,1)S(1)}, bf16[2,7,7,16,1024]{4,3,2,1,0:T(8,128)(2,1)}, u32[]{:S(2)}) copy-start(bf16[2,7,7,16,1024]{4,3,2,1,0:T(8,128)(2,1)} %inverse_ref.25) | copy-start | bytes 9633796
  2.7 9.5 %collective-permute-start.11 = (s16[912,128]{1,0:T(8,128)(2,1)S(1)}, s16[912,128]{1,0:T(8,128)(2,1)S(1)}, u32[]{:S(2)}, u32[]{:S(2)}) collective-permute-start(s16[912,128]{1,0:T(8,128)(2,1)S(1)} %get-tuple-element.58), channel_id=1, source_target_pairs={{0,8},{8,0},{16,24},{24,16},{1,9},{9,1},{17,25},{25,17},{2,10},{10... | collective-permute-start | bytes 700424 | tf_op jit(solution)/shard_map/ppermute | solution.py:424
  5.7 11.0 %collective-permute-start = (s16[912,128]{1,0:T(8,128)(2,1)S(1)}, s16[912,128]{1,0:T(8,128)(2,1)S(1)}, u32[]{:S(2)}, u32[]{:S(2)}) collective-permute-start(s16[912,128]{1,0:T(8,128)(2,1)S(1)} %get-tuple-element.41), channel_id=1, source_target_pairs={{0,8},{8,0},{16,24},{24,16},{1,9},{9,1},{17,25},{25,17},{2,10},{10... | collective-permute-start | bytes 700424 | tf_op jit(solution)/shard_map/ppermute | solution.py:424
  5.7 12.7 %collective-permute-start.2 = (f32[2,7,2,1024]{3,2,1,0:T(2,128)S(1)}, f32[2,7,2,1024]{3,2,1,0:T(2,128)S(1)}, u32[]{:S(2)}, u32[]{:S(2)}) collective-permute-start(f32[2,7,2,1024]{3,2,1,0:T(2,128)S(1)} %get-tuple-element.42), channel_id=1, source_target_pairs={{0,2},{2,0},{4,6},{6,4},{1,3},{3,1},{5,7},{7,5},{8,10},{10,8},{12,... | collective-permute-start | bytes 344072 | tf_op jit(solution)/shard_map/ppermute | solution.py:426
  7.8 10.7 %collective-permute-start.3 = (f32[2,7,2,1024]{3,2,1,0:T(2,128)S(1)}, f32[2,7,2,1024]{3,2,1,0:T(2,128)S(1)}, u32[]{:S(2)}, u32[]{:S(2)}) collective-permute-start(f32[2,7,2,1024]{3,2,1,0:T(2,128)S(1)} %get-tuple-element.43), channel_id=1, source_target_pairs={{0,0},{2,4},{4,2},{6,6},{1,1},{3,5},{5,3},{7,7},{8,8},{10,12},{12,... | collective-permute-start | bytes 344072 | tf_op jit(solution)/shard_map/ppermute | solution.py:426
  8.4 10.1 %collective-permute-start.4 = (f32[2,7,16,128]{3,2,1,0:T(8,128)S(1)}, f32[2,7,16,128]{3,2,1,0:T(8,128)S(1)}, u32[]{:S(2)}, u32[]{:S(2)}) collective-permute-start(f32[2,7,16,128]{3,2,1,0:T(8,128)S(1)} %get-tuple-element.44), channel_id=1, source_target_pairs={{0,1},{1,0},{2,3},{3,2},{4,5},{5,4},{6,7},{7,6},{8,9},{9,8},{10,11... | collective-permute-start | bytes 344072 | tf_op jit(solution)/shard_map/ppermute | solution.py:425
  12.2 17.3 %collective-permute-start.12 = (s16[912,128]{1,0:T(8,128)(2,1)S(1)}, s16[912,128]{1,0:T(8,128)(2,1)S(1)}, u32[]{:S(2)}, u32[]{:S(2)}) collective-permute-start(s16[912,128]{1,0:T(8,128)(2,1)S(1)} %get-tuple-element.58), channel_id=1, source_target_pairs={{0,0},{8,16},{16,8},{24,24},{1,1},{9,17},{17,9},{25,25},{2,2},{10,... | collective-permute-start | bytes 700424 | tf_op jit(solution)/shard_map/ppermute | solution.py:432
  16.6 17.4 %collective-permute-start.1 = (s16[912,128]{1,0:T(8,128)(2,1)S(1)}, s16[912,128]{1,0:T(8,128)(2,1)S(1)}, u32[]{:S(2)}, u32[]{:S(2)}) collective-permute-start(s16[912,128]{1,0:T(8,128)(2,1)S(1)} %get-tuple-element.41), channel_id=1, source_target_pairs={{0,0},{8,16},{16,8},{24,24},{1,1},{9,17},{17,9},{25,25},{2,2},{10,... | collective-permute-start | bytes 700424 | tf_op jit(solution)/shard_map/ppermute | solution.py:432
  19.4 10.1 %collective-permute-start.13 = (s16[464,128]{1,0:T(8,128)(2,1)S(1)}, s16[464,128]{1,0:T(8,128)(2,1)S(1)}, u32[]{:S(2)}, u32[]{:S(2)}) collective-permute-start(s16[464,128]{1,0:T(8,128)(2,1)S(1)} %get-tuple-element.60), channel_id=1, source_target_pairs={{0,8},{8,0},{16,16},{24,24},{1,9},{9,1},{17,17},{25,25},{2,10},{10... | collective-permute-start | bytes 356360 | tf_op jit(solution)/shard_map/ppermute | solution.py:452
  26.1 7.9 %collective-permute-start.5 = (s16[464,128]{1,0:T(8,128)(2,1)S(1)}, s16[464,128]{1,0:T(8,128)(2,1)S(1)}, u32[]{:S(2)}, u32[]{:S(2)}) collective-permute-start(s16[464,128]{1,0:T(8,128)(2,1)S(1)} %get-tuple-element.46), channel_id=1, source_target_pairs={{0,8},{8,0},{16,16},{24,24},{1,9},{9,1},{17,17},{25,25},{2,10},{10... | collective-permute-start | bytes 356360 | tf_op jit(solution)/shard_map/ppermute | solution.py:452
  29.5 5.2 %collective-permute-start.14 = (s16[464,128]{1,0:T(8,128)(2,1)S(1)}, s16[464,128]{1,0:T(8,128)(2,1)S(1)}, u32[]{:S(2)}, u32[]{:S(2)}) collective-permute-start(s16[464,128]{1,0:T(8,128)(2,1)S(1)} %get-tuple-element.62), channel_id=1, source_target_pairs={{0,0},{8,16},{16,8},{24,24},{1,1},{9,17},{17,9},{25,25},{2,2},{10,... | collective-permute-start | bytes 356360 | tf_op jit(solution)/shard_map/ppermute | solution.py:452
  34.1 1.5 %collective-permute-start.6 = (s16[464,128]{1,0:T(8,128)(2,1)S(1)}, s16[464,128]{1,0:T(8,128)(2,1)S(1)}, u32[]{:S(2)}, u32[]{:S(2)}) collective-permute-start(s16[464,128]{1,0:T(8,128)(2,1)S(1)} %get-tuple-element.48), channel_id=1, source_target_pairs={{0,0},{8,16},{16,8},{24,24},{1,1},{9,17},{17,9},{25,25},{2,2},{10,... | collective-permute-start | bytes 356360 | tf_op jit(solution)/shard_map/ppermute | solution.py:452
  34.9 1.5 %collective-permute-start.15 = (s16[464,128]{1,0:T(8,128)(2,1)S(1)}, s16[464,128]{1,0:T(8,128)(2,1)S(1)}, u32[]{:S(2)}, u32[]{:S(2)}) collective-permute-start(s16[464,128]{1,0:T(8,128)(2,1)S(1)} %get-tuple-element.64), channel_id=1, source_target_pairs={{0,0},{8,8},{16,24},{24,16},{1,1},{9,9},{17,25},{25,17},{2,2},{10,... | collective-permute-start | bytes 356360 | tf_op jit(solution)/shard_map/ppermute | solution.py:452
  35.6 1.5 %collective-permute-start.7 = (s16[464,128]{1,0:T(8,128)(2,1)S(1)}, s16[464,128]{1,0:T(8,128)(2,1)S(1)}, u32[]{:S(2)}, u32[]{:S(2)}) collective-permute-start(s16[464,128]{1,0:T(8,128)(2,1)S(1)} %get-tuple-element.50), channel_id=1, source_target_pairs={{0,0},{8,8},{16,24},{24,16},{1,1},{9,9},{17,25},{25,17},{2,2},{10,... | collective-permute-start | bytes 356360 | tf_op jit(solution)/shard_map/ppermute | solution.py:452
  36.4 1.5 %collective-permute-start.16 = (s16[464,128]{1,0:T(8,128)(2,1)S(1)}, s16[464,128]{1,0:T(8,128)(2,1)S(1)}, u32[]{:S(2)}, u32[]{:S(2)}) collective-permute-start(s16[464,128]{1,0:T(8,128)(2,1)S(1)} %get-tuple-element.66), channel_id=1, source_target_pairs={{0,0},{8,8},{16,24},{24,16},{1,1},{9,9},{17,25},{25,17},{2,2},{10,... | collective-permute-start | bytes 356360 | tf_op jit(solution)/shard_map/ppermute | solution.py:452
  37.2 1.5 %collective-permute-start.8 = (s16[464,128]{1,0:T(8,128)(2,1)S(1)}, s16[464,128]{1,0:T(8,128)(2,1)S(1)}, u32[]{:S(2)}, u32[]{:S(2)}) collective-permute-start(s16[464,128]{1,0:T(8,128)(2,1)S(1)} %get-tuple-element.52), channel_id=1, source_target_pairs={{0,0},{8,8},{16,24},{24,16},{1,1},{9,9},{17,25},{25,17},{2,2},{10,... | collective-permute-start | bytes 356360 | tf_op jit(solution)/shard_map/ppermute | solution.py:452
  38.0 1.5 %collective-permute-start.17 = (s16[464,128]{1,0:T(8,128)(2,1)S(1)}, s16[464,128]{1,0:T(8,128)(2,1)S(1)}, u32[]{:S(2)}, u32[]{:S(2)}) collective-permute-start(s16[464,128]{1,0:T(8,128)(2,1)S(1)} %get-tuple-element.68), channel_id=1, source_target_pairs={{0,0},{8,16},{16,8},{24,24},{1,1},{9,17},{17,9},{25,25},{2,2},{10,... | collective-permute-start | bytes 356360 | tf_op jit(solution)/shard_map/ppermute | solution.py:465
  38.7 25.1 %collective-permute-start.9 = (s16[464,128]{1,0:T(8,128)(2,1)S(1)}, s16[464,128]{1,0:T(8,128)(2,1)S(1)}, u32[]{:S(2)}, u32[]{:S(2)}) collective-permute-start(s16[464,128]{1,0:T(8,128)(2,1)S(1)} %get-tuple-element.54), channel_id=1, source_target_pairs={{0,0},{8,16},{16,8},{24,24},{1,1},{9,17},{17,9},{25,25},{2,2},{10,... | collective-permute-start | bytes 356360 | tf_op jit(solution)/shard_map/ppermute | solution.py:465
  39.7 28.3 %collective-permute-start.18 = (s16[464,128]{1,0:T(8,128)(2,1)S(1)}, s16[464,128]{1,0:T(8,128)(2,1)S(1)}, u32[]{:S(2)}, u32[]{:S(2)}) collective-permute-start(s16[464,128]{1,0:T(8,128)(2,1)S(1)} %get-tuple-element.70), channel_id=1, source_target_pairs={{0,8},{8,0},{16,16},{24,24},{1,9},{9,1},{17,17},{25,25},{2,10},{10... | collective-permute-start | bytes 356360 | tf_op jit(solution)/shard_map/ppermute | solution.py:465
  63.9 6.9 %collective-permute-start.10 = (s16[464,128]{1,0:T(8,128)(2,1)S(1)}, s16[464,128]{1,0:T(8,128)(2,1)S(1)}, u32[]{:S(2)}, u32[]{:S(2)}) collective-permute-start(s16[464,128]{1,0:T(8,128)(2,1)S(1)} %get-tuple-element.56), channel_id=1, source_target_pairs={{0,8},{8,0},{16,16},{24,24},{1,9},{9,1},{17,17},{25,25},{2,10},{10... | collective-permute-start | bytes 356360 | tf_op jit(solution)/shard_map/ppermute | solution.py:465

commit v3 on v2

--- a/solution.py
+++ b/solution.py
@@ -20,7 +20,8 @@
 LANES = 128
 TOP = 32767.0
 VMEM = pltpu.VMEM
-CHUNKS = 2
+CHUNKS = 4
+HALO_CHUNKS = 2
 
 
 def scale_of(code):
@@ -47,26 +48,21 @@
     return coded_ref[index * rows : (index + 1) * rows, :].astype(jnp.int32).astype(jnp.float32) * scale
 
 
-def encode_kernel(chunks, both_k, state_ref, wall_ref, *outs):
+def encode_kernel(start, width, state_ref, out_ref):
+    planes, nv, rows, _ = state_ref.shape
+    places = [
+        (p, v, start + b * LANES) for p in range(planes) for v in range(nv) for b in range(width // LANES)
+    ]
+    most = None
+    for p, v, at in places:
+        size = jnp.abs(state_ref[p, v, :, at : at + LANES])
+        most = size if most is None else jnp.maximum(most, size)
+    blocks = [(lambda p=p, v=v, at=at: state_ref[p, v, :, at : at + LANES]) for p, v, at in places]
+    put_coded(blocks, most, out_ref, rows)
+
+
+def edges_kernel(both_k, state_ref, after_ref, j_first, j_second, *edges_k):
     planes, nv, rows, columns = state_ref.shape
-    coded, (j_first, j_second), edges_k, open_ref = outs[:chunks], outs[chunks : chunks + 2], outs[chunks + 2 : -1], outs[-1]
-    width = columns // chunks
-    for chunk, out_ref in enumerate(coded):
-        places = [
-            (p, v, chunk * width + b * LANES)
-            for p in range(planes)
-            for v in range(nv)
-            for b in range(width // LANES)
-        ]
-        most = None
-        for p, v, at in places:
-            size = jnp.abs(state_ref[p, v, :, at : at + LANES])
-            most = size if most is None else jnp.maximum(most, size)
-        blocks = [
-            (lambda p=p, v=v, at=at: state_ref[p, v, :, at : at + LANES]) for p, v, at in places
-        ]
-        put_coded(blocks, most, out_ref, rows)
-    open_ref[...] = 1.0 - wall_ref[...].astype(jnp.float32)
 
     def rows_for(next_ref, previous_ref):
         for p in range(planes):
@@ -112,8 +108,9 @@
             columns_for_next(edges_k[1])
 
 
-def local_kernel(state_ref, *refs):
-    x_outs, rows_pad = refs[:-1], refs[-1]
+def local_kernel(state_ref, wall_ref, *refs):
+    x_outs, open_ref, rows_pad = refs[:-2], refs[-2], refs[-1]
+    open_ref[...] = 1.0 - wall_ref[...].astype(jnp.float32)
     planes, nv, rows, columns = state_ref.shape
     width = columns // len(x_outs)
     nothing = jnp.zeros((rows, LANES), jnp.float32)
@@ -141,15 +138,6 @@
                 x_out[p, v] = total
 
 
-def add_plane_terms(coded, x_ref, p, v, block, terms, scale, per):
-    nv, rows = x_ref.shape[1:3]
-    own = slice(block * LANES, (block + 1) * LANES)
-    total = x_ref[p, v, :, own]
-    for q, factor in terms:
-        total += factor * get_coded(coded, (q * nv + v) * per + block, rows, scale)
-    return total
-
-
 def terms_ahead(planes, p):
     found = [(p + shift - planes, factor) for shift, factor in ((1, NEAR), (2, FAR))]
     return [(q, factor) for q, factor in found if q >= 0]
@@ -160,21 +148,25 @@
     return [(q, factor) for q, factor in found if q < planes]
 
 
-def halo_kernel(chunk, chunks, counts, j_first, j_second, edges_k, neighbour, open_ref, x_in, x_out):
-    planes, nv, rows, width = x_out.shape
+def halo_kernel(half, halves, counts, j_first, j_second, edges_k, neighbour, open_ref, x_ins, x_outs):
+    planes, nv, rows, width = x_outs[0].shape
     per = width // LANES
-    start = chunk * width
+    parts = len(x_outs)
+    start = half * parts * width
     place_i, place_j, place_k = (lax.axis_index(name) for name in ("ia", "ja", "ka"))
     count_i, count_j, count_k = counts
-    scale = get_scale(neighbour, planes * nv * per, rows)
+    scale = get_scale(neighbour, planes * nv * per * parts, rows)
     even_i = place_i % 2 == 0
 
     def with_planes(terms_of):
         for p in range(planes):
             for v in range(nv):
-                for block in range(per):
-                    own = slice(block * LANES, (block + 1) * LANES)
-                    x_out[p, v, :, own] = add_plane_terms(neighbour, x_in, p, v, block, terms_of(planes, p), scale, per)
+                for block in range(per * parts):
+                    own = slice(block % per * LANES, (block % per + 1) * LANES)
+                    total = x_ins[block // per][p, v, :, own]
+                    for q, factor in terms_of(planes, p):
+                        total += factor * get_coded(neighbour, (q * nv + v) * per * parts + block, rows, scale)
+                    x_outs[block // per][p, v, :, own] = total
 
     takes_ahead = jnp.logical_and(even_i, place_i + 1 < count_i)
     takes_behind = jnp.logical_not(even_i)
@@ -184,6 +176,7 @@
         pl.when(place_i == count_i - 1)(lambda: with_planes(lambda planes, p: []))
 
     even_j = place_j % 2 == 0
+    odd_j = jnp.logical_not(even_j)
     from_next = place_j + 1 < count_j
     from_previous = place_j > 0
 
@@ -191,11 +184,12 @@
         at = 0 if low else rows - 2
         for p in range(planes):
             for v in range(nv):
-                x_out[p, v, at : at + 2, :] += ref[p, v, :, start : start + width]
+                for part, x_out in enumerate(x_outs):
+                    first = start + part * width
+                    x_out[p, v, at : at + 2, :] += ref[p, v, :, first : first + width]
 
     pl.when(jnp.logical_and(even_j, from_next))(lambda: add_rows(j_first, False))
     pl.when(jnp.logical_and(even_j, from_previous))(lambda: add_rows(j_second, True))
-    odd_j = jnp.logical_not(even_j)
     pl.when(odd_j)(lambda: add_rows(j_first, True))
     pl.when(jnp.logical_and(odd_j, from_next))(lambda: add_rows(j_second, False))
 
@@ -204,23 +198,26 @@
 
     def add_columns(ref, low):
         at = 0 if low else width - LANES
+        x_out = x_outs[0 if low else -1]
         for p in range(planes):
             for v in range(nv):
                 x_out[p, v, :, at : at + LANES] += ref[p, v]
 
-    if chunk == 0:
+    if half == 0:
         pl.when(odd_k)(lambda: add_columns(edges_k[0], True))
         if len(edges_k) > 1:
             pl.when(jnp.logical_and(even_k, place_k > 0))(lambda: add_columns(edges_k[1], True))
-    if chunk == chunks - 1:
+    if half == halves - 1:
         pl.when(jnp.logical_and(even_k, place_k + 1 < count_k))(lambda: add_columns(edges_k[0], False))
         if len(edges_k) > 1:
             pl.when(jnp.logical_and(odd_k, place_k + 1 < count_k))(lambda: add_columns(edges_k[1], False))
 
     for p in range(planes):
-        open_cells = open_ref[p, :, start : start + width]
-        for v in range(nv):
-            x_out[p, v] = open_cells * x_out[p, v]
+        for part, x_out in enumerate(x_outs):
+            first = start + part * width
+            open_cells = open_ref[p, :, first : first + width]
+            for v in range(nv):
+                x_out[p, v] = open_cells * x_out[p, v]
 
 
 def apply_block(inverse_ref, p, at, vector):
@@ -234,7 +231,7 @@
     return result
 
 
-def forward_part(chunk, hop, count, inverse_ref, coupling_ref, open_ref, neighbour, face, x_in, x_out, send):
+def forward_part(chunk, parts, hop, count, inverse_ref, coupling_ref, open_ref, neighbour, face, x_in, x_out, send):
     planes, nv, rows, width = x_out.shape
     per = width // LANES
     first = hop == 0
@@ -246,7 +243,8 @@
         elif hop < count - 1:
             terms_of = terms_ahead
     if terms_of is not None:
-        scale = get_scale(neighbour, planes * nv * per, rows)
+        scale = get_scale(neighbour, planes * nv * per * parts, rows)
+    skip = chunk % parts * per
     most = None
     for block in range(per):
         own = slice(block * LANES, (block + 1) * LANES)
@@ -264,7 +262,7 @@
                 if terms_of is not None:
                     extra = None
                     for q, weight in terms_of(planes, p):
-                        term = weight * get_coded(neighbour, (q * nv + v) * per + block, rows, scale)
+                        term = weight * get_coded(neighbour, (q * nv + v) * per * parts + skip + block, rows, scale)
                         extra = term if extra is None else extra + term
                     if extra is not None:
                         entry += open_cells * extra
@@ -320,14 +318,15 @@
         put_face(0, most, x_out, send)
 
 
-def forward_kernel(chunk, hop, count, inverse_ref, coupling_ref, open_ref, neighbour, face, x_in, x_out, send):
+def forward_kernel(chunk, parts, hop, count, inverse_ref, coupling_ref, open_ref, neighbour, face, x_in, x_out, send):
     active = lax.axis_index("ia") == hop
     last = hop == count - 1
 
     @pl.when(active)
     def _():
         forward_part(
-            chunk, hop, count, inverse_ref, coupling_ref, open_ref, neighbour, face, x_in, x_out, None if last else send
+            chunk, parts, hop, count, inverse_ref, coupling_ref, open_ref, neighbour, face, x_in, x_out,
+            None if last else send,
         )
         if last:
             backward_part(chunk, True, inverse_ref, coupling_ref, None, x_out, x_out, send)
@@ -372,7 +371,7 @@
     return pl.BlockSpec(memory_space=VMEM)
 
 
-def call(kernel, operands, outs, name, alias=None, scratch=()):
+def call(kernel, operands, outs, name, alias=None, scratch=(), cost=None):
     return pl.pallas_call(
         kernel,
         in_specs=[whole()] * len(operands),
@@ -380,7 +379,8 @@
         out_shape=outs,
         scratch_shapes=list(scratch),
         input_output_aliases=alias or {},
-        compiler_params=pltpu.CompilerParams(vmem_limit_bytes=24 * 2**20),
+        compiler_params=pltpu.CompilerParams(vmem_limit_bytes=12 * 2**20),
+        cost_estimate=cost,
         name=name,
     )(*operands)
 
@@ -392,21 +392,16 @@
     return list(enumerate(partner))
 
 
-def swap_of(count, low):
-    partner = list(range(count))
-    partner[low], partner[low + 1] = low + 1, low
-    return list(enumerate(partner))
-
-
 def shards(state, inverse, coupling, wall):
     planes, nv, rows, columns = state.shape
-    chunks = CHUNKS
+    chunks, halves = CHUNKS, HALO_CHUNKS
+    parts = chunks // halves
     width = columns // chunks
     per = width // LANES
     counts = count, count_j, count_k = [lax.axis_size(name) for name in ("ia", "ja", "ka")]
     sets_k = 1 if count_k == 2 else 2
 
-    halo_code = jax.ShapeDtypeStruct(((planes * nv * per + 1) * rows, LANES), jnp.int16)
+    halo_code = jax.ShapeDtypeStruct(((planes * nv * per * parts + 1) * rows, LANES), jnp.int16)
     face_code = jax.ShapeDtypeStruct(((nv * per + 1) * rows, LANES), jnp.int16)
     full = jax.ShapeDtypeStruct(state.shape, jnp.float32)
     part = jax.ShapeDtypeStruct((planes, nv, rows, width), jnp.float32)
@@ -414,55 +409,67 @@
     edge_k = jax.ShapeDtypeStruct((planes, nv, rows, LANES), jnp.float32)
     cells = jax.ShapeDtypeStruct((planes, rows, columns), jnp.float32)
 
+    coded = []
+    for h in range(halves):
+        kernel = functools.partial(encode_kernel, h * parts * width, parts * width)
+        coded += call(kernel, [state], [halo_code], "encode")
+    near = [lax.ppermute(coded[h], "ia", swaps(count, 0)) for h in range(halves)]
     made = call(
-        functools.partial(encode_kernel, chunks, sets_k == 2),
-        [state, wall],
-        [halo_code] * chunks + [edge_j] * 2 + [edge_k] * sets_k + [cells],
-        "encode",
+        functools.partial(edges_kernel, sets_k == 2), [state, coded[-1]], [edge_j] * 2 + [edge_k] * sets_k, "edges"
     )
-    coded, edges_j, edges_k, open_cells = made[:chunks], made[chunks : chunks + 2], made[chunks + 2 : -1], made[-1]
-    near = [lax.ppermute(coded[c], "ia", swaps(count, 0)) for c in range(chunks)]
+    edges_j, edges_k = made[:2], made[2:]
     edges_k = [lax.ppermute(edge, "ka", swaps(count_k, s)) for s, edge in enumerate(edges_k)]
     edges_j = [lax.ppermute(edge, "ja", swaps(count_j, s)) for s, edge in enumerate(edges_j)]
-    local = call(local_kernel, [state], [part] * chunks, "local", None, [VMEM((rows + 16, width), jnp.float32)])
-
-    x, far = [], []
-    for c in range(chunks):
-        later, _ = lax.optimization_barrier((coded[c], near[c]))
-        far.append(lax.ppermute(later, "ia", swaps(count, 1)))
-
-        def kernel(*refs, c=c):
-            rest = refs[2 + sets_k :]
-            halo_kernel(c, chunks, counts, *refs[:2], refs[2 : 2 + sets_k], *rest)
-
-        operands = [*edges_j, *edges_k, near[c], open_cells, local[c]]
-        x += call(kernel, operands, [part], "halo", {len(operands) - 1: 0})
-
-    face = [None] * chunks
-    for hop in range(count):
+    size = state.size
+    *local, open_cells = call(
+        local_kernel,
+        [state, wall],
+        [part] * chunks + [cells],
+        "local",
+        None,
+        [VMEM((rows + 16, width), jnp.float32)],
+        pl.CostEstimate(flops=40 * size, bytes_accessed=10 * size, transcendentals=0),
+    )
+
+    def hop_pair(value, source, target):
+        return lax.ppermute(value, "ia", [(source, target)])
+
+    gated = lax.optimization_barrier((*coded, open_cells, *edges_j, *edges_k))[:halves]
+    far = [lax.ppermute(value, "ia", swaps(count, 1)) for value in gated]
+    x, face = [], [None] * chunks
+    for h in range(halves):
+        def kernel(*refs, h=h):
+            rest = refs[2 + sets_k : 4 + sets_k]
+            xs = refs[4 + sets_k :]
+            halo_kernel(h, halves, counts, *refs[:2], refs[2 : 2 + sets_k], *rest, xs[:parts], xs[parts:])
+
+        operands = [*edges_j, *edges_k, near[h], open_cells, *local[h * parts : (h + 1) * parts]]
+        first = len(operands) - parts
+        x += call(kernel, operands, [part] * parts, "halo", {first + i: i for i in range(parts)})
+        for c in range(h * parts, (h + 1) * parts):
+            def kernel(inverse_ref, coupling_ref, *refs, c=c):
+                forward_kernel(c, parts, 0, count, inverse_ref, coupling_ref, None, None, None, *refs)
+
+            x[c], send = call(kernel, [inverse, coupling, x[c]], [part, face_code], "forward", {2: 0})
+            face[c] = hop_pair(send, 0, 1)
+
+    for hop in range(1, count):
         for c in range(chunks):
-            if hop == 0:
-                def kernel(inverse_ref, coupling_ref, *refs, c=c):
-                    forward_kernel(c, 0, count, inverse_ref, coupling_ref, None, None, None, *refs)
-                operands = [inverse, coupling, x[c]]
-            else:
-                kernel = functools.partial(forward_kernel, c, hop, count)
-                operands = [inverse, coupling, open_cells, far[c], face[c], x[c]]
-            x[c], send = call(kernel, operands, [part, face_code], "forward", {len(operands) - 1: 0})
-            face[c] = lax.ppermute(send, "ia", swap_of(count, min(hop, count - 2)))
-    for hop in reversed(range(count - 1)):
+            kernel = functools.partial(forward_kernel, c, parts, hop, count)
+            operands = [inverse, coupling, open_cells, far[c // parts], face[c], x[c]]
+            x[c], send = call(kernel, operands, [part, face_code], "forward", {5: 0})
+            face[c] = hop_pair(send, hop, hop + 1) if hop < count - 1 else hop_pair(send, hop, hop - 1)
+    for hop in reversed(range(1, count - 1)):
         for c in range(chunks):
-            if hop == 0 and c == chunks - 1:
-                operands = [inverse, coupling, face[c], *x]
-                return call(functools.partial(final_kernel, c), operands, [full], "last")[0]
-            if hop == 0:
-                def kernel(*refs, c=c):
-                    backward_kernel(c, 0, *refs, None)
-                (x[c],) = call(kernel, [inverse, coupling, face[c], x[c]], [part], "backward", {3: 0})
-                continue
             kernel = functools.partial(backward_kernel, c, hop)
             x[c], send = call(kernel, [inverse, coupling, face[c], x[c]], [part, face_code], "backward", {3: 0})
-            face[c] = lax.ppermute(send, "ia", swap_of(count, hop - 1))
+            face[c] = hop_pair(send, hop, hop - 1)
+    for c in range(chunks - 1):
+        def kernel(*refs, c=c):
+            backward_kernel(c, 0, *refs, None)
+
+        (x[c],) = call(kernel, [inverse, coupling, face[c], x[c]], [part], "backward", {3: 0})
+    return call(functools.partial(final_kernel, chunks - 1), [inverse, coupling, face[-1], *x], [full], "last")[0]
 
 
 def solution(mesh):

time: 72.7 us -> 64.1 us (0.88)
  the two profiles are of different devices: /device:TPU:0 before, /device:TPU:8 now
where the time goes in v3:
time: 64.1 us; the launch traced here: 63.4 us
  starting transfers between devices  39.2 us (61%)
  waiting for transfers between devices  14.2 us (22%)
  Pallas kernels  6.77 us (11%)
  local copies, waits for them, and re-layouts  2.32 us (4%)
  between operations  0.96 us (1%)
    ppermute x24, starting transfers between devices, hop_pair(): return lax.ppermute(value, 'ia', [(source, target)])  30.5 us
    ppermute x24, waiting for transfers between devices, hop_pair(): return lax.ppermute(value, 'ia', [(source, target)])  14.2 us
    pallas_call x34, Pallas kernels, call(): pl.pallas_call(kernel, in_specs=[whole()] * len(operands), out_specs=[who...  6.77 us
    ppermute x2, starting transfers between devices, shards(): lax.ppermute(edge, 'ja', swaps(count_j, s))  5.11 us
    unnamed x40, local copies, waits for them, and re-layouts  2.32 us
    ppermute x2, starting transfers between devices, shards(): lax.ppermute(coded[h], 'ia', swaps(count, 0))  2.16 us
    ppermute x2, starting transfers between devices, shards(): far = [lax.ppermute(value, 'ia', swaps(count, 1)) for value in gated]  1.35 us
  transfers between devices with their start and end apart: 31, of which 4 were waited for; matrix products, arithmetic and copies ran while one was open for 0% of the time, Pallas kernels for 9%

profile of v3, /device:TPU:8, one launch (start us, length us, event | category | flops | bytes accessed | tf_op | source)
XLA Modules:
  0.0 63.4 jit_solution(3457042255525393743)
XLA Ops:
  0.0 1.3 %copy-done.14 = f32[2,7,16,1024]{3,2,1,0:T(8,128)S(1)} copy-done((f32[2,7,16,1024]{3,2,1,0:T(8,128)S(1)}, f32[2,7,16,1024]{3,2,1,0:T(8,128)}, u32[]{:S(2)}) %copy-start.14) | copy-done | bytes 917528
  1.5 1.6 %collective-permute-start.4 = (s16[912,128]{1,0:T(8,128)(2,1)S(1)}, s16[912,128]{1,0:T(8,128)(2,1)S(1)}, u32[]{:S(2)}, u32[]{:S(2)}) collective-permute-start(s16[912,128]{1,0:T(8,128)(2,1)S(1)} %encode.3.after_ref), channel_id=1, source_target_pairs={{0,8},{8,0},{16,24},{24,16},{1,9},{9,1},{17,25},{25,17},{2,10},{10... | collective-permute-start | bytes 700424 | tf_op jit(solution)/shard_map/ppermute | solution.py:416
  3.3 0.5 collective-permute-start
  3.8 4.6 %collective-permute-start.1 = (f32[2,7,2,1024]{3,2,1,0:T(2,128)S(1)}, f32[2,7,2,1024]{3,2,1,0:T(2,128)S(1)}, u32[]{:S(2)}, u32[]{:S(2)}) collective-permute-start(f32[2,7,2,1024]{3,2,1,0:T(2,128)S(1)} %get-tuple-element.69), channel_id=1, source_target_pairs={{0,0},{2,4},{4,2},{6,6},{1,1},{3,5},{5,3},{7,7},{8,8},{10,12},{12,... | collective-permute-start | bytes 344072 | tf_op jit(solution)/shard_map/ppermute | solution.py:422
  8.6 0.6 collective-permute-start.12
  9.2 0.9 %copy-done.19 = s32[2,16,1024]{2,1,0:T(8,128)S(1)} copy-done((s32[2,16,1024]{2,1,0:T(8,128)S(1)}, s32[2,16,1024]{2,1,0:T(8,128)}, u32[]{:S(2)}) %copy-start.19) | copy-done | bytes 131096
  10.1 1.4 %local.1 = (f32[2,7,16,256]{3,2,1,0:T(8,128)S(1)}, f32[2,7,16,256]{3,2,1,0:T(8,128)S(1)}, f32[2,7,16,256]{3,2,1,0:T(8,128)S(1)}, f32[2,7,16,256]{3,2,1,0:T(8,128)S(1)}, f32[2,16,1024]{2,1,0:T(8,128)S(1)}) custom-call(f32[2,7,16,1024]{3,2,1,0:T(8,128)S(1)} %copy-done.14, s32[2,16,1024]{2,1,0:T(8,128)S(1)} %copy-done.19), custom_call_target="tpu_custom_call" | custom-call | flops 9175040 | bytes 2293760 | tf_op jit(solution)/shard_map/local/pallas_call | solution.py:375
  11.5 0.7 %collective-permute-start.3 = (s16[912,128]{1,0:T(8,128)(2,1)S(1)}, s16[912,128]{1,0:T(8,128)(2,1)S(1)}, u32[]{:S(2)}, u32[]{:S(2)}) collective-permute-start(s16[912,128]{1,0:T(8,128)(2,1)S(1)} %encode.3.after_ref), channel_id=1, source_target_pairs={{0,0},{8,16},{16,8},{24,24},{1,1},{9,17},{17,9},{25,25},{2,2},{10,... | collective-permute-start | bytes 700424 | tf_op jit(solution)/shard_map/ppermute | solution.py:438
  12.2 0.7 %collective-permute-start.11 = (s16[912,128]{1,0:T(8,128)(2,1)S(1)}, s16[912,128]{1,0:T(8,128)(2,1)S(1)}, u32[]{:S(2)}, u32[]{:S(2)}) collective-permute-start(s16[912,128]{1,0:T(8,128)(2,1)S(1)} %encode.2), channel_id=1, source_target_pairs={{0,0},{8,16},{16,8},{24,24},{1,1},{9,17},{17,9},{25,25},{2,2},{10,... | collective-permute-start | bytes 700424 | tf_op jit(solution)/shard_map/ppermute | solution.py:438
  12.9 0.3 halo.2
  13.2 0.3 forward.28
  13.5 8.6 %collective-permute-start.25 = (s16[240,128]{1,0:T(8,128)(2,1)S(1)}, s16[240,128]{1,0:T(8,128)(2,1)S(1)}, u32[]{:S(2)}, u32[]{:S(2)}) collective-permute-start(s16[240,128]{1,0:T(8,128)(2,1)S(1)} %get-tuple-element.116), channel_id=1, source_target_pairs={{0,8},{1,9},{2,10},{3,11},{4,12},{5,13},{6,14},{7,15}} | collective-permute-start | bytes 184328 | tf_op jit(solution)/shard_map/ppermute | solution.py:435
  22.1 0.3 halo.3
  22.4 0.3 forward.24
  22.7 1.3 %collective-permute-start.19 = (s16[240,128]{1,0:T(8,128)(2,1)S(1)}, s16[240,128]{1,0:T(8,128)(2,1)S(1)}, u32[]{:S(2)}, u32[]{:S(2)}) collective-permute-start(s16[240,128]{1,0:T(8,128)(2,1)S(1)} %get-tuple-element.103), channel_id=1, source_target_pairs={{0,8},{1,9},{2,10},{3,11},{4,12},{5,13},{6,14},{7,15}} | collective-permute-start | bytes 184328 | tf_op jit(solution)/shard_map/ppermute | solution.py:435
  24.0 0.3 forward.20
  24.2 1.3 %collective-permute-start.13 = (s16[240,128]{1,0:T(8,128)(2,1)S(1)}, s16[240,128]{1,0:T(8,128)(2,1)S(1)}, u32[]{:S(2)}, u32[]{:S(2)}) collective-permute-start(s16[240,128]{1,0:T(8,128)(2,1)S(1)} %get-tuple-element.90), channel_id=1, source_target_pairs={{0,8},{1,9},{2,10},{3,11},{4,12},{5,13},{6,14},{7,15}} | collective-permute-start | bytes 184328 | tf_op jit(solution)/shard_map/ppermute | solution.py:435
  25.6 0.3 forward.16
  25.9 2.5 %collective-permute-start.5 = (s16[240,128]{1,0:T(8,128)(2,1)S(1)}, s16[240,128]{1,0:T(8,128)(2,1)S(1)}, u32[]{:S(2)}, u32[]{:S(2)}) collective-permute-start(s16[240,128]{1,0:T(8,128)(2,1)S(1)} %get-tuple-element.75), channel_id=1, source_target_pairs={{0,8},{1,9},{2,10},{3,11},{4,12},{5,13},{6,14},{7,15}} | collective-permute-start | bytes 184328 | tf_op jit(solution)/shard_map/ppermute | solution.py:435
  28.4 0.7 %collective-permute-start.26 = (s16[240,128]{1,0:T(8,128)(2,1)S(1)}, s16[240,128]{1,0:T(8,128)(2,1)S(1)}, u32[]{:S(2)}, u32[]{:S(2)}) collective-permute-start(s16[240,128]{1,0:T(8,128)(2,1)S(1)} %get-tuple-element.118), channel_id=1, source_target_pairs={{8,16},{9,17},{10,18},{11,19},{12,20},{13,21},{14,22},{15,23}} | collective-permute-start | bytes 184328 | tf_op jit(solution)/shard_map/ppermute | solution.py:435
  29.2 0.7 %collective-permute-start.20 = (s16[240,128]{1,0:T(8,128)(2,1)S(1)}, s16[240,128]{1,0:T(8,128)(2,1)S(1)}, u32[]{:S(2)}, u32[]{:S(2)}) collective-permute-start(s16[240,128]{1,0:T(8,128)(2,1)S(1)} %get-tuple-element.105), channel_id=1, source_target_pairs={{8,16},{9,17},{10,18},{11,19},{12,20},{13,21},{14,22},{15,23}} | collective-permute-start | bytes 184328 | tf_op jit(solution)/shard_map/ppermute | solution.py:435
  29.9 0.7 %collective-permute-start.14 = (s16[240,128]{1,0:T(8,128)(2,1)S(1)}, s16[240,128]{1,0:T(8,128)(2,1)S(1)}, u32[]{:S(2)}, u32[]{:S(2)}) collective-permute-start(s16[240,128]{1,0:T(8,128)(2,1)S(1)} %get-tuple-element.92), channel_id=1, source_target_pairs={{8,16},{9,17},{10,18},{11,19},{12,20},{13,21},{14,22},{15,23}} | collective-permute-start | bytes 184328 | tf_op jit(solution)/shard_map/ppermute | solution.py:435
  30.6 0.7 %collective-permute-start.6 = (s16[240,128]{1,0:T(8,128)(2,1)S(1)}, s16[240,128]{1,0:T(8,128)(2,1)S(1)}, u32[]{:S(2)}, u32[]{:S(2)}) collective-permute-start(s16[240,128]{1,0:T(8,128)(2,1)S(1)} %get-tuple-element.77), channel_id=1, source_target_pairs={{8,16},{9,17},{10,18},{11,19},{12,20},{13,21},{14,22},{15,23}} | collective-permute-start | bytes 184328 | tf_op jit(solution)/shard_map/ppermute | solution.py:435
  31.4 0.7 %collective-permute-start.27 = (s16[240,128]{1,0:T(8,128)(2,1)S(1)}, s16[240,128]{1,0:T(8,128)(2,1)S(1)}, u32[]{:S(2)}, u32[]{:S(2)}) collective-permute-start(s16[240,128]{1,0:T(8,128)(2,1)S(1)} %get-tuple-element.120), channel_id=1, source_target_pairs={{16,24},{17,25},{18,26},{19,27},{20,28},{21,29},{22,30},{23,31}} | collective-permute-start | bytes 184328 | tf_op jit(solution)/shard_map/ppermute | solution.py:435
  32.1 0.7 %collective-permute-start.21 = (s16[240,128]{1,0:T(8,128)(2,1)S(1)}, s16[240,128]{1,0:T(8,128)(2,1)S(1)}, u32[]{:S(2)}, u32[]{:S(2)}) collective-permute-start(s16[240,128]{1,0:T(8,128)(2,1)S(1)} %get-tuple-element.107), channel_id=1, source_target_pairs={{16,24},{17,25},{18,26},{19,27},{20,28},{21,29},{22,30},{23,31}} | collective-permute-start | bytes 184328 | tf_op jit(solution)/shard_map/ppermute | solution.py:435
  32.9 0.7 %collective-permute-start.15 = (s16[240,128]{1,0:T(8,128)(2,1)S(1)}, s16[240,128]{1,0:T(8,128)(2,1)S(1)}, u32[]{:S(2)}, u32[]{:S(2)}) collective-permute-start(s16[240,128]{1,0:T(8,128)(2,1)S(1)} %get-tuple-element.94), channel_id=1, source_target_pairs={{16,24},{17,25},{18,26},{19,27},{20,28},{21,29},{22,30},{23,31}} | collective-permute-start | bytes 184328 | tf_op jit(solution)/shard_map/ppermute | solution.py:435
  33.6 0.7 %collective-permute-start.7 = (s16[240,128]{1,0:T(8,128)(2,1)S(1)}, s16[240,128]{1,0:T(8,128)(2,1)S(1)}, u32[]{:S(2)}, u32[]{:S(2)}) collective-permute-start(s16[240,128]{1,0:T(8,128)(2,1)S(1)} %get-tuple-element.79), channel_id=1, source_target_pairs={{16,24},{17,25},{18,26},{19,27},{20,28},{21,29},{22,30},{23,31}} | collective-permute-start | bytes 184328 | tf_op jit(solution)/shard_map/ppermute | solution.py:435
  34.4 0.7 %collective-permute-start.28 = (s16[240,128]{1,0:T(8,128)(2,1)S(1)}, s16[240,128]{1,0:T(8,128)(2,1)S(1)}, u32[]{:S(2)}, u32[]{:S(2)}) collective-permute-start(s16[240,128]{1,0:T(8,128)(2,1)S(1)} %get-tuple-element.122), channel_id=1, source_target_pairs={{24,16},{25,17},{26,18},{27,19},{28,20},{29,21},{30,22},{31,23}} | collective-permute-start | bytes 184328 | tf_op jit(solution)/shard_map/ppermute | solution.py:435
  35.1 0.7 %collective-permute-start.22 = (s16[240,128]{1,0:T(8,128)(2,1)S(1)}, s16[240,128]{1,0:T(8,128)(2,1)S(1)}, u32[]{:S(2)}, u32[]{:S(2)}) collective-permute-start(s16[240,128]{1,0:T(8,128)(2,1)S(1)} %get-tuple-element.109), channel_id=1, source_target_pairs={{24,16},{25,17},{26,18},{27,19},{28,20},{29,21},{30,22},{31,23}} | collective-permute-start | bytes 184328 | tf_op jit(solution)/shard_map/ppermute | solution.py:435
  35.9 0.8 %collective-permute-start.16 = (s16[240,128]{1,0:T(8,128)(2,1)S(1)}, s16[240,128]{1,0:T(8,128)(2,1)S(1)}, u32[]{:S(2)}, u32[]{:S(2)}) collective-permute-start(s16[240,128]{1,0:T(8,128)(2,1)S(1)} %get-tuple-element.96), channel_id=1, source_target_pairs={{24,16},{25,17},{26,18},{27,19},{28,20},{29,21},{30,22},{31,23}} | collective-permute-start | bytes 184328 | tf_op jit(solution)/shard_map/ppermute | solution.py:435
  36.8 0.8 %collective-permute-start.8 = (s16[240,128]{1,0:T(8,128)(2,1)S(1)}, s16[240,128]{1,0:T(8,128)(2,1)S(1)}, u32[]{:S(2)}, u32[]{:S(2)}) collective-permute-start(s16[240,128]{1,0:T(8,128)(2,1)S(1)} %get-tuple-element.81), channel_id=1, source_target_pairs={{24,16},{25,17},{26,18},{27,19},{28,20},{29,21},{30,22},{31,23}} | collective-permute-start | bytes 184328 | tf_op jit(solution)/shard_map/ppermute | solution.py:435
  37.7 0.8 %collective-permute-start.29 = (s16[240,128]{1,0:T(8,128)(2,1)S(1)}, s16[240,128]{1,0:T(8,128)(2,1)S(1)}, u32[]{:S(2)}, u32[]{:S(2)}) collective-permute-start(s16[240,128]{1,0:T(8,128)(2,1)S(1)} %get-tuple-element.124), channel_id=1, source_target_pairs={{16,8},{17,9},{18,10},{19,11},{20,12},{21,13},{22,14},{23,15}} | collective-permute-start | bytes 184328 | tf_op jit(solution)/shard_map/ppermute | solution.py:435
  38.6 0.8 %collective-permute-start.23 = (s16[240,128]{1,0:T(8,128)(2,1)S(1)}, s16[240,128]{1,0:T(8,128)(2,1)S(1)}, u32[]{:S(2)}, u32[]{:S(2)}) collective-permute-start(s16[240,128]{1,0:T(8,128)(2,1)S(1)} %get-tuple-element.111), channel_id=1, source_target_pairs={{16,8},{17,9},{18,10},{19,11},{20,12},{21,13},{22,14},{23,15}} | collective-permute-start | bytes 184328 | tf_op jit(solution)/shard_map/ppermute | solution.py:435
  39.4 0.2 backward.13
  39.7 0.8 %collective-permute-start.17 = (s16[240,128]{1,0:T(8,128)(2,1)S(1)}, s16[240,128]{1,0:T(8,128)(2,1)S(1)}, u32[]{:S(2)}, u32[]{:S(2)}) collective-permute-start(s16[240,128]{1,0:T(8,128)(2,1)S(1)} %get-tuple-element.98), channel_id=1, source_target_pairs={{16,8},{17,9},{18,10},{19,11},{20,12},{21,13},{22,14},{23,15}} | collective-permute-start | bytes 184328 | tf_op jit(solution)/shard_map/ppermute | solution.py:435
  40.6 0.8 %collective-permute-start.9 = (s16[240,128]{1,0:T(8,128)(2,1)S(1)}, s16[240,128]{1,0:T(8,128)(2,1)S(1)}, u32[]{:S(2)}, u32[]{:S(2)}) collective-permute-start(s16[240,128]{1,0:T(8,128)(2,1)S(1)} %get-tuple-element.83), channel_id=1, source_target_pairs={{16,8},{17,9},{18,10},{19,11},{20,12},{21,13},{22,14},{23,15}} | collective-permute-start | bytes 184328 | tf_op jit(solution)/shard_map/ppermute | solution.py:435
  41.5 1.4 %collective-permute-start.30 = (s16[240,128]{1,0:T(8,128)(2,1)S(1)}, s16[240,128]{1,0:T(8,128)(2,1)S(1)}, u32[]{:S(2)}, u32[]{:S(2)}) collective-permute-start(s16[240,128]{1,0:T(8,128)(2,1)S(1)} %get-tuple-element.126), channel_id=1, source_target_pairs={{8,0},{9,1},{10,2},{11,3},{12,4},{13,5},{14,6},{15,7}} | collective-permute-start | bytes 184328 | tf_op jit(solution)/shard_map/ppermute | solution.py:435
  43.0 1.4 %collective-permute-start.24 = (s16[240,128]{1,0:T(8,128)(2,1)S(1)}, s16[240,128]{1,0:T(8,128)(2,1)S(1)}, u32[]{:S(2)}, u32[]{:S(2)}) collective-permute-start(s16[240,128]{1,0:T(8,128)(2,1)S(1)} %get-tuple-element.113), channel_id=1, source_target_pairs={{8,0},{9,1},{10,2},{11,3},{12,4},{13,5},{14,6},{15,7}} | collective-permute-start | bytes 184328 | tf_op jit(solution)/shard_map/ppermute | solution.py:435
  44.5 1.3 %collective-permute-start.18 = (s16[240,128]{1,0:T(8,128)(2,1)S(1)}, s16[240,128]{1,0:T(8,128)(2,1)S(1)}, u32[]{:S(2)}, u32[]{:S(2)}) collective-permute-start(s16[240,128]{1,0:T(8,128)(2,1)S(1)} %get-tuple-element.100), channel_id=1, source_target_pairs={{8,0},{9,1},{10,2},{11,3},{12,4},{13,5},{14,6},{15,7}} | collective-permute-start | bytes 184328 | tf_op jit(solution)/shard_map/ppermute | solution.py:435
  45.9 1.3 %collective-permute-start.10 = (s16[240,128]{1,0:T(8,128)(2,1)S(1)}, s16[240,128]{1,0:T(8,128)(2,1)S(1)}, u32[]{:S(2)}, u32[]{:S(2)}) collective-permute-start(s16[240,128]{1,0:T(8,128)(2,1)S(1)} %get-tuple-element.85), channel_id=1, source_target_pairs={{8,0},{9,1},{10,2},{11,3},{12,4},{13,5},{14,6},{15,7}} | collective-permute-start | bytes 184328 | tf_op jit(solution)/shard_map/ppermute | solution.py:435
  47.2 9.8 %collective-permute-done.30.refs_2_ = s16[240,128]{1,0:T(8,128)(2,1)S(1)} collective-permute-done((s16[240,128]{1,0:T(8,128)(2,1)S(1)}, s16[240,128]{1,0:T(8,128)(2,1)S(1)}, u32[]{:S(2)}, u32[]{:S(2)}) %collective-permute-start.30) | collective-permute-done | bytes 61472 | tf_op jit(solution)/shard_map/ppermute | solution.py:435
  57.0 0.3 backward.21.refs_2_
  57.3 1.7 %collective-permute-done.24.refs_2_ = s16[240,128]{1,0:T(8,128)(2,1)S(1)} collective-permute-done((s16[240,128]{1,0:T(8,128)(2,1)S(1)}, s16[240,128]{1,0:T(8,128)(2,1)S(1)}, u32[]{:S(2)}, u32[]{:S(2)}) %collective-permute-start.24) | collective-permute-done | bytes 61472 | tf_op jit(solution)/shard_map/ppermute | solution.py:435
  59.0 0.3 backward.18.refs_1_
  59.3 1.2 %collective-permute-done.18.refs_2_ = s16[240,128]{1,0:T(8,128)(2,1)S(1)} collective-permute-done((s16[240,128]{1,0:T(8,128)(2,1)S(1)}, s16[240,128]{1,0:T(8,128)(2,1)S(1)}, u32[]{:S(2)}, u32[]{:S(2)}) %collective-permute-start.18) | collective-permute-done | bytes 61472 | tf_op jit(solution)/shard_map/ppermute | solution.py:435
  60.4 0.3 backward.15.refs_0_
  60.7 1.5 %collective-permute-done.10.face = s16[240,128]{1,0:T(8,128)(2,1)S(1)} collective-permute-done((s16[240,128]{1,0:T(8,128)(2,1)S(1)}, s16[240,128]{1,0:T(8,128)(2,1)S(1)}, u32[]{:S(2)}, u32[]{:S(2)}) %collective-permute-start.10) | collective-permute-done | bytes 61472 | tf_op jit(solution)/shard_map/ppermute | solution.py:435
  62.2 1.2 %last.1 = f32[2,7,16,1024]{3,2,1,0:T(8,128)} custom-call(bf16[2,7,7,16,1024]{4,3,2,1,0:T(8,128)(2,1)S(1)} %copy-done, f32[2,2,16,1024]{3,2,1,0:T(8,128)S(1)} %copy-done.1, s16[240,128]{1,0:T(8,128)(2,1)S(1)} %collective-permute-done.10.face, f32[2,7,16,256]{3,2,1,0:T(8,128)S(1)} %backward.15.refs_0_, f32[2,7,16,256]{3,2,1,0:T(8,128)S(1)} %backward.18.refs_1_, ...), custom_call_target="tpu_custom_call" | custom-call | tf_op jit(solution)/shard_map/last/pallas_call | solution.py:375
  (88 shorter events, 1.6 us)
Async XLA Ops:
  0.0 13.2 %copy-start = (bf16[2,7,7,16,1024]{4,3,2,1,0:T(8,128)(2,1)S(1)}, bf16[2,7,7,16,1024]{4,3,2,1,0:T(8,128)(2,1)}, u32[]{:S(2)}) copy-start(bf16[2,7,7,16,1024]{4,3,2,1,0:T(8,128)(2,1)} %inverse_ref.49) | copy-start | bytes 9633796
  1.3 11.9 %copy-start.1 = (f32[2,2,16,1024]{3,2,1,0:T(8,128)S(1)}, f32[2,2,16,1024]{3,2,1,0:T(8,128)}, u32[]{:S(2)}) copy-start(f32[2,2,16,1024]{3,2,1,0:T(8,128)} %coupling_ref.49) | copy-start | bytes 786436
  1.5 11.4 %collective-permute-start.4 = (s16[912,128]{1,0:T(8,128)(2,1)S(1)}, s16[912,128]{1,0:T(8,128)(2,1)S(1)}, u32[]{:S(2)}, u32[]{:S(2)}) collective-permute-start(s16[912,128]{1,0:T(8,128)(2,1)S(1)} %encode.3.after_ref), channel_id=1, source_target_pairs={{0,8},{8,0},{16,24},{24,16},{1,9},{9,1},{17,25},{25,17},{2,10},{10... | collective-permute-start | bytes 700424 | tf_op jit(solution)/shard_map/ppermute | solution.py:416
  3.3 8.3 %collective-permute-start = (f32[2,7,2,1024]{3,2,1,0:T(2,128)S(1)}, f32[2,7,2,1024]{3,2,1,0:T(2,128)S(1)}, u32[]{:S(2)}, u32[]{:S(2)}) collective-permute-start(f32[2,7,2,1024]{3,2,1,0:T(2,128)S(1)} %get-tuple-element.68), channel_id=1, source_target_pairs={{0,2},{2,0},{4,6},{6,4},{1,3},{3,1},{5,7},{7,5},{8,10},{10,8},{12,... | collective-permute-start | bytes 344072 | tf_op jit(solution)/shard_map/ppermute | solution.py:422
  3.8 7.7 %collective-permute-start.1 = (f32[2,7,2,1024]{3,2,1,0:T(2,128)S(1)}, f32[2,7,2,1024]{3,2,1,0:T(2,128)S(1)}, u32[]{:S(2)}, u32[]{:S(2)}) collective-permute-start(f32[2,7,2,1024]{3,2,1,0:T(2,128)S(1)} %get-tuple-element.69), channel_id=1, source_target_pairs={{0,0},{2,4},{4,2},{6,6},{1,1},{3,5},{5,3},{7,7},{8,8},{10,12},{12,... | collective-permute-start | bytes 344072 | tf_op jit(solution)/shard_map/ppermute | solution.py:422
  8.4 3.2 %collective-permute-start.2 = (f32[2,7,16,128]{3,2,1,0:T(8,128)S(1)}, f32[2,7,16,128]{3,2,1,0:T(8,128)S(1)}, u32[]{:S(2)}, u32[]{:S(2)}) collective-permute-start(f32[2,7,16,128]{3,2,1,0:T(8,128)S(1)} %get-tuple-element.70), channel_id=1, source_target_pairs={{0,1},{1,0},{2,3},{3,2},{4,5},{5,4},{6,7},{7,6},{8,9},{9,8},{10,11... | collective-permute-start | bytes 344072 | tf_op jit(solution)/shard_map/ppermute | solution.py:421
  8.6 13.5 %collective-permute-start.12 = (s16[912,128]{1,0:T(8,128)(2,1)S(1)}, s16[912,128]{1,0:T(8,128)(2,1)S(1)}, u32[]{:S(2)}, u32[]{:S(2)}) collective-permute-start(s16[912,128]{1,0:T(8,128)(2,1)S(1)} %encode.2), channel_id=1, source_target_pairs={{0,8},{8,0},{16,24},{24,16},{1,9},{9,1},{17,25},{25,17},{2,10},{10... | collective-permute-start | bytes 700424 | tf_op jit(solution)/shard_map/ppermute | solution.py:416
  11.5 16.8 %collective-permute-start.3 = (s16[912,128]{1,0:T(8,128)(2,1)S(1)}, s16[912,128]{1,0:T(8,128)(2,1)S(1)}, u32[]{:S(2)}, u32[]{:S(2)}) collective-permute-start(s16[912,128]{1,0:T(8,128)(2,1)S(1)} %encode.3.after_ref), channel_id=1, source_target_pairs={{0,0},{8,16},{16,8},{24,24},{1,1},{9,17},{17,9},{25,25},{2,2},{10,... | collective-permute-start | bytes 700424 | tf_op jit(solution)/shard_map/ppermute | solution.py:438
  12.2 16.9 %collective-permute-start.11 = (s16[912,128]{1,0:T(8,128)(2,1)S(1)}, s16[912,128]{1,0:T(8,128)(2,1)S(1)}, u32[]{:S(2)}, u32[]{:S(2)}) collective-permute-start(s16[912,128]{1,0:T(8,128)(2,1)S(1)} %encode.2), channel_id=1, source_target_pairs={{0,0},{8,16},{16,8},{24,24},{1,1},{9,17},{17,9},{25,25},{2,2},{10,... | collective-permute-start | bytes 700424 | tf_op jit(solution)/shard_map/ppermute | solution.py:438
  13.5 12.3 %collective-permute-start.25 = (s16[240,128]{1,0:T(8,128)(2,1)S(1)}, s16[240,128]{1,0:T(8,128)(2,1)S(1)}, u32[]{:S(2)}, u32[]{:S(2)}) collective-permute-start(s16[240,128]{1,0:T(8,128)(2,1)S(1)} %get-tuple-element.116), channel_id=1, source_target_pairs={{0,8},{1,9},{2,10},{3,11},{4,12},{5,13},{6,14},{7,15}} | collective-permute-start | bytes 184328 | tf_op jit(solution)/shard_map/ppermute | solution.py:435
  22.7 6.4 %collective-permute-start.19 = (s16[240,128]{1,0:T(8,128)(2,1)S(1)}, s16[240,128]{1,0:T(8,128)(2,1)S(1)}, u32[]{:S(2)}, u32[]{:S(2)}) collective-permute-start(s16[240,128]{1,0:T(8,128)(2,1)S(1)} %get-tuple-element.103), channel_id=1, source_target_pairs={{0,8},{1,9},{2,10},{3,11},{4,12},{5,13},{6,14},{7,15}} | collective-permute-start | bytes 184328 | tf_op jit(solution)/shard_map/ppermute | solution.py:435
  24.2 5.6 %collective-permute-start.13 = (s16[240,128]{1,0:T(8,128)(2,1)S(1)}, s16[240,128]{1,0:T(8,128)(2,1)S(1)}, u32[]{:S(2)}, u32[]{:S(2)}) collective-permute-start(s16[240,128]{1,0:T(8,128)(2,1)S(1)} %get-tuple-element.90), channel_id=1, source_target_pairs={{0,8},{1,9},{2,10},{3,11},{4,12},{5,13},{6,14},{7,15}} | collective-permute-start | bytes 184328 | tf_op jit(solution)/shard_map/ppermute | solution.py:435
  25.9 4.7 %collective-permute-start.5 = (s16[240,128]{1,0:T(8,128)(2,1)S(1)}, s16[240,128]{1,0:T(8,128)(2,1)S(1)}, u32[]{:S(2)}, u32[]{:S(2)}) collective-permute-start(s16[240,128]{1,0:T(8,128)(2,1)S(1)} %get-tuple-element.75), channel_id=1, source_target_pairs={{0,8},{1,9},{2,10},{3,11},{4,12},{5,13},{6,14},{7,15}} | collective-permute-start | bytes 184328 | tf_op jit(solution)/shard_map/ppermute | solution.py:435
  28.4 2.9 %collective-permute-start.26 = (s16[240,128]{1,0:T(8,128)(2,1)S(1)}, s16[240,128]{1,0:T(8,128)(2,1)S(1)}, u32[]{:S(2)}, u32[]{:S(2)}) collective-permute-start(s16[240,128]{1,0:T(8,128)(2,1)S(1)} %get-tuple-element.118), channel_id=1, source_target_pairs={{8,16},{9,17},{10,18},{11,19},{12,20},{13,21},{14,22},{15,23}} | collective-permute-start | bytes 184328 | tf_op jit(solution)/shard_map/ppermute | solution.py:435
  29.2 2.9 %collective-permute-start.20 = (s16[240,128]{1,0:T(8,128)(2,1)S(1)}, s16[240,128]{1,0:T(8,128)(2,1)S(1)}, u32[]{:S(2)}, u32[]{:S(2)}) collective-permute-start(s16[240,128]{1,0:T(8,128)(2,1)S(1)} %get-tuple-element.105), channel_id=1, source_target_pairs={{8,16},{9,17},{10,18},{11,19},{12,20},{13,21},{14,22},{15,23}} | collective-permute-start | bytes 184328 | tf_op jit(solution)/shard_map/ppermute | solution.py:435
  29.9 2.9 %collective-permute-start.14 = (s16[240,128]{1,0:T(8,128)(2,1)S(1)}, s16[240,128]{1,0:T(8,128)(2,1)S(1)}, u32[]{:S(2)}, u32[]{:S(2)}) collective-permute-start(s16[240,128]{1,0:T(8,128)(2,1)S(1)} %get-tuple-element.92), channel_id=1, source_target_pairs={{8,16},{9,17},{10,18},{11,19},{12,20},{13,21},{14,22},{15,23}} | collective-permute-start | bytes 184328 | tf_op jit(solution)/shard_map/ppermute | solution.py:435
  30.6 2.9 %collective-permute-start.6 = (s16[240,128]{1,0:T(8,128)(2,1)S(1)}, s16[240,128]{1,0:T(8,128)(2,1)S(1)}, u32[]{:S(2)}, u32[]{:S(2)}) collective-permute-start(s16[240,128]{1,0:T(8,128)(2,1)S(1)} %get-tuple-element.77), channel_id=1, source_target_pairs={{8,16},{9,17},{10,18},{11,19},{12,20},{13,21},{14,22},{15,23}} | collective-permute-start | bytes 184328 | tf_op jit(solution)/shard_map/ppermute | solution.py:435
  31.4 2.9 %collective-permute-start.27 = (s16[240,128]{1,0:T(8,128)(2,1)S(1)}, s16[240,128]{1,0:T(8,128)(2,1)S(1)}, u32[]{:S(2)}, u32[]{:S(2)}) collective-permute-start(s16[240,128]{1,0:T(8,128)(2,1)S(1)} %get-tuple-element.120), channel_id=1, source_target_pairs={{16,24},{17,25},{18,26},{19,27},{20,28},{21,29},{22,30},{23,31}} | collective-permute-start | bytes 184328 | tf_op jit(solution)/shard_map/ppermute | solution.py:435
  32.1 2.9 %collective-permute-start.21 = (s16[240,128]{1,0:T(8,128)(2,1)S(1)}, s16[240,128]{1,0:T(8,128)(2,1)S(1)}, u32[]{:S(2)}, u32[]{:S(2)}) collective-permute-start(s16[240,128]{1,0:T(8,128)(2,1)S(1)} %get-tuple-element.107), channel_id=1, source_target_pairs={{16,24},{17,25},{18,26},{19,27},{20,28},{21,29},{22,30},{23,31}} | collective-permute-start | bytes 184328 | tf_op jit(solution)/shard_map/ppermute | solution.py:435
  32.9 2.9 %collective-permute-start.15 = (s16[240,128]{1,0:T(8,128)(2,1)S(1)}, s16[240,128]{1,0:T(8,128)(2,1)S(1)}, u32[]{:S(2)}, u32[]{:S(2)}) collective-permute-start(s16[240,128]{1,0:T(8,128)(2,1)S(1)} %get-tuple-element.94), channel_id=1, source_target_pairs={{16,24},{17,25},{18,26},{19,27},{20,28},{21,29},{22,30},{23,31}} | collective-permute-start | bytes 184328 | tf_op jit(solution)/shard_map/ppermute | solution.py:435
  33.6 3.1 %collective-permute-start.7 = (s16[240,128]{1,0:T(8,128)(2,1)S(1)}, s16[240,128]{1,0:T(8,128)(2,1)S(1)}, u32[]{:S(2)}, u32[]{:S(2)}) collective-permute-start(s16[240,128]{1,0:T(8,128)(2,1)S(1)} %get-tuple-element.79), channel_id=1, source_target_pairs={{16,24},{17,25},{18,26},{19,27},{20,28},{21,29},{22,30},{23,31}} | collective-permute-start | bytes 184328 | tf_op jit(solution)/shard_map/ppermute | solution.py:435
  34.4 3.2 %collective-permute-start.28 = (s16[240,128]{1,0:T(8,128)(2,1)S(1)}, s16[240,128]{1,0:T(8,128)(2,1)S(1)}, u32[]{:S(2)}, u32[]{:S(2)}) collective-permute-start(s16[240,128]{1,0:T(8,128)(2,1)S(1)} %get-tuple-element.122), channel_id=1, source_target_pairs={{24,16},{25,17},{26,18},{27,19},{28,20},{29,21},{30,22},{31,23}} | collective-permute-start | bytes 184328 | tf_op jit(solution)/shard_map/ppermute | solution.py:435
  35.1 1.7 %copy-start.6 = (f32[2,7,16,256]{3,2,1,0:T(8,128)}, f32[2,7,16,256]{3,2,1,0:T(8,128)S(1)}, u32[]{:S(2)}) copy-start(f32[2,7,16,256]{3,2,1,0:T(8,128)S(1)} %get-tuple-element.110.x_in) | copy-start | bytes 688132
  35.1 3.4 %collective-permute-start.22 = (s16[240,128]{1,0:T(8,128)(2,1)S(1)}, s16[240,128]{1,0:T(8,128)(2,1)S(1)}, u32[]{:S(2)}, u32[]{:S(2)}) collective-permute-start(s16[240,128]{1,0:T(8,128)(2,1)S(1)} %get-tuple-element.109), channel_id=1, source_target_pairs={{24,16},{25,17},{26,18},{27,19},{28,20},{29,21},{30,22},{31,23}} | collective-permute-start | bytes 184328 | tf_op jit(solution)/shard_map/ppermute | solution.py:435
  35.8 1.8 %copy-start.2 = (f32[2,7,16,256]{3,2,1,0:T(8,128)}, f32[2,7,16,256]{3,2,1,0:T(8,128)S(1)}, u32[]{:S(2)}) copy-start(f32[2,7,16,256]{3,2,1,0:T(8,128)S(1)} %get-tuple-element.97.x_in) | copy-start | bytes 688132
  35.9 1.7 %copy-start.11 = (f32[2,7,16,256]{3,2,1,0:T(8,128)S(1)}, f32[2,7,16,256]{3,2,1,0:T(8,128)}, u32[]{:S(2)}) copy-start(f32[2,7,16,256]{3,2,1,0:T(8,128)} %copy-done.10) | copy-start | bytes 688132
  35.9 3.5 %collective-permute-start.16 = (s16[240,128]{1,0:T(8,128)(2,1)S(1)}, s16[240,128]{1,0:T(8,128)(2,1)S(1)}, u32[]{:S(2)}, u32[]{:S(2)}) collective-permute-start(s16[240,128]{1,0:T(8,128)(2,1)S(1)} %get-tuple-element.96), channel_id=1, source_target_pairs={{24,16},{25,17},{26,18},{27,19},{28,20},{29,21},{30,22},{31,23}} | collective-permute-start | bytes 184328 | tf_op jit(solution)/shard_map/ppermute | solution.py:435
  36.7 1.8 %copy-start.15 = (f32[2,7,16,256]{3,2,1,0:T(8,128)}, f32[2,7,16,256]{3,2,1,0:T(8,128)S(1)}, u32[]{:S(2)}) copy-start(f32[2,7,16,256]{3,2,1,0:T(8,128)S(1)} %get-tuple-element.82.x_in) | copy-start | bytes 688132
  36.8 1.7 %copy-start.7 = (f32[2,7,16,256]{3,2,1,0:T(8,128)S(1)}, f32[2,7,16,256]{3,2,1,0:T(8,128)}, u32[]{:S(2)}) copy-start(f32[2,7,16,256]{3,2,1,0:T(8,128)} %copy-done.6) | copy-start | bytes 688132
  36.8 3.7 %collective-permute-start.8 = (s16[240,128]{1,0:T(8,128)(2,1)S(1)}, s16[240,128]{1,0:T(8,128)(2,1)S(1)}, u32[]{:S(2)}, u32[]{:S(2)}) collective-permute-start(s16[240,128]{1,0:T(8,128)(2,1)S(1)} %get-tuple-element.81), channel_id=1, source_target_pairs={{24,16},{25,17},{26,18},{27,19},{28,20},{29,21},{30,22},{31,23}} | collective-permute-start | bytes 184328 | tf_op jit(solution)/shard_map/ppermute | solution.py:435
  37.7 2.0 %copy-start.12 = (f32[2,7,16,256]{3,2,1,0:T(8,128)}, f32[2,7,16,256]{3,2,1,0:T(8,128)S(1)}, u32[]{:S(2)}) copy-start(f32[2,7,16,256]{3,2,1,0:T(8,128)S(1)} %get-tuple-element.125.x_in) | copy-start | bytes 688132
  37.7 1.7 %copy-start.3 = (f32[2,7,16,256]{3,2,1,0:T(8,128)S(1)}, f32[2,7,16,256]{3,2,1,0:T(8,128)}, u32[]{:S(2)}) copy-start(f32[2,7,16,256]{3,2,1,0:T(8,128)} %copy-done.2) | copy-start | bytes 688132
  37.7 3.7 %collective-permute-start.29 = (s16[240,128]{1,0:T(8,128)(2,1)S(1)}, s16[240,128]{1,0:T(8,128)(2,1)S(1)}, u32[]{:S(2)}, u32[]{:S(2)}) collective-permute-start(s16[240,128]{1,0:T(8,128)(2,1)S(1)} %get-tuple-element.124), channel_id=1, source_target_pairs={{16,8},{17,9},{18,10},{19,11},{20,12},{21,13},{22,14},{23,15}} | collective-permute-start | bytes 184328 | tf_op jit(solution)/shard_map/ppermute | solution.py:435
  38.6 2.0 %copy-start.8 = (f32[2,7,16,256]{3,2,1,0:T(8,128)}, f32[2,7,16,256]{3,2,1,0:T(8,128)S(1)}, u32[]{:S(2)}) copy-start(f32[2,7,16,256]{3,2,1,0:T(8,128)S(1)} %get-tuple-element.112.x_in) | copy-start | bytes 688132
  38.6 1.9 %copy-start.16 = (f32[2,7,16,256]{3,2,1,0:T(8,128)S(1)}, f32[2,7,16,256]{3,2,1,0:T(8,128)}, u32[]{:S(2)}) copy-start(f32[2,7,16,256]{3,2,1,0:T(8,128)} %copy-done.15) | copy-start | bytes 688132
  38.6 4.3 %collective-permute-start.23 = (s16[240,128]{1,0:T(8,128)(2,1)S(1)}, s16[240,128]{1,0:T(8,128)(2,1)S(1)}, u32[]{:S(2)}, u32[]{:S(2)}) collective-permute-start(s16[240,128]{1,0:T(8,128)(2,1)S(1)} %get-tuple-element.111), channel_id=1, source_target_pairs={{16,8},{17,9},{18,10},{19,11},{20,12},{21,13},{22,14},{23,15}} | collective-permute-start | bytes 184328 | tf_op jit(solution)/shard_map/ppermute | solution.py:435
  39.7 1.8 %copy-start.4 = (f32[2,7,16,256]{3,2,1,0:T(8,128)}, f32[2,7,16,256]{3,2,1,0:T(8,128)S(1)}, u32[]{:S(2)}) copy-start(f32[2,7,16,256]{3,2,1,0:T(8,128)S(1)} %get-tuple-element.99.x_in) | copy-start | bytes 688132
  39.7 1.7 %copy-start.13 = (f32[2,7,16,256]{3,2,1,0:T(8,128)S(1)}, f32[2,7,16,256]{3,2,1,0:T(8,128)}, u32[]{:S(2)}) copy-start(f32[2,7,16,256]{3,2,1,0:T(8,128)} %copy-done.12) | copy-start | bytes 688132
  39.7 4.8 %collective-permute-start.17 = (s16[240,128]{1,0:T(8,128)(2,1)S(1)}, s16[240,128]{1,0:T(8,128)(2,1)S(1)}, u32[]{:S(2)}, u32[]{:S(2)}) collective-permute-start(s16[240,128]{1,0:T(8,128)(2,1)S(1)} %get-tuple-element.98), channel_id=1, source_target_pairs={{16,8},{17,9},{18,10},{19,11},{20,12},{21,13},{22,14},{23,15}} | collective-permute-start | bytes 184328 | tf_op jit(solution)/shard_map/ppermute | solution.py:435
  40.6 2.4 %copy-start.17 = (f32[2,7,16,256]{3,2,1,0:T(8,128)}, f32[2,7,16,256]{3,2,1,0:T(8,128)S(1)}, u32[]{:S(2)}) copy-start(f32[2,7,16,256]{3,2,1,0:T(8,128)S(1)} %get-tuple-element.84.x_in) | copy-start | bytes 688132
  40.6 2.4 %copy-start.9 = (f32[2,7,16,256]{3,2,1,0:T(8,128)S(1)}, f32[2,7,16,256]{3,2,1,0:T(8,128)}, u32[]{:S(2)}) copy-start(f32[2,7,16,256]{3,2,1,0:T(8,128)} %copy-done.8) | copy-start | bytes 688132
  40.6 5.2 %collective-permute-start.9 = (s16[240,128]{1,0:T(8,128)(2,1)S(1)}, s16[240,128]{1,0:T(8,128)(2,1)S(1)}, u32[]{:S(2)}, u32[]{:S(2)}) collective-permute-start(s16[240,128]{1,0:T(8,128)(2,1)S(1)} %get-tuple-element.83), channel_id=1, source_target_pairs={{16,8},{17,9},{18,10},{19,11},{20,12},{21,13},{22,14},{23,15}} | collective-permute-start | bytes 184328 | tf_op jit(solution)/shard_map/ppermute | solution.py:435
  41.5 3.0 %copy-start.5 = (f32[2,7,16,256]{3,2,1,0:T(8,128)S(1)}, f32[2,7,16,256]{3,2,1,0:T(8,128)}, u32[]{:S(2)}) copy-start(f32[2,7,16,256]{3,2,1,0:T(8,128)} %copy-done.4) | copy-start | bytes 688132
  41.5 15.5 %collective-permute-start.30 = (s16[240,128]{1,0:T(8,128)(2,1)S(1)}, s16[240,128]{1,0:T(8,128)(2,1)S(1)}, u32[]{:S(2)}, u32[]{:S(2)}) collective-permute-start(s16[240,128]{1,0:T(8,128)(2,1)S(1)} %get-tuple-element.126), channel_id=1, source_target_pairs={{8,0},{9,1},{10,2},{11,3},{12,4},{13,5},{14,6},{15,7}} | collective-permute-start | bytes 184328 | tf_op jit(solution)/shard_map/ppermute | solution.py:435
  43.0 2.8 %copy-start.18 = (f32[2,7,16,256]{3,2,1,0:T(8,128)S(1)}, f32[2,7,16,256]{3,2,1,0:T(8,128)}, u32[]{:S(2)}) copy-start(f32[2,7,16,256]{3,2,1,0:T(8,128)} %copy-done.17) | copy-start | bytes 688132
  43.0 15.9 %collective-permute-start.24 = (s16[240,128]{1,0:T(8,128)(2,1)S(1)}, s16[240,128]{1,0:T(8,128)(2,1)S(1)}, u32[]{:S(2)}, u32[]{:S(2)}) collective-permute-start(s16[240,128]{1,0:T(8,128)(2,1)S(1)} %get-tuple-element.113), channel_id=1, source_target_pairs={{8,0},{9,1},{10,2},{11,3},{12,4},{13,5},{14,6},{15,7}} | collective-permute-start | bytes 184328 | tf_op jit(solution)/shard_map/ppermute | solution.py:435
  44.5 15.9 %collective-permute-start.18 = (s16[240,128]{1,0:T(8,128)(2,1)S(1)}, s16[240,128]{1,0:T(8,128)(2,1)S(1)}, u32[]{:S(2)}, u32[]{:S(2)}) collective-permute-start(s16[240,128]{1,0:T(8,128)(2,1)S(1)} %get-tuple-element.100), channel_id=1, source_target_pairs={{8,0},{9,1},{10,2},{11,3},{12,4},{13,5},{14,6},{15,7}} | collective-permute-start | bytes 184328 | tf_op jit(solution)/shard_map/ppermute | solution.py:435
  45.9 16.3 %collective-permute-start.10 = (s16[240,128]{1,0:T(8,128)(2,1)S(1)}, s16[240,128]{1,0:T(8,128)(2,1)S(1)}, u32[]{:S(2)}, u32[]{:S(2)}) collective-permute-start(s16[240,128]{1,0:T(8,128)(2,1)S(1)} %get-tuple-element.85), channel_id=1, source_target_pairs={{8,0},{9,1},{10,2},{11,3},{12,4},{13,5},{14,6},{15,7}} | collective-permute-start | bytes 184328 | tf_op jit(solution)/shard_map/ppermute | solution.py:435
  (3 other events, 3.7 us)

commit v4 on v3

--- a/solution.py
+++ b/solution.py
@@ -20,7 +20,7 @@
 LANES = 128
 TOP = 32767.0
 VMEM = pltpu.VMEM
-CHUNKS = 4
+CHUNKS = 2
 HALO_CHUNKS = 2
 
 
@@ -109,8 +109,9 @@
 
 
 def local_kernel(state_ref, wall_ref, *refs):
-    x_outs, open_ref, rows_pad = refs[:-2], refs[-2], refs[-1]
-    open_ref[...] = 1.0 - wall_ref[...].astype(jnp.float32)
+    x_outs, (open_ref, rows_pad, wall_here, done) = refs[:-4], refs[-4:]
+    copy = pltpu.make_async_copy(wall_ref, wall_here, done)
+    copy.start()
     planes, nv, rows, columns = state_ref.shape
     width = columns // len(x_outs)
     nothing = jnp.zeros((rows, LANES), jnp.float32)
@@ -136,6 +137,8 @@
                 two = pltpu.roll(wide, 2, 1) + pltpu.roll(wide, span - 2, 1)
                 total += (NEAR * one + FAR * two)[:, LANES : LANES + width]
                 x_out[p, v] = total
+    copy.wait()
+    open_ref[...] = 1.0 - wall_here[...].astype(jnp.float32)
 
 
 def terms_ahead(planes, p):
@@ -169,11 +172,11 @@
                     x_outs[block // per][p, v, :, own] = total
 
     takes_ahead = jnp.logical_and(even_i, place_i + 1 < count_i)
-    takes_behind = jnp.logical_not(even_i)
+    takes_behind = jnp.logical_not(even_i) if half == 0 else place_i == 1
     pl.when(takes_ahead)(lambda: with_planes(terms_ahead))
     pl.when(takes_behind)(lambda: with_planes(terms_behind))
-    if count_i % 2:
-        pl.when(place_i == count_i - 1)(lambda: with_planes(lambda planes, p: []))
+    neither = jnp.logical_not(jnp.logical_or(takes_ahead, takes_behind))
+    pl.when(neither)(lambda: with_planes(lambda planes, p: []))
 
     even_j = place_j % 2 == 0
     odd_j = jnp.logical_not(even_j)
@@ -231,19 +234,12 @@
     return result
 
 
-def forward_part(chunk, parts, hop, count, inverse_ref, coupling_ref, open_ref, neighbour, face, x_in, x_out, send):
+def forward_part(chunk, parts, first, inverse_ref, coupling_ref, open_ref, messages, face, x_in, x_out, send):
     planes, nv, rows, width = x_out.shape
     per = width // LANES
-    first = hop == 0
-    terms_of = None
     if not first:
         face_scale = get_scale(face, nv * per, rows)
-        if hop % 2 == 0:
-            terms_of = terms_behind
-        elif hop < count - 1:
-            terms_of = terms_ahead
-    if terms_of is not None:
-        scale = get_scale(neighbour, planes * nv * per * parts, rows)
+    scales = [get_scale(coded, planes * nv * per * parts, rows) for coded, _ in messages]
     skip = chunk % parts * per
     most = None
     for block in range(per):
@@ -254,18 +250,19 @@
             running = [get_coded(face, v * per + block, rows, face_scale) for v in range(nv)]
         for p in range(planes):
             factor = coupling_ref[p, 0, :, at : at + LANES]
-            if terms_of is not None:
+            if messages:
                 open_cells = open_ref[p, :, at : at + LANES]
             right = []
             for v in range(nv):
                 entry = x_in[p, v, :, own]
-                if terms_of is not None:
-                    extra = None
+                extra = None
+                for (coded, terms_of), scale in zip(messages, scales):
                     for q, weight in terms_of(planes, p):
-                        term = weight * get_coded(neighbour, (q * nv + v) * per * parts + skip + block, rows, scale)
+                        index = (q * nv + v) * per * parts + skip + block
+                        term = weight * get_coded(coded, index, rows, scale)
                         extra = term if extra is None else extra + term
-                    if extra is not None:
-                        entry += open_cells * extra
+                if extra is not None:
+                    entry += open_cells * extra
                 if running is not None:
                     entry += factor * running[v]
                 right.append(entry)
@@ -318,14 +315,20 @@
         put_face(0, most, x_out, send)
 
 
-def forward_kernel(chunk, parts, hop, count, inverse_ref, coupling_ref, open_ref, neighbour, face, x_in, x_out, send):
+def forward_kernel(chunk, parts, hop, count, kinds, inverse_ref, coupling_ref, *refs):
     active = lax.axis_index("ia") == hop
-    last = hop == count - 1
+    first, last = hop == 0, hop == count - 1
+    x_in, x_out, send = refs[-3:]
+    open_ref = face = None
+    messages = []
+    if not first:
+        open_ref, face = refs[0], refs[1]
+        messages = list(zip(refs[2:-3], kinds))
 
     @pl.when(active)
     def _():
         forward_part(
-            chunk, parts, hop, count, inverse_ref, coupling_ref, open_ref, neighbour, face, x_in, x_out,
+            chunk, parts, first, inverse_ref, coupling_ref, open_ref, messages, face, x_in, x_out,
             None if last else send,
         )
         if last:
@@ -371,10 +374,10 @@
     return pl.BlockSpec(memory_space=VMEM)
 
 
-def call(kernel, operands, outs, name, alias=None, scratch=(), cost=None):
+def call(kernel, operands, outs, name, alias=None, scratch=(), cost=None, far=()):
     return pl.pallas_call(
         kernel,
-        in_specs=[whole()] * len(operands),
+        in_specs=[pl.BlockSpec(memory_space=pl.ANY) if i in far else whole() for i in range(len(operands))],
         out_specs=[whole()] * len(outs),
         out_shape=outs,
         scratch_shapes=list(scratch),
@@ -413,7 +416,8 @@
     for h in range(halves):
         kernel = functools.partial(encode_kernel, h * parts * width, parts * width)
         coded += call(kernel, [state], [halo_code], "encode")
-    near = [lax.ppermute(coded[h], "ia", swaps(count, 0)) for h in range(halves)]
+    to_even = [(i + 1, i) for i in range(0, count - 1, 2)]
+    near = [lax.ppermute(coded[h], "ia", swaps(count, 0) if h == 0 else to_even + [(0, 1)]) for h in range(halves)]
     made = call(
         functools.partial(edges_kernel, sets_k == 2), [state, coded[-1]], [edge_j] * 2 + [edge_k] * sets_k, "edges"
     )
@@ -427,16 +431,21 @@
         [part] * chunks + [cells],
         "local",
         None,
-        [VMEM((rows + 16, width), jnp.float32)],
+        [VMEM((rows + 16, width), jnp.float32), VMEM(wall.shape, wall.dtype), pltpu.SemaphoreType.DMA],
         pl.CostEstimate(flops=40 * size, bytes_accessed=10 * size, transcendentals=0),
+        (1,),
     )
 
     def hop_pair(value, source, target):
-        return lax.ppermute(value, "ia", [(source, target)])
-
-    gated = lax.optimization_barrier((*coded, open_cells, *edges_j, *edges_k))[:halves]
-    far = [lax.ppermute(value, "ia", swaps(count, 1)) for value in gated]
-    x, face = [], [None] * chunks
+        low = min(source, target)
+        return lax.ppermute(value, "ia", swaps(count, 0) if low % 2 == 0 and count % 2 == 0 else [(source, target)])
+
+    to_odd = [(i + 1, i) for i in range(1, count - 1, 2)]
+    gates = [edges_k] + [[*edges_k, open_cells]] * (halves - 1)
+    gated = [lax.optimization_barrier((value, *gate))[0] for value, gate in zip(coded, gates)]
+    far_ahead = [lax.ppermute(value, "ia", to_odd) for value in gated]
+
+    x, sent, face = [], [], [None] * chunks
     for h in range(halves):
         def kernel(*refs, h=h):
             rest = refs[2 + sets_k : 4 + sets_k]
@@ -447,17 +456,26 @@
         first = len(operands) - parts
         x += call(kernel, operands, [part] * parts, "halo", {first + i: i for i in range(parts)})
         for c in range(h * parts, (h + 1) * parts):
-            def kernel(inverse_ref, coupling_ref, *refs, c=c):
-                forward_kernel(c, parts, 0, count, inverse_ref, coupling_ref, None, None, None, *refs)
-
+            kernel = functools.partial(forward_kernel, c, parts, 0, count, ())
             x[c], send = call(kernel, [inverse, coupling, x[c]], [part, face_code], "forward", {2: 0})
             face[c] = hop_pair(send, 0, 1)
+            sent.append(send)
+
+    gated = lax.optimization_barrier((*coded, sent[0]))[:halves]
+    to_behind = [[(i, i + 1) for i in range(1, count - 1) if h or i % 2] for h in range(halves)]
+    far_behind = [lax.ppermute(gated[h], "ia", to_behind[h]) for h in range(halves)]
 
     for hop in range(1, count):
         for c in range(chunks):
-            kernel = functools.partial(forward_kernel, c, parts, hop, count)
-            operands = [inverse, coupling, open_cells, far[c // parts], face[c], x[c]]
-            x[c], send = call(kernel, operands, [part, face_code], "forward", {5: 0})
+            h = c // parts
+            messages, kinds = [], []
+            if hop % 2 and hop < count - 1:
+                messages, kinds = messages + [far_ahead[h]], kinds + [terms_ahead]
+            if hop >= 2 and (hop % 2 == 0 or h):
+                messages, kinds = messages + [far_behind[h]], kinds + [terms_behind]
+            kernel = functools.partial(forward_kernel, c, parts, hop, count, kinds)
+            operands = [inverse, coupling, open_cells, face[c], *messages, x[c]]
+            x[c], send = call(kernel, operands, [part, face_code], "forward", {len(operands) - 1: 0})
             face[c] = hop_pair(send, hop, hop + 1) if hop < count - 1 else hop_pair(send, hop, hop - 1)
     for hop in reversed(range(1, count - 1)):
         for c in range(chunks):

time: 64.1 us -> 67.2 us (1.048)
  starting transfers between devices: 39.2 us -> 44.9 us
  waiting for transfers between devices: 14.2 us -> 13.2 us
    ppermute x28 -> x18, starting transfers between devices: 34 us -> 39.8 us  [the longest x12 33.1 us: hop_pair(): lax.ppermute(value, 'ia', swaps(count, 0) if low % 2 == 0 and count % 2 =...]
    ppermute x28 -> x18, waiting for transfers between devices: 14.2 us -> 13.2 us  [the longest x12 13.2 us: hop_pair(): lax.ppermute(value, 'ia', swaps(count, 0) if low % 2 == 0 and count % 2 =...]
    pallas_call x34 -> x20, Pallas kernels: 6.77 us -> 6.25 us  [call(): pl.pallas_call(kernel, in_specs=[pl.BlockSpec(memory_space=pl.ANY) if i i...]
    unnamed x40 -> x8, local copies, waits for them, and re-layouts: 2.32 us -> 2.24 us
  transfers between devices with their start and end apart: 31 -> 21, of which waited for: 4 -> 8; matrix products, arithmetic and copies ran while one was open for 0% -> 0% of each run, Pallas kernels for 9% -> 7%
where the time goes in v4:
time: 67.2 us; the launch traced here: 66.9 us
  starting transfers between devices  44.9 us (67%)
  waiting for transfers between devices  13.2 us (20%)
  Pallas kernels  6.25 us (9%)
  local copies, waits for them, and re-layouts  2.24 us (3%)
    ppermute x12, starting transfers between devices, hop_pair(): lax.ppermute(value, 'ia', swaps(count, 0) if low % 2 == 0 and count % 2 =...  33.1 us
    ppermute x12, waiting for transfers between devices, hop_pair(): lax.ppermute(value, 'ia', swaps(count, 0) if low % 2 == 0 and count % 2 =...  13.2 us
    pallas_call x20, Pallas kernels, call(): pl.pallas_call(kernel, in_specs=[pl.BlockSpec(memory_space=pl.ANY) if i i...  6.25 us
    ppermute x2, starting transfers between devices, shards(): lax.ppermute(edge, 'ja', swaps(count_j, s))  5.1 us
    ppermute x2, starting transfers between devices, shards(): lax.ppermute(coded[h], 'ia', swaps(count, 0) if h == 0 else to_even + [(0...  3.99 us
    unnamed x8, local copies, waits for them, and re-layouts  2.24 us
    ppermute x2, starting transfers between devices, shards(): far_ahead = [lax.ppermute(value, 'ia', to_odd) for value in gated]  1.35 us
    ppermute x2, starting transfers between devices, shards(): lax.ppermute(gated[h], 'ia', to_behind[h])  1.35 us
  transfers between devices with their start and end apart: 21, of which 8 were waited for; matrix products, arithmetic and copies ran while one was open for 0% of the time, Pallas kernels for 7%

profile of v4, /device:TPU:8, one launch (start us, length us, event | category | flops | bytes accessed | tf_op | source)
XLA Modules:
  0.0 66.9 jit_solution(16811091859981220405)
XLA Ops:
  0.0 1.3 %copy-done.2 = f32[2,7,16,1024]{3,2,1,0:T(8,128)S(1)} copy-done((f32[2,7,16,1024]{3,2,1,0:T(8,128)S(1)}, f32[2,7,16,1024]{3,2,1,0:T(8,128)}, u32[]{:S(2)}) %copy-start.2) | copy-done | bytes 917528
  1.3 0.2 encode.2.after_ref
  1.5 0.2 edges.1
  1.7 0.1 collective-permute-start.2
  1.8 0.2 encode.3
  2.0 1.6 %collective-permute-start.7 = (s16[912,128]{1,0:T(8,128)(2,1)S(1)}, s16[912,128]{1,0:T(8,128)(2,1)S(1)}, u32[]{:S(2)}, u32[]{:S(2)}) collective-permute-start(s16[912,128]{1,0:T(8,128)(2,1)S(1)} %encode.3), channel_id=1, source_target_pairs={{0,8},{8,0},{16,24},{24,16},{1,9},{9,1},{17,25},{25,17},{2,10},{10... | collective-permute-start | bytes 700424 | tf_op jit(solution)/shard_map/ppermute | solution.py:420
  3.5 2.4 %collective-permute-start.3 = (s16[912,128]{1,0:T(8,128)(2,1)S(1)}, s16[912,128]{1,0:T(8,128)(2,1)S(1)}, u32[]{:S(2)}, u32[]{:S(2)}) collective-permute-start(s16[912,128]{1,0:T(8,128)(2,1)S(1)} %encode.2.after_ref), channel_id=1, source_target_pairs={{8,0},{24,16},{0,8},{9,1},{25,17},{1,9},{10,2},{26,18},{2,10},{11,... | collective-permute-start | bytes 700424 | tf_op jit(solution)/shard_map/ppermute | solution.py:420
  6.0 0.1 collective-permute-start
  6.1 0.7 %collective-permute-start.14 = (s16[912,128]{1,0:T(8,128)(2,1)S(1)}, s16[912,128]{1,0:T(8,128)(2,1)S(1)}, u32[]{:S(2)}, u32[]{:S(2)}) collective-permute-start(s16[912,128]{1,0:T(8,128)(2,1)S(1)} %encode.3), channel_id=1, source_target_pairs={{16,8},{17,9},{18,10},{19,11},{20,12},{21,13},{22,14},{23,15}} | collective-permute-start | bytes 700424 | tf_op jit(solution)/shard_map/ppermute | solution.py:446
  6.7 5.0 %collective-permute-start.1 = (f32[2,7,2,1024]{3,2,1,0:T(2,128)S(1)}, f32[2,7,2,1024]{3,2,1,0:T(2,128)S(1)}, u32[]{:S(2)}, u32[]{:S(2)}) collective-permute-start(f32[2,7,2,1024]{3,2,1,0:T(2,128)S(1)} %get-tuple-element.41), channel_id=1, source_target_pairs={{0,0},{2,4},{4,2},{6,6},{1,1},{3,5},{5,3},{7,7},{8,8},{10,12},{12,... | collective-permute-start | bytes 344072 | tf_op jit(solution)/shard_map/ppermute | solution.py:426
  11.8 0.9 %copy-done.3 = s32[2,16,1024]{2,1,0:T(8,128)S(1)} copy-done((s32[2,16,1024]{2,1,0:T(8,128)S(1)}, s32[2,16,1024]{2,1,0:T(8,128)}, u32[]{:S(2)}) %copy-start.3) | copy-done | bytes 131096
  12.7 1.3 %local.1 = (f32[2,7,16,512]{3,2,1,0:T(8,128)S(1)}, f32[2,7,16,512]{3,2,1,0:T(8,128)S(1)}, f32[2,16,1024]{2,1,0:T(8,128)S(1)}) custom-call(f32[2,7,16,1024]{3,2,1,0:T(8,128)S(1)} %copy-done.2, s32[2,16,1024]{2,1,0:T(8,128)S(1)} %copy-done.3), custom_call_target="tpu_custom_call" | custom-call | flops 9175040 | bytes 2293760 | tf_op jit(solution)/shard_map/local/pallas_call | solution.py:378
  14.0 0.7 %collective-permute-start.5 = (s16[912,128]{1,0:T(8,128)(2,1)S(1)}, s16[912,128]{1,0:T(8,128)(2,1)S(1)}, u32[]{:S(2)}, u32[]{:S(2)}) collective-permute-start(s16[912,128]{1,0:T(8,128)(2,1)S(1)} %encode.2.after_ref), channel_id=1, source_target_pairs={{16,8},{17,9},{18,10},{19,11},{20,12},{21,13},{22,14},{23,15}} | collective-permute-start | bytes 700424 | tf_op jit(solution)/shard_map/ppermute | solution.py:446
  14.7 0.4 halo.3.refs_0_
  15.1 0.5 forward.10
  15.6 2.4 %collective-permute-start.13 = (s16[464,128]{1,0:T(8,128)(2,1)S(1)}, s16[464,128]{1,0:T(8,128)(2,1)S(1)}, u32[]{:S(2)}, u32[]{:S(2)}) collective-permute-start(s16[464,128]{1,0:T(8,128)(2,1)S(1)} %get-tuple-element.49), channel_id=1, source_target_pairs={{0,8},{8,0},{16,24},{24,16},{1,9},{9,1},{17,25},{25,17},{2,10},{10... | collective-permute-start | bytes 356360 | tf_op jit(solution)/shard_map/ppermute | solution.py:441
  18.0 0.4 halo.2.refs_0_
  18.4 0.5 forward.8
  18.9 0.1 collective-permute-start.4
  19.0 0.7 %collective-permute-start.16 = (s16[912,128]{1,0:T(8,128)(2,1)S(1)}, s16[912,128]{1,0:T(8,128)(2,1)S(1)}, u32[]{:S(2)}, u32[]{:S(2)}) collective-permute-start(s16[912,128]{1,0:T(8,128)(2,1)S(1)} %encode.3), channel_id=1, source_target_pairs={{8,16},{9,17},{10,18},{11,19},{12,20},{13,21},{14,22},{15,23}} | collective-permute-start | bytes 700424 | tf_op jit(solution)/shard_map/ppermute | solution.py:466
  19.7 0.7 %collective-permute-start.8 = (s16[912,128]{1,0:T(8,128)(2,1)S(1)}, s16[912,128]{1,0:T(8,128)(2,1)S(1)}, u32[]{:S(2)}, u32[]{:S(2)}) collective-permute-start(s16[912,128]{1,0:T(8,128)(2,1)S(1)} %encode.2.after_ref), channel_id=1, source_target_pairs={{8,16},{16,24},{9,17},{17,25},{10,18},{18,26},{11,19},{19,27},{12,... | collective-permute-start | bytes 700424 | tf_op jit(solution)/shard_map/ppermute | solution.py:466
  20.4 0.9 %collective-permute-done.13.refs_1_ = s16[464,128]{1,0:T(8,128)(2,1)S(1)} collective-permute-done((s16[464,128]{1,0:T(8,128)(2,1)S(1)}, s16[464,128]{1,0:T(8,128)(2,1)S(1)}, u32[]{:S(2)}, u32[]{:S(2)}) %collective-permute-start.13) | collective-permute-done | bytes 118816 | tf_op jit(solution)/shard_map/ppermute | solution.py:441
  21.3 0.1 forward.13
  21.4 0.7 collective-permute-start.15
  22.1 1.8 %collective-permute-done.4.refs_1_ = s16[464,128]{1,0:T(8,128)(2,1)S(1)} collective-permute-done((s16[464,128]{1,0:T(8,128)(2,1)S(1)}, s16[464,128]{1,0:T(8,128)(2,1)S(1)}, u32[]{:S(2)}, u32[]{:S(2)}) %collective-permute-start.4) | collective-permute-done | bytes 118816 | tf_op jit(solution)/shard_map/ppermute | solution.py:441
  23.8 0.1 forward.9
  23.9 0.7 collective-permute-start.6
  24.6 0.1 forward.14
  24.7 15.0 %collective-permute-start.17 = (s16[464,128]{1,0:T(8,128)(2,1)S(1)}, s16[464,128]{1,0:T(8,128)(2,1)S(1)}, u32[]{:S(2)}, u32[]{:S(2)}) collective-permute-start(s16[464,128]{1,0:T(8,128)(2,1)S(1)} %get-tuple-element.64), channel_id=1, source_target_pairs={{0,8},{8,0},{16,24},{24,16},{1,9},{9,1},{17,25},{25,17},{2,10},{10... | collective-permute-start | bytes 356360 | tf_op jit(solution)/shard_map/ppermute | solution.py:441
  39.7 0.1 forward.11
  39.7 2.5 %collective-permute-start.9 = (s16[464,128]{1,0:T(8,128)(2,1)S(1)}, s16[464,128]{1,0:T(8,128)(2,1)S(1)}, u32[]{:S(2)}, u32[]{:S(2)}) collective-permute-start(s16[464,128]{1,0:T(8,128)(2,1)S(1)} %get-tuple-element.52), channel_id=1, source_target_pairs={{0,8},{8,0},{16,24},{24,16},{1,9},{9,1},{17,25},{25,17},{2,10},{10... | collective-permute-start | bytes 356360 | tf_op jit(solution)/shard_map/ppermute | solution.py:441
  42.2 2.9 %collective-permute-done.17.refs_1_ = s16[464,128]{1,0:T(8,128)(2,1)S(1)} collective-permute-done((s16[464,128]{1,0:T(8,128)(2,1)S(1)}, s16[464,128]{1,0:T(8,128)(2,1)S(1)}, u32[]{:S(2)}, u32[]{:S(2)}) %collective-permute-start.17) | collective-permute-done | bytes 118816 | tf_op jit(solution)/shard_map/ppermute | solution.py:441
  45.1 0.1 forward.15
  45.2 0.4 collective-permute-start.18
  45.6 1.7 %collective-permute-done.9.refs_1_ = s16[464,128]{1,0:T(8,128)(2,1)S(1)} collective-permute-done((s16[464,128]{1,0:T(8,128)(2,1)S(1)}, s16[464,128]{1,0:T(8,128)(2,1)S(1)}, u32[]{:S(2)}, u32[]{:S(2)}) %collective-permute-start.9) | collective-permute-done | bytes 118816 | tf_op jit(solution)/shard_map/ppermute | solution.py:441
  47.3 1.1 %collective-permute-start.10 = (s16[464,128]{1,0:T(8,128)(2,1)S(1)}, s16[464,128]{1,0:T(8,128)(2,1)S(1)}, u32[]{:S(2)}, u32[]{:S(2)}) collective-permute-start(s16[464,128]{1,0:T(8,128)(2,1)S(1)} %get-tuple-element.54), channel_id=1, source_target_pairs={{0,8},{8,0},{16,24},{24,16},{1,9},{9,1},{17,25},{25,17},{2,10},{10... | collective-permute-start | bytes 356360 | tf_op jit(solution)/shard_map/ppermute | solution.py:441
  48.4 1.6 %collective-permute-done.18.face = s16[464,128]{1,0:T(8,128)(2,1)S(1)} collective-permute-done((s16[464,128]{1,0:T(8,128)(2,1)S(1)}, s16[464,128]{1,0:T(8,128)(2,1)S(1)}, u32[]{:S(2)}, u32[]{:S(2)}) %collective-permute-start.18) | collective-permute-done | bytes 118816 | tf_op jit(solution)/shard_map/ppermute | solution.py:441
  50.1 0.7 collective-permute-start.19
  50.8 1.4 %collective-permute-done.10.face = s16[464,128]{1,0:T(8,128)(2,1)S(1)} collective-permute-done((s16[464,128]{1,0:T(8,128)(2,1)S(1)}, s16[464,128]{1,0:T(8,128)(2,1)S(1)}, u32[]{:S(2)}, u32[]{:S(2)}) %collective-permute-start.10) | collective-permute-done | bytes 118816 | tf_op jit(solution)/shard_map/ppermute | solution.py:441
  52.2 0.1 backward.5
  52.3 0.7 collective-permute-start.11
  53.0 0.1 backward.8
  53.1 7.5 %collective-permute-start.20 = (s16[464,128]{1,0:T(8,128)(2,1)S(1)}, s16[464,128]{1,0:T(8,128)(2,1)S(1)}, u32[]{:S(2)}, u32[]{:S(2)}) collective-permute-start(s16[464,128]{1,0:T(8,128)(2,1)S(1)} %get-tuple-element.70), channel_id=1, source_target_pairs={{0,8},{8,0},{16,24},{24,16},{1,9},{9,1},{17,25},{25,17},{2,10},{10... | collective-permute-start | bytes 356360 | tf_op jit(solution)/shard_map/ppermute | solution.py:441
  60.6 1.5 %collective-permute-start.12 = (s16[464,128]{1,0:T(8,128)(2,1)S(1)}, s16[464,128]{1,0:T(8,128)(2,1)S(1)}, u32[]{:S(2)}, u32[]{:S(2)}) collective-permute-start(s16[464,128]{1,0:T(8,128)(2,1)S(1)} %get-tuple-element.58), channel_id=1, source_target_pairs={{0,8},{8,0},{16,24},{24,16},{1,9},{9,1},{17,25},{25,17},{2,10},{10... | collective-permute-start | bytes 356360 | tf_op jit(solution)/shard_map/ppermute | solution.py:441
  62.1 1.2 %collective-permute-done.20.refs_2_ = s16[464,128]{1,0:T(8,128)(2,1)S(1)} collective-permute-done((s16[464,128]{1,0:T(8,128)(2,1)S(1)}, s16[464,128]{1,0:T(8,128)(2,1)S(1)}, u32[]{:S(2)}, u32[]{:S(2)}) %collective-permute-start.20) | collective-permute-done | bytes 118816 | tf_op jit(solution)/shard_map/ppermute | solution.py:441
  63.4 0.6 backward.9.refs_0_
  63.9 1.6 %collective-permute-done.12.face = s16[464,128]{1,0:T(8,128)(2,1)S(1)} collective-permute-done((s16[464,128]{1,0:T(8,128)(2,1)S(1)}, s16[464,128]{1,0:T(8,128)(2,1)S(1)}, u32[]{:S(2)}, u32[]{:S(2)}) %collective-permute-start.12) | collective-permute-done | bytes 118816 | tf_op jit(solution)/shard_map/ppermute | solution.py:441
  65.5 1.4 %last.1 = f32[2,7,16,1024]{3,2,1,0:T(8,128)} custom-call(bf16[2,7,7,16,1024]{4,3,2,1,0:T(8,128)(2,1)S(1)} %copy-done, f32[2,2,16,1024]{3,2,1,0:T(8,128)S(1)} %copy-done.1, s16[464,128]{1,0:T(8,128)(2,1)S(1)} %collective-permute-done.12.face, f32[2,7,16,512]{3,2,1,0:T(8,128)S(1)} %backward.9.refs_0_, f32[2,7,16,512]{3,2,1,0:T(8,128)S(1)} %get-tuple-element.72.refs_1_), custom_call_target="tpu_custom_call" | custom-call | tf_op jit(solution)/shard_map/last/pallas_call | solution.py:378
  (22 shorter events, 0.2 us)
Async XLA Ops:
  0.0 15.1 %copy-start = (bf16[2,7,7,16,1024]{4,3,2,1,0:T(8,128)(2,1)S(1)}, bf16[2,7,7,16,1024]{4,3,2,1,0:T(8,128)(2,1)}, u32[]{:S(2)}) copy-start(bf16[2,7,7,16,1024]{4,3,2,1,0:T(8,128)(2,1)} %inverse_ref.25) | copy-start | bytes 9633796
  0.0 1.3 %copy-start.2 = (f32[2,7,16,1024]{3,2,1,0:T(8,128)S(1)}, f32[2,7,16,1024]{3,2,1,0:T(8,128)}, u32[]{:S(2)}) copy-start(f32[2,7,16,1024]{3,2,1,0:T(8,128)} %state_ref.7) | copy-start | bytes 2752516
  1.3 13.8 %copy-start.1 = (f32[2,2,16,1024]{3,2,1,0:T(8,128)S(1)}, f32[2,2,16,1024]{3,2,1,0:T(8,128)}, u32[]{:S(2)}) copy-start(f32[2,2,16,1024]{3,2,1,0:T(8,128)} %coupling_ref.25) | copy-start | bytes 786436
  1.7 4.3 %collective-permute-start.2 = (f32[2,7,16,128]{3,2,1,0:T(8,128)S(1)}, f32[2,7,16,128]{3,2,1,0:T(8,128)S(1)}, u32[]{:S(2)}, u32[]{:S(2)}) collective-permute-start(f32[2,7,16,128]{3,2,1,0:T(8,128)S(1)} %get-tuple-element.42), channel_id=1, source_target_pairs={{0,1},{1,0},{2,3},{3,2},{4,5},{5,4},{6,7},{7,6},{8,9},{9,8},{10,11... | collective-permute-start | bytes 344072 | tf_op jit(solution)/shard_map/ppermute | solution.py:425
  2.0 12.8 %collective-permute-start.7 = (s16[912,128]{1,0:T(8,128)(2,1)S(1)}, s16[912,128]{1,0:T(8,128)(2,1)S(1)}, u32[]{:S(2)}, u32[]{:S(2)}) collective-permute-start(s16[912,128]{1,0:T(8,128)(2,1)S(1)} %encode.3), channel_id=1, source_target_pairs={{0,8},{8,0},{16,24},{24,16},{1,9},{9,1},{17,25},{25,17},{2,10},{10... | collective-permute-start | bytes 700424 | tf_op jit(solution)/shard_map/ppermute | solution.py:420
  3.5 14.5 %collective-permute-start.3 = (s16[912,128]{1,0:T(8,128)(2,1)S(1)}, s16[912,128]{1,0:T(8,128)(2,1)S(1)}, u32[]{:S(2)}, u32[]{:S(2)}) collective-permute-start(s16[912,128]{1,0:T(8,128)(2,1)S(1)} %encode.2.after_ref), channel_id=1, source_target_pairs={{8,0},{24,16},{0,8},{9,1},{25,17},{1,9},{10,2},{26,18},{2,10},{11,... | collective-permute-start | bytes 700424 | tf_op jit(solution)/shard_map/ppermute | solution.py:420
  6.0 8.0 %collective-permute-start = (f32[2,7,2,1024]{3,2,1,0:T(2,128)S(1)}, f32[2,7,2,1024]{3,2,1,0:T(2,128)S(1)}, u32[]{:S(2)}, u32[]{:S(2)}) collective-permute-start(f32[2,7,2,1024]{3,2,1,0:T(2,128)S(1)} %get-tuple-element.40), channel_id=1, source_target_pairs={{0,2},{2,0},{4,6},{6,4},{1,3},{3,1},{5,7},{7,5},{8,10},{10,8},{12,... | collective-permute-start | bytes 344072 | tf_op jit(solution)/shard_map/ppermute | solution.py:426
  6.1 13.6 %collective-permute-start.14 = (s16[912,128]{1,0:T(8,128)(2,1)S(1)}, s16[912,128]{1,0:T(8,128)(2,1)S(1)}, u32[]{:S(2)}, u32[]{:S(2)}) collective-permute-start(s16[912,128]{1,0:T(8,128)(2,1)S(1)} %encode.3), channel_id=1, source_target_pairs={{16,8},{17,9},{18,10},{19,11},{20,12},{21,13},{22,14},{23,15}} | collective-permute-start | bytes 700424 | tf_op jit(solution)/shard_map/ppermute | solution.py:446
  6.7 8.0 %collective-permute-start.1 = (f32[2,7,2,1024]{3,2,1,0:T(2,128)S(1)}, f32[2,7,2,1024]{3,2,1,0:T(2,128)S(1)}, u32[]{:S(2)}, u32[]{:S(2)}) collective-permute-start(f32[2,7,2,1024]{3,2,1,0:T(2,128)S(1)} %get-tuple-element.41), channel_id=1, source_target_pairs={{0,0},{2,4},{4,2},{6,6},{1,1},{3,5},{5,3},{7,7},{8,8},{10,12},{12,... | collective-permute-start | bytes 344072 | tf_op jit(solution)/shard_map/ppermute | solution.py:426
  11.8 0.9 %copy-start.3 = (s32[2,16,1024]{2,1,0:T(8,128)S(1)}, s32[2,16,1024]{2,1,0:T(8,128)}, u32[]{:S(2)}) copy-start(s32[2,16,1024]{2,1,0:T(8,128)} %wall_ref.1) | copy-start | bytes 393220
  14.0 8.0 %collective-permute-start.5 = (s16[912,128]{1,0:T(8,128)(2,1)S(1)}, s16[912,128]{1,0:T(8,128)(2,1)S(1)}, u32[]{:S(2)}, u32[]{:S(2)}) collective-permute-start(s16[912,128]{1,0:T(8,128)(2,1)S(1)} %encode.2.after_ref), channel_id=1, source_target_pairs={{16,8},{17,9},{18,10},{19,11},{20,12},{21,13},{22,14},{23,15}} | collective-permute-start | bytes 700424 | tf_op jit(solution)/shard_map/ppermute | solution.py:446
  15.6 5.7 %collective-permute-start.13 = (s16[464,128]{1,0:T(8,128)(2,1)S(1)}, s16[464,128]{1,0:T(8,128)(2,1)S(1)}, u32[]{:S(2)}, u32[]{:S(2)}) collective-permute-start(s16[464,128]{1,0:T(8,128)(2,1)S(1)} %get-tuple-element.49), channel_id=1, source_target_pairs={{0,8},{8,0},{16,24},{24,16},{1,9},{9,1},{17,25},{25,17},{2,10},{10... | collective-permute-start | bytes 356360 | tf_op jit(solution)/shard_map/ppermute | solution.py:441
  18.9 4.9 %collective-permute-start.4 = (s16[464,128]{1,0:T(8,128)(2,1)S(1)}, s16[464,128]{1,0:T(8,128)(2,1)S(1)}, u32[]{:S(2)}, u32[]{:S(2)}) collective-permute-start(s16[464,128]{1,0:T(8,128)(2,1)S(1)} %get-tuple-element.44), channel_id=1, source_target_pairs={{0,8},{8,0},{16,24},{24,16},{1,9},{9,1},{17,25},{25,17},{2,10},{10... | collective-permute-start | bytes 356360 | tf_op jit(solution)/shard_map/ppermute | solution.py:441
  19.0 5.6 %collective-permute-start.16 = (s16[912,128]{1,0:T(8,128)(2,1)S(1)}, s16[912,128]{1,0:T(8,128)(2,1)S(1)}, u32[]{:S(2)}, u32[]{:S(2)}) collective-permute-start(s16[912,128]{1,0:T(8,128)(2,1)S(1)} %encode.3), channel_id=1, source_target_pairs={{8,16},{9,17},{10,18},{11,19},{12,20},{13,21},{14,22},{15,23}} | collective-permute-start | bytes 700424 | tf_op jit(solution)/shard_map/ppermute | solution.py:466
  19.7 20.0 %collective-permute-start.8 = (s16[912,128]{1,0:T(8,128)(2,1)S(1)}, s16[912,128]{1,0:T(8,128)(2,1)S(1)}, u32[]{:S(2)}, u32[]{:S(2)}) collective-permute-start(s16[912,128]{1,0:T(8,128)(2,1)S(1)} %encode.2.after_ref), channel_id=1, source_target_pairs={{8,16},{16,24},{9,17},{17,25},{10,18},{18,26},{11,19},{19,27},{12,... | collective-permute-start | bytes 700424 | tf_op jit(solution)/shard_map/ppermute | solution.py:466
  21.4 3.2 %collective-permute-start.15 = (s16[464,128]{1,0:T(8,128)(2,1)S(1)}, s16[464,128]{1,0:T(8,128)(2,1)S(1)}, u32[]{:S(2)}, u32[]{:S(2)}) collective-permute-start(s16[464,128]{1,0:T(8,128)(2,1)S(1)} %get-tuple-element.61), channel_id=1, source_target_pairs={{8,16},{9,17},{10,18},{11,19},{12,20},{13,21},{14,22},{15,23}} | collective-permute-start | bytes 356360 | tf_op jit(solution)/shard_map/ppermute | solution.py:441
  23.9 15.8 %collective-permute-start.6 = (s16[464,128]{1,0:T(8,128)(2,1)S(1)}, s16[464,128]{1,0:T(8,128)(2,1)S(1)}, u32[]{:S(2)}, u32[]{:S(2)}) collective-permute-start(s16[464,128]{1,0:T(8,128)(2,1)S(1)} %get-tuple-element.47), channel_id=1, source_target_pairs={{8,16},{9,17},{10,18},{11,19},{12,20},{13,21},{14,22},{15,23}} | collective-permute-start | bytes 356360 | tf_op jit(solution)/shard_map/ppermute | solution.py:441
  24.7 20.4 %collective-permute-start.17 = (s16[464,128]{1,0:T(8,128)(2,1)S(1)}, s16[464,128]{1,0:T(8,128)(2,1)S(1)}, u32[]{:S(2)}, u32[]{:S(2)}) collective-permute-start(s16[464,128]{1,0:T(8,128)(2,1)S(1)} %get-tuple-element.64), channel_id=1, source_target_pairs={{0,8},{8,0},{16,24},{24,16},{1,9},{9,1},{17,25},{25,17},{2,10},{10... | collective-permute-start | bytes 356360 | tf_op jit(solution)/shard_map/ppermute | solution.py:441
  39.7 7.5 %collective-permute-start.9 = (s16[464,128]{1,0:T(8,128)(2,1)S(1)}, s16[464,128]{1,0:T(8,128)(2,1)S(1)}, u32[]{:S(2)}, u32[]{:S(2)}) collective-permute-start(s16[464,128]{1,0:T(8,128)(2,1)S(1)} %get-tuple-element.52), channel_id=1, source_target_pairs={{0,8},{8,0},{16,24},{24,16},{1,9},{9,1},{17,25},{25,17},{2,10},{10... | collective-permute-start | bytes 356360 | tf_op jit(solution)/shard_map/ppermute | solution.py:441
  45.2 4.9 %collective-permute-start.18 = (s16[464,128]{1,0:T(8,128)(2,1)S(1)}, s16[464,128]{1,0:T(8,128)(2,1)S(1)}, u32[]{:S(2)}, u32[]{:S(2)}) collective-permute-start(s16[464,128]{1,0:T(8,128)(2,1)S(1)} %get-tuple-element.66), channel_id=1, source_target_pairs={{0,8},{8,0},{16,24},{24,16},{1,9},{9,1},{17,25},{25,17},{2,10},{10... | collective-permute-start | bytes 356360 | tf_op jit(solution)/shard_map/ppermute | solution.py:441
  47.3 4.9 %collective-permute-start.10 = (s16[464,128]{1,0:T(8,128)(2,1)S(1)}, s16[464,128]{1,0:T(8,128)(2,1)S(1)}, u32[]{:S(2)}, u32[]{:S(2)}) collective-permute-start(s16[464,128]{1,0:T(8,128)(2,1)S(1)} %get-tuple-element.54), channel_id=1, source_target_pairs={{0,8},{8,0},{16,24},{24,16},{1,9},{9,1},{17,25},{25,17},{2,10},{10... | collective-permute-start | bytes 356360 | tf_op jit(solution)/shard_map/ppermute | solution.py:441
  50.1 2.9 %collective-permute-start.19 = (s16[464,128]{1,0:T(8,128)(2,1)S(1)}, s16[464,128]{1,0:T(8,128)(2,1)S(1)}, u32[]{:S(2)}, u32[]{:S(2)}) collective-permute-start(s16[464,128]{1,0:T(8,128)(2,1)S(1)} %get-tuple-element.68), channel_id=1, source_target_pairs={{16,8},{17,9},{18,10},{19,11},{20,12},{21,13},{22,14},{23,15}} | collective-permute-start | bytes 356360 | tf_op jit(solution)/shard_map/ppermute | solution.py:441
  52.3 8.2 %collective-permute-start.11 = (s16[464,128]{1,0:T(8,128)(2,1)S(1)}, s16[464,128]{1,0:T(8,128)(2,1)S(1)}, u32[]{:S(2)}, u32[]{:S(2)}) collective-permute-start(s16[464,128]{1,0:T(8,128)(2,1)S(1)} %get-tuple-element.56), channel_id=1, source_target_pairs={{16,8},{17,9},{18,10},{19,11},{20,12},{21,13},{22,14},{23,15}} | collective-permute-start | bytes 356360 | tf_op jit(solution)/shard_map/ppermute | solution.py:441
  53.1 10.3 %collective-permute-start.20 = (s16[464,128]{1,0:T(8,128)(2,1)S(1)}, s16[464,128]{1,0:T(8,128)(2,1)S(1)}, u32[]{:S(2)}, u32[]{:S(2)}) collective-permute-start(s16[464,128]{1,0:T(8,128)(2,1)S(1)} %get-tuple-element.70), channel_id=1, source_target_pairs={{0,8},{8,0},{16,24},{24,16},{1,9},{9,1},{17,25},{25,17},{2,10},{10... | collective-permute-start | bytes 356360 | tf_op jit(solution)/shard_map/ppermute | solution.py:441
  60.6 4.9 %collective-permute-start.12 = (s16[464,128]{1,0:T(8,128)(2,1)S(1)}, s16[464,128]{1,0:T(8,128)(2,1)S(1)}, u32[]{:S(2)}, u32[]{:S(2)}) collective-permute-start(s16[464,128]{1,0:T(8,128)(2,1)S(1)} %get-tuple-element.58), channel_id=1, source_target_pairs={{0,8},{8,0},{16,24},{24,16},{1,9},{9,1},{17,25},{25,17},{2,10},{10... | collective-permute-start | bytes 356360 | tf_op jit(solution)/shard_map/ppermute | solution.py:441

commit v5 on v3

--- a/solution.py
+++ b/solution.py
@@ -20,7 +20,7 @@
 LANES = 128
 TOP = 32767.0
 VMEM = pltpu.VMEM
-CHUNKS = 4
+CHUNKS = 2
 HALO_CHUNKS = 2
 
 
@@ -386,6 +386,8 @@
 
 
 def swaps(count, first):
+    if count % 2 == 0:
+        return [(i, (i + 1 if i % 2 == first else i - 1) % count) for i in range(count)]
     partner = list(range(count))
     for i in range(first, count - 1, 2):
         partner[i], partner[i + 1] = i + 1, i
@@ -432,11 +434,15 @@
     )
 
     def hop_pair(value, source, target):
-        return lax.ppermute(value, "ia", [(source, target)])
-
-    gated = lax.optimization_barrier((*coded, open_cells, *edges_j, *edges_k))[:halves]
-    far = [lax.ppermute(value, "ia", swaps(count, 1)) for value in gated]
-    x, face = [], [None] * chunks
+        return lax.ppermute(value, "ia", swaps(count, min(source, target) % 2))
+
+    def pass_on(h, *gate):
+        passed = near[h] if count == 4 else coded[h]
+        if gate:
+            passed = lax.optimization_barrier((passed, *gate))[0]
+        return lax.ppermute(passed, "ia", [(i, i ^ 2) for i in range(4)] if count == 4 else swaps(count, 1))
+
+    x, far, face = [], [pass_on(0)], [None] * chunks
     for h in range(halves):
         def kernel(*refs, h=h):
             rest = refs[2 + sets_k : 4 + sets_k]
@@ -452,6 +458,8 @@
 
             x[c], send = call(kernel, [inverse, coupling, x[c]], [part, face_code], "forward", {2: 0})
             face[c] = hop_pair(send, 0, 1)
+        if h:
+            far.append(pass_on(h, send))
 
     for hop in range(1, count):
         for c in range(chunks):

time: 64.1 us -> 58.5 us (0.913)
  the two profiles are of different devices: /device:TPU:8 before, /device:TPU:0 now
where the time goes in v5:
time: 58.5 us; the launch traced here: 58.4 us
  starting transfers between devices  35.9 us (61%)
  waiting for transfers between devices  14.1 us (24%)
  Pallas kernels  5.99 us (10%)
  local copies, waits for them, and re-layouts  2.24 us (4%)
    ppermute x12, starting transfers between devices, hop_pair(): return lax.ppermute(value, 'ia', swaps(count, min(source, target) % 2))  25.2 us
    ppermute x12, waiting for transfers between devices, hop_pair(): return lax.ppermute(value, 'ia', swaps(count, min(source, target) % 2))  12.2 us
    pallas_call x20, Pallas kernels, call(): pl.pallas_call(kernel, in_specs=[whole()] * len(operands), out_specs=[who...  5.99 us
    ppermute x2, starting transfers between devices, shards(): lax.ppermute(edge, 'ja', swaps(count_j, s))  4.62 us
    ppermute x2, starting transfers between devices, shards(): lax.ppermute(coded[h], 'ia', swaps(count, 0))  3.08 us
    ppermute x2, starting transfers between devices, pass_on(): lax.ppermute(passed, 'ia', [(i, i ^ 2) for i in range(4)] if count == 4 e...  2.97 us
    unnamed x8, local copies, waits for them, and re-layouts  2.24 us
    ppermute x2, waiting for transfers between devices, shards(): lax.ppermute(edge, 'ja', swaps(count_j, s))  1.2 us
  transfers between devices with their start and end apart: 19, of which 14 were waited for; matrix products, arithmetic and copies ran while one was open for 0% of the time, Pallas kernels for 8%

profile of v5, /device:TPU:0, one launch (start us, length us, event | category | flops | bytes accessed | tf_op | source)
XLA Modules:
  0.0 58.4 jit_solution(4673306986730827274)
XLA Ops:
  0.0 1.3 %copy-done.2 = f32[2,7,16,1024]{3,2,1,0:T(8,128)S(1)} copy-done((f32[2,7,16,1024]{3,2,1,0:T(8,128)S(1)}, f32[2,7,16,1024]{3,2,1,0:T(8,128)}, u32[]{:S(2)}) %copy-start.2) | copy-done | bytes 917528
  1.3 0.2 encode.3
  1.5 3.0 %collective-permute-start.11 = (s16[912,128]{1,0:T(8,128)(2,1)S(1)}, s16[912,128]{1,0:T(8,128)(2,1)S(1)}, u32[]{:S(2)}, u32[]{:S(2)}) collective-permute-start(s16[912,128]{1,0:T(8,128)(2,1)S(1)} %encode.3), channel_id=1, source_target_pairs={{0,8},{8,0},{16,24},{24,16},{1,9},{9,1},{17,25},{25,17},{2,10},{10... | collective-permute-start | bytes 700424 | tf_op jit(solution)/shard_map/ppermute | solution.py:418
  4.5 0.2 encode.2.after_ref
  4.7 0.1 collective-permute-start
  4.7 0.2 edges.1
  5.0 2.1 %collective-permute-start.1 = (f32[2,7,2,1024]{3,2,1,0:T(2,128)S(1)}, f32[2,7,2,1024]{3,2,1,0:T(2,128)S(1)}, u32[]{:S(2)}, u32[]{:S(2)}) collective-permute-start(f32[2,7,2,1024]{3,2,1,0:T(2,128)S(1)} %get-tuple-element.37), channel_id=1, source_target_pairs={{0,2},{2,0},{4,6},{6,4},{1,3},{3,1},{5,7},{7,5},{8,10},{10,8},{12,... | collective-permute-start | bytes 344072 | tf_op jit(solution)/shard_map/ppermute | solution.py:424
  7.1 2.5 %collective-permute-start.2 = (f32[2,7,2,1024]{3,2,1,0:T(2,128)S(1)}, f32[2,7,2,1024]{3,2,1,0:T(2,128)S(1)}, u32[]{:S(2)}, u32[]{:S(2)}) collective-permute-start(f32[2,7,2,1024]{3,2,1,0:T(2,128)S(1)} %get-tuple-element.38), channel_id=1, source_target_pairs={{0,6},{2,4},{4,2},{6,0},{1,7},{3,5},{5,3},{7,1},{8,14},{10,12},{12... | collective-permute-start | bytes 344072 | tf_op jit(solution)/shard_map/ppermute | solution.py:424
  9.6 0.9 %copy-done.3 = s32[2,16,1024]{2,1,0:T(8,128)S(1)} copy-done((s32[2,16,1024]{2,1,0:T(8,128)S(1)}, s32[2,16,1024]{2,1,0:T(8,128)}, u32[]{:S(2)}) %copy-start.3) | copy-done | bytes 131096
  10.5 1.2 %local.1 = (f32[2,7,16,512]{3,2,1,0:T(8,128)S(1)}, f32[2,7,16,512]{3,2,1,0:T(8,128)S(1)}, f32[2,16,1024]{2,1,0:T(8,128)S(1)}) custom-call(f32[2,7,16,1024]{3,2,1,0:T(8,128)S(1)} %copy-done.2, s32[2,16,1024]{2,1,0:T(8,128)S(1)} %copy-done.3), custom_call_target="tpu_custom_call" | custom-call | flops 9175040 | bytes 2293760 | tf_op jit(solution)/shard_map/local/pallas_call | solution.py:375
  11.7 1.6 %collective-permute-start.12 = (s16[912,128]{1,0:T(8,128)(2,1)S(1)}, s16[912,128]{1,0:T(8,128)(2,1)S(1)}, u32[]{:S(2)}, u32[]{:S(2)}) collective-permute-start(s16[912,128]{1,0:T(8,128)(2,1)S(1)} %collective-permute-done.11.refs_3_), channel_id=1, source_target_pairs={{0,16},{8,24},{16,0},{24,8},{1,17},{9,25},{17,1},{25,9},{2,18},{10... | collective-permute-start | bytes 700424 | tf_op jit(solution)/shard_map/ppermute | solution.py:443
  13.3 1.2 %collective-permute-done.2.refs_1_ = f32[2,7,2,1024]{3,2,1,0:T(2,128)S(1)} collective-permute-done((f32[2,7,2,1024]{3,2,1,0:T(2,128)S(1)}, f32[2,7,2,1024]{3,2,1,0:T(2,128)S(1)}, u32[]{:S(2)}, u32[]{:S(2)}) %collective-permute-start.2) | collective-permute-done | bytes 114720 | tf_op jit(solution)/shard_map/ppermute | solution.py:424
  14.5 0.7 %collective-permute-done.refs_3_ = s16[912,128]{1,0:T(8,128)(2,1)S(1)} collective-permute-done((s16[912,128]{1,0:T(8,128)(2,1)S(1)}, s16[912,128]{1,0:T(8,128)(2,1)S(1)}, u32[]{:S(2)}, u32[]{:S(2)}) %collective-permute-start) | collective-permute-done | bytes 233504 | tf_op jit(solution)/shard_map/ppermute | solution.py:418
  15.2 0.3 halo.2.refs_0_
  15.6 0.5 forward.8
  16.1 1.4 %collective-permute-start.4 = (s16[912,128]{1,0:T(8,128)(2,1)S(1)}, s16[912,128]{1,0:T(8,128)(2,1)S(1)}, u32[]{:S(2)}, u32[]{:S(2)}) collective-permute-start(s16[912,128]{1,0:T(8,128)(2,1)S(1)} %collective-permute-done.refs_3_), channel_id=1, source_target_pairs={{0,16},{8,24},{16,0},{24,8},{1,17},{9,25},{17,1},{25,9},{2,18},{10... | collective-permute-start | bytes 700424 | tf_op jit(solution)/shard_map/ppermute | solution.py:443
  17.5 0.3 halo.3.refs_0_
  17.8 0.5 forward.12
  18.4 1.1 %collective-permute-start.13 = (s16[464,128]{1,0:T(8,128)(2,1)S(1)}, s16[464,128]{1,0:T(8,128)(2,1)S(1)}, u32[]{:S(2)}, u32[]{:S(2)}) collective-permute-start(s16[464,128]{1,0:T(8,128)(2,1)S(1)} %get-tuple-element.54), channel_id=1, source_target_pairs={{0,8},{8,0},{16,24},{24,16},{1,9},{9,1},{17,25},{25,17},{2,10},{10... | collective-permute-start | bytes 356360 | tf_op jit(solution)/shard_map/ppermute | solution.py:437
  19.5 1.0 %collective-permute-start.5 = (s16[464,128]{1,0:T(8,128)(2,1)S(1)}, s16[464,128]{1,0:T(8,128)(2,1)S(1)}, u32[]{:S(2)}, u32[]{:S(2)}) collective-permute-start(s16[464,128]{1,0:T(8,128)(2,1)S(1)} %get-tuple-element.41), channel_id=1, source_target_pairs={{0,8},{8,0},{16,24},{24,16},{1,9},{9,1},{17,25},{25,17},{2,10},{10... | collective-permute-start | bytes 356360 | tf_op jit(solution)/shard_map/ppermute | solution.py:437
  20.5 3.1 %collective-permute-done.13.face = s16[464,128]{1,0:T(8,128)(2,1)S(1)} collective-permute-done((s16[464,128]{1,0:T(8,128)(2,1)S(1)}, s16[464,128]{1,0:T(8,128)(2,1)S(1)}, u32[]{:S(2)}, u32[]{:S(2)}) %collective-permute-start.13) | collective-permute-done | bytes 118816 | tf_op jit(solution)/shard_map/ppermute | solution.py:437
  23.5 0.1 forward.13
  23.6 1.0 %collective-permute-start.14 = (s16[464,128]{1,0:T(8,128)(2,1)S(1)}, s16[464,128]{1,0:T(8,128)(2,1)S(1)}, u32[]{:S(2)}, u32[]{:S(2)}) collective-permute-start(s16[464,128]{1,0:T(8,128)(2,1)S(1)} %get-tuple-element.56), channel_id=1, source_target_pairs={{0,24},{8,16},{16,8},{24,0},{1,25},{9,17},{17,9},{25,1},{2,26},{10... | collective-permute-start | bytes 356360 | tf_op jit(solution)/shard_map/ppermute | solution.py:437
  24.6 1.0 %collective-permute-done.5.face = s16[464,128]{1,0:T(8,128)(2,1)S(1)} collective-permute-done((s16[464,128]{1,0:T(8,128)(2,1)S(1)}, s16[464,128]{1,0:T(8,128)(2,1)S(1)}, u32[]{:S(2)}, u32[]{:S(2)}) %collective-permute-start.5) | collective-permute-done | bytes 118816 | tf_op jit(solution)/shard_map/ppermute | solution.py:437
  25.7 0.1 forward.9
  25.7 2.9 %collective-permute-start.6 = (s16[464,128]{1,0:T(8,128)(2,1)S(1)}, s16[464,128]{1,0:T(8,128)(2,1)S(1)}, u32[]{:S(2)}, u32[]{:S(2)}) collective-permute-start(s16[464,128]{1,0:T(8,128)(2,1)S(1)} %get-tuple-element.44), channel_id=1, source_target_pairs={{0,24},{8,16},{16,8},{24,0},{1,25},{9,17},{17,9},{25,1},{2,26},{10... | collective-permute-start | bytes 356360 | tf_op jit(solution)/shard_map/ppermute | solution.py:437
  28.7 0.8 %collective-permute-done.14.face = s16[464,128]{1,0:T(8,128)(2,1)S(1)} collective-permute-done((s16[464,128]{1,0:T(8,128)(2,1)S(1)}, s16[464,128]{1,0:T(8,128)(2,1)S(1)}, u32[]{:S(2)}, u32[]{:S(2)}) %collective-permute-start.14) | collective-permute-done | bytes 118816 | tf_op jit(solution)/shard_map/ppermute | solution.py:437
  29.5 0.1 forward.14
  29.6 2.4 %collective-permute-start.15 = (s16[464,128]{1,0:T(8,128)(2,1)S(1)}, s16[464,128]{1,0:T(8,128)(2,1)S(1)}, u32[]{:S(2)}, u32[]{:S(2)}) collective-permute-start(s16[464,128]{1,0:T(8,128)(2,1)S(1)} %get-tuple-element.58), channel_id=1, source_target_pairs={{0,8},{8,0},{16,24},{24,16},{1,9},{9,1},{17,25},{25,17},{2,10},{10... | collective-permute-start | bytes 356360 | tf_op jit(solution)/shard_map/ppermute | solution.py:437
  32.0 0.9 %collective-permute-done.6.face = s16[464,128]{1,0:T(8,128)(2,1)S(1)} collective-permute-done((s16[464,128]{1,0:T(8,128)(2,1)S(1)}, s16[464,128]{1,0:T(8,128)(2,1)S(1)}, u32[]{:S(2)}, u32[]{:S(2)}) %collective-permute-start.6) | collective-permute-done | bytes 118816 | tf_op jit(solution)/shard_map/ppermute | solution.py:437
  32.9 1.9 %collective-permute-start.7 = (s16[464,128]{1,0:T(8,128)(2,1)S(1)}, s16[464,128]{1,0:T(8,128)(2,1)S(1)}, u32[]{:S(2)}, u32[]{:S(2)}) collective-permute-start(s16[464,128]{1,0:T(8,128)(2,1)S(1)} %get-tuple-element.46), channel_id=1, source_target_pairs={{0,8},{8,0},{16,24},{24,16},{1,9},{9,1},{17,25},{25,17},{2,10},{10... | collective-permute-start | bytes 356360 | tf_op jit(solution)/shard_map/ppermute | solution.py:437
  34.7 1.0 %collective-permute-done.15.face = s16[464,128]{1,0:T(8,128)(2,1)S(1)} collective-permute-done((s16[464,128]{1,0:T(8,128)(2,1)S(1)}, s16[464,128]{1,0:T(8,128)(2,1)S(1)}, u32[]{:S(2)}, u32[]{:S(2)}) %collective-permute-start.15) | collective-permute-done | bytes 118816 | tf_op jit(solution)/shard_map/ppermute | solution.py:437
  35.8 2.4 %collective-permute-start.16 = (s16[464,128]{1,0:T(8,128)(2,1)S(1)}, s16[464,128]{1,0:T(8,128)(2,1)S(1)}, u32[]{:S(2)}, u32[]{:S(2)}) collective-permute-start(s16[464,128]{1,0:T(8,128)(2,1)S(1)} %get-tuple-element.60), channel_id=1, source_target_pairs={{0,8},{8,0},{16,24},{24,16},{1,9},{9,1},{17,25},{25,17},{2,10},{10... | collective-permute-start | bytes 356360 | tf_op jit(solution)/shard_map/ppermute | solution.py:437
  38.2 0.4 collective-permute-done.7.face
  38.7 1.9 %collective-permute-start.8 = (s16[464,128]{1,0:T(8,128)(2,1)S(1)}, s16[464,128]{1,0:T(8,128)(2,1)S(1)}, u32[]{:S(2)}, u32[]{:S(2)}) collective-permute-start(s16[464,128]{1,0:T(8,128)(2,1)S(1)} %get-tuple-element.48), channel_id=1, source_target_pairs={{0,8},{8,0},{16,24},{24,16},{1,9},{9,1},{17,25},{25,17},{2,10},{10... | collective-permute-start | bytes 356360 | tf_op jit(solution)/shard_map/ppermute | solution.py:437
  40.6 1.0 %collective-permute-done.16.face = s16[464,128]{1,0:T(8,128)(2,1)S(1)} collective-permute-done((s16[464,128]{1,0:T(8,128)(2,1)S(1)}, s16[464,128]{1,0:T(8,128)(2,1)S(1)}, u32[]{:S(2)}, u32[]{:S(2)}) %collective-permute-start.16) | collective-permute-done | bytes 118816 | tf_op jit(solution)/shard_map/ppermute | solution.py:437
  41.6 2.2 %collective-permute-start.17 = (s16[464,128]{1,0:T(8,128)(2,1)S(1)}, s16[464,128]{1,0:T(8,128)(2,1)S(1)}, u32[]{:S(2)}, u32[]{:S(2)}) collective-permute-start(s16[464,128]{1,0:T(8,128)(2,1)S(1)} %get-tuple-element.62), channel_id=1, source_target_pairs={{0,24},{8,16},{16,8},{24,0},{1,25},{9,17},{17,9},{25,1},{2,26},{10... | collective-permute-start | bytes 356360 | tf_op jit(solution)/shard_map/ppermute | solution.py:437
  43.8 0.1 collective-permute-done.8.face
  44.0 4.4 %collective-permute-start.9 = (s16[464,128]{1,0:T(8,128)(2,1)S(1)}, s16[464,128]{1,0:T(8,128)(2,1)S(1)}, u32[]{:S(2)}, u32[]{:S(2)}) collective-permute-start(s16[464,128]{1,0:T(8,128)(2,1)S(1)} %get-tuple-element.50), channel_id=1, source_target_pairs={{0,24},{8,16},{16,8},{24,0},{1,25},{9,17},{17,9},{25,1},{2,26},{10... | collective-permute-start | bytes 356360 | tf_op jit(solution)/shard_map/ppermute | solution.py:437
  48.4 0.9 %collective-permute-done.17.face = s16[464,128]{1,0:T(8,128)(2,1)S(1)} collective-permute-done((s16[464,128]{1,0:T(8,128)(2,1)S(1)}, s16[464,128]{1,0:T(8,128)(2,1)S(1)}, u32[]{:S(2)}, u32[]{:S(2)}) %collective-permute-start.17) | collective-permute-done | bytes 118816 | tf_op jit(solution)/shard_map/ppermute | solution.py:437
  49.2 0.1 backward.8
  49.3 2.1 %collective-permute-start.18 = (s16[464,128]{1,0:T(8,128)(2,1)S(1)}, s16[464,128]{1,0:T(8,128)(2,1)S(1)}, u32[]{:S(2)}, u32[]{:S(2)}) collective-permute-start(s16[464,128]{1,0:T(8,128)(2,1)S(1)} %get-tuple-element.64), channel_id=1, source_target_pairs={{0,8},{8,0},{16,24},{24,16},{1,9},{9,1},{17,25},{25,17},{2,10},{10... | collective-permute-start | bytes 356360 | tf_op jit(solution)/shard_map/ppermute | solution.py:437
  51.4 0.6 %collective-permute-done.9.face = s16[464,128]{1,0:T(8,128)(2,1)S(1)} collective-permute-done((s16[464,128]{1,0:T(8,128)(2,1)S(1)}, s16[464,128]{1,0:T(8,128)(2,1)S(1)}, u32[]{:S(2)}, u32[]{:S(2)}) %collective-permute-start.9) | collective-permute-done | bytes 118816 | tf_op jit(solution)/shard_map/ppermute | solution.py:437
  52.0 1.9 %collective-permute-start.10 = (s16[464,128]{1,0:T(8,128)(2,1)S(1)}, s16[464,128]{1,0:T(8,128)(2,1)S(1)}, u32[]{:S(2)}, u32[]{:S(2)}) collective-permute-start(s16[464,128]{1,0:T(8,128)(2,1)S(1)} %get-tuple-element.52), channel_id=1, source_target_pairs={{0,8},{8,0},{16,24},{24,16},{1,9},{9,1},{17,25},{25,17},{2,10},{10... | collective-permute-start | bytes 356360 | tf_op jit(solution)/shard_map/ppermute | solution.py:437
  53.9 0.3 collective-permute-done.18.refs_2_
  54.2 0.6 backward.9.refs_0_
  54.8 2.2 %collective-permute-done.10.face = s16[464,128]{1,0:T(8,128)(2,1)S(1)} collective-permute-done((s16[464,128]{1,0:T(8,128)(2,1)S(1)}, s16[464,128]{1,0:T(8,128)(2,1)S(1)}, u32[]{:S(2)}, u32[]{:S(2)}) %collective-permute-start.10) | collective-permute-done | bytes 118816 | tf_op jit(solution)/shard_map/ppermute | solution.py:437
  56.9 1.4 %last.1 = f32[2,7,16,1024]{3,2,1,0:T(8,128)} custom-call(bf16[2,7,7,16,1024]{4,3,2,1,0:T(8,128)(2,1)S(1)} %copy-done, f32[2,2,16,1024]{3,2,1,0:T(8,128)S(1)} %copy-done.1, s16[464,128]{1,0:T(8,128)(2,1)S(1)} %collective-permute-done.10.face, f32[2,7,16,512]{3,2,1,0:T(8,128)S(1)} %backward.9.refs_0_, f32[2,7,16,512]{3,2,1,0:T(8,128)S(1)} %get-tuple-element.66.refs_1_), custom_call_target="tpu_custom_call" | custom-call | tf_op jit(solution)/shard_map/last/pallas_call | solution.py:375
  (18 shorter events, 0.4 us)
Async XLA Ops:
  0.0 15.6 %copy-start = (bf16[2,7,7,16,1024]{4,3,2,1,0:T(8,128)(2,1)S(1)}, bf16[2,7,7,16,1024]{4,3,2,1,0:T(8,128)(2,1)}, u32[]{:S(2)}) copy-start(bf16[2,7,7,16,1024]{4,3,2,1,0:T(8,128)(2,1)} %inverse_ref.25) | copy-start | bytes 9633796
  0.0 1.3 %copy-start.2 = (f32[2,7,16,1024]{3,2,1,0:T(8,128)S(1)}, f32[2,7,16,1024]{3,2,1,0:T(8,128)}, u32[]{:S(2)}) copy-start(f32[2,7,16,1024]{3,2,1,0:T(8,128)} %state_ref.7) | copy-start | bytes 2752516
  1.3 14.2 %copy-start.1 = (f32[2,2,16,1024]{3,2,1,0:T(8,128)S(1)}, f32[2,2,16,1024]{3,2,1,0:T(8,128)}, u32[]{:S(2)}) copy-start(f32[2,2,16,1024]{3,2,1,0:T(8,128)} %coupling_ref.25) | copy-start | bytes 786436
  1.5 10.2 %collective-permute-start.11 = (s16[912,128]{1,0:T(8,128)(2,1)S(1)}, s16[912,128]{1,0:T(8,128)(2,1)S(1)}, u32[]{:S(2)}, u32[]{:S(2)}) collective-permute-start(s16[912,128]{1,0:T(8,128)(2,1)S(1)} %encode.3), channel_id=1, source_target_pairs={{0,8},{8,0},{16,24},{24,16},{1,9},{9,1},{17,25},{25,17},{2,10},{10... | collective-permute-start | bytes 700424 | tf_op jit(solution)/shard_map/ppermute | solution.py:418
  4.7 10.5 %collective-permute-start = (s16[912,128]{1,0:T(8,128)(2,1)S(1)}, s16[912,128]{1,0:T(8,128)(2,1)S(1)}, u32[]{:S(2)}, u32[]{:S(2)}) collective-permute-start(s16[912,128]{1,0:T(8,128)(2,1)S(1)} %encode.2.after_ref), channel_id=1, source_target_pairs={{0,8},{8,0},{16,24},{24,16},{1,9},{9,1},{17,25},{25,17},{2,10},{10... | collective-permute-start | bytes 700424 | tf_op jit(solution)/shard_map/ppermute | solution.py:418
  5.0 8.3 %collective-permute-start.1 = (f32[2,7,2,1024]{3,2,1,0:T(2,128)S(1)}, f32[2,7,2,1024]{3,2,1,0:T(2,128)S(1)}, u32[]{:S(2)}, u32[]{:S(2)}) collective-permute-start(f32[2,7,2,1024]{3,2,1,0:T(2,128)S(1)} %get-tuple-element.37), channel_id=1, source_target_pairs={{0,2},{2,0},{4,6},{6,4},{1,3},{3,1},{5,7},{7,5},{8,10},{10,8},{12,... | collective-permute-start | bytes 344072 | tf_op jit(solution)/shard_map/ppermute | solution.py:424
  7.1 7.3 %collective-permute-start.2 = (f32[2,7,2,1024]{3,2,1,0:T(2,128)S(1)}, f32[2,7,2,1024]{3,2,1,0:T(2,128)S(1)}, u32[]{:S(2)}, u32[]{:S(2)}) collective-permute-start(f32[2,7,2,1024]{3,2,1,0:T(2,128)S(1)} %get-tuple-element.38), channel_id=1, source_target_pairs={{0,6},{2,4},{4,2},{6,0},{1,7},{3,5},{5,3},{7,1},{8,14},{10,12},{12... | collective-permute-start | bytes 344072 | tf_op jit(solution)/shard_map/ppermute | solution.py:424
  9.6 4.9 %collective-permute-start.3 = (f32[2,7,16,128]{3,2,1,0:T(8,128)S(1)}, f32[2,7,16,128]{3,2,1,0:T(8,128)S(1)}, u32[]{:S(2)}, u32[]{:S(2)}) collective-permute-start(f32[2,7,16,128]{3,2,1,0:T(8,128)S(1)} %get-tuple-element.39), channel_id=1, source_target_pairs={{0,1},{1,0},{2,3},{3,2},{4,5},{5,4},{6,7},{7,6},{8,9},{9,8},{10,11... | collective-permute-start | bytes 344072 | tf_op jit(solution)/shard_map/ppermute | solution.py:423
  9.6 0.9 %copy-start.3 = (s32[2,16,1024]{2,1,0:T(8,128)S(1)}, s32[2,16,1024]{2,1,0:T(8,128)}, u32[]{:S(2)}) copy-start(s32[2,16,1024]{2,1,0:T(8,128)} %wall_ref.1) | copy-start | bytes 393220
  11.7 11.9 %collective-permute-start.12 = (s16[912,128]{1,0:T(8,128)(2,1)S(1)}, s16[912,128]{1,0:T(8,128)(2,1)S(1)}, u32[]{:S(2)}, u32[]{:S(2)}) collective-permute-start(s16[912,128]{1,0:T(8,128)(2,1)S(1)} %collective-permute-done.11.refs_3_), channel_id=1, source_target_pairs={{0,16},{8,24},{16,0},{24,8},{1,17},{9,25},{17,1},{25,9},{2,18},{10... | collective-permute-start | bytes 700424 | tf_op jit(solution)/shard_map/ppermute | solution.py:443
  16.1 9.6 %collective-permute-start.4 = (s16[912,128]{1,0:T(8,128)(2,1)S(1)}, s16[912,128]{1,0:T(8,128)(2,1)S(1)}, u32[]{:S(2)}, u32[]{:S(2)}) collective-permute-start(s16[912,128]{1,0:T(8,128)(2,1)S(1)} %collective-permute-done.refs_3_), channel_id=1, source_target_pairs={{0,16},{8,24},{16,0},{24,8},{1,17},{9,25},{17,1},{25,9},{2,18},{10... | collective-permute-start | bytes 700424 | tf_op jit(solution)/shard_map/ppermute | solution.py:443
  18.4 5.2 %collective-permute-start.13 = (s16[464,128]{1,0:T(8,128)(2,1)S(1)}, s16[464,128]{1,0:T(8,128)(2,1)S(1)}, u32[]{:S(2)}, u32[]{:S(2)}) collective-permute-start(s16[464,128]{1,0:T(8,128)(2,1)S(1)} %get-tuple-element.54), channel_id=1, source_target_pairs={{0,8},{8,0},{16,24},{24,16},{1,9},{9,1},{17,25},{25,17},{2,10},{10... | collective-permute-start | bytes 356360 | tf_op jit(solution)/shard_map/ppermute | solution.py:437
  19.5 6.2 %collective-permute-start.5 = (s16[464,128]{1,0:T(8,128)(2,1)S(1)}, s16[464,128]{1,0:T(8,128)(2,1)S(1)}, u32[]{:S(2)}, u32[]{:S(2)}) collective-permute-start(s16[464,128]{1,0:T(8,128)(2,1)S(1)} %get-tuple-element.41), channel_id=1, source_target_pairs={{0,8},{8,0},{16,24},{24,16},{1,9},{9,1},{17,25},{25,17},{2,10},{10... | collective-permute-start | bytes 356360 | tf_op jit(solution)/shard_map/ppermute | solution.py:437
  23.6 5.9 %collective-permute-start.14 = (s16[464,128]{1,0:T(8,128)(2,1)S(1)}, s16[464,128]{1,0:T(8,128)(2,1)S(1)}, u32[]{:S(2)}, u32[]{:S(2)}) collective-permute-start(s16[464,128]{1,0:T(8,128)(2,1)S(1)} %get-tuple-element.56), channel_id=1, source_target_pairs={{0,24},{8,16},{16,8},{24,0},{1,25},{9,17},{17,9},{25,1},{2,26},{10... | collective-permute-start | bytes 356360 | tf_op jit(solution)/shard_map/ppermute | solution.py:437
  25.7 7.1 %collective-permute-start.6 = (s16[464,128]{1,0:T(8,128)(2,1)S(1)}, s16[464,128]{1,0:T(8,128)(2,1)S(1)}, u32[]{:S(2)}, u32[]{:S(2)}) collective-permute-start(s16[464,128]{1,0:T(8,128)(2,1)S(1)} %get-tuple-element.44), channel_id=1, source_target_pairs={{0,24},{8,16},{16,8},{24,0},{1,25},{9,17},{17,9},{25,1},{2,26},{10... | collective-permute-start | bytes 356360 | tf_op jit(solution)/shard_map/ppermute | solution.py:437
  29.6 6.2 %collective-permute-start.15 = (s16[464,128]{1,0:T(8,128)(2,1)S(1)}, s16[464,128]{1,0:T(8,128)(2,1)S(1)}, u32[]{:S(2)}, u32[]{:S(2)}) collective-permute-start(s16[464,128]{1,0:T(8,128)(2,1)S(1)} %get-tuple-element.58), channel_id=1, source_target_pairs={{0,8},{8,0},{16,24},{24,16},{1,9},{9,1},{17,25},{25,17},{2,10},{10... | collective-permute-start | bytes 356360 | tf_op jit(solution)/shard_map/ppermute | solution.py:437
  32.9 5.7 %collective-permute-start.7 = (s16[464,128]{1,0:T(8,128)(2,1)S(1)}, s16[464,128]{1,0:T(8,128)(2,1)S(1)}, u32[]{:S(2)}, u32[]{:S(2)}) collective-permute-start(s16[464,128]{1,0:T(8,128)(2,1)S(1)} %get-tuple-element.46), channel_id=1, source_target_pairs={{0,8},{8,0},{16,24},{24,16},{1,9},{9,1},{17,25},{25,17},{2,10},{10... | collective-permute-start | bytes 356360 | tf_op jit(solution)/shard_map/ppermute | solution.py:437
  35.8 5.7 %collective-permute-start.16 = (s16[464,128]{1,0:T(8,128)(2,1)S(1)}, s16[464,128]{1,0:T(8,128)(2,1)S(1)}, u32[]{:S(2)}, u32[]{:S(2)}) collective-permute-start(s16[464,128]{1,0:T(8,128)(2,1)S(1)} %get-tuple-element.60), channel_id=1, source_target_pairs={{0,8},{8,0},{16,24},{24,16},{1,9},{9,1},{17,25},{25,17},{2,10},{10... | collective-permute-start | bytes 356360 | tf_op jit(solution)/shard_map/ppermute | solution.py:437
  38.7 5.3 %collective-permute-start.8 = (s16[464,128]{1,0:T(8,128)(2,1)S(1)}, s16[464,128]{1,0:T(8,128)(2,1)S(1)}, u32[]{:S(2)}, u32[]{:S(2)}) collective-permute-start(s16[464,128]{1,0:T(8,128)(2,1)S(1)} %get-tuple-element.48), channel_id=1, source_target_pairs={{0,8},{8,0},{16,24},{24,16},{1,9},{9,1},{17,25},{25,17},{2,10},{10... | collective-permute-start | bytes 356360 | tf_op jit(solution)/shard_map/ppermute | solution.py:437
  41.6 7.6 %collective-permute-start.17 = (s16[464,128]{1,0:T(8,128)(2,1)S(1)}, s16[464,128]{1,0:T(8,128)(2,1)S(1)}, u32[]{:S(2)}, u32[]{:S(2)}) collective-permute-start(s16[464,128]{1,0:T(8,128)(2,1)S(1)} %get-tuple-element.62), channel_id=1, source_target_pairs={{0,24},{8,16},{16,8},{24,0},{1,25},{9,17},{17,9},{25,1},{2,26},{10... | collective-permute-start | bytes 356360 | tf_op jit(solution)/shard_map/ppermute | solution.py:437
  44.0 8.0 %collective-permute-start.9 = (s16[464,128]{1,0:T(8,128)(2,1)S(1)}, s16[464,128]{1,0:T(8,128)(2,1)S(1)}, u32[]{:S(2)}, u32[]{:S(2)}) collective-permute-start(s16[464,128]{1,0:T(8,128)(2,1)S(1)} %get-tuple-element.50), channel_id=1, source_target_pairs={{0,24},{8,16},{16,8},{24,0},{1,25},{9,17},{17,9},{25,1},{2,26},{10... | collective-permute-start | bytes 356360 | tf_op jit(solution)/shard_map/ppermute | solution.py:437
  49.3 4.9 %collective-permute-start.18 = (s16[464,128]{1,0:T(8,128)(2,1)S(1)}, s16[464,128]{1,0:T(8,128)(2,1)S(1)}, u32[]{:S(2)}, u32[]{:S(2)}) collective-permute-start(s16[464,128]{1,0:T(8,128)(2,1)S(1)} %get-tuple-element.64), channel_id=1, source_target_pairs={{0,8},{8,0},{16,24},{24,16},{1,9},{9,1},{17,25},{25,17},{2,10},{10... | collective-permute-start | bytes 356360 | tf_op jit(solution)/shard_map/ppermute | solution.py:437
  52.0 4.9 %collective-permute-start.10 = (s16[464,128]{1,0:T(8,128)(2,1)S(1)}, s16[464,128]{1,0:T(8,128)(2,1)S(1)}, u32[]{:S(2)}, u32[]{:S(2)}) collective-permute-start(s16[464,128]{1,0:T(8,128)(2,1)S(1)} %get-tuple-element.52), channel_id=1, source_target_pairs={{0,8},{8,0},{16,24},{24,16},{1,9},{9,1},{17,25},{25,17},{2,10},{10... | collective-permute-start | bytes 356360 | tf_op jit(solution)/shard_map/ppermute | solution.py:437

commit v6 on v5

--- a/solution.py
+++ b/solution.py
@@ -348,6 +348,14 @@
         x_out[...] = x_in[...]
 
 
+def first_kernel(chunk, parts, count, inverse_ref, coupling_ref, *refs):
+    forward_kernel(chunk, parts, 0, count, inverse_ref, coupling_ref, None, None, None, *refs)
+
+
+def unsent_kernel(chunk, *refs):
+    backward_kernel(chunk, 0, *refs, None)
+
+
 def final_kernel(chunk, inverse_ref, coupling_ref, face, *refs):
     parts, out = refs[:-1], refs[-1]
     width = parts[0].shape[3]
@@ -442,41 +450,54 @@
             passed = lax.optimization_barrier((passed, *gate))[0]
         return lax.ppermute(passed, "ia", [(i, i ^ 2) for i in range(4)] if count == 4 else swaps(count, 1))
 
-    x, far, face = [], [pass_on(0)], [None] * chunks
-    for h in range(halves):
-        def kernel(*refs, h=h):
+    last_step = 2 * count - 2
+    x, sent, face, far = list(local), {}, [None] * chunks, [pass_on(0, open_cells)]
+
+    def halo(h):
+        def kernel(*refs):
             rest = refs[2 + sets_k : 4 + sets_k]
             xs = refs[4 + sets_k :]
             halo_kernel(h, halves, counts, *refs[:2], refs[2 : 2 + sets_k], *rest, xs[:parts], xs[parts:])
 
-        operands = [*edges_j, *edges_k, near[h], open_cells, *local[h * parts : (h + 1) * parts]]
+        own = slice(h * parts, (h + 1) * parts)
+        operands = [*edges_j, *edges_k, near[h], open_cells, *x[own]]
         first = len(operands) - parts
-        x += call(kernel, operands, [part] * parts, "halo", {first + i: i for i in range(parts)})
-        for c in range(h * parts, (h + 1) * parts):
-            def kernel(inverse_ref, coupling_ref, *refs, c=c):
-                forward_kernel(c, parts, 0, count, inverse_ref, coupling_ref, None, None, None, *refs)
-
-            x[c], send = call(kernel, [inverse, coupling, x[c]], [part, face_code], "forward", {2: 0})
-            face[c] = hop_pair(send, 0, 1)
-        if h:
-            far.append(pass_on(h, send))
-
-    for hop in range(1, count):
+        x[own] = call(kernel, operands, [part] * parts, "halo", {first + i: i for i in range(parts)})
+
+    def step(c, k):
+        hop = min(k, last_step - k)
+        forward = k < count
+        gate = sent.get((c - 1, k + 1))
+        entry = x[c] if gate is None else lax.optimization_barrier((x[c], gate))[0]
+        if k == 0:
+            kernel = functools.partial(first_kernel, c, parts, count)
+            operands = [inverse, coupling, entry]
+        elif forward:
+            kernel = functools.partial(forward_kernel, c, parts, hop, count)
+            operands = [inverse, coupling, open_cells, far[c // parts], face[c], entry]
+        elif k < last_step:
+            kernel = functools.partial(backward_kernel, c, hop)
+            operands = [inverse, coupling, face[c], entry]
+        else:
+            kernel = functools.partial(unsent_kernel, c)
+            operands = [inverse, coupling, face[c], entry]
+        alias = {len(operands) - 1: 0}
+        name = "forward" if forward else "backward"
+        if k == last_step:
+            (x[c],) = call(kernel, operands, [part], name, alias)
+            return
+        x[c], sent[c, k] = call(kernel, operands, [part, face_code], name, alias)
+        face[c] = hop_pair(sent[c, k], hop, hop + 1 if k < count - 1 else hop - 1)
+
+    halo(0)
+    step(0, 0)
+    for h in range(1, halves):
+        far.append(pass_on(h, sent[0, 0]))
+        halo(h)
+    for turn in range(1, last_step + chunks):
         for c in range(chunks):
-            kernel = functools.partial(forward_kernel, c, parts, hop, count)
-            operands = [inverse, coupling, open_cells, far[c // parts], face[c], x[c]]
-            x[c], send = call(kernel, operands, [part, face_code], "forward", {5: 0})
-            face[c] = hop_pair(send, hop, hop + 1) if hop < count - 1 else hop_pair(send, hop, hop - 1)
-    for hop in reversed(range(1, count - 1)):
-        for c in range(chunks):
-            kernel = functools.partial(backward_kernel, c, hop)
-            x[c], send = call(kernel, [inverse, coupling, face[c], x[c]], [part, face_code], "backward", {3: 0})
-            face[c] = hop_pair(send, hop, hop - 1)
-    for c in range(chunks - 1):
-        def kernel(*refs, c=c):
-            backward_kernel(c, 0, *refs, None)
-
-        (x[c],) = call(kernel, [inverse, coupling, face[c], x[c]], [part], "backward", {3: 0})
+            if 0 <= turn - c <= last_step and (c, turn - c) != (chunks - 1, last_step):
+                step(c, turn - c)
     return call(functools.partial(final_kernel, chunks - 1), [inverse, coupling, face[-1], *x], [full], "last")[0]
 
 

time: 58.5 us -> 61.2 us (1.046)
  waiting for transfers between devices: 14.1 us -> 20.9 us
  starting transfers between devices: 35.9 us -> 31.9 us
    ppermute x12, waiting for transfers between devices: 12.2 us -> 19.7 us  [hop_pair(): return lax.ppermute(value, 'ia', swaps(count, min(source, target) % 2))]
    ppermute x12, starting transfers between devices: 25.2 us -> 21.1 us  [hop_pair(): return lax.ppermute(value, 'ia', swaps(count, min(source, target) % 2))]
    ppermute x2, waiting for transfers between devices: 0.74 us -> 0.01 us  [shards(): lax.ppermute(coded[h], 'ia', swaps(count, 0))]
  transfers between devices with their start and end apart: 19 -> 19, of which waited for: 14 -> 12; matrix products, arithmetic and copies ran while one was open for 0% -> 0% of each run, Pallas kernels for 8% -> 7%
where the time goes in v6:
time: 61.2 us; the launch traced here: 61 us
  starting transfers between devices  31.9 us (52%)
  waiting for transfers between devices  20.9 us (34%)
  Pallas kernels  6 us (10%)
  local copies, waits for them, and re-layouts  2.13 us (3%)
    ppermute x12, starting transfers between devices, hop_pair(): return lax.ppermute(value, 'ia', swaps(count, min(source, target) % 2))  21.1 us
    ppermute x12, waiting for transfers between devices, hop_pair(): return lax.ppermute(value, 'ia', swaps(count, min(source, target) % 2))  19.7 us
    pallas_call x20, Pallas kernels, call(): pl.pallas_call(kernel, in_specs=[whole()] * len(operands), out_specs=[who...  6 us
    ppermute x2, starting transfers between devices, shards(): lax.ppermute(edge, 'ja', swaps(count_j, s))  4.62 us
    ppermute x2, starting transfers between devices, pass_on(): lax.ppermute(passed, 'ia', [(i, i ^ 2) for i in range(4)] if count == 4 e...  3.1 us
    ppermute x2, starting transfers between devices, shards(): lax.ppermute(coded[h], 'ia', swaps(count, 0))  3.08 us
    unnamed x8, local copies, waits for them, and re-layouts  2.13 us
  transfers between devices with their start and end apart: 19, of which 12 were waited for; matrix products, arithmetic and copies ran while one was open for 0% of the time, Pallas kernels for 7%

profile of v6, /device:TPU:0, one launch (start us, length us, event | category | flops | bytes accessed | tf_op | source)
XLA Modules:
  0.0 61.0 jit_solution(6818832092943611215)
XLA Ops:
  0.0 1.2 %copy-done.2 = f32[2,7,16,1024]{3,2,1,0:T(8,128)S(1)} copy-done((f32[2,7,16,1024]{3,2,1,0:T(8,128)S(1)}, f32[2,7,16,1024]{3,2,1,0:T(8,128)}, u32[]{:S(2)}) %copy-start.2) | copy-done | bytes 917528
  1.2 0.2 encode.3
  1.4 3.0 %collective-permute-start.4 = (s16[912,128]{1,0:T(8,128)(2,1)S(1)}, s16[912,128]{1,0:T(8,128)(2,1)S(1)}, u32[]{:S(2)}, u32[]{:S(2)}) collective-permute-start(s16[912,128]{1,0:T(8,128)(2,1)S(1)} %encode.3), channel_id=1, source_target_pairs={{0,8},{8,0},{16,24},{24,16},{1,9},{9,1},{17,25},{25,17},{2,10},{10... | collective-permute-start | bytes 700424 | tf_op jit(solution)/shard_map/ppermute | solution.py:426
  4.4 0.2 encode.2.after_ref
  4.6 0.1 collective-permute-start
  4.6 0.2 edges.1
  4.9 2.1 %collective-permute-start.1 = (f32[2,7,2,1024]{3,2,1,0:T(2,128)S(1)}, f32[2,7,2,1024]{3,2,1,0:T(2,128)S(1)}, u32[]{:S(2)}, u32[]{:S(2)}) collective-permute-start(f32[2,7,2,1024]{3,2,1,0:T(2,128)S(1)} %get-tuple-element.43), channel_id=1, source_target_pairs={{0,2},{2,0},{4,6},{6,4},{1,3},{3,1},{5,7},{7,5},{8,10},{10,8},{12,... | collective-permute-start | bytes 344072 | tf_op jit(solution)/shard_map/ppermute | solution.py:432
  7.0 2.5 %collective-permute-start.2 = (f32[2,7,2,1024]{3,2,1,0:T(2,128)S(1)}, f32[2,7,2,1024]{3,2,1,0:T(2,128)S(1)}, u32[]{:S(2)}, u32[]{:S(2)}) collective-permute-start(f32[2,7,2,1024]{3,2,1,0:T(2,128)S(1)} %get-tuple-element.44), channel_id=1, source_target_pairs={{0,6},{2,4},{4,2},{6,0},{1,7},{3,5},{5,3},{7,1},{8,14},{10,12},{12... | collective-permute-start | bytes 344072 | tf_op jit(solution)/shard_map/ppermute | solution.py:432
  9.5 0.9 %copy-done.3 = s32[2,16,1024]{2,1,0:T(8,128)S(1)} copy-done((s32[2,16,1024]{2,1,0:T(8,128)S(1)}, s32[2,16,1024]{2,1,0:T(8,128)}, u32[]{:S(2)}) %copy-start.3) | copy-done | bytes 131096
  10.4 1.2 %local.1 = (f32[2,7,16,512]{3,2,1,0:T(8,128)S(1)}, f32[2,7,16,512]{3,2,1,0:T(8,128)S(1)}, f32[2,16,1024]{2,1,0:T(8,128)S(1)}) custom-call(f32[2,7,16,1024]{3,2,1,0:T(8,128)S(1)} %copy-done.2, s32[2,16,1024]{2,1,0:T(8,128)S(1)} %copy-done.3), custom_call_target="tpu_custom_call" | custom-call | flops 9175040 | bytes 2293760 | tf_op jit(solution)/shard_map/local/pallas_call | solution.py:383
  11.6 1.6 %collective-permute-start.6 = (s16[912,128]{1,0:T(8,128)(2,1)S(1)}, s16[912,128]{1,0:T(8,128)(2,1)S(1)}, u32[]{:S(2)}, u32[]{:S(2)}) collective-permute-start(s16[912,128]{1,0:T(8,128)(2,1)S(1)} %collective-permute-done.4.refs_3_), channel_id=1, source_target_pairs={{0,16},{8,24},{16,0},{24,8},{1,17},{9,25},{17,1},{25,9},{2,18},{10... | collective-permute-start | bytes 700424 | tf_op jit(solution)/shard_map/ppermute | solution.py:451
  13.2 1.2 %collective-permute-done.2.refs_1_ = f32[2,7,2,1024]{3,2,1,0:T(2,128)S(1)} collective-permute-done((f32[2,7,2,1024]{3,2,1,0:T(2,128)S(1)}, f32[2,7,2,1024]{3,2,1,0:T(2,128)S(1)}, u32[]{:S(2)}, u32[]{:S(2)}) %collective-permute-start.2) | collective-permute-done | bytes 114720 | tf_op jit(solution)/shard_map/ppermute | solution.py:432
  14.4 0.3 halo.2.refs_0_
  14.7 0.5 forward.8
  15.2 1.1 %collective-permute-start.7 = (s16[464,128]{1,0:T(8,128)(2,1)S(1)}, s16[464,128]{1,0:T(8,128)(2,1)S(1)}, u32[]{:S(2)}, u32[]{:S(2)}) collective-permute-start(s16[464,128]{1,0:T(8,128)(2,1)S(1)} %get-tuple-element.47), channel_id=1, source_target_pairs={{0,8},{8,0},{16,24},{24,16},{1,9},{9,1},{17,25},{25,17},{2,10},{10... | collective-permute-start | bytes 356360 | tf_op jit(solution)/shard_map/ppermute | solution.py:445
  16.4 1.5 %collective-permute-start.5 = (s16[912,128]{1,0:T(8,128)(2,1)S(1)}, s16[912,128]{1,0:T(8,128)(2,1)S(1)}, u32[]{:S(2)}, u32[]{:S(2)}) collective-permute-start(s16[912,128]{1,0:T(8,128)(2,1)S(1)} %collective-permute-done.refs_3_), channel_id=1, source_target_pairs={{0,16},{8,24},{16,0},{24,8},{1,17},{9,25},{17,1},{25,9},{2,18},{10... | collective-permute-start | bytes 700424 | tf_op jit(solution)/shard_map/ppermute | solution.py:451
  17.9 2.3 %collective-permute-done.7.face = s16[464,128]{1,0:T(8,128)(2,1)S(1)} collective-permute-done((s16[464,128]{1,0:T(8,128)(2,1)S(1)}, s16[464,128]{1,0:T(8,128)(2,1)S(1)}, u32[]{:S(2)}, u32[]{:S(2)}) %collective-permute-start.7) | collective-permute-done | bytes 118816 | tf_op jit(solution)/shard_map/ppermute | solution.py:445
  20.1 0.1 forward.9
  20.2 2.5 %collective-permute-start.9 = (s16[464,128]{1,0:T(8,128)(2,1)S(1)}, s16[464,128]{1,0:T(8,128)(2,1)S(1)}, u32[]{:S(2)}, u32[]{:S(2)}) collective-permute-start(s16[464,128]{1,0:T(8,128)(2,1)S(1)} %get-tuple-element.52), channel_id=1, source_target_pairs={{0,24},{8,16},{16,8},{24,0},{1,25},{9,17},{17,9},{25,1},{2,26},{10... | collective-permute-start | bytes 356360 | tf_op jit(solution)/shard_map/ppermute | solution.py:445
  22.7 0.4 halo.3.refs_0_
  23.1 0.5 forward.10
  23.6 0.1 collective-permute-start.8
  23.7 3.0 %collective-permute-done.9.face = s16[464,128]{1,0:T(8,128)(2,1)S(1)} collective-permute-done((s16[464,128]{1,0:T(8,128)(2,1)S(1)}, s16[464,128]{1,0:T(8,128)(2,1)S(1)}, u32[]{:S(2)}, u32[]{:S(2)}) %collective-permute-start.9) | collective-permute-done | bytes 118816 | tf_op jit(solution)/shard_map/ppermute | solution.py:445
  26.7 0.1 forward.11
  26.7 2.4 %collective-permute-start.11 = (s16[464,128]{1,0:T(8,128)(2,1)S(1)}, s16[464,128]{1,0:T(8,128)(2,1)S(1)}, u32[]{:S(2)}, u32[]{:S(2)}) collective-permute-start(s16[464,128]{1,0:T(8,128)(2,1)S(1)} %get-tuple-element.57), channel_id=1, source_target_pairs={{0,8},{8,0},{16,24},{24,16},{1,9},{9,1},{17,25},{25,17},{2,10},{10... | collective-permute-start | bytes 356360 | tf_op jit(solution)/shard_map/ppermute | solution.py:445
  29.2 0.6 %collective-permute-done.8.face = s16[464,128]{1,0:T(8,128)(2,1)S(1)} collective-permute-done((s16[464,128]{1,0:T(8,128)(2,1)S(1)}, s16[464,128]{1,0:T(8,128)(2,1)S(1)}, u32[]{:S(2)}, u32[]{:S(2)}) %collective-permute-start.8) | collective-permute-done | bytes 118816 | tf_op jit(solution)/shard_map/ppermute | solution.py:445
  29.8 0.1 forward.12
  29.9 1.3 %collective-permute-start.10 = (s16[464,128]{1,0:T(8,128)(2,1)S(1)}, s16[464,128]{1,0:T(8,128)(2,1)S(1)}, u32[]{:S(2)}, u32[]{:S(2)}) collective-permute-start(s16[464,128]{1,0:T(8,128)(2,1)S(1)} %get-tuple-element.59), channel_id=1, source_target_pairs={{0,24},{8,16},{16,8},{24,0},{1,25},{9,17},{17,9},{25,1},{2,26},{10... | collective-permute-start | bytes 356360 | tf_op jit(solution)/shard_map/ppermute | solution.py:445
  31.2 2.0 %collective-permute-done.11.face = s16[464,128]{1,0:T(8,128)(2,1)S(1)} collective-permute-done((s16[464,128]{1,0:T(8,128)(2,1)S(1)}, s16[464,128]{1,0:T(8,128)(2,1)S(1)}, u32[]{:S(2)}, u32[]{:S(2)}) %collective-permute-start.11) | collective-permute-done | bytes 118816 | tf_op jit(solution)/shard_map/ppermute | solution.py:445
  33.3 0.1 forward.13
  33.3 1.8 %collective-permute-start.13 = (s16[464,128]{1,0:T(8,128)(2,1)S(1)}, s16[464,128]{1,0:T(8,128)(2,1)S(1)}, u32[]{:S(2)}, u32[]{:S(2)}) collective-permute-start(s16[464,128]{1,0:T(8,128)(2,1)S(1)} %get-tuple-element.62), channel_id=1, source_target_pairs={{0,8},{8,0},{16,24},{24,16},{1,9},{9,1},{17,25},{25,17},{2,10},{10... | collective-permute-start | bytes 356360 | tf_op jit(solution)/shard_map/ppermute | solution.py:445
  35.2 1.0 %collective-permute-done.10.face = s16[464,128]{1,0:T(8,128)(2,1)S(1)} collective-permute-done((s16[464,128]{1,0:T(8,128)(2,1)S(1)}, s16[464,128]{1,0:T(8,128)(2,1)S(1)}, u32[]{:S(2)}, u32[]{:S(2)}) %collective-permute-start.10) | collective-permute-done | bytes 118816 | tf_op jit(solution)/shard_map/ppermute | solution.py:445
  36.2 0.1 forward.14
  36.2 1.4 %collective-permute-start.12 = (s16[464,128]{1,0:T(8,128)(2,1)S(1)}, s16[464,128]{1,0:T(8,128)(2,1)S(1)}, u32[]{:S(2)}, u32[]{:S(2)}) collective-permute-start(s16[464,128]{1,0:T(8,128)(2,1)S(1)} %get-tuple-element.64), channel_id=1, source_target_pairs={{0,8},{8,0},{16,24},{24,16},{1,9},{9,1},{17,25},{25,17},{2,10},{10... | collective-permute-start | bytes 356360 | tf_op jit(solution)/shard_map/ppermute | solution.py:445
  37.7 0.6 %collective-permute-done.13.face = s16[464,128]{1,0:T(8,128)(2,1)S(1)} collective-permute-done((s16[464,128]{1,0:T(8,128)(2,1)S(1)}, s16[464,128]{1,0:T(8,128)(2,1)S(1)}, u32[]{:S(2)}, u32[]{:S(2)}) %collective-permute-start.13) | collective-permute-done | bytes 118816 | tf_op jit(solution)/shard_map/ppermute | solution.py:445
  38.4 3.4 %collective-permute-start.15 = (s16[464,128]{1,0:T(8,128)(2,1)S(1)}, s16[464,128]{1,0:T(8,128)(2,1)S(1)}, u32[]{:S(2)}, u32[]{:S(2)}) collective-permute-start(s16[464,128]{1,0:T(8,128)(2,1)S(1)} %get-tuple-element.67), channel_id=1, source_target_pairs={{0,24},{8,16},{16,8},{24,0},{1,25},{9,17},{17,9},{25,1},{2,26},{10... | collective-permute-start | bytes 356360 | tf_op jit(solution)/shard_map/ppermute | solution.py:445
  41.8 0.6 collective-permute-done.12.face
  42.5 1.4 %collective-permute-start.14 = (s16[464,128]{1,0:T(8,128)(2,1)S(1)}, s16[464,128]{1,0:T(8,128)(2,1)S(1)}, u32[]{:S(2)}, u32[]{:S(2)}) collective-permute-start(s16[464,128]{1,0:T(8,128)(2,1)S(1)} %get-tuple-element.69), channel_id=1, source_target_pairs={{0,8},{8,0},{16,24},{24,16},{1,9},{9,1},{17,25},{25,17},{2,10},{10... | collective-permute-start | bytes 356360 | tf_op jit(solution)/shard_map/ppermute | solution.py:445
  43.9 1.0 %collective-permute-done.15.face = s16[464,128]{1,0:T(8,128)(2,1)S(1)} collective-permute-done((s16[464,128]{1,0:T(8,128)(2,1)S(1)}, s16[464,128]{1,0:T(8,128)(2,1)S(1)}, u32[]{:S(2)}, u32[]{:S(2)}) %collective-permute-start.15) | collective-permute-done | bytes 118816 | tf_op jit(solution)/shard_map/ppermute | solution.py:445
  45.0 3.0 %collective-permute-done.14.face = s16[464,128]{1,0:T(8,128)(2,1)S(1)} collective-permute-done((s16[464,128]{1,0:T(8,128)(2,1)S(1)}, s16[464,128]{1,0:T(8,128)(2,1)S(1)}, u32[]{:S(2)}, u32[]{:S(2)}) %collective-permute-start.14) | collective-permute-done | bytes 118816 | tf_op jit(solution)/shard_map/ppermute | solution.py:445
  47.9 0.1 backward.7
  48.0 3.3 %collective-permute-start.16 = (s16[464,128]{1,0:T(8,128)(2,1)S(1)}, s16[464,128]{1,0:T(8,128)(2,1)S(1)}, u32[]{:S(2)}, u32[]{:S(2)}) collective-permute-start(s16[464,128]{1,0:T(8,128)(2,1)S(1)} %get-tuple-element.74), channel_id=1, source_target_pairs={{0,24},{8,16},{16,8},{24,0},{1,25},{9,17},{17,9},{25,1},{2,26},{10... | collective-permute-start | bytes 356360 | tf_op jit(solution)/shard_map/ppermute | solution.py:445
  51.3 0.4 collective-permute-start.18
  51.7 3.0 %collective-permute-done.16.face = s16[464,128]{1,0:T(8,128)(2,1)S(1)} collective-permute-done((s16[464,128]{1,0:T(8,128)(2,1)S(1)}, s16[464,128]{1,0:T(8,128)(2,1)S(1)}, u32[]{:S(2)}, u32[]{:S(2)}) %collective-permute-start.16) | collective-permute-done | bytes 118816 | tf_op jit(solution)/shard_map/ppermute | solution.py:445
  54.7 1.7 %collective-permute-start.17 = (s16[464,128]{1,0:T(8,128)(2,1)S(1)}, s16[464,128]{1,0:T(8,128)(2,1)S(1)}, u32[]{:S(2)}, u32[]{:S(2)}) collective-permute-start(s16[464,128]{1,0:T(8,128)(2,1)S(1)} %get-tuple-element.76), channel_id=1, source_target_pairs={{0,8},{8,0},{16,24},{24,16},{1,9},{9,1},{17,25},{25,17},{2,10},{10... | collective-permute-start | bytes 356360 | tf_op jit(solution)/shard_map/ppermute | solution.py:445
  56.4 0.6 backward.9.refs_0_
  57.0 2.6 %collective-permute-done.17.face = s16[464,128]{1,0:T(8,128)(2,1)S(1)} collective-permute-done((s16[464,128]{1,0:T(8,128)(2,1)S(1)}, s16[464,128]{1,0:T(8,128)(2,1)S(1)}, u32[]{:S(2)}, u32[]{:S(2)}) %collective-permute-start.17) | collective-permute-done | bytes 118816 | tf_op jit(solution)/shard_map/ppermute | solution.py:445
  59.6 1.4 %last.1 = f32[2,7,16,1024]{3,2,1,0:T(8,128)} custom-call(bf16[2,7,7,16,1024]{4,3,2,1,0:T(8,128)(2,1)S(1)} %copy-done, f32[2,2,16,1024]{3,2,1,0:T(8,128)S(1)} %copy-done.1, s16[464,128]{1,0:T(8,128)(2,1)S(1)} %collective-permute-done.17.face, f32[2,7,16,512]{3,2,1,0:T(8,128)S(1)} %backward.9.refs_0_, f32[2,7,16,512]{3,2,1,0:T(8,128)S(1)} %get-tuple-element.78.refs_1_), custom_call_target="tpu_custom_call" | custom-call | tf_op jit(solution)/shard_map/last/pallas_call | solution.py:383
  (18 shorter events, 0.3 us)
Async XLA Ops:
  0.0 14.7 %copy-start.1 = (f32[2,2,16,1024]{3,2,1,0:T(8,128)S(1)}, f32[2,2,16,1024]{3,2,1,0:T(8,128)}, u32[]{:S(2)}) copy-start(f32[2,2,16,1024]{3,2,1,0:T(8,128)} %coupling_ref.25) | copy-start | bytes 786436
  0.0 1.2 %copy-start.2 = (f32[2,7,16,1024]{3,2,1,0:T(8,128)S(1)}, f32[2,7,16,1024]{3,2,1,0:T(8,128)}, u32[]{:S(2)}) copy-start(f32[2,7,16,1024]{3,2,1,0:T(8,128)} %state_ref.7) | copy-start | bytes 2752516
  1.2 13.5 %copy-start = (bf16[2,7,7,16,1024]{4,3,2,1,0:T(8,128)(2,1)S(1)}, bf16[2,7,7,16,1024]{4,3,2,1,0:T(8,128)(2,1)}, u32[]{:S(2)}) copy-start(bf16[2,7,7,16,1024]{4,3,2,1,0:T(8,128)(2,1)} %inverse_ref.25) | copy-start | bytes 9633796
  1.4 10.2 %collective-permute-start.4 = (s16[912,128]{1,0:T(8,128)(2,1)S(1)}, s16[912,128]{1,0:T(8,128)(2,1)S(1)}, u32[]{:S(2)}, u32[]{:S(2)}) collective-permute-start(s16[912,128]{1,0:T(8,128)(2,1)S(1)} %encode.3), channel_id=1, source_target_pairs={{0,8},{8,0},{16,24},{24,16},{1,9},{9,1},{17,25},{25,17},{2,10},{10... | collective-permute-start | bytes 700424 | tf_op jit(solution)/shard_map/ppermute | solution.py:426
  4.6 11.8 %collective-permute-start = (s16[912,128]{1,0:T(8,128)(2,1)S(1)}, s16[912,128]{1,0:T(8,128)(2,1)S(1)}, u32[]{:S(2)}, u32[]{:S(2)}) collective-permute-start(s16[912,128]{1,0:T(8,128)(2,1)S(1)} %encode.2.after_ref), channel_id=1, source_target_pairs={{0,8},{8,0},{16,24},{24,16},{1,9},{9,1},{17,25},{25,17},{2,10},{10... | collective-permute-start | bytes 700424 | tf_op jit(solution)/shard_map/ppermute | solution.py:426
  4.9 8.3 %collective-permute-start.1 = (f32[2,7,2,1024]{3,2,1,0:T(2,128)S(1)}, f32[2,7,2,1024]{3,2,1,0:T(2,128)S(1)}, u32[]{:S(2)}, u32[]{:S(2)}) collective-permute-start(f32[2,7,2,1024]{3,2,1,0:T(2,128)S(1)} %get-tuple-element.43), channel_id=1, source_target_pairs={{0,2},{2,0},{4,6},{6,4},{1,3},{3,1},{5,7},{7,5},{8,10},{10,8},{12,... | collective-permute-start | bytes 344072 | tf_op jit(solution)/shard_map/ppermute | solution.py:432
  7.0 7.3 %collective-permute-start.2 = (f32[2,7,2,1024]{3,2,1,0:T(2,128)S(1)}, f32[2,7,2,1024]{3,2,1,0:T(2,128)S(1)}, u32[]{:S(2)}, u32[]{:S(2)}) collective-permute-start(f32[2,7,2,1024]{3,2,1,0:T(2,128)S(1)} %get-tuple-element.44), channel_id=1, source_target_pairs={{0,6},{2,4},{4,2},{6,0},{1,7},{3,5},{5,3},{7,1},{8,14},{10,12},{12... | collective-permute-start | bytes 344072 | tf_op jit(solution)/shard_map/ppermute | solution.py:432
  9.5 4.9 %collective-permute-start.3 = (f32[2,7,16,128]{3,2,1,0:T(8,128)S(1)}, f32[2,7,16,128]{3,2,1,0:T(8,128)S(1)}, u32[]{:S(2)}, u32[]{:S(2)}) collective-permute-start(f32[2,7,16,128]{3,2,1,0:T(8,128)S(1)} %get-tuple-element.45), channel_id=1, source_target_pairs={{0,1},{1,0},{2,3},{3,2},{4,5},{5,4},{6,7},{7,6},{8,9},{9,8},{10,11... | collective-permute-start | bytes 344072 | tf_op jit(solution)/shard_map/ppermute | solution.py:431
  9.5 0.9 %copy-start.3 = (s32[2,16,1024]{2,1,0:T(8,128)S(1)}, s32[2,16,1024]{2,1,0:T(8,128)}, u32[]{:S(2)}) copy-start(s32[2,16,1024]{2,1,0:T(8,128)} %wall_ref.1) | copy-start | bytes 393220
  11.6 8.6 %collective-permute-start.6 = (s16[912,128]{1,0:T(8,128)(2,1)S(1)}, s16[912,128]{1,0:T(8,128)(2,1)S(1)}, u32[]{:S(2)}, u32[]{:S(2)}) collective-permute-start(s16[912,128]{1,0:T(8,128)(2,1)S(1)} %collective-permute-done.4.refs_3_), channel_id=1, source_target_pairs={{0,16},{8,24},{16,0},{24,8},{1,17},{9,25},{17,1},{25,9},{2,18},{10... | collective-permute-start | bytes 700424 | tf_op jit(solution)/shard_map/ppermute | solution.py:451
  15.2 4.9 %collective-permute-start.7 = (s16[464,128]{1,0:T(8,128)(2,1)S(1)}, s16[464,128]{1,0:T(8,128)(2,1)S(1)}, u32[]{:S(2)}, u32[]{:S(2)}) collective-permute-start(s16[464,128]{1,0:T(8,128)(2,1)S(1)} %get-tuple-element.47), channel_id=1, source_target_pairs={{0,8},{8,0},{16,24},{24,16},{1,9},{9,1},{17,25},{25,17},{2,10},{10... | collective-permute-start | bytes 356360 | tf_op jit(solution)/shard_map/ppermute | solution.py:445
  16.4 12.8 %collective-permute-start.5 = (s16[912,128]{1,0:T(8,128)(2,1)S(1)}, s16[912,128]{1,0:T(8,128)(2,1)S(1)}, u32[]{:S(2)}, u32[]{:S(2)}) collective-permute-start(s16[912,128]{1,0:T(8,128)(2,1)S(1)} %collective-permute-done.refs_3_), channel_id=1, source_target_pairs={{0,16},{8,24},{16,0},{24,8},{1,17},{9,25},{17,1},{25,9},{2,18},{10... | collective-permute-start | bytes 700424 | tf_op jit(solution)/shard_map/ppermute | solution.py:451
  20.2 6.5 %collective-permute-start.9 = (s16[464,128]{1,0:T(8,128)(2,1)S(1)}, s16[464,128]{1,0:T(8,128)(2,1)S(1)}, u32[]{:S(2)}, u32[]{:S(2)}) collective-permute-start(s16[464,128]{1,0:T(8,128)(2,1)S(1)} %get-tuple-element.52), channel_id=1, source_target_pairs={{0,24},{8,16},{16,8},{24,0},{1,25},{9,17},{17,9},{25,1},{2,26},{10... | collective-permute-start | bytes 356360 | tf_op jit(solution)/shard_map/ppermute | solution.py:445
  23.6 6.2 %collective-permute-start.8 = (s16[464,128]{1,0:T(8,128)(2,1)S(1)}, s16[464,128]{1,0:T(8,128)(2,1)S(1)}, u32[]{:S(2)}, u32[]{:S(2)}) collective-permute-start(s16[464,128]{1,0:T(8,128)(2,1)S(1)} %get-tuple-element.54), channel_id=1, source_target_pairs={{0,8},{8,0},{16,24},{24,16},{1,9},{9,1},{17,25},{25,17},{2,10},{10... | collective-permute-start | bytes 356360 | tf_op jit(solution)/shard_map/ppermute | solution.py:445
  26.7 6.5 %collective-permute-start.11 = (s16[464,128]{1,0:T(8,128)(2,1)S(1)}, s16[464,128]{1,0:T(8,128)(2,1)S(1)}, u32[]{:S(2)}, u32[]{:S(2)}) collective-permute-start(s16[464,128]{1,0:T(8,128)(2,1)S(1)} %get-tuple-element.57), channel_id=1, source_target_pairs={{0,8},{8,0},{16,24},{24,16},{1,9},{9,1},{17,25},{25,17},{2,10},{10... | collective-permute-start | bytes 356360 | tf_op jit(solution)/shard_map/ppermute | solution.py:445
  29.9 6.3 %collective-permute-start.10 = (s16[464,128]{1,0:T(8,128)(2,1)S(1)}, s16[464,128]{1,0:T(8,128)(2,1)S(1)}, u32[]{:S(2)}, u32[]{:S(2)}) collective-permute-start(s16[464,128]{1,0:T(8,128)(2,1)S(1)} %get-tuple-element.59), channel_id=1, source_target_pairs={{0,24},{8,16},{16,8},{24,0},{1,25},{9,17},{17,9},{25,1},{2,26},{10... | collective-permute-start | bytes 356360 | tf_op jit(solution)/shard_map/ppermute | solution.py:445
  33.3 5.0 %collective-permute-start.13 = (s16[464,128]{1,0:T(8,128)(2,1)S(1)}, s16[464,128]{1,0:T(8,128)(2,1)S(1)}, u32[]{:S(2)}, u32[]{:S(2)}) collective-permute-start(s16[464,128]{1,0:T(8,128)(2,1)S(1)} %get-tuple-element.62), channel_id=1, source_target_pairs={{0,8},{8,0},{16,24},{24,16},{1,9},{9,1},{17,25},{25,17},{2,10},{10... | collective-permute-start | bytes 356360 | tf_op jit(solution)/shard_map/ppermute | solution.py:445
  36.2 6.2 %collective-permute-start.12 = (s16[464,128]{1,0:T(8,128)(2,1)S(1)}, s16[464,128]{1,0:T(8,128)(2,1)S(1)}, u32[]{:S(2)}, u32[]{:S(2)}) collective-permute-start(s16[464,128]{1,0:T(8,128)(2,1)S(1)} %get-tuple-element.64), channel_id=1, source_target_pairs={{0,8},{8,0},{16,24},{24,16},{1,9},{9,1},{17,25},{25,17},{2,10},{10... | collective-permute-start | bytes 356360 | tf_op jit(solution)/shard_map/ppermute | solution.py:445
  38.4 6.5 %collective-permute-start.15 = (s16[464,128]{1,0:T(8,128)(2,1)S(1)}, s16[464,128]{1,0:T(8,128)(2,1)S(1)}, u32[]{:S(2)}, u32[]{:S(2)}) collective-permute-start(s16[464,128]{1,0:T(8,128)(2,1)S(1)} %get-tuple-element.67), channel_id=1, source_target_pairs={{0,24},{8,16},{16,8},{24,0},{1,25},{9,17},{17,9},{25,1},{2,26},{10... | collective-permute-start | bytes 356360 | tf_op jit(solution)/shard_map/ppermute | solution.py:445
  42.5 5.4 %collective-permute-start.14 = (s16[464,128]{1,0:T(8,128)(2,1)S(1)}, s16[464,128]{1,0:T(8,128)(2,1)S(1)}, u32[]{:S(2)}, u32[]{:S(2)}) collective-permute-start(s16[464,128]{1,0:T(8,128)(2,1)S(1)} %get-tuple-element.69), channel_id=1, source_target_pairs={{0,8},{8,0},{16,24},{24,16},{1,9},{9,1},{17,25},{25,17},{2,10},{10... | collective-permute-start | bytes 356360 | tf_op jit(solution)/shard_map/ppermute | solution.py:445
  48.0 6.7 %collective-permute-start.16 = (s16[464,128]{1,0:T(8,128)(2,1)S(1)}, s16[464,128]{1,0:T(8,128)(2,1)S(1)}, u32[]{:S(2)}, u32[]{:S(2)}) collective-permute-start(s16[464,128]{1,0:T(8,128)(2,1)S(1)} %get-tuple-element.74), channel_id=1, source_target_pairs={{0,24},{8,16},{16,8},{24,0},{1,25},{9,17},{17,9},{25,1},{2,26},{10... | collective-permute-start | bytes 356360 | tf_op jit(solution)/shard_map/ppermute | solution.py:445
  51.3 5.2 %collective-permute-start.18 = (s16[464,128]{1,0:T(8,128)(2,1)S(1)}, s16[464,128]{1,0:T(8,128)(2,1)S(1)}, u32[]{:S(2)}, u32[]{:S(2)}) collective-permute-start(s16[464,128]{1,0:T(8,128)(2,1)S(1)} %get-tuple-element.72), channel_id=1, source_target_pairs={{0,8},{8,0},{16,24},{24,16},{1,9},{9,1},{17,25},{25,17},{2,10},{10... | collective-permute-start | bytes 356360 | tf_op jit(solution)/shard_map/ppermute | solution.py:445
  54.7 4.9 %collective-permute-start.17 = (s16[464,128]{1,0:T(8,128)(2,1)S(1)}, s16[464,128]{1,0:T(8,128)(2,1)S(1)}, u32[]{:S(2)}, u32[]{:S(2)}) collective-permute-start(s16[464,128]{1,0:T(8,128)(2,1)S(1)} %get-tuple-element.76), channel_id=1, source_target_pairs={{0,8},{8,0},{16,24},{24,16},{1,9},{9,1},{17,25},{25,17},{2,10},{10... | collective-permute-start | bytes 356360 | tf_op jit(solution)/shard_map/ppermute | solution.py:445

commit v7 on v6

--- a/solution.py
+++ b/solution.py
@@ -442,7 +442,7 @@
     )
 
     def hop_pair(value, source, target):
-        return lax.ppermute(value, "ia", swaps(count, min(source, target) % 2))
+        return lax.ppermute(value, "ia", [(source, target)])
 
     def pass_on(h, *gate):
         passed = near[h] if count == 4 else coded[h]
@@ -467,7 +467,7 @@
     def step(c, k):
         hop = min(k, last_step - k)
         forward = k < count
-        gate = sent.get((c - 1, k + 1))
+        gate = sent.get((c - 1, 0)) if k == 0 else None
         entry = x[c] if gate is None else lax.optimization_barrier((x[c], gate))[0]
         if k == 0:
             kernel = functools.partial(first_kernel, c, parts, count)
@@ -490,14 +490,13 @@
         face[c] = hop_pair(sent[c, k], hop, hop + 1 if k < count - 1 else hop - 1)
 
     halo(0)
-    step(0, 0)
     for h in range(1, halves):
-        far.append(pass_on(h, sent[0, 0]))
+        far.append(pass_on(h, x[0]))
         halo(h)
-    for turn in range(1, last_step + chunks):
+    for k in range(last_step + 1):
         for c in range(chunks):
-            if 0 <= turn - c <= last_step and (c, turn - c) != (chunks - 1, last_step):
-                step(c, turn - c)
+            if (c, k) != (chunks - 1, last_step):
+                step(c, k)
     return call(functools.partial(final_kernel, chunks - 1), [inverse, coupling, face[-1], *x], [full], "last")[0]
 
 

time: 61.2 us -> 61.1 us (level)
  starting transfers between devices: 31.9 us -> 23.2 us
  waiting for transfers between devices: 20.9 us -> 28.8 us
    ppermute x12, starting transfers between devices: 21.1 us -> 12.2 us  [hop_pair(): return lax.ppermute(value, 'ia', [(source, target)])]
    ppermute x12, waiting for transfers between devices: 19.7 us -> 27.2 us  [hop_pair(): return lax.ppermute(value, 'ia', [(source, target)])]
  transfers between devices with their start and end apart: 19 -> 19, of which waited for: 12 -> 6; matrix products, arithmetic and copies ran while one was open for 0% -> 0% of each run, Pallas kernels for 7% -> 8%
where the time goes in v7:
time: 61.1 us; the launch traced here: 60.8 us
  waiting for transfers between devices  28.8 us (47%)
  starting transfers between devices  23.2 us (38%)
  Pallas kernels  6.31 us (10%)
  local copies, waits for them, and re-layouts  2.13 us (3%)
    ppermute x12, waiting for transfers between devices, hop_pair(): return lax.ppermute(value, 'ia', [(source, target)])  27.2 us
    ppermute x12, starting transfers between devices, hop_pair(): return lax.ppermute(value, 'ia', [(source, target)])  12.2 us
    pallas_call x20, Pallas kernels, call(): pl.pallas_call(kernel, in_specs=[whole()] * len(operands), out_specs=[who...  6.31 us
    ppermute x2, starting transfers between devices, shards(): lax.ppermute(edge, 'ja', swaps(count_j, s))  4.62 us
    ppermute x2, starting transfers between devices, pass_on(): lax.ppermute(passed, 'ia', [(i, i ^ 2) for i in range(4)] if count == 4 e...  3.35 us
    ppermute x2, starting transfers between devices, shards(): lax.ppermute(coded[h], 'ia', swaps(count, 0))  3.08 us
    unnamed x8, local copies, waits for them, and re-layouts  2.13 us
  transfers between devices with their start and end apart: 19, of which 6 were waited for; matrix products, arithmetic and copies ran while one was open for 0% of the time, Pallas kernels for 8%

profile of v7, /device:TPU:0, one launch (start us, length us, event | category | flops | bytes accessed | tf_op | source)
XLA Modules:
  0.0 60.8 jit_solution(11021732648727344152)
XLA Ops:
  0.0 1.2 %copy-done.2 = f32[2,7,16,1024]{3,2,1,0:T(8,128)S(1)} copy-done((f32[2,7,16,1024]{3,2,1,0:T(8,128)S(1)}, f32[2,7,16,1024]{3,2,1,0:T(8,128)}, u32[]{:S(2)}) %copy-start.2) | copy-done | bytes 917528
  1.2 0.2 encode.3
  1.4 3.0 %collective-permute-start.4 = (s16[912,128]{1,0:T(8,128)(2,1)S(1)}, s16[912,128]{1,0:T(8,128)(2,1)S(1)}, u32[]{:S(2)}, u32[]{:S(2)}) collective-permute-start(s16[912,128]{1,0:T(8,128)(2,1)S(1)} %encode.3), channel_id=1, source_target_pairs={{0,8},{8,0},{16,24},{24,16},{1,9},{9,1},{17,25},{25,17},{2,10},{10... | collective-permute-start | bytes 700424 | tf_op jit(solution)/shard_map/ppermute | solution.py:426
  4.4 0.2 encode.2.after_ref
  4.6 0.1 collective-permute-start
  4.6 0.2 edges.1
  4.9 2.1 %collective-permute-start.1 = (f32[2,7,2,1024]{3,2,1,0:T(2,128)S(1)}, f32[2,7,2,1024]{3,2,1,0:T(2,128)S(1)}, u32[]{:S(2)}, u32[]{:S(2)}) collective-permute-start(f32[2,7,2,1024]{3,2,1,0:T(2,128)S(1)} %get-tuple-element.39), channel_id=1, source_target_pairs={{0,2},{2,0},{4,6},{6,4},{1,3},{3,1},{5,7},{7,5},{8,10},{10,8},{12,... | collective-permute-start | bytes 344072 | tf_op jit(solution)/shard_map/ppermute | solution.py:432
  7.0 2.5 %collective-permute-start.2 = (f32[2,7,2,1024]{3,2,1,0:T(2,128)S(1)}, f32[2,7,2,1024]{3,2,1,0:T(2,128)S(1)}, u32[]{:S(2)}, u32[]{:S(2)}) collective-permute-start(f32[2,7,2,1024]{3,2,1,0:T(2,128)S(1)} %get-tuple-element.40), channel_id=1, source_target_pairs={{0,6},{2,4},{4,2},{6,0},{1,7},{3,5},{5,3},{7,1},{8,14},{10,12},{12... | collective-permute-start | bytes 344072 | tf_op jit(solution)/shard_map/ppermute | solution.py:432
  9.5 0.0 collective-permute-start.3
  9.5 0.9 %copy-done.3 = s32[2,16,1024]{2,1,0:T(8,128)S(1)} copy-done((s32[2,16,1024]{2,1,0:T(8,128)S(1)}, s32[2,16,1024]{2,1,0:T(8,128)}, u32[]{:S(2)}) %copy-start.3) | copy-done | bytes 131096
  10.4 1.2 %local.1 = (f32[2,7,16,512]{3,2,1,0:T(8,128)S(1)}, f32[2,7,16,512]{3,2,1,0:T(8,128)S(1)}, f32[2,16,1024]{2,1,0:T(8,128)S(1)}) custom-call(f32[2,7,16,1024]{3,2,1,0:T(8,128)S(1)} %copy-done.2, s32[2,16,1024]{2,1,0:T(8,128)S(1)} %copy-done.3), custom_call_target="tpu_custom_call" | custom-call | flops 9175040 | bytes 2293760 | tf_op jit(solution)/shard_map/local/pallas_call | solution.py:383
  11.6 0.0 collective-permute-done.4.refs_3_
  11.6 1.6 %collective-permute-start.12 = (s16[912,128]{1,0:T(8,128)(2,1)S(1)}, s16[912,128]{1,0:T(8,128)(2,1)S(1)}, u32[]{:S(2)}, u32[]{:S(2)}) collective-permute-start(s16[912,128]{1,0:T(8,128)(2,1)S(1)} %collective-permute-done.4.refs_3_), channel_id=1, source_target_pairs={{0,16},{8,24},{16,0},{24,8},{1,17},{9,25},{17,1},{25,9},{2,18},{10... | collective-permute-start | bytes 700424 | tf_op jit(solution)/shard_map/ppermute | solution.py:451
  13.2 1.2 %collective-permute-done.2.refs_1_ = f32[2,7,2,1024]{3,2,1,0:T(2,128)S(1)} collective-permute-done((f32[2,7,2,1024]{3,2,1,0:T(2,128)S(1)}, f32[2,7,2,1024]{3,2,1,0:T(2,128)S(1)}, u32[]{:S(2)}, u32[]{:S(2)}) %collective-permute-start.2) | collective-permute-done | bytes 114720 | tf_op jit(solution)/shard_map/ppermute | solution.py:432
  14.4 0.3 halo.2.refs_0_
  14.7 0.4 collective-permute-done.refs_3_
  15.1 1.8 %collective-permute-start.5 = (s16[912,128]{1,0:T(8,128)(2,1)S(1)}, s16[912,128]{1,0:T(8,128)(2,1)S(1)}, u32[]{:S(2)}, u32[]{:S(2)}) collective-permute-start(s16[912,128]{1,0:T(8,128)(2,1)S(1)} %collective-permute-done.refs_3_), channel_id=1, source_target_pairs={{0,16},{8,24},{16,0},{24,8},{1,17},{9,25},{17,1},{25,9},{2,18},{10... | collective-permute-start | bytes 700424 | tf_op jit(solution)/shard_map/ppermute | solution.py:451
  16.9 0.5 forward.8
  17.4 3.0 %collective-permute-start.13 = (s16[464,128]{1,0:T(8,128)(2,1)S(1)}, s16[464,128]{1,0:T(8,128)(2,1)S(1)}, u32[]{:S(2)}, u32[]{:S(2)}) collective-permute-start(s16[464,128]{1,0:T(8,128)(2,1)S(1)} %get-tuple-element.45), channel_id=1, source_target_pairs={{0,8},{1,9},{2,10},{3,11},{4,12},{5,13},{6,14},{7,15}} | collective-permute-start | bytes 356360 | tf_op jit(solution)/shard_map/ppermute | solution.py:445
  20.3 0.4 halo.3.refs_0_
  20.7 0.5 forward.9
  21.2 1.3 %collective-permute-start.6 = (s16[464,128]{1,0:T(8,128)(2,1)S(1)}, s16[464,128]{1,0:T(8,128)(2,1)S(1)}, u32[]{:S(2)}, u32[]{:S(2)}) collective-permute-start(s16[464,128]{1,0:T(8,128)(2,1)S(1)} %get-tuple-element.47), channel_id=1, source_target_pairs={{0,8},{1,9},{2,10},{3,11},{4,12},{5,13},{6,14},{7,15}} | collective-permute-start | bytes 356360 | tf_op jit(solution)/shard_map/ppermute | solution.py:445
  22.5 1.3 %collective-permute-done.13.face = s16[464,128]{1,0:T(8,128)(2,1)S(1)} collective-permute-done((s16[464,128]{1,0:T(8,128)(2,1)S(1)}, s16[464,128]{1,0:T(8,128)(2,1)S(1)}, u32[]{:S(2)}, u32[]{:S(2)}) %collective-permute-start.13) | collective-permute-done | bytes 118816 | tf_op jit(solution)/shard_map/ppermute | solution.py:445
  23.9 0.1 forward.13
  23.9 0.7 %collective-permute-start.14 = (s16[464,128]{1,0:T(8,128)(2,1)S(1)}, s16[464,128]{1,0:T(8,128)(2,1)S(1)}, u32[]{:S(2)}, u32[]{:S(2)}) collective-permute-start(s16[464,128]{1,0:T(8,128)(2,1)S(1)} %get-tuple-element.60), channel_id=1, source_target_pairs={{8,16},{9,17},{10,18},{11,19},{12,20},{13,21},{14,22},{15,23}} | collective-permute-start | bytes 356360 | tf_op jit(solution)/shard_map/ppermute | solution.py:445
  24.6 0.5 collective-permute-done.6.face
  25.1 0.1 forward.10
  25.2 0.7 %collective-permute-start.7 = (s16[464,128]{1,0:T(8,128)(2,1)S(1)}, s16[464,128]{1,0:T(8,128)(2,1)S(1)}, u32[]{:S(2)}, u32[]{:S(2)}) collective-permute-start(s16[464,128]{1,0:T(8,128)(2,1)S(1)} %get-tuple-element.49), channel_id=1, source_target_pairs={{8,16},{9,17},{10,18},{11,19},{12,20},{13,21},{14,22},{15,23}} | collective-permute-start | bytes 356360 | tf_op jit(solution)/shard_map/ppermute | solution.py:445
  25.9 0.1 forward.14
  26.0 0.7 %collective-permute-start.15 = (s16[464,128]{1,0:T(8,128)(2,1)S(1)}, s16[464,128]{1,0:T(8,128)(2,1)S(1)}, u32[]{:S(2)}, u32[]{:S(2)}) collective-permute-start(s16[464,128]{1,0:T(8,128)(2,1)S(1)} %get-tuple-element.62), channel_id=1, source_target_pairs={{16,24},{17,25},{18,26},{19,27},{20,28},{21,29},{22,30},{23,31}} | collective-permute-start | bytes 356360 | tf_op jit(solution)/shard_map/ppermute | solution.py:445
  26.6 0.1 forward.11
  26.7 0.7 %collective-permute-start.8 = (s16[464,128]{1,0:T(8,128)(2,1)S(1)}, s16[464,128]{1,0:T(8,128)(2,1)S(1)}, u32[]{:S(2)}, u32[]{:S(2)}) collective-permute-start(s16[464,128]{1,0:T(8,128)(2,1)S(1)} %get-tuple-element.51), channel_id=1, source_target_pairs={{16,24},{17,25},{18,26},{19,27},{20,28},{21,29},{22,30},{23,31}} | collective-permute-start | bytes 356360 | tf_op jit(solution)/shard_map/ppermute | solution.py:445
  27.4 0.1 forward.15
  27.5 0.7 %collective-permute-start.16 = (s16[464,128]{1,0:T(8,128)(2,1)S(1)}, s16[464,128]{1,0:T(8,128)(2,1)S(1)}, u32[]{:S(2)}, u32[]{:S(2)}) collective-permute-start(s16[464,128]{1,0:T(8,128)(2,1)S(1)} %get-tuple-element.64), channel_id=1, source_target_pairs={{24,16},{25,17},{26,18},{27,19},{28,20},{29,21},{30,22},{31,23}} | collective-permute-start | bytes 356360 | tf_op jit(solution)/shard_map/ppermute | solution.py:445
  28.2 0.1 forward.12
  28.3 0.7 %collective-permute-start.9 = (s16[464,128]{1,0:T(8,128)(2,1)S(1)}, s16[464,128]{1,0:T(8,128)(2,1)S(1)}, u32[]{:S(2)}, u32[]{:S(2)}) collective-permute-start(s16[464,128]{1,0:T(8,128)(2,1)S(1)} %get-tuple-element.53), channel_id=1, source_target_pairs={{24,16},{25,17},{26,18},{27,19},{28,20},{29,21},{30,22},{31,23}} | collective-permute-start | bytes 356360 | tf_op jit(solution)/shard_map/ppermute | solution.py:445
  29.0 0.1 backward.7
  29.1 0.7 %collective-permute-start.17 = (s16[464,128]{1,0:T(8,128)(2,1)S(1)}, s16[464,128]{1,0:T(8,128)(2,1)S(1)}, u32[]{:S(2)}, u32[]{:S(2)}) collective-permute-start(s16[464,128]{1,0:T(8,128)(2,1)S(1)} %get-tuple-element.66), channel_id=1, source_target_pairs={{16,8},{17,9},{18,10},{19,11},{20,12},{21,13},{22,14},{23,15}} | collective-permute-start | bytes 356360 | tf_op jit(solution)/shard_map/ppermute | solution.py:445
  29.7 0.1 backward.5
  29.8 0.7 %collective-permute-start.10 = (s16[464,128]{1,0:T(8,128)(2,1)S(1)}, s16[464,128]{1,0:T(8,128)(2,1)S(1)}, u32[]{:S(2)}, u32[]{:S(2)}) collective-permute-start(s16[464,128]{1,0:T(8,128)(2,1)S(1)} %get-tuple-element.55), channel_id=1, source_target_pairs={{16,8},{17,9},{18,10},{19,11},{20,12},{21,13},{22,14},{23,15}} | collective-permute-start | bytes 356360 | tf_op jit(solution)/shard_map/ppermute | solution.py:445
  30.5 0.3 backward.8
  30.8 1.3 %collective-permute-start.18 = (s16[464,128]{1,0:T(8,128)(2,1)S(1)}, s16[464,128]{1,0:T(8,128)(2,1)S(1)}, u32[]{:S(2)}, u32[]{:S(2)}) collective-permute-start(s16[464,128]{1,0:T(8,128)(2,1)S(1)} %get-tuple-element.68), channel_id=1, source_target_pairs={{8,0},{9,1},{10,2},{11,3},{12,4},{13,5},{14,6},{15,7}} | collective-permute-start | bytes 356360 | tf_op jit(solution)/shard_map/ppermute | solution.py:445
  32.1 0.1 backward.6
  32.2 1.3 %collective-permute-start.11 = (s16[464,128]{1,0:T(8,128)(2,1)S(1)}, s16[464,128]{1,0:T(8,128)(2,1)S(1)}, u32[]{:S(2)}, u32[]{:S(2)}) collective-permute-start(s16[464,128]{1,0:T(8,128)(2,1)S(1)} %get-tuple-element.57), channel_id=1, source_target_pairs={{8,0},{9,1},{10,2},{11,3},{12,4},{13,5},{14,6},{15,7}} | collective-permute-start | bytes 356360 | tf_op jit(solution)/shard_map/ppermute | solution.py:445
  33.5 24.0 %collective-permute-done.18.refs_2_ = s16[464,128]{1,0:T(8,128)(2,1)S(1)} collective-permute-done((s16[464,128]{1,0:T(8,128)(2,1)S(1)}, s16[464,128]{1,0:T(8,128)(2,1)S(1)}, u32[]{:S(2)}, u32[]{:S(2)}) %collective-permute-start.18) | collective-permute-done | bytes 118816 | tf_op jit(solution)/shard_map/ppermute | solution.py:445
  57.5 0.6 backward.9.refs_0_
  58.1 1.3 %collective-permute-done.11.face = s16[464,128]{1,0:T(8,128)(2,1)S(1)} collective-permute-done((s16[464,128]{1,0:T(8,128)(2,1)S(1)}, s16[464,128]{1,0:T(8,128)(2,1)S(1)}, u32[]{:S(2)}, u32[]{:S(2)}) %collective-permute-start.11) | collective-permute-done | bytes 118816 | tf_op jit(solution)/shard_map/ppermute | solution.py:445
  59.4 1.4 %last.1 = f32[2,7,16,1024]{3,2,1,0:T(8,128)} custom-call(bf16[2,7,7,16,1024]{4,3,2,1,0:T(8,128)(2,1)S(1)} %copy-done, f32[2,2,16,1024]{3,2,1,0:T(8,128)S(1)} %copy-done.1, s16[464,128]{1,0:T(8,128)(2,1)S(1)} %collective-permute-done.11.face, f32[2,7,16,512]{3,2,1,0:T(8,128)S(1)} %backward.9.refs_0_, f32[2,7,16,512]{3,2,1,0:T(8,128)S(1)} %get-tuple-element.70.refs_1_), custom_call_target="tpu_custom_call" | custom-call | tf_op jit(solution)/shard_map/last/pallas_call | solution.py:383
  (18 shorter events, 0.0 us)
Async XLA Ops:
  0.0 16.9 %copy-start.1 = (f32[2,2,16,1024]{3,2,1,0:T(8,128)S(1)}, f32[2,2,16,1024]{3,2,1,0:T(8,128)}, u32[]{:S(2)}) copy-start(f32[2,2,16,1024]{3,2,1,0:T(8,128)} %coupling_ref.25) | copy-start | bytes 786436
  0.0 1.2 %copy-start.2 = (f32[2,7,16,1024]{3,2,1,0:T(8,128)S(1)}, f32[2,7,16,1024]{3,2,1,0:T(8,128)}, u32[]{:S(2)}) copy-start(f32[2,7,16,1024]{3,2,1,0:T(8,128)} %state_ref.7) | copy-start | bytes 2752516
  1.2 15.6 %copy-start = (bf16[2,7,7,16,1024]{4,3,2,1,0:T(8,128)(2,1)S(1)}, bf16[2,7,7,16,1024]{4,3,2,1,0:T(8,128)(2,1)}, u32[]{:S(2)}) copy-start(bf16[2,7,7,16,1024]{4,3,2,1,0:T(8,128)(2,1)} %inverse_ref.25) | copy-start | bytes 9633796
  1.4 10.2 %collective-permute-start.4 = (s16[912,128]{1,0:T(8,128)(2,1)S(1)}, s16[912,128]{1,0:T(8,128)(2,1)S(1)}, u32[]{:S(2)}, u32[]{:S(2)}) collective-permute-start(s16[912,128]{1,0:T(8,128)(2,1)S(1)} %encode.3), channel_id=1, source_target_pairs={{0,8},{8,0},{16,24},{24,16},{1,9},{9,1},{17,25},{25,17},{2,10},{10... | collective-permute-start | bytes 700424 | tf_op jit(solution)/shard_map/ppermute | solution.py:426
  4.6 10.5 %collective-permute-start = (s16[912,128]{1,0:T(8,128)(2,1)S(1)}, s16[912,128]{1,0:T(8,128)(2,1)S(1)}, u32[]{:S(2)}, u32[]{:S(2)}) collective-permute-start(s16[912,128]{1,0:T(8,128)(2,1)S(1)} %encode.2.after_ref), channel_id=1, source_target_pairs={{0,8},{8,0},{16,24},{24,16},{1,9},{9,1},{17,25},{25,17},{2,10},{10... | collective-permute-start | bytes 700424 | tf_op jit(solution)/shard_map/ppermute | solution.py:426
  4.9 8.3 %collective-permute-start.1 = (f32[2,7,2,1024]{3,2,1,0:T(2,128)S(1)}, f32[2,7,2,1024]{3,2,1,0:T(2,128)S(1)}, u32[]{:S(2)}, u32[]{:S(2)}) collective-permute-start(f32[2,7,2,1024]{3,2,1,0:T(2,128)S(1)} %get-tuple-element.39), channel_id=1, source_target_pairs={{0,2},{2,0},{4,6},{6,4},{1,3},{3,1},{5,7},{7,5},{8,10},{10,8},{12,... | collective-permute-start | bytes 344072 | tf_op jit(solution)/shard_map/ppermute | solution.py:432
  7.0 7.3 %collective-permute-start.2 = (f32[2,7,2,1024]{3,2,1,0:T(2,128)S(1)}, f32[2,7,2,1024]{3,2,1,0:T(2,128)S(1)}, u32[]{:S(2)}, u32[]{:S(2)}) collective-permute-start(f32[2,7,2,1024]{3,2,1,0:T(2,128)S(1)} %get-tuple-element.40), channel_id=1, source_target_pairs={{0,6},{2,4},{4,2},{6,0},{1,7},{3,5},{5,3},{7,1},{8,14},{10,12},{12... | collective-permute-start | bytes 344072 | tf_op jit(solution)/shard_map/ppermute | solution.py:432
  9.5 4.9 %collective-permute-start.3 = (f32[2,7,16,128]{3,2,1,0:T(8,128)S(1)}, f32[2,7,16,128]{3,2,1,0:T(8,128)S(1)}, u32[]{:S(2)}, u32[]{:S(2)}) collective-permute-start(f32[2,7,16,128]{3,2,1,0:T(8,128)S(1)} %get-tuple-element.41), channel_id=1, source_target_pairs={{0,1},{1,0},{2,3},{3,2},{4,5},{5,4},{6,7},{7,6},{8,9},{9,8},{10,11... | collective-permute-start | bytes 344072 | tf_op jit(solution)/shard_map/ppermute | solution.py:431
  9.5 0.9 %copy-start.3 = (s32[2,16,1024]{2,1,0:T(8,128)S(1)}, s32[2,16,1024]{2,1,0:T(8,128)}, u32[]{:S(2)}) copy-start(s32[2,16,1024]{2,1,0:T(8,128)} %wall_ref.1) | copy-start | bytes 393220
  11.6 12.3 %collective-permute-start.12 = (s16[912,128]{1,0:T(8,128)(2,1)S(1)}, s16[912,128]{1,0:T(8,128)(2,1)S(1)}, u32[]{:S(2)}, u32[]{:S(2)}) collective-permute-start(s16[912,128]{1,0:T(8,128)(2,1)S(1)} %collective-permute-done.4.refs_3_), channel_id=1, source_target_pairs={{0,16},{8,24},{16,0},{24,8},{1,17},{9,25},{17,1},{25,9},{2,18},{10... | collective-permute-start | bytes 700424 | tf_op jit(solution)/shard_map/ppermute | solution.py:451
  15.1 10.0 %collective-permute-start.5 = (s16[912,128]{1,0:T(8,128)(2,1)S(1)}, s16[912,128]{1,0:T(8,128)(2,1)S(1)}, u32[]{:S(2)}, u32[]{:S(2)}) collective-permute-start(s16[912,128]{1,0:T(8,128)(2,1)S(1)} %collective-permute-done.refs_3_), channel_id=1, source_target_pairs={{0,16},{8,24},{16,0},{24,8},{1,17},{9,25},{17,1},{25,9},{2,18},{10... | collective-permute-start | bytes 700424 | tf_op jit(solution)/shard_map/ppermute | solution.py:451
  17.4 6.5 %collective-permute-start.13 = (s16[464,128]{1,0:T(8,128)(2,1)S(1)}, s16[464,128]{1,0:T(8,128)(2,1)S(1)}, u32[]{:S(2)}, u32[]{:S(2)}) collective-permute-start(s16[464,128]{1,0:T(8,128)(2,1)S(1)} %get-tuple-element.45), channel_id=1, source_target_pairs={{0,8},{1,9},{2,10},{3,11},{4,12},{5,13},{6,14},{7,15}} | collective-permute-start | bytes 356360 | tf_op jit(solution)/shard_map/ppermute | solution.py:445
  21.2 3.9 %collective-permute-start.6 = (s16[464,128]{1,0:T(8,128)(2,1)S(1)}, s16[464,128]{1,0:T(8,128)(2,1)S(1)}, u32[]{:S(2)}, u32[]{:S(2)}) collective-permute-start(s16[464,128]{1,0:T(8,128)(2,1)S(1)} %get-tuple-element.47), channel_id=1, source_target_pairs={{0,8},{1,9},{2,10},{3,11},{4,12},{5,13},{6,14},{7,15}} | collective-permute-start | bytes 356360 | tf_op jit(solution)/shard_map/ppermute | solution.py:445
  23.9 2.0 %collective-permute-start.14 = (s16[464,128]{1,0:T(8,128)(2,1)S(1)}, s16[464,128]{1,0:T(8,128)(2,1)S(1)}, u32[]{:S(2)}, u32[]{:S(2)}) collective-permute-start(s16[464,128]{1,0:T(8,128)(2,1)S(1)} %get-tuple-element.60), channel_id=1, source_target_pairs={{8,16},{9,17},{10,18},{11,19},{12,20},{13,21},{14,22},{15,23}} | collective-permute-start | bytes 356360 | tf_op jit(solution)/shard_map/ppermute | solution.py:445
  25.2 1.5 %collective-permute-start.7 = (s16[464,128]{1,0:T(8,128)(2,1)S(1)}, s16[464,128]{1,0:T(8,128)(2,1)S(1)}, u32[]{:S(2)}, u32[]{:S(2)}) collective-permute-start(s16[464,128]{1,0:T(8,128)(2,1)S(1)} %get-tuple-element.49), channel_id=1, source_target_pairs={{8,16},{9,17},{10,18},{11,19},{12,20},{13,21},{14,22},{15,23}} | collective-permute-start | bytes 356360 | tf_op jit(solution)/shard_map/ppermute | solution.py:445
  26.0 1.5 %collective-permute-start.15 = (s16[464,128]{1,0:T(8,128)(2,1)S(1)}, s16[464,128]{1,0:T(8,128)(2,1)S(1)}, u32[]{:S(2)}, u32[]{:S(2)}) collective-permute-start(s16[464,128]{1,0:T(8,128)(2,1)S(1)} %get-tuple-element.62), channel_id=1, source_target_pairs={{16,24},{17,25},{18,26},{19,27},{20,28},{21,29},{22,30},{23,31}} | collective-permute-start | bytes 356360 | tf_op jit(solution)/shard_map/ppermute | solution.py:445
  26.7 1.5 %collective-permute-start.8 = (s16[464,128]{1,0:T(8,128)(2,1)S(1)}, s16[464,128]{1,0:T(8,128)(2,1)S(1)}, u32[]{:S(2)}, u32[]{:S(2)}) collective-permute-start(s16[464,128]{1,0:T(8,128)(2,1)S(1)} %get-tuple-element.51), channel_id=1, source_target_pairs={{16,24},{17,25},{18,26},{19,27},{20,28},{21,29},{22,30},{23,31}} | collective-permute-start | bytes 356360 | tf_op jit(solution)/shard_map/ppermute | solution.py:445
  27.5 1.5 %collective-permute-start.16 = (s16[464,128]{1,0:T(8,128)(2,1)S(1)}, s16[464,128]{1,0:T(8,128)(2,1)S(1)}, u32[]{:S(2)}, u32[]{:S(2)}) collective-permute-start(s16[464,128]{1,0:T(8,128)(2,1)S(1)} %get-tuple-element.64), channel_id=1, source_target_pairs={{24,16},{25,17},{26,18},{27,19},{28,20},{29,21},{30,22},{31,23}} | collective-permute-start | bytes 356360 | tf_op jit(solution)/shard_map/ppermute | solution.py:445
  28.3 1.5 %collective-permute-start.9 = (s16[464,128]{1,0:T(8,128)(2,1)S(1)}, s16[464,128]{1,0:T(8,128)(2,1)S(1)}, u32[]{:S(2)}, u32[]{:S(2)}) collective-permute-start(s16[464,128]{1,0:T(8,128)(2,1)S(1)} %get-tuple-element.53), channel_id=1, source_target_pairs={{24,16},{25,17},{26,18},{27,19},{28,20},{29,21},{30,22},{31,23}} | collective-permute-start | bytes 356360 | tf_op jit(solution)/shard_map/ppermute | solution.py:445
  29.1 1.5 %collective-permute-start.17 = (s16[464,128]{1,0:T(8,128)(2,1)S(1)}, s16[464,128]{1,0:T(8,128)(2,1)S(1)}, u32[]{:S(2)}, u32[]{:S(2)}) collective-permute-start(s16[464,128]{1,0:T(8,128)(2,1)S(1)} %get-tuple-element.66), channel_id=1, source_target_pairs={{16,8},{17,9},{18,10},{19,11},{20,12},{21,13},{22,14},{23,15}} | collective-permute-start | bytes 356360 | tf_op jit(solution)/shard_map/ppermute | solution.py:445
  29.8 2.3 %collective-permute-start.10 = (s16[464,128]{1,0:T(8,128)(2,1)S(1)}, s16[464,128]{1,0:T(8,128)(2,1)S(1)}, u32[]{:S(2)}, u32[]{:S(2)}) collective-permute-start(s16[464,128]{1,0:T(8,128)(2,1)S(1)} %get-tuple-element.55), channel_id=1, source_target_pairs={{16,8},{17,9},{18,10},{19,11},{20,12},{21,13},{22,14},{23,15}} | collective-permute-start | bytes 356360 | tf_op jit(solution)/shard_map/ppermute | solution.py:445
  30.8 26.7 %collective-permute-start.18 = (s16[464,128]{1,0:T(8,128)(2,1)S(1)}, s16[464,128]{1,0:T(8,128)(2,1)S(1)}, u32[]{:S(2)}, u32[]{:S(2)}) collective-permute-start(s16[464,128]{1,0:T(8,128)(2,1)S(1)} %get-tuple-element.68), channel_id=1, source_target_pairs={{8,0},{9,1},{10,2},{11,3},{12,4},{13,5},{14,6},{15,7}} | collective-permute-start | bytes 356360 | tf_op jit(solution)/shard_map/ppermute | solution.py:445
  32.2 27.2 %collective-permute-start.11 = (s16[464,128]{1,0:T(8,128)(2,1)S(1)}, s16[464,128]{1,0:T(8,128)(2,1)S(1)}, u32[]{:S(2)}, u32[]{:S(2)}) collective-permute-start(s16[464,128]{1,0:T(8,128)(2,1)S(1)} %get-tuple-element.57), channel_id=1, source_target_pairs={{8,0},{9,1},{10,2},{11,3},{12,4},{13,5},{14,6},{15,7}} | collective-permute-start | bytes 356360 | tf_op jit(solution)/shard_map/ppermute | solution.py:445

commit v8 on v7

--- a/solution.py
+++ b/solution.py
@@ -442,7 +442,8 @@
     )
 
     def hop_pair(value, source, target):
-        return lax.ppermute(value, "ia", [(source, target)])
+        exchange = min(source, target) % 2 == 0 and count % 2 == 0
+        return lax.ppermute(value, "ia", swaps(count, 0) if exchange else [(source, target)])
 
     def pass_on(h, *gate):
         passed = near[h] if count == 4 else coded[h]
@@ -490,12 +491,13 @@
         face[c] = hop_pair(sent[c, k], hop, hop + 1 if k < count - 1 else hop - 1)
 
     halo(0)
+    step(0, 0)
     for h in range(1, halves):
-        far.append(pass_on(h, x[0]))
+        far.append(pass_on(h, sent[0, 0]))
         halo(h)
     for k in range(last_step + 1):
         for c in range(chunks):
-            if (c, k) != (chunks - 1, last_step):
+            if (c, k) not in ((0, 0), (chunks - 1, last_step)):
                 step(c, k)
     return call(functools.partial(final_kernel, chunks - 1), [inverse, coupling, face[-1], *x], [full], "last")[0]
 

time: 61.1 us -> 58.5 us (0.957)
  waiting for transfers between devices: 28.8 us -> 17.2 us
  starting transfers between devices: 23.2 us -> 32.5 us
    ppermute x12, waiting for transfers between devices: 27.2 us -> 15.4 us  [hop_pair(): lax.ppermute(value, 'ia', swaps(count, 0) if exchange else [(source, targ...]
    ppermute x12, starting transfers between devices: 12.2 us -> 21.6 us  [hop_pair(): lax.ppermute(value, 'ia', swaps(count, 0) if exchange else [(source, targ...]
  transfers between devices with their start and end apart: 19 -> 19, of which waited for: 6 -> 10; matrix products, arithmetic and copies ran while one was open for 0% -> 0% of each run, Pallas kernels for 8% -> 8%
where the time goes in v8:
time: 58.5 us; the launch traced here: 58.3 us
  starting transfers between devices  32.5 us (56%)
  waiting for transfers between devices  17.2 us (29%)
  Pallas kernels  6.22 us (11%)
  local copies, waits for them, and re-layouts  2.13 us (4%)
    ppermute x12, starting transfers between devices, hop_pair(): lax.ppermute(value, 'ia', swaps(count, 0) if exchange else [(source, targ...  21.6 us
    ppermute x12, waiting for transfers between devices, hop_pair(): lax.ppermute(value, 'ia', swaps(count, 0) if exchange else [(source, targ...  15.4 us
    pallas_call x20, Pallas kernels, call(): pl.pallas_call(kernel, in_specs=[whole()] * len(operands), out_specs=[who...  6.22 us
    ppermute x2, starting transfers between devices, shards(): lax.ppermute(edge, 'ja', swaps(count_j, s))  4.62 us
    ppermute x2, starting transfers between devices, pass_on(): lax.ppermute(passed, 'ia', [(i, i ^ 2) for i in range(4)] if count == 4 e...  3.19 us
    ppermute x2, starting transfers between devices, shards(): lax.ppermute(coded[h], 'ia', swaps(count, 0))  3.08 us
    unnamed x8, local copies, waits for them, and re-layouts  2.13 us
    ppermute x2, waiting for transfers between devices, shards(): lax.ppermute(edge, 'ja', swaps(count_j, s))  1.2 us
  transfers between devices with their start and end apart: 19, of which 10 were waited for; matrix products, arithmetic and copies ran while one was open for 0% of the time, Pallas kernels for 8%

profile of v8, /device:TPU:0, one launch (start us, length us, event | category | flops | bytes accessed | tf_op | source)
XLA Modules:
  0.0 58.3 jit_solution(6130924064840000584)
XLA Ops:
  0.0 1.2 %copy-done.2 = f32[2,7,16,1024]{3,2,1,0:T(8,128)S(1)} copy-done((f32[2,7,16,1024]{3,2,1,0:T(8,128)S(1)}, f32[2,7,16,1024]{3,2,1,0:T(8,128)}, u32[]{:S(2)}) %copy-start.2) | copy-done | bytes 917528
  1.2 0.2 encode.3
  1.4 3.0 %collective-permute-start.4 = (s16[912,128]{1,0:T(8,128)(2,1)S(1)}, s16[912,128]{1,0:T(8,128)(2,1)S(1)}, u32[]{:S(2)}, u32[]{:S(2)}) collective-permute-start(s16[912,128]{1,0:T(8,128)(2,1)S(1)} %encode.3), channel_id=1, source_target_pairs={{0,8},{8,0},{16,24},{24,16},{1,9},{9,1},{17,25},{25,17},{2,10},{10... | collective-permute-start | bytes 700424 | tf_op jit(solution)/shard_map/ppermute | solution.py:426
  4.4 0.2 encode.2.after_ref
  4.6 0.1 collective-permute-start
  4.6 0.2 edges.1
  4.9 2.1 %collective-permute-start.1 = (f32[2,7,2,1024]{3,2,1,0:T(2,128)S(1)}, f32[2,7,2,1024]{3,2,1,0:T(2,128)S(1)}, u32[]{:S(2)}, u32[]{:S(2)}) collective-permute-start(f32[2,7,2,1024]{3,2,1,0:T(2,128)S(1)} %get-tuple-element.39), channel_id=1, source_target_pairs={{0,2},{2,0},{4,6},{6,4},{1,3},{3,1},{5,7},{7,5},{8,10},{10,8},{12,... | collective-permute-start | bytes 344072 | tf_op jit(solution)/shard_map/ppermute | solution.py:432
  7.0 2.5 %collective-permute-start.2 = (f32[2,7,2,1024]{3,2,1,0:T(2,128)S(1)}, f32[2,7,2,1024]{3,2,1,0:T(2,128)S(1)}, u32[]{:S(2)}, u32[]{:S(2)}) collective-permute-start(f32[2,7,2,1024]{3,2,1,0:T(2,128)S(1)} %get-tuple-element.40), channel_id=1, source_target_pairs={{0,6},{2,4},{4,2},{6,0},{1,7},{3,5},{5,3},{7,1},{8,14},{10,12},{12... | collective-permute-start | bytes 344072 | tf_op jit(solution)/shard_map/ppermute | solution.py:432
  9.5 0.9 %copy-done.3 = s32[2,16,1024]{2,1,0:T(8,128)S(1)} copy-done((s32[2,16,1024]{2,1,0:T(8,128)S(1)}, s32[2,16,1024]{2,1,0:T(8,128)}, u32[]{:S(2)}) %copy-start.3) | copy-done | bytes 131096
  10.4 1.2 %local.1 = (f32[2,7,16,512]{3,2,1,0:T(8,128)S(1)}, f32[2,7,16,512]{3,2,1,0:T(8,128)S(1)}, f32[2,16,1024]{2,1,0:T(8,128)S(1)}) custom-call(f32[2,7,16,1024]{3,2,1,0:T(8,128)S(1)} %copy-done.2, s32[2,16,1024]{2,1,0:T(8,128)S(1)} %copy-done.3), custom_call_target="tpu_custom_call" | custom-call | flops 9175040 | bytes 2293760 | tf_op jit(solution)/shard_map/local/pallas_call | solution.py:383
  11.6 1.6 %collective-permute-start.12 = (s16[912,128]{1,0:T(8,128)(2,1)S(1)}, s16[912,128]{1,0:T(8,128)(2,1)S(1)}, u32[]{:S(2)}, u32[]{:S(2)}) collective-permute-start(s16[912,128]{1,0:T(8,128)(2,1)S(1)} %collective-permute-done.4.refs_3_), channel_id=1, source_target_pairs={{0,16},{8,24},{16,0},{24,8},{1,17},{9,25},{17,1},{25,9},{2,18},{10... | collective-permute-start | bytes 700424 | tf_op jit(solution)/shard_map/ppermute | solution.py:452
  13.2 1.2 %collective-permute-done.2.refs_1_ = f32[2,7,2,1024]{3,2,1,0:T(2,128)S(1)} collective-permute-done((f32[2,7,2,1024]{3,2,1,0:T(2,128)S(1)}, f32[2,7,2,1024]{3,2,1,0:T(2,128)S(1)}, u32[]{:S(2)}, u32[]{:S(2)}) %collective-permute-start.2) | collective-permute-done | bytes 114720 | tf_op jit(solution)/shard_map/ppermute | solution.py:432
  14.4 0.3 halo.2.refs_0_
  14.7 0.5 forward.8
  15.3 1.6 %collective-permute-start.5 = (s16[912,128]{1,0:T(8,128)(2,1)S(1)}, s16[912,128]{1,0:T(8,128)(2,1)S(1)}, u32[]{:S(2)}, u32[]{:S(2)}) collective-permute-start(s16[912,128]{1,0:T(8,128)(2,1)S(1)} %collective-permute-done.refs_3_), channel_id=1, source_target_pairs={{0,16},{8,24},{16,0},{24,8},{1,17},{9,25},{17,1},{25,9},{2,18},{10... | collective-permute-start | bytes 700424 | tf_op jit(solution)/shard_map/ppermute | solution.py:452
  16.9 1.5 %collective-permute-start.13 = (s16[464,128]{1,0:T(8,128)(2,1)S(1)}, s16[464,128]{1,0:T(8,128)(2,1)S(1)}, u32[]{:S(2)}, u32[]{:S(2)}) collective-permute-start(s16[464,128]{1,0:T(8,128)(2,1)S(1)} %get-tuple-element.43), channel_id=1, source_target_pairs={{0,8},{8,0},{16,24},{24,16},{1,9},{9,1},{17,25},{25,17},{2,10},{10... | collective-permute-start | bytes 356360 | tf_op jit(solution)/shard_map/ppermute | solution.py:446
  18.4 0.4 halo.3.refs_0_
  18.7 0.5 forward.9
  19.3 0.1 collective-permute-start.6
  19.4 3.5 %collective-permute-done.13.face = s16[464,128]{1,0:T(8,128)(2,1)S(1)} collective-permute-done((s16[464,128]{1,0:T(8,128)(2,1)S(1)}, s16[464,128]{1,0:T(8,128)(2,1)S(1)}, u32[]{:S(2)}, u32[]{:S(2)}) %collective-permute-start.13) | collective-permute-done | bytes 118816 | tf_op jit(solution)/shard_map/ppermute | solution.py:446
  22.8 0.1 forward.13
  22.9 0.7 %collective-permute-start.14 = (s16[464,128]{1,0:T(8,128)(2,1)S(1)}, s16[464,128]{1,0:T(8,128)(2,1)S(1)}, u32[]{:S(2)}, u32[]{:S(2)}) collective-permute-start(s16[464,128]{1,0:T(8,128)(2,1)S(1)} %get-tuple-element.60), channel_id=1, source_target_pairs={{8,16},{9,17},{10,18},{11,19},{12,20},{13,21},{14,22},{15,23}} | collective-permute-start | bytes 356360 | tf_op jit(solution)/shard_map/ppermute | solution.py:446
  23.6 0.6 collective-permute-done.6.face
  24.2 0.6 %collective-permute-done.5.neighbour = s16[912,128]{1,0:T(8,128)(2,1)S(1)} collective-permute-done((s16[912,128]{1,0:T(8,128)(2,1)S(1)}, s16[912,128]{1,0:T(8,128)(2,1)S(1)}, u32[]{:S(2)}, u32[]{:S(2)}) %collective-permute-start.5) | collective-permute-done | bytes 233504 | tf_op jit(solution)/shard_map/ppermute | solution.py:452
  24.7 0.1 forward.10
  24.8 0.7 %collective-permute-start.7 = (s16[464,128]{1,0:T(8,128)(2,1)S(1)}, s16[464,128]{1,0:T(8,128)(2,1)S(1)}, u32[]{:S(2)}, u32[]{:S(2)}) collective-permute-start(s16[464,128]{1,0:T(8,128)(2,1)S(1)} %get-tuple-element.49), channel_id=1, source_target_pairs={{8,16},{9,17},{10,18},{11,19},{12,20},{13,21},{14,22},{15,23}} | collective-permute-start | bytes 356360 | tf_op jit(solution)/shard_map/ppermute | solution.py:446
  25.5 0.1 forward.14
  25.6 4.3 %collective-permute-start.15 = (s16[464,128]{1,0:T(8,128)(2,1)S(1)}, s16[464,128]{1,0:T(8,128)(2,1)S(1)}, u32[]{:S(2)}, u32[]{:S(2)}) collective-permute-start(s16[464,128]{1,0:T(8,128)(2,1)S(1)} %get-tuple-element.62), channel_id=1, source_target_pairs={{0,8},{8,0},{16,24},{24,16},{1,9},{9,1},{17,25},{25,17},{2,10},{10... | collective-permute-start | bytes 356360 | tf_op jit(solution)/shard_map/ppermute | solution.py:446
  29.9 0.1 forward.11
  29.9 3.5 %collective-permute-start.8 = (s16[464,128]{1,0:T(8,128)(2,1)S(1)}, s16[464,128]{1,0:T(8,128)(2,1)S(1)}, u32[]{:S(2)}, u32[]{:S(2)}) collective-permute-start(s16[464,128]{1,0:T(8,128)(2,1)S(1)} %get-tuple-element.51), channel_id=1, source_target_pairs={{0,8},{8,0},{16,24},{24,16},{1,9},{9,1},{17,25},{25,17},{2,10},{10... | collective-permute-start | bytes 356360 | tf_op jit(solution)/shard_map/ppermute | solution.py:446
  33.5 2.9 %collective-permute-done.15.face = s16[464,128]{1,0:T(8,128)(2,1)S(1)} collective-permute-done((s16[464,128]{1,0:T(8,128)(2,1)S(1)}, s16[464,128]{1,0:T(8,128)(2,1)S(1)}, u32[]{:S(2)}, u32[]{:S(2)}) %collective-permute-start.15) | collective-permute-done | bytes 118816 | tf_op jit(solution)/shard_map/ppermute | solution.py:446
  36.3 0.1 forward.15
  36.4 0.1 collective-permute-start.16
  36.5 2.4 %collective-permute-done.8.face = s16[464,128]{1,0:T(8,128)(2,1)S(1)} collective-permute-done((s16[464,128]{1,0:T(8,128)(2,1)S(1)}, s16[464,128]{1,0:T(8,128)(2,1)S(1)}, u32[]{:S(2)}, u32[]{:S(2)}) %collective-permute-start.8) | collective-permute-done | bytes 118816 | tf_op jit(solution)/shard_map/ppermute | solution.py:446
  38.9 0.1 forward.12
  38.9 0.3 collective-permute-start.9
  39.3 2.4 %collective-permute-done.16.face = s16[464,128]{1,0:T(8,128)(2,1)S(1)} collective-permute-done((s16[464,128]{1,0:T(8,128)(2,1)S(1)}, s16[464,128]{1,0:T(8,128)(2,1)S(1)}, u32[]{:S(2)}, u32[]{:S(2)}) %collective-permute-start.16) | collective-permute-done | bytes 118816 | tf_op jit(solution)/shard_map/ppermute | solution.py:446
  41.7 0.1 backward.7
  41.8 0.7 %collective-permute-start.17 = (s16[464,128]{1,0:T(8,128)(2,1)S(1)}, s16[464,128]{1,0:T(8,128)(2,1)S(1)}, u32[]{:S(2)}, u32[]{:S(2)}) collective-permute-start(s16[464,128]{1,0:T(8,128)(2,1)S(1)} %get-tuple-element.66), channel_id=1, source_target_pairs={{16,8},{17,9},{18,10},{19,11},{20,12},{21,13},{22,14},{23,15}} | collective-permute-start | bytes 356360 | tf_op jit(solution)/shard_map/ppermute | solution.py:446
  42.5 1.4 %collective-permute-done.9.face = s16[464,128]{1,0:T(8,128)(2,1)S(1)} collective-permute-done((s16[464,128]{1,0:T(8,128)(2,1)S(1)}, s16[464,128]{1,0:T(8,128)(2,1)S(1)}, u32[]{:S(2)}, u32[]{:S(2)}) %collective-permute-start.9) | collective-permute-done | bytes 118816 | tf_op jit(solution)/shard_map/ppermute | solution.py:446
  43.9 0.7 %collective-permute-start.10 = (s16[464,128]{1,0:T(8,128)(2,1)S(1)}, s16[464,128]{1,0:T(8,128)(2,1)S(1)}, u32[]{:S(2)}, u32[]{:S(2)}) collective-permute-start(s16[464,128]{1,0:T(8,128)(2,1)S(1)} %get-tuple-element.55), channel_id=1, source_target_pairs={{16,8},{17,9},{18,10},{19,11},{20,12},{21,13},{22,14},{23,15}} | collective-permute-start | bytes 356360 | tf_op jit(solution)/shard_map/ppermute | solution.py:446
  44.6 0.3 backward.8
  44.9 6.8 %collective-permute-start.18 = (s16[464,128]{1,0:T(8,128)(2,1)S(1)}, s16[464,128]{1,0:T(8,128)(2,1)S(1)}, u32[]{:S(2)}, u32[]{:S(2)}) collective-permute-start(s16[464,128]{1,0:T(8,128)(2,1)S(1)} %get-tuple-element.68), channel_id=1, source_target_pairs={{0,8},{8,0},{16,24},{24,16},{1,9},{9,1},{17,25},{25,17},{2,10},{10... | collective-permute-start | bytes 356360 | tf_op jit(solution)/shard_map/ppermute | solution.py:446
  51.7 2.3 %collective-permute-start.11 = (s16[464,128]{1,0:T(8,128)(2,1)S(1)}, s16[464,128]{1,0:T(8,128)(2,1)S(1)}, u32[]{:S(2)}, u32[]{:S(2)}) collective-permute-start(s16[464,128]{1,0:T(8,128)(2,1)S(1)} %get-tuple-element.57), channel_id=1, source_target_pairs={{0,8},{8,0},{16,24},{24,16},{1,9},{9,1},{17,25},{25,17},{2,10},{10... | collective-permute-start | bytes 356360 | tf_op jit(solution)/shard_map/ppermute | solution.py:446
  54.0 0.4 collective-permute-done.18.refs_2_
  54.4 0.6 backward.9.refs_0_
  55.0 1.8 %collective-permute-done.11.face = s16[464,128]{1,0:T(8,128)(2,1)S(1)} collective-permute-done((s16[464,128]{1,0:T(8,128)(2,1)S(1)}, s16[464,128]{1,0:T(8,128)(2,1)S(1)}, u32[]{:S(2)}, u32[]{:S(2)}) %collective-permute-start.11) | collective-permute-done | bytes 118816 | tf_op jit(solution)/shard_map/ppermute | solution.py:446
  56.9 1.4 %last.1 = f32[2,7,16,1024]{3,2,1,0:T(8,128)} custom-call(bf16[2,7,7,16,1024]{4,3,2,1,0:T(8,128)(2,1)S(1)} %copy-done, f32[2,2,16,1024]{3,2,1,0:T(8,128)S(1)} %copy-done.1, s16[464,128]{1,0:T(8,128)(2,1)S(1)} %collective-permute-done.11.face, f32[2,7,16,512]{3,2,1,0:T(8,128)S(1)} %backward.9.refs_0_, f32[2,7,16,512]{3,2,1,0:T(8,128)S(1)} %get-tuple-element.70.refs_1_), custom_call_target="tpu_custom_call" | custom-call | tf_op jit(solution)/shard_map/last/pallas_call | solution.py:383
  (18 shorter events, 0.2 us)
Async XLA Ops:
  0.0 14.7 %copy-start.1 = (f32[2,2,16,1024]{3,2,1,0:T(8,128)S(1)}, f32[2,2,16,1024]{3,2,1,0:T(8,128)}, u32[]{:S(2)}) copy-start(f32[2,2,16,1024]{3,2,1,0:T(8,128)} %coupling_ref.25) | copy-start | bytes 786436
  0.0 1.2 %copy-start.2 = (f32[2,7,16,1024]{3,2,1,0:T(8,128)S(1)}, f32[2,7,16,1024]{3,2,1,0:T(8,128)}, u32[]{:S(2)}) copy-start(f32[2,7,16,1024]{3,2,1,0:T(8,128)} %state_ref.7) | copy-start | bytes 2752516
  1.2 13.5 %copy-start = (bf16[2,7,7,16,1024]{4,3,2,1,0:T(8,128)(2,1)S(1)}, bf16[2,7,7,16,1024]{4,3,2,1,0:T(8,128)(2,1)}, u32[]{:S(2)}) copy-start(bf16[2,7,7,16,1024]{4,3,2,1,0:T(8,128)(2,1)} %inverse_ref.25) | copy-start | bytes 9633796
  1.4 10.2 %collective-permute-start.4 = (s16[912,128]{1,0:T(8,128)(2,1)S(1)}, s16[912,128]{1,0:T(8,128)(2,1)S(1)}, u32[]{:S(2)}, u32[]{:S(2)}) collective-permute-start(s16[912,128]{1,0:T(8,128)(2,1)S(1)} %encode.3), channel_id=1, source_target_pairs={{0,8},{8,0},{16,24},{24,16},{1,9},{9,1},{17,25},{25,17},{2,10},{10... | collective-permute-start | bytes 700424 | tf_op jit(solution)/shard_map/ppermute | solution.py:426
  4.6 10.7 %collective-permute-start = (s16[912,128]{1,0:T(8,128)(2,1)S(1)}, s16[912,128]{1,0:T(8,128)(2,1)S(1)}, u32[]{:S(2)}, u32[]{:S(2)}) collective-permute-start(s16[912,128]{1,0:T(8,128)(2,1)S(1)} %encode.2.after_ref), channel_id=1, source_target_pairs={{0,8},{8,0},{16,24},{24,16},{1,9},{9,1},{17,25},{25,17},{2,10},{10... | collective-permute-start | bytes 700424 | tf_op jit(solution)/shard_map/ppermute | solution.py:426
  4.9 8.3 %collective-permute-start.1 = (f32[2,7,2,1024]{3,2,1,0:T(2,128)S(1)}, f32[2,7,2,1024]{3,2,1,0:T(2,128)S(1)}, u32[]{:S(2)}, u32[]{:S(2)}) collective-permute-start(f32[2,7,2,1024]{3,2,1,0:T(2,128)S(1)} %get-tuple-element.39), channel_id=1, source_target_pairs={{0,2},{2,0},{4,6},{6,4},{1,3},{3,1},{5,7},{7,5},{8,10},{10,8},{12,... | collective-permute-start | bytes 344072 | tf_op jit(solution)/shard_map/ppermute | solution.py:432
  7.0 7.3 %collective-permute-start.2 = (f32[2,7,2,1024]{3,2,1,0:T(2,128)S(1)}, f32[2,7,2,1024]{3,2,1,0:T(2,128)S(1)}, u32[]{:S(2)}, u32[]{:S(2)}) collective-permute-start(f32[2,7,2,1024]{3,2,1,0:T(2,128)S(1)} %get-tuple-element.40), channel_id=1, source_target_pairs={{0,6},{2,4},{4,2},{6,0},{1,7},{3,5},{5,3},{7,1},{8,14},{10,12},{12... | collective-permute-start | bytes 344072 | tf_op jit(solution)/shard_map/ppermute | solution.py:432
  9.5 4.9 %collective-permute-start.3 = (f32[2,7,16,128]{3,2,1,0:T(8,128)S(1)}, f32[2,7,16,128]{3,2,1,0:T(8,128)S(1)}, u32[]{:S(2)}, u32[]{:S(2)}) collective-permute-start(f32[2,7,16,128]{3,2,1,0:T(8,128)S(1)} %get-tuple-element.41), channel_id=1, source_target_pairs={{0,1},{1,0},{2,3},{3,2},{4,5},{5,4},{6,7},{7,6},{8,9},{9,8},{10,11... | collective-permute-start | bytes 344072 | tf_op jit(solution)/shard_map/ppermute | solution.py:431
  9.5 0.9 %copy-start.3 = (s32[2,16,1024]{2,1,0:T(8,128)S(1)}, s32[2,16,1024]{2,1,0:T(8,128)}, u32[]{:S(2)}) copy-start(s32[2,16,1024]{2,1,0:T(8,128)} %wall_ref.1) | copy-start | bytes 393220
  11.6 11.3 %collective-permute-start.12 = (s16[912,128]{1,0:T(8,128)(2,1)S(1)}, s16[912,128]{1,0:T(8,128)(2,1)S(1)}, u32[]{:S(2)}, u32[]{:S(2)}) collective-permute-start(s16[912,128]{1,0:T(8,128)(2,1)S(1)} %collective-permute-done.4.refs_3_), channel_id=1, source_target_pairs={{0,16},{8,24},{16,0},{24,8},{1,17},{9,25},{17,1},{25,9},{2,18},{10... | collective-permute-start | bytes 700424 | tf_op jit(solution)/shard_map/ppermute | solution.py:452
  15.3 9.5 %collective-permute-start.5 = (s16[912,128]{1,0:T(8,128)(2,1)S(1)}, s16[912,128]{1,0:T(8,128)(2,1)S(1)}, u32[]{:S(2)}, u32[]{:S(2)}) collective-permute-start(s16[912,128]{1,0:T(8,128)(2,1)S(1)} %collective-permute-done.refs_3_), channel_id=1, source_target_pairs={{0,16},{8,24},{16,0},{24,8},{1,17},{9,25},{17,1},{25,9},{2,18},{10... | collective-permute-start | bytes 700424 | tf_op jit(solution)/shard_map/ppermute | solution.py:452
  16.9 6.0 %collective-permute-start.13 = (s16[464,128]{1,0:T(8,128)(2,1)S(1)}, s16[464,128]{1,0:T(8,128)(2,1)S(1)}, u32[]{:S(2)}, u32[]{:S(2)}) collective-permute-start(s16[464,128]{1,0:T(8,128)(2,1)S(1)} %get-tuple-element.43), channel_id=1, source_target_pairs={{0,8},{8,0},{16,24},{24,16},{1,9},{9,1},{17,25},{25,17},{2,10},{10... | collective-permute-start | bytes 356360 | tf_op jit(solution)/shard_map/ppermute | solution.py:446
  19.3 4.9 %collective-permute-start.6 = (s16[464,128]{1,0:T(8,128)(2,1)S(1)}, s16[464,128]{1,0:T(8,128)(2,1)S(1)}, u32[]{:S(2)}, u32[]{:S(2)}) collective-permute-start(s16[464,128]{1,0:T(8,128)(2,1)S(1)} %get-tuple-element.47), channel_id=1, source_target_pairs={{0,8},{8,0},{16,24},{24,16},{1,9},{9,1},{17,25},{25,17},{2,10},{10... | collective-permute-start | bytes 356360 | tf_op jit(solution)/shard_map/ppermute | solution.py:446
  22.9 2.6 %collective-permute-start.14 = (s16[464,128]{1,0:T(8,128)(2,1)S(1)}, s16[464,128]{1,0:T(8,128)(2,1)S(1)}, u32[]{:S(2)}, u32[]{:S(2)}) collective-permute-start(s16[464,128]{1,0:T(8,128)(2,1)S(1)} %get-tuple-element.60), channel_id=1, source_target_pairs={{8,16},{9,17},{10,18},{11,19},{12,20},{13,21},{14,22},{15,23}} | collective-permute-start | bytes 356360 | tf_op jit(solution)/shard_map/ppermute | solution.py:446
  24.8 5.1 %collective-permute-start.7 = (s16[464,128]{1,0:T(8,128)(2,1)S(1)}, s16[464,128]{1,0:T(8,128)(2,1)S(1)}, u32[]{:S(2)}, u32[]{:S(2)}) collective-permute-start(s16[464,128]{1,0:T(8,128)(2,1)S(1)} %get-tuple-element.49), channel_id=1, source_target_pairs={{8,16},{9,17},{10,18},{11,19},{12,20},{13,21},{14,22},{15,23}} | collective-permute-start | bytes 356360 | tf_op jit(solution)/shard_map/ppermute | solution.py:446
  25.6 10.8 %collective-permute-start.15 = (s16[464,128]{1,0:T(8,128)(2,1)S(1)}, s16[464,128]{1,0:T(8,128)(2,1)S(1)}, u32[]{:S(2)}, u32[]{:S(2)}) collective-permute-start(s16[464,128]{1,0:T(8,128)(2,1)S(1)} %get-tuple-element.62), channel_id=1, source_target_pairs={{0,8},{8,0},{16,24},{24,16},{1,9},{9,1},{17,25},{25,17},{2,10},{10... | collective-permute-start | bytes 356360 | tf_op jit(solution)/shard_map/ppermute | solution.py:446
  29.9 8.9 %collective-permute-start.8 = (s16[464,128]{1,0:T(8,128)(2,1)S(1)}, s16[464,128]{1,0:T(8,128)(2,1)S(1)}, u32[]{:S(2)}, u32[]{:S(2)}) collective-permute-start(s16[464,128]{1,0:T(8,128)(2,1)S(1)} %get-tuple-element.51), channel_id=1, source_target_pairs={{0,8},{8,0},{16,24},{24,16},{1,9},{9,1},{17,25},{25,17},{2,10},{10... | collective-permute-start | bytes 356360 | tf_op jit(solution)/shard_map/ppermute | solution.py:446
  36.4 5.3 %collective-permute-start.16 = (s16[464,128]{1,0:T(8,128)(2,1)S(1)}, s16[464,128]{1,0:T(8,128)(2,1)S(1)}, u32[]{:S(2)}, u32[]{:S(2)}) collective-permute-start(s16[464,128]{1,0:T(8,128)(2,1)S(1)} %get-tuple-element.64), channel_id=1, source_target_pairs={{0,8},{8,0},{16,24},{24,16},{1,9},{9,1},{17,25},{25,17},{2,10},{10... | collective-permute-start | bytes 356360 | tf_op jit(solution)/shard_map/ppermute | solution.py:446
  38.9 4.9 %collective-permute-start.9 = (s16[464,128]{1,0:T(8,128)(2,1)S(1)}, s16[464,128]{1,0:T(8,128)(2,1)S(1)}, u32[]{:S(2)}, u32[]{:S(2)}) collective-permute-start(s16[464,128]{1,0:T(8,128)(2,1)S(1)} %get-tuple-element.53), channel_id=1, source_target_pairs={{0,8},{8,0},{16,24},{24,16},{1,9},{9,1},{17,25},{25,17},{2,10},{10... | collective-permute-start | bytes 356360 | tf_op jit(solution)/shard_map/ppermute | solution.py:446
  41.8 2.8 %collective-permute-start.17 = (s16[464,128]{1,0:T(8,128)(2,1)S(1)}, s16[464,128]{1,0:T(8,128)(2,1)S(1)}, u32[]{:S(2)}, u32[]{:S(2)}) collective-permute-start(s16[464,128]{1,0:T(8,128)(2,1)S(1)} %get-tuple-element.66), channel_id=1, source_target_pairs={{16,8},{17,9},{18,10},{19,11},{20,12},{21,13},{22,14},{23,15}} | collective-permute-start | bytes 356360 | tf_op jit(solution)/shard_map/ppermute | solution.py:446
  43.9 7.7 %collective-permute-start.10 = (s16[464,128]{1,0:T(8,128)(2,1)S(1)}, s16[464,128]{1,0:T(8,128)(2,1)S(1)}, u32[]{:S(2)}, u32[]{:S(2)}) collective-permute-start(s16[464,128]{1,0:T(8,128)(2,1)S(1)} %get-tuple-element.55), channel_id=1, source_target_pairs={{16,8},{17,9},{18,10},{19,11},{20,12},{21,13},{22,14},{23,15}} | collective-permute-start | bytes 356360 | tf_op jit(solution)/shard_map/ppermute | solution.py:446
  44.9 9.6 %collective-permute-start.18 = (s16[464,128]{1,0:T(8,128)(2,1)S(1)}, s16[464,128]{1,0:T(8,128)(2,1)S(1)}, u32[]{:S(2)}, u32[]{:S(2)}) collective-permute-start(s16[464,128]{1,0:T(8,128)(2,1)S(1)} %get-tuple-element.68), channel_id=1, source_target_pairs={{0,8},{8,0},{16,24},{24,16},{1,9},{9,1},{17,25},{25,17},{2,10},{10... | collective-permute-start | bytes 356360 | tf_op jit(solution)/shard_map/ppermute | solution.py:446
  51.7 5.2 %collective-permute-start.11 = (s16[464,128]{1,0:T(8,128)(2,1)S(1)}, s16[464,128]{1,0:T(8,128)(2,1)S(1)}, u32[]{:S(2)}, u32[]{:S(2)}) collective-permute-start(s16[464,128]{1,0:T(8,128)(2,1)S(1)} %get-tuple-element.57), channel_id=1, source_target_pairs={{0,8},{8,0},{16,24},{24,16},{1,9},{9,1},{17,25},{25,17},{2,10},{10... | collective-permute-start | bytes 356360 | tf_op jit(solution)/shard_map/ppermute | solution.py:446

commit v9 on v8

--- a/solution.py
+++ b/solution.py
@@ -442,8 +442,9 @@
     )
 
     def hop_pair(value, source, target):
-        exchange = min(source, target) % 2 == 0 and count % 2 == 0
-        return lax.ppermute(value, "ia", swaps(count, 0) if exchange else [(source, target)])
+        first = min(source, target) % 2
+        exchange = count % 2 == 0 and (first == 0 or source < target)
+        return lax.ppermute(value, "ia", swaps(count, first) if exchange else [(source, target)])
 
     def pass_on(h, *gate):
         passed = near[h] if count == 4 else coded[h]

time: 58.5 us -> 59.3 us (1.014)
  starting transfers between devices: 32.5 us -> 33.2 us
    ppermute x12, starting transfers between devices: 21.6 us -> 22.3 us  [hop_pair(): lax.ppermute(value, 'ia', swaps(count, first) if exchange else [(source,...]
  transfers between devices with their start and end apart: 19 -> 19, of which waited for: 10 -> 11; matrix products, arithmetic and copies ran while one was open for 0% -> 0% of each run, Pallas kernels for 8% -> 8%
where the time goes in v9:
time: 59.3 us; the launch traced here: 59.2 us
  starting transfers between devices  33.2 us (56%)
  waiting for transfers between devices  17.4 us (29%)
  Pallas kernels  6.2 us (10%)
  local copies, waits for them, and re-layouts  2.13 us (4%)
    ppermute x12, starting transfers between devices, hop_pair(): lax.ppermute(value, 'ia', swaps(count, first) if exchange else [(source,...  22.3 us
    ppermute x12, waiting for transfers between devices, hop_pair(): lax.ppermute(value, 'ia', swaps(count, first) if exchange else [(source,...  15.4 us
    pallas_call x20, Pallas kernels, call(): pl.pallas_call(kernel, in_specs=[whole()] * len(operands), out_specs=[who...  6.2 us
    ppermute x2, starting transfers between devices, shards(): lax.ppermute(edge, 'ja', swaps(count_j, s))  4.62 us
    ppermute x2, starting transfers between devices, pass_on(): lax.ppermute(passed, 'ia', [(i, i ^ 2) for i in range(4)] if count == 4 e...  3.19 us
    ppermute x2, starting transfers between devices, shards(): lax.ppermute(coded[h], 'ia', swaps(count, 0))  3.08 us
    unnamed x8, local copies, waits for them, and re-layouts  2.13 us
    ppermute x2, waiting for transfers between devices, shards(): lax.ppermute(edge, 'ja', swaps(count_j, s))  1.2 us
  transfers between devices with their start and end apart: 19, of which 11 were waited for; matrix products, arithmetic and copies ran while one was open for 0% of the time, Pallas kernels for 8%

profile of v9, /device:TPU:0, one launch (start us, length us, event | category | flops | bytes accessed | tf_op | source)
XLA Modules:
  0.0 59.2 jit_solution(4397296194434026631)
XLA Ops:
  0.0 1.2 %copy-done.2 = f32[2,7,16,1024]{3,2,1,0:T(8,128)S(1)} copy-done((f32[2,7,16,1024]{3,2,1,0:T(8,128)S(1)}, f32[2,7,16,1024]{3,2,1,0:T(8,128)}, u32[]{:S(2)}) %copy-start.2) | copy-done | bytes 917528
  1.2 0.2 encode.3
  1.4 3.0 %collective-permute-start.4 = (s16[912,128]{1,0:T(8,128)(2,1)S(1)}, s16[912,128]{1,0:T(8,128)(2,1)S(1)}, u32[]{:S(2)}, u32[]{:S(2)}) collective-permute-start(s16[912,128]{1,0:T(8,128)(2,1)S(1)} %encode.3), channel_id=1, source_target_pairs={{0,8},{8,0},{16,24},{24,16},{1,9},{9,1},{17,25},{25,17},{2,10},{10... | collective-permute-start | bytes 700424 | tf_op jit(solution)/shard_map/ppermute | solution.py:426
  4.4 0.2 encode.2.after_ref
  4.6 0.1 collective-permute-start
  4.6 0.2 edges.1
  4.9 2.1 %collective-permute-start.1 = (f32[2,7,2,1024]{3,2,1,0:T(2,128)S(1)}, f32[2,7,2,1024]{3,2,1,0:T(2,128)S(1)}, u32[]{:S(2)}, u32[]{:S(2)}) collective-permute-start(f32[2,7,2,1024]{3,2,1,0:T(2,128)S(1)} %get-tuple-element.39), channel_id=1, source_target_pairs={{0,2},{2,0},{4,6},{6,4},{1,3},{3,1},{5,7},{7,5},{8,10},{10,8},{12,... | collective-permute-start | bytes 344072 | tf_op jit(solution)/shard_map/ppermute | solution.py:432
  7.0 2.5 %collective-permute-start.2 = (f32[2,7,2,1024]{3,2,1,0:T(2,128)S(1)}, f32[2,7,2,1024]{3,2,1,0:T(2,128)S(1)}, u32[]{:S(2)}, u32[]{:S(2)}) collective-permute-start(f32[2,7,2,1024]{3,2,1,0:T(2,128)S(1)} %get-tuple-element.40), channel_id=1, source_target_pairs={{0,6},{2,4},{4,2},{6,0},{1,7},{3,5},{5,3},{7,1},{8,14},{10,12},{12... | collective-permute-start | bytes 344072 | tf_op jit(solution)/shard_map/ppermute | solution.py:432
  9.5 0.9 %copy-done.3 = s32[2,16,1024]{2,1,0:T(8,128)S(1)} copy-done((s32[2,16,1024]{2,1,0:T(8,128)S(1)}, s32[2,16,1024]{2,1,0:T(8,128)}, u32[]{:S(2)}) %copy-start.3) | copy-done | bytes 131096
  10.4 1.2 %local.1 = (f32[2,7,16,512]{3,2,1,0:T(8,128)S(1)}, f32[2,7,16,512]{3,2,1,0:T(8,128)S(1)}, f32[2,16,1024]{2,1,0:T(8,128)S(1)}) custom-call(f32[2,7,16,1024]{3,2,1,0:T(8,128)S(1)} %copy-done.2, s32[2,16,1024]{2,1,0:T(8,128)S(1)} %copy-done.3), custom_call_target="tpu_custom_call" | custom-call | flops 9175040 | bytes 2293760 | tf_op jit(solution)/shard_map/local/pallas_call | solution.py:383
  11.6 1.6 %collective-permute-start.12 = (s16[912,128]{1,0:T(8,128)(2,1)S(1)}, s16[912,128]{1,0:T(8,128)(2,1)S(1)}, u32[]{:S(2)}, u32[]{:S(2)}) collective-permute-start(s16[912,128]{1,0:T(8,128)(2,1)S(1)} %collective-permute-done.4.refs_3_), channel_id=1, source_target_pairs={{0,16},{8,24},{16,0},{24,8},{1,17},{9,25},{17,1},{25,9},{2,18},{10... | collective-permute-start | bytes 700424 | tf_op jit(solution)/shard_map/ppermute | solution.py:453
  13.2 1.2 %collective-permute-done.2.refs_1_ = f32[2,7,2,1024]{3,2,1,0:T(2,128)S(1)} collective-permute-done((f32[2,7,2,1024]{3,2,1,0:T(2,128)S(1)}, f32[2,7,2,1024]{3,2,1,0:T(2,128)S(1)}, u32[]{:S(2)}, u32[]{:S(2)}) %collective-permute-start.2) | collective-permute-done | bytes 114720 | tf_op jit(solution)/shard_map/ppermute | solution.py:432
  14.4 0.3 halo.2.refs_0_
  14.7 0.5 forward.8
  15.3 1.6 %collective-permute-start.5 = (s16[912,128]{1,0:T(8,128)(2,1)S(1)}, s16[912,128]{1,0:T(8,128)(2,1)S(1)}, u32[]{:S(2)}, u32[]{:S(2)}) collective-permute-start(s16[912,128]{1,0:T(8,128)(2,1)S(1)} %collective-permute-done.refs_3_), channel_id=1, source_target_pairs={{0,16},{8,24},{16,0},{24,8},{1,17},{9,25},{17,1},{25,9},{2,18},{10... | collective-permute-start | bytes 700424 | tf_op jit(solution)/shard_map/ppermute | solution.py:453
  16.9 1.5 %collective-permute-start.13 = (s16[464,128]{1,0:T(8,128)(2,1)S(1)}, s16[464,128]{1,0:T(8,128)(2,1)S(1)}, u32[]{:S(2)}, u32[]{:S(2)}) collective-permute-start(s16[464,128]{1,0:T(8,128)(2,1)S(1)} %get-tuple-element.43), channel_id=1, source_target_pairs={{0,8},{8,0},{16,24},{24,16},{1,9},{9,1},{17,25},{25,17},{2,10},{10... | collective-permute-start | bytes 356360 | tf_op jit(solution)/shard_map/ppermute | solution.py:447
  18.4 0.4 halo.3.refs_0_
  18.7 0.5 forward.9
  19.3 0.1 collective-permute-start.6
  19.4 3.5 %collective-permute-done.13.face = s16[464,128]{1,0:T(8,128)(2,1)S(1)} collective-permute-done((s16[464,128]{1,0:T(8,128)(2,1)S(1)}, s16[464,128]{1,0:T(8,128)(2,1)S(1)}, u32[]{:S(2)}, u32[]{:S(2)}) %collective-permute-start.13) | collective-permute-done | bytes 118816 | tf_op jit(solution)/shard_map/ppermute | solution.py:447
  22.8 0.1 forward.13
  22.9 0.6 %collective-permute-start.14 = (s16[464,128]{1,0:T(8,128)(2,1)S(1)}, s16[464,128]{1,0:T(8,128)(2,1)S(1)}, u32[]{:S(2)}, u32[]{:S(2)}) collective-permute-start(s16[464,128]{1,0:T(8,128)(2,1)S(1)} %get-tuple-element.60), channel_id=1, source_target_pairs={{0,24},{8,16},{16,8},{24,0},{1,25},{9,17},{17,9},{25,1},{2,26},{10... | collective-permute-start | bytes 356360 | tf_op jit(solution)/shard_map/ppermute | solution.py:447
  23.5 1.6 %collective-permute-done.6.face = s16[464,128]{1,0:T(8,128)(2,1)S(1)} collective-permute-done((s16[464,128]{1,0:T(8,128)(2,1)S(1)}, s16[464,128]{1,0:T(8,128)(2,1)S(1)}, u32[]{:S(2)}, u32[]{:S(2)}) %collective-permute-start.6) | collective-permute-done | bytes 118816 | tf_op jit(solution)/shard_map/ppermute | solution.py:447
  25.2 0.8 %collective-permute-done.5.neighbour = s16[912,128]{1,0:T(8,128)(2,1)S(1)} collective-permute-done((s16[912,128]{1,0:T(8,128)(2,1)S(1)}, s16[912,128]{1,0:T(8,128)(2,1)S(1)}, u32[]{:S(2)}, u32[]{:S(2)}) %collective-permute-start.5) | collective-permute-done | bytes 233504 | tf_op jit(solution)/shard_map/ppermute | solution.py:453
  26.0 0.1 forward.10
  26.1 3.8 %collective-permute-start.7 = (s16[464,128]{1,0:T(8,128)(2,1)S(1)}, s16[464,128]{1,0:T(8,128)(2,1)S(1)}, u32[]{:S(2)}, u32[]{:S(2)}) collective-permute-start(s16[464,128]{1,0:T(8,128)(2,1)S(1)} %get-tuple-element.49), channel_id=1, source_target_pairs={{0,24},{8,16},{16,8},{24,0},{1,25},{9,17},{17,9},{25,1},{2,26},{10... | collective-permute-start | bytes 356360 | tf_op jit(solution)/shard_map/ppermute | solution.py:447
  29.9 0.1 forward.14
  29.9 0.1 collective-permute-start.15
  30.0 3.4 %collective-permute-done.7.face = s16[464,128]{1,0:T(8,128)(2,1)S(1)} collective-permute-done((s16[464,128]{1,0:T(8,128)(2,1)S(1)}, s16[464,128]{1,0:T(8,128)(2,1)S(1)}, u32[]{:S(2)}, u32[]{:S(2)}) %collective-permute-start.7) | collective-permute-done | bytes 118816 | tf_op jit(solution)/shard_map/ppermute | solution.py:447
  33.5 0.1 forward.11
  33.5 1.9 %collective-permute-start.8 = (s16[464,128]{1,0:T(8,128)(2,1)S(1)}, s16[464,128]{1,0:T(8,128)(2,1)S(1)}, u32[]{:S(2)}, u32[]{:S(2)}) collective-permute-start(s16[464,128]{1,0:T(8,128)(2,1)S(1)} %get-tuple-element.51), channel_id=1, source_target_pairs={{0,8},{8,0},{16,24},{24,16},{1,9},{9,1},{17,25},{25,17},{2,10},{10... | collective-permute-start | bytes 356360 | tf_op jit(solution)/shard_map/ppermute | solution.py:447
  35.4 0.7 %collective-permute-done.15.face = s16[464,128]{1,0:T(8,128)(2,1)S(1)} collective-permute-done((s16[464,128]{1,0:T(8,128)(2,1)S(1)}, s16[464,128]{1,0:T(8,128)(2,1)S(1)}, u32[]{:S(2)}, u32[]{:S(2)}) %collective-permute-start.15) | collective-permute-done | bytes 118816 | tf_op jit(solution)/shard_map/ppermute | solution.py:447
  36.1 0.1 forward.15
  36.1 0.7 %collective-permute-start.16 = (s16[464,128]{1,0:T(8,128)(2,1)S(1)}, s16[464,128]{1,0:T(8,128)(2,1)S(1)}, u32[]{:S(2)}, u32[]{:S(2)}) collective-permute-start(s16[464,128]{1,0:T(8,128)(2,1)S(1)} %get-tuple-element.64), channel_id=1, source_target_pairs={{0,8},{8,0},{16,24},{24,16},{1,9},{9,1},{17,25},{25,17},{2,10},{10... | collective-permute-start | bytes 356360 | tf_op jit(solution)/shard_map/ppermute | solution.py:447
  36.8 1.8 %collective-permute-done.8.face = s16[464,128]{1,0:T(8,128)(2,1)S(1)} collective-permute-done((s16[464,128]{1,0:T(8,128)(2,1)S(1)}, s16[464,128]{1,0:T(8,128)(2,1)S(1)}, u32[]{:S(2)}, u32[]{:S(2)}) %collective-permute-start.8) | collective-permute-done | bytes 118816 | tf_op jit(solution)/shard_map/ppermute | solution.py:447
  38.6 0.1 forward.12
  38.7 2.1 %collective-permute-start.9 = (s16[464,128]{1,0:T(8,128)(2,1)S(1)}, s16[464,128]{1,0:T(8,128)(2,1)S(1)}, u32[]{:S(2)}, u32[]{:S(2)}) collective-permute-start(s16[464,128]{1,0:T(8,128)(2,1)S(1)} %get-tuple-element.53), channel_id=1, source_target_pairs={{0,8},{8,0},{16,24},{24,16},{1,9},{9,1},{17,25},{25,17},{2,10},{10... | collective-permute-start | bytes 356360 | tf_op jit(solution)/shard_map/ppermute | solution.py:447
  40.8 0.6 %collective-permute-done.16.face = s16[464,128]{1,0:T(8,128)(2,1)S(1)} collective-permute-done((s16[464,128]{1,0:T(8,128)(2,1)S(1)}, s16[464,128]{1,0:T(8,128)(2,1)S(1)}, u32[]{:S(2)}, u32[]{:S(2)}) %collective-permute-start.16) | collective-permute-done | bytes 118816 | tf_op jit(solution)/shard_map/ppermute | solution.py:447
  41.5 0.7 %collective-permute-start.17 = (s16[464,128]{1,0:T(8,128)(2,1)S(1)}, s16[464,128]{1,0:T(8,128)(2,1)S(1)}, u32[]{:S(2)}, u32[]{:S(2)}) collective-permute-start(s16[464,128]{1,0:T(8,128)(2,1)S(1)} %get-tuple-element.66), channel_id=1, source_target_pairs={{16,8},{17,9},{18,10},{19,11},{20,12},{21,13},{22,14},{23,15}} | collective-permute-start | bytes 356360 | tf_op jit(solution)/shard_map/ppermute | solution.py:447
  42.2 1.4 %collective-permute-done.9.face = s16[464,128]{1,0:T(8,128)(2,1)S(1)} collective-permute-done((s16[464,128]{1,0:T(8,128)(2,1)S(1)}, s16[464,128]{1,0:T(8,128)(2,1)S(1)}, u32[]{:S(2)}, u32[]{:S(2)}) %collective-permute-start.9) | collective-permute-done | bytes 118816 | tf_op jit(solution)/shard_map/ppermute | solution.py:447
  43.7 0.7 %collective-permute-start.10 = (s16[464,128]{1,0:T(8,128)(2,1)S(1)}, s16[464,128]{1,0:T(8,128)(2,1)S(1)}, u32[]{:S(2)}, u32[]{:S(2)}) collective-permute-start(s16[464,128]{1,0:T(8,128)(2,1)S(1)} %get-tuple-element.55), channel_id=1, source_target_pairs={{16,8},{17,9},{18,10},{19,11},{20,12},{21,13},{22,14},{23,15}} | collective-permute-start | bytes 356360 | tf_op jit(solution)/shard_map/ppermute | solution.py:447
  44.4 0.3 backward.8
  44.6 7.8 %collective-permute-start.18 = (s16[464,128]{1,0:T(8,128)(2,1)S(1)}, s16[464,128]{1,0:T(8,128)(2,1)S(1)}, u32[]{:S(2)}, u32[]{:S(2)}) collective-permute-start(s16[464,128]{1,0:T(8,128)(2,1)S(1)} %get-tuple-element.68), channel_id=1, source_target_pairs={{0,8},{8,0},{16,24},{24,16},{1,9},{9,1},{17,25},{25,17},{2,10},{10... | collective-permute-start | bytes 356360 | tf_op jit(solution)/shard_map/ppermute | solution.py:447
  52.5 2.4 %collective-permute-start.11 = (s16[464,128]{1,0:T(8,128)(2,1)S(1)}, s16[464,128]{1,0:T(8,128)(2,1)S(1)}, u32[]{:S(2)}, u32[]{:S(2)}) collective-permute-start(s16[464,128]{1,0:T(8,128)(2,1)S(1)} %get-tuple-element.57), channel_id=1, source_target_pairs={{0,8},{8,0},{16,24},{24,16},{1,9},{9,1},{17,25},{25,17},{2,10},{10... | collective-permute-start | bytes 356360 | tf_op jit(solution)/shard_map/ppermute | solution.py:447
  54.9 0.3 collective-permute-done.18.refs_2_
  55.2 0.6 backward.9.refs_0_
  55.8 1.9 %collective-permute-done.11.face = s16[464,128]{1,0:T(8,128)(2,1)S(1)} collective-permute-done((s16[464,128]{1,0:T(8,128)(2,1)S(1)}, s16[464,128]{1,0:T(8,128)(2,1)S(1)}, u32[]{:S(2)}, u32[]{:S(2)}) %collective-permute-start.11) | collective-permute-done | bytes 118816 | tf_op jit(solution)/shard_map/ppermute | solution.py:447
  57.7 1.4 %last.1 = f32[2,7,16,1024]{3,2,1,0:T(8,128)} custom-call(bf16[2,7,7,16,1024]{4,3,2,1,0:T(8,128)(2,1)S(1)} %copy-done, f32[2,2,16,1024]{3,2,1,0:T(8,128)S(1)} %copy-done.1, s16[464,128]{1,0:T(8,128)(2,1)S(1)} %collective-permute-done.11.face, f32[2,7,16,512]{3,2,1,0:T(8,128)S(1)} %backward.9.refs_0_, f32[2,7,16,512]{3,2,1,0:T(8,128)S(1)} %get-tuple-element.70.refs_1_), custom_call_target="tpu_custom_call" | custom-call | tf_op jit(solution)/shard_map/last/pallas_call | solution.py:383
  (18 shorter events, 0.2 us)
Async XLA Ops:
  0.0 14.7 %copy-start.1 = (f32[2,2,16,1024]{3,2,1,0:T(8,128)S(1)}, f32[2,2,16,1024]{3,2,1,0:T(8,128)}, u32[]{:S(2)}) copy-start(f32[2,2,16,1024]{3,2,1,0:T(8,128)} %coupling_ref.25) | copy-start | bytes 786436
  0.0 1.2 %copy-start.2 = (f32[2,7,16,1024]{3,2,1,0:T(8,128)S(1)}, f32[2,7,16,1024]{3,2,1,0:T(8,128)}, u32[]{:S(2)}) copy-start(f32[2,7,16,1024]{3,2,1,0:T(8,128)} %state_ref.7) | copy-start | bytes 2752516
  1.2 13.5 %copy-start = (bf16[2,7,7,16,1024]{4,3,2,1,0:T(8,128)(2,1)S(1)}, bf16[2,7,7,16,1024]{4,3,2,1,0:T(8,128)(2,1)}, u32[]{:S(2)}) copy-start(bf16[2,7,7,16,1024]{4,3,2,1,0:T(8,128)(2,1)} %inverse_ref.25) | copy-start | bytes 9633796
  1.4 10.2 %collective-permute-start.4 = (s16[912,128]{1,0:T(8,128)(2,1)S(1)}, s16[912,128]{1,0:T(8,128)(2,1)S(1)}, u32[]{:S(2)}, u32[]{:S(2)}) collective-permute-start(s16[912,128]{1,0:T(8,128)(2,1)S(1)} %encode.3), channel_id=1, source_target_pairs={{0,8},{8,0},{16,24},{24,16},{1,9},{9,1},{17,25},{25,17},{2,10},{10... | collective-permute-start | bytes 700424 | tf_op jit(solution)/shard_map/ppermute | solution.py:426
  4.6 10.7 %collective-permute-start = (s16[912,128]{1,0:T(8,128)(2,1)S(1)}, s16[912,128]{1,0:T(8,128)(2,1)S(1)}, u32[]{:S(2)}, u32[]{:S(2)}) collective-permute-start(s16[912,128]{1,0:T(8,128)(2,1)S(1)} %encode.2.after_ref), channel_id=1, source_target_pairs={{0,8},{8,0},{16,24},{24,16},{1,9},{9,1},{17,25},{25,17},{2,10},{10... | collective-permute-start | bytes 700424 | tf_op jit(solution)/shard_map/ppermute | solution.py:426
  4.9 8.3 %collective-permute-start.1 = (f32[2,7,2,1024]{3,2,1,0:T(2,128)S(1)}, f32[2,7,2,1024]{3,2,1,0:T(2,128)S(1)}, u32[]{:S(2)}, u32[]{:S(2)}) collective-permute-start(f32[2,7,2,1024]{3,2,1,0:T(2,128)S(1)} %get-tuple-element.39), channel_id=1, source_target_pairs={{0,2},{2,0},{4,6},{6,4},{1,3},{3,1},{5,7},{7,5},{8,10},{10,8},{12,... | collective-permute-start | bytes 344072 | tf_op jit(solution)/shard_map/ppermute | solution.py:432
  7.0 7.3 %collective-permute-start.2 = (f32[2,7,2,1024]{3,2,1,0:T(2,128)S(1)}, f32[2,7,2,1024]{3,2,1,0:T(2,128)S(1)}, u32[]{:S(2)}, u32[]{:S(2)}) collective-permute-start(f32[2,7,2,1024]{3,2,1,0:T(2,128)S(1)} %get-tuple-element.40), channel_id=1, source_target_pairs={{0,6},{2,4},{4,2},{6,0},{1,7},{3,5},{5,3},{7,1},{8,14},{10,12},{12... | collective-permute-start | bytes 344072 | tf_op jit(solution)/shard_map/ppermute | solution.py:432
  9.5 4.9 %collective-permute-start.3 = (f32[2,7,16,128]{3,2,1,0:T(8,128)S(1)}, f32[2,7,16,128]{3,2,1,0:T(8,128)S(1)}, u32[]{:S(2)}, u32[]{:S(2)}) collective-permute-start(f32[2,7,16,128]{3,2,1,0:T(8,128)S(1)} %get-tuple-element.41), channel_id=1, source_target_pairs={{0,1},{1,0},{2,3},{3,2},{4,5},{5,4},{6,7},{7,6},{8,9},{9,8},{10,11... | collective-permute-start | bytes 344072 | tf_op jit(solution)/shard_map/ppermute | solution.py:431
  9.5 0.9 %copy-start.3 = (s32[2,16,1024]{2,1,0:T(8,128)S(1)}, s32[2,16,1024]{2,1,0:T(8,128)}, u32[]{:S(2)}) copy-start(s32[2,16,1024]{2,1,0:T(8,128)} %wall_ref.1) | copy-start | bytes 393220
  11.6 11.3 %collective-permute-start.12 = (s16[912,128]{1,0:T(8,128)(2,1)S(1)}, s16[912,128]{1,0:T(8,128)(2,1)S(1)}, u32[]{:S(2)}, u32[]{:S(2)}) collective-permute-start(s16[912,128]{1,0:T(8,128)(2,1)S(1)} %collective-permute-done.4.refs_3_), channel_id=1, source_target_pairs={{0,16},{8,24},{16,0},{24,8},{1,17},{9,25},{17,1},{25,9},{2,18},{10... | collective-permute-start | bytes 700424 | tf_op jit(solution)/shard_map/ppermute | solution.py:453
  15.3 10.8 %collective-permute-start.5 = (s16[912,128]{1,0:T(8,128)(2,1)S(1)}, s16[912,128]{1,0:T(8,128)(2,1)S(1)}, u32[]{:S(2)}, u32[]{:S(2)}) collective-permute-start(s16[912,128]{1,0:T(8,128)(2,1)S(1)} %collective-permute-done.refs_3_), channel_id=1, source_target_pairs={{0,16},{8,24},{16,0},{24,8},{1,17},{9,25},{17,1},{25,9},{2,18},{10... | collective-permute-start | bytes 700424 | tf_op jit(solution)/shard_map/ppermute | solution.py:453
  16.9 6.0 %collective-permute-start.13 = (s16[464,128]{1,0:T(8,128)(2,1)S(1)}, s16[464,128]{1,0:T(8,128)(2,1)S(1)}, u32[]{:S(2)}, u32[]{:S(2)}) collective-permute-start(s16[464,128]{1,0:T(8,128)(2,1)S(1)} %get-tuple-element.43), channel_id=1, source_target_pairs={{0,8},{8,0},{16,24},{24,16},{1,9},{9,1},{17,25},{25,17},{2,10},{10... | collective-permute-start | bytes 356360 | tf_op jit(solution)/shard_map/ppermute | solution.py:447
  19.3 5.9 %collective-permute-start.6 = (s16[464,128]{1,0:T(8,128)(2,1)S(1)}, s16[464,128]{1,0:T(8,128)(2,1)S(1)}, u32[]{:S(2)}, u32[]{:S(2)}) collective-permute-start(s16[464,128]{1,0:T(8,128)(2,1)S(1)} %get-tuple-element.47), channel_id=1, source_target_pairs={{0,8},{8,0},{16,24},{24,16},{1,9},{9,1},{17,25},{25,17},{2,10},{10... | collective-permute-start | bytes 356360 | tf_op jit(solution)/shard_map/ppermute | solution.py:447
  22.9 7.0 %collective-permute-start.14 = (s16[464,128]{1,0:T(8,128)(2,1)S(1)}, s16[464,128]{1,0:T(8,128)(2,1)S(1)}, u32[]{:S(2)}, u32[]{:S(2)}) collective-permute-start(s16[464,128]{1,0:T(8,128)(2,1)S(1)} %get-tuple-element.60), channel_id=1, source_target_pairs={{0,24},{8,16},{16,8},{24,0},{1,25},{9,17},{17,9},{25,1},{2,26},{10... | collective-permute-start | bytes 356360 | tf_op jit(solution)/shard_map/ppermute | solution.py:447
  26.1 7.4 %collective-permute-start.7 = (s16[464,128]{1,0:T(8,128)(2,1)S(1)}, s16[464,128]{1,0:T(8,128)(2,1)S(1)}, u32[]{:S(2)}, u32[]{:S(2)}) collective-permute-start(s16[464,128]{1,0:T(8,128)(2,1)S(1)} %get-tuple-element.49), channel_id=1, source_target_pairs={{0,24},{8,16},{16,8},{24,0},{1,25},{9,17},{17,9},{25,1},{2,26},{10... | collective-permute-start | bytes 356360 | tf_op jit(solution)/shard_map/ppermute | solution.py:447
  29.9 6.2 %collective-permute-start.15 = (s16[464,128]{1,0:T(8,128)(2,1)S(1)}, s16[464,128]{1,0:T(8,128)(2,1)S(1)}, u32[]{:S(2)}, u32[]{:S(2)}) collective-permute-start(s16[464,128]{1,0:T(8,128)(2,1)S(1)} %get-tuple-element.62), channel_id=1, source_target_pairs={{0,8},{8,0},{16,24},{24,16},{1,9},{9,1},{17,25},{25,17},{2,10},{10... | collective-permute-start | bytes 356360 | tf_op jit(solution)/shard_map/ppermute | solution.py:447
  33.5 5.1 %collective-permute-start.8 = (s16[464,128]{1,0:T(8,128)(2,1)S(1)}, s16[464,128]{1,0:T(8,128)(2,1)S(1)}, u32[]{:S(2)}, u32[]{:S(2)}) collective-permute-start(s16[464,128]{1,0:T(8,128)(2,1)S(1)} %get-tuple-element.51), channel_id=1, source_target_pairs={{0,8},{8,0},{16,24},{24,16},{1,9},{9,1},{17,25},{25,17},{2,10},{10... | collective-permute-start | bytes 356360 | tf_op jit(solution)/shard_map/ppermute | solution.py:447
  36.1 5.3 %collective-permute-start.16 = (s16[464,128]{1,0:T(8,128)(2,1)S(1)}, s16[464,128]{1,0:T(8,128)(2,1)S(1)}, u32[]{:S(2)}, u32[]{:S(2)}) collective-permute-start(s16[464,128]{1,0:T(8,128)(2,1)S(1)} %get-tuple-element.64), channel_id=1, source_target_pairs={{0,8},{8,0},{16,24},{24,16},{1,9},{9,1},{17,25},{25,17},{2,10},{10... | collective-permute-start | bytes 356360 | tf_op jit(solution)/shard_map/ppermute | solution.py:447
  38.7 4.9 %collective-permute-start.9 = (s16[464,128]{1,0:T(8,128)(2,1)S(1)}, s16[464,128]{1,0:T(8,128)(2,1)S(1)}, u32[]{:S(2)}, u32[]{:S(2)}) collective-permute-start(s16[464,128]{1,0:T(8,128)(2,1)S(1)} %get-tuple-element.53), channel_id=1, source_target_pairs={{0,8},{8,0},{16,24},{24,16},{1,9},{9,1},{17,25},{25,17},{2,10},{10... | collective-permute-start | bytes 356360 | tf_op jit(solution)/shard_map/ppermute | solution.py:447
  41.5 2.9 %collective-permute-start.17 = (s16[464,128]{1,0:T(8,128)(2,1)S(1)}, s16[464,128]{1,0:T(8,128)(2,1)S(1)}, u32[]{:S(2)}, u32[]{:S(2)}) collective-permute-start(s16[464,128]{1,0:T(8,128)(2,1)S(1)} %get-tuple-element.66), channel_id=1, source_target_pairs={{16,8},{17,9},{18,10},{19,11},{20,12},{21,13},{22,14},{23,15}} | collective-permute-start | bytes 356360 | tf_op jit(solution)/shard_map/ppermute | solution.py:447
  43.7 8.7 %collective-permute-start.10 = (s16[464,128]{1,0:T(8,128)(2,1)S(1)}, s16[464,128]{1,0:T(8,128)(2,1)S(1)}, u32[]{:S(2)}, u32[]{:S(2)}) collective-permute-start(s16[464,128]{1,0:T(8,128)(2,1)S(1)} %get-tuple-element.55), channel_id=1, source_target_pairs={{16,8},{17,9},{18,10},{19,11},{20,12},{21,13},{22,14},{23,15}} | collective-permute-start | bytes 356360 | tf_op jit(solution)/shard_map/ppermute | solution.py:447
  44.6 10.6 %collective-permute-start.18 = (s16[464,128]{1,0:T(8,128)(2,1)S(1)}, s16[464,128]{1,0:T(8,128)(2,1)S(1)}, u32[]{:S(2)}, u32[]{:S(2)}) collective-permute-start(s16[464,128]{1,0:T(8,128)(2,1)S(1)} %get-tuple-element.68), channel_id=1, source_target_pairs={{0,8},{8,0},{16,24},{24,16},{1,9},{9,1},{17,25},{25,17},{2,10},{10... | collective-permute-start | bytes 356360 | tf_op jit(solution)/shard_map/ppermute | solution.py:447
  52.5 5.3 %collective-permute-start.11 = (s16[464,128]{1,0:T(8,128)(2,1)S(1)}, s16[464,128]{1,0:T(8,128)(2,1)S(1)}, u32[]{:S(2)}, u32[]{:S(2)}) collective-permute-start(s16[464,128]{1,0:T(8,128)(2,1)S(1)} %get-tuple-element.57), channel_id=1, source_target_pairs={{0,8},{8,0},{16,24},{24,16},{1,9},{9,1},{17,25},{25,17},{2,10},{10... | collective-permute-start | bytes 356360 | tf_op jit(solution)/shard_map/ppermute | solution.py:447

commit v10 on v5

--- a/solution.py
+++ b/solution.py
@@ -434,7 +434,9 @@
     )
 
     def hop_pair(value, source, target):
-        return lax.ppermute(value, "ia", swaps(count, min(source, target) % 2))
+        first = min(source, target) % 2
+        exchange = count % 2 == 0 and (first == 0 or source < target)
+        return lax.ppermute(value, "ia", swaps(count, first) if exchange else [(source, target)])
 
     def pass_on(h, *gate):
         passed = near[h] if count == 4 else coded[h]

time: 58.5 us -> 59.5 us (1.017)
  starting transfers between devices: 35.9 us -> 37.1 us
    ppermute x12, starting transfers between devices: 25.2 us -> 26.4 us  [hop_pair(): lax.ppermute(value, 'ia', swaps(count, first) if exchange else [(source,...]
  transfers between devices with their start and end apart: 19 -> 19, of which waited for: 14 -> 12; matrix products, arithmetic and copies ran while one was open for 0% -> 0% of each run, Pallas kernels for 8% -> 8%
where the time goes in v10:
time: 59.5 us; the launch traced here: 59.3 us
  starting transfers between devices  37.1 us (62%)
  waiting for transfers between devices  13.6 us (23%)
  Pallas kernels  6.19 us (10%)
  local copies, waits for them, and re-layouts  2.24 us (4%)
    ppermute x12, starting transfers between devices, hop_pair(): lax.ppermute(value, 'ia', swaps(count, first) if exchange else [(source,...  26.4 us
    ppermute x12, waiting for transfers between devices, hop_pair(): lax.ppermute(value, 'ia', swaps(count, first) if exchange else [(source,...  11.7 us
    pallas_call x20, Pallas kernels, call(): pl.pallas_call(kernel, in_specs=[whole()] * len(operands), out_specs=[who...  6.19 us
    ppermute x2, starting transfers between devices, shards(): lax.ppermute(edge, 'ja', swaps(count_j, s))  4.62 us
    ppermute x2, starting transfers between devices, shards(): lax.ppermute(coded[h], 'ia', swaps(count, 0))  3.08 us
    ppermute x2, starting transfers between devices, pass_on(): lax.ppermute(passed, 'ia', [(i, i ^ 2) for i in range(4)] if count == 4 e...  2.97 us
    unnamed x8, local copies, waits for them, and re-layouts  2.24 us
    ppermute x2, waiting for transfers between devices, shards(): lax.ppermute(edge, 'ja', swaps(count_j, s))  1.2 us
  transfers between devices with their start and end apart: 19, of which 12 were waited for; matrix products, arithmetic and copies ran while one was open for 0% of the time, Pallas kernels for 8%

profile of v10, /device:TPU:0, one launch (start us, length us, event | category | flops | bytes accessed | tf_op | source)
XLA Modules:
  0.0 59.3 jit_solution(579728801608070774)
XLA Ops:
  0.0 1.3 %copy-done.2 = f32[2,7,16,1024]{3,2,1,0:T(8,128)S(1)} copy-done((f32[2,7,16,1024]{3,2,1,0:T(8,128)S(1)}, f32[2,7,16,1024]{3,2,1,0:T(8,128)}, u32[]{:S(2)}) %copy-start.2) | copy-done | bytes 917528
  1.3 0.2 encode.3
  1.5 3.0 %collective-permute-start.11 = (s16[912,128]{1,0:T(8,128)(2,1)S(1)}, s16[912,128]{1,0:T(8,128)(2,1)S(1)}, u32[]{:S(2)}, u32[]{:S(2)}) collective-permute-start(s16[912,128]{1,0:T(8,128)(2,1)S(1)} %encode.3), channel_id=1, source_target_pairs={{0,8},{8,0},{16,24},{24,16},{1,9},{9,1},{17,25},{25,17},{2,10},{10... | collective-permute-start | bytes 700424 | tf_op jit(solution)/shard_map/ppermute | solution.py:418
  4.5 0.2 encode.2.after_ref
  4.7 0.1 collective-permute-start
  4.7 0.2 edges.1
  5.0 2.1 %collective-permute-start.1 = (f32[2,7,2,1024]{3,2,1,0:T(2,128)S(1)}, f32[2,7,2,1024]{3,2,1,0:T(2,128)S(1)}, u32[]{:S(2)}, u32[]{:S(2)}) collective-permute-start(f32[2,7,2,1024]{3,2,1,0:T(2,128)S(1)} %get-tuple-element.37), channel_id=1, source_target_pairs={{0,2},{2,0},{4,6},{6,4},{1,3},{3,1},{5,7},{7,5},{8,10},{10,8},{12,... | collective-permute-start | bytes 344072 | tf_op jit(solution)/shard_map/ppermute | solution.py:424
  7.1 2.5 %collective-permute-start.2 = (f32[2,7,2,1024]{3,2,1,0:T(2,128)S(1)}, f32[2,7,2,1024]{3,2,1,0:T(2,128)S(1)}, u32[]{:S(2)}, u32[]{:S(2)}) collective-permute-start(f32[2,7,2,1024]{3,2,1,0:T(2,128)S(1)} %get-tuple-element.38), channel_id=1, source_target_pairs={{0,6},{2,4},{4,2},{6,0},{1,7},{3,5},{5,3},{7,1},{8,14},{10,12},{12... | collective-permute-start | bytes 344072 | tf_op jit(solution)/shard_map/ppermute | solution.py:424
  9.6 0.9 %copy-done.3 = s32[2,16,1024]{2,1,0:T(8,128)S(1)} copy-done((s32[2,16,1024]{2,1,0:T(8,128)S(1)}, s32[2,16,1024]{2,1,0:T(8,128)}, u32[]{:S(2)}) %copy-start.3) | copy-done | bytes 131096
  10.5 1.2 %local.1 = (f32[2,7,16,512]{3,2,1,0:T(8,128)S(1)}, f32[2,7,16,512]{3,2,1,0:T(8,128)S(1)}, f32[2,16,1024]{2,1,0:T(8,128)S(1)}) custom-call(f32[2,7,16,1024]{3,2,1,0:T(8,128)S(1)} %copy-done.2, s32[2,16,1024]{2,1,0:T(8,128)S(1)} %copy-done.3), custom_call_target="tpu_custom_call" | custom-call | flops 9175040 | bytes 2293760 | tf_op jit(solution)/shard_map/local/pallas_call | solution.py:375
  11.7 1.6 %collective-permute-start.12 = (s16[912,128]{1,0:T(8,128)(2,1)S(1)}, s16[912,128]{1,0:T(8,128)(2,1)S(1)}, u32[]{:S(2)}, u32[]{:S(2)}) collective-permute-start(s16[912,128]{1,0:T(8,128)(2,1)S(1)} %collective-permute-done.11.refs_3_), channel_id=1, source_target_pairs={{0,16},{8,24},{16,0},{24,8},{1,17},{9,25},{17,1},{25,9},{2,18},{10... | collective-permute-start | bytes 700424 | tf_op jit(solution)/shard_map/ppermute | solution.py:445
  13.3 1.2 %collective-permute-done.2.refs_1_ = f32[2,7,2,1024]{3,2,1,0:T(2,128)S(1)} collective-permute-done((f32[2,7,2,1024]{3,2,1,0:T(2,128)S(1)}, f32[2,7,2,1024]{3,2,1,0:T(2,128)S(1)}, u32[]{:S(2)}, u32[]{:S(2)}) %collective-permute-start.2) | collective-permute-done | bytes 114720 | tf_op jit(solution)/shard_map/ppermute | solution.py:424
  14.5 0.7 %collective-permute-done.refs_3_ = s16[912,128]{1,0:T(8,128)(2,1)S(1)} collective-permute-done((s16[912,128]{1,0:T(8,128)(2,1)S(1)}, s16[912,128]{1,0:T(8,128)(2,1)S(1)}, u32[]{:S(2)}, u32[]{:S(2)}) %collective-permute-start) | collective-permute-done | bytes 233504 | tf_op jit(solution)/shard_map/ppermute | solution.py:418
  15.2 0.3 halo.2.refs_0_
  15.6 0.5 forward.8
  16.1 1.4 %collective-permute-start.4 = (s16[912,128]{1,0:T(8,128)(2,1)S(1)}, s16[912,128]{1,0:T(8,128)(2,1)S(1)}, u32[]{:S(2)}, u32[]{:S(2)}) collective-permute-start(s16[912,128]{1,0:T(8,128)(2,1)S(1)} %collective-permute-done.refs_3_), channel_id=1, source_target_pairs={{0,16},{8,24},{16,0},{24,8},{1,17},{9,25},{17,1},{25,9},{2,18},{10... | collective-permute-start | bytes 700424 | tf_op jit(solution)/shard_map/ppermute | solution.py:445
  17.5 0.3 halo.3.refs_0_
  17.8 0.5 forward.12
  18.4 1.1 %collective-permute-start.13 = (s16[464,128]{1,0:T(8,128)(2,1)S(1)}, s16[464,128]{1,0:T(8,128)(2,1)S(1)}, u32[]{:S(2)}, u32[]{:S(2)}) collective-permute-start(s16[464,128]{1,0:T(8,128)(2,1)S(1)} %get-tuple-element.54), channel_id=1, source_target_pairs={{0,8},{8,0},{16,24},{24,16},{1,9},{9,1},{17,25},{25,17},{2,10},{10... | collective-permute-start | bytes 356360 | tf_op jit(solution)/shard_map/ppermute | solution.py:439
  19.5 1.0 %collective-permute-start.5 = (s16[464,128]{1,0:T(8,128)(2,1)S(1)}, s16[464,128]{1,0:T(8,128)(2,1)S(1)}, u32[]{:S(2)}, u32[]{:S(2)}) collective-permute-start(s16[464,128]{1,0:T(8,128)(2,1)S(1)} %get-tuple-element.41), channel_id=1, source_target_pairs={{0,8},{8,0},{16,24},{24,16},{1,9},{9,1},{17,25},{25,17},{2,10},{10... | collective-permute-start | bytes 356360 | tf_op jit(solution)/shard_map/ppermute | solution.py:439
  20.5 3.1 %collective-permute-done.13.face = s16[464,128]{1,0:T(8,128)(2,1)S(1)} collective-permute-done((s16[464,128]{1,0:T(8,128)(2,1)S(1)}, s16[464,128]{1,0:T(8,128)(2,1)S(1)}, u32[]{:S(2)}, u32[]{:S(2)}) %collective-permute-start.13) | collective-permute-done | bytes 118816 | tf_op jit(solution)/shard_map/ppermute | solution.py:439
  23.5 0.1 forward.13
  23.6 1.0 %collective-permute-start.14 = (s16[464,128]{1,0:T(8,128)(2,1)S(1)}, s16[464,128]{1,0:T(8,128)(2,1)S(1)}, u32[]{:S(2)}, u32[]{:S(2)}) collective-permute-start(s16[464,128]{1,0:T(8,128)(2,1)S(1)} %get-tuple-element.56), channel_id=1, source_target_pairs={{0,24},{8,16},{16,8},{24,0},{1,25},{9,17},{17,9},{25,1},{2,26},{10... | collective-permute-start | bytes 356360 | tf_op jit(solution)/shard_map/ppermute | solution.py:439
  24.6 1.0 %collective-permute-done.5.face = s16[464,128]{1,0:T(8,128)(2,1)S(1)} collective-permute-done((s16[464,128]{1,0:T(8,128)(2,1)S(1)}, s16[464,128]{1,0:T(8,128)(2,1)S(1)}, u32[]{:S(2)}, u32[]{:S(2)}) %collective-permute-start.5) | collective-permute-done | bytes 118816 | tf_op jit(solution)/shard_map/ppermute | solution.py:439
  25.7 0.1 forward.9
  25.7 2.9 %collective-permute-start.6 = (s16[464,128]{1,0:T(8,128)(2,1)S(1)}, s16[464,128]{1,0:T(8,128)(2,1)S(1)}, u32[]{:S(2)}, u32[]{:S(2)}) collective-permute-start(s16[464,128]{1,0:T(8,128)(2,1)S(1)} %get-tuple-element.44), channel_id=1, source_target_pairs={{0,24},{8,16},{16,8},{24,0},{1,25},{9,17},{17,9},{25,1},{2,26},{10... | collective-permute-start | bytes 356360 | tf_op jit(solution)/shard_map/ppermute | solution.py:439
  28.7 0.8 %collective-permute-done.14.face = s16[464,128]{1,0:T(8,128)(2,1)S(1)} collective-permute-done((s16[464,128]{1,0:T(8,128)(2,1)S(1)}, s16[464,128]{1,0:T(8,128)(2,1)S(1)}, u32[]{:S(2)}, u32[]{:S(2)}) %collective-permute-start.14) | collective-permute-done | bytes 118816 | tf_op jit(solution)/shard_map/ppermute | solution.py:439
  29.5 0.1 forward.14
  29.6 2.4 %collective-permute-start.15 = (s16[464,128]{1,0:T(8,128)(2,1)S(1)}, s16[464,128]{1,0:T(8,128)(2,1)S(1)}, u32[]{:S(2)}, u32[]{:S(2)}) collective-permute-start(s16[464,128]{1,0:T(8,128)(2,1)S(1)} %get-tuple-element.58), channel_id=1, source_target_pairs={{0,8},{8,0},{16,24},{24,16},{1,9},{9,1},{17,25},{25,17},{2,10},{10... | collective-permute-start | bytes 356360 | tf_op jit(solution)/shard_map/ppermute | solution.py:439
  32.0 0.9 %collective-permute-done.6.face = s16[464,128]{1,0:T(8,128)(2,1)S(1)} collective-permute-done((s16[464,128]{1,0:T(8,128)(2,1)S(1)}, s16[464,128]{1,0:T(8,128)(2,1)S(1)}, u32[]{:S(2)}, u32[]{:S(2)}) %collective-permute-start.6) | collective-permute-done | bytes 118816 | tf_op jit(solution)/shard_map/ppermute | solution.py:439
  32.8 0.1 forward.10
  32.9 1.9 %collective-permute-start.7 = (s16[464,128]{1,0:T(8,128)(2,1)S(1)}, s16[464,128]{1,0:T(8,128)(2,1)S(1)}, u32[]{:S(2)}, u32[]{:S(2)}) collective-permute-start(s16[464,128]{1,0:T(8,128)(2,1)S(1)} %get-tuple-element.46), channel_id=1, source_target_pairs={{0,8},{8,0},{16,24},{24,16},{1,9},{9,1},{17,25},{25,17},{2,10},{10... | collective-permute-start | bytes 356360 | tf_op jit(solution)/shard_map/ppermute | solution.py:439
  34.7 1.0 %collective-permute-done.15.face = s16[464,128]{1,0:T(8,128)(2,1)S(1)} collective-permute-done((s16[464,128]{1,0:T(8,128)(2,1)S(1)}, s16[464,128]{1,0:T(8,128)(2,1)S(1)}, u32[]{:S(2)}, u32[]{:S(2)}) %collective-permute-start.15) | collective-permute-done | bytes 118816 | tf_op jit(solution)/shard_map/ppermute | solution.py:439
  35.7 0.1 forward.15
  35.8 2.4 %collective-permute-start.16 = (s16[464,128]{1,0:T(8,128)(2,1)S(1)}, s16[464,128]{1,0:T(8,128)(2,1)S(1)}, u32[]{:S(2)}, u32[]{:S(2)}) collective-permute-start(s16[464,128]{1,0:T(8,128)(2,1)S(1)} %get-tuple-element.60), channel_id=1, source_target_pairs={{0,8},{8,0},{16,24},{24,16},{1,9},{9,1},{17,25},{25,17},{2,10},{10... | collective-permute-start | bytes 356360 | tf_op jit(solution)/shard_map/ppermute | solution.py:439
  38.2 0.4 collective-permute-done.7.face
  38.7 1.9 %collective-permute-start.8 = (s16[464,128]{1,0:T(8,128)(2,1)S(1)}, s16[464,128]{1,0:T(8,128)(2,1)S(1)}, u32[]{:S(2)}, u32[]{:S(2)}) collective-permute-start(s16[464,128]{1,0:T(8,128)(2,1)S(1)} %get-tuple-element.48), channel_id=1, source_target_pairs={{0,8},{8,0},{16,24},{24,16},{1,9},{9,1},{17,25},{25,17},{2,10},{10... | collective-permute-start | bytes 356360 | tf_op jit(solution)/shard_map/ppermute | solution.py:439
  40.6 0.8 %collective-permute-done.16.face = s16[464,128]{1,0:T(8,128)(2,1)S(1)} collective-permute-done((s16[464,128]{1,0:T(8,128)(2,1)S(1)}, s16[464,128]{1,0:T(8,128)(2,1)S(1)}, u32[]{:S(2)}, u32[]{:S(2)}) %collective-permute-start.16) | collective-permute-done | bytes 118816 | tf_op jit(solution)/shard_map/ppermute | solution.py:439
  41.5 0.7 %collective-permute-start.17 = (s16[464,128]{1,0:T(8,128)(2,1)S(1)}, s16[464,128]{1,0:T(8,128)(2,1)S(1)}, u32[]{:S(2)}, u32[]{:S(2)}) collective-permute-start(s16[464,128]{1,0:T(8,128)(2,1)S(1)} %get-tuple-element.62), channel_id=1, source_target_pairs={{16,8},{17,9},{18,10},{19,11},{20,12},{21,13},{22,14},{23,15}} | collective-permute-start | bytes 356360 | tf_op jit(solution)/shard_map/ppermute | solution.py:439
  42.1 1.4 %collective-permute-done.8.face = s16[464,128]{1,0:T(8,128)(2,1)S(1)} collective-permute-done((s16[464,128]{1,0:T(8,128)(2,1)S(1)}, s16[464,128]{1,0:T(8,128)(2,1)S(1)}, u32[]{:S(2)}, u32[]{:S(2)}) %collective-permute-start.8) | collective-permute-done | bytes 118816 | tf_op jit(solution)/shard_map/ppermute | solution.py:439
  43.6 0.7 %collective-permute-start.9 = (s16[464,128]{1,0:T(8,128)(2,1)S(1)}, s16[464,128]{1,0:T(8,128)(2,1)S(1)}, u32[]{:S(2)}, u32[]{:S(2)}) collective-permute-start(s16[464,128]{1,0:T(8,128)(2,1)S(1)} %get-tuple-element.50), channel_id=1, source_target_pairs={{16,8},{17,9},{18,10},{19,11},{20,12},{21,13},{22,14},{23,15}} | collective-permute-start | bytes 356360 | tf_op jit(solution)/shard_map/ppermute | solution.py:439
  44.3 0.3 backward.8
  44.6 8.2 %collective-permute-start.18 = (s16[464,128]{1,0:T(8,128)(2,1)S(1)}, s16[464,128]{1,0:T(8,128)(2,1)S(1)}, u32[]{:S(2)}, u32[]{:S(2)}) collective-permute-start(s16[464,128]{1,0:T(8,128)(2,1)S(1)} %get-tuple-element.64), channel_id=1, source_target_pairs={{0,8},{8,0},{16,24},{24,16},{1,9},{9,1},{17,25},{25,17},{2,10},{10... | collective-permute-start | bytes 356360 | tf_op jit(solution)/shard_map/ppermute | solution.py:439
  52.9 2.2 %collective-permute-start.10 = (s16[464,128]{1,0:T(8,128)(2,1)S(1)}, s16[464,128]{1,0:T(8,128)(2,1)S(1)}, u32[]{:S(2)}, u32[]{:S(2)}) collective-permute-start(s16[464,128]{1,0:T(8,128)(2,1)S(1)} %get-tuple-element.52), channel_id=1, source_target_pairs={{0,8},{8,0},{16,24},{24,16},{1,9},{9,1},{17,25},{25,17},{2,10},{10... | collective-permute-start | bytes 356360 | tf_op jit(solution)/shard_map/ppermute | solution.py:439
  55.1 0.5 collective-permute-done.18.refs_2_
  55.6 0.6 backward.9.refs_0_
  56.2 1.7 %collective-permute-done.10.face = s16[464,128]{1,0:T(8,128)(2,1)S(1)} collective-permute-done((s16[464,128]{1,0:T(8,128)(2,1)S(1)}, s16[464,128]{1,0:T(8,128)(2,1)S(1)}, u32[]{:S(2)}, u32[]{:S(2)}) %collective-permute-start.10) | collective-permute-done | bytes 118816 | tf_op jit(solution)/shard_map/ppermute | solution.py:439
  57.9 1.4 %last.1 = f32[2,7,16,1024]{3,2,1,0:T(8,128)} custom-call(bf16[2,7,7,16,1024]{4,3,2,1,0:T(8,128)(2,1)S(1)} %copy-done, f32[2,2,16,1024]{3,2,1,0:T(8,128)S(1)} %copy-done.1, s16[464,128]{1,0:T(8,128)(2,1)S(1)} %collective-permute-done.10.face, f32[2,7,16,512]{3,2,1,0:T(8,128)S(1)} %backward.9.refs_0_, f32[2,7,16,512]{3,2,1,0:T(8,128)S(1)} %get-tuple-element.66.refs_1_), custom_call_target="tpu_custom_call" | custom-call | tf_op jit(solution)/shard_map/last/pallas_call | solution.py:375
  (18 shorter events, 0.3 us)
Async XLA Ops:
  0.0 15.6 %copy-start = (bf16[2,7,7,16,1024]{4,3,2,1,0:T(8,128)(2,1)S(1)}, bf16[2,7,7,16,1024]{4,3,2,1,0:T(8,128)(2,1)}, u32[]{:S(2)}) copy-start(bf16[2,7,7,16,1024]{4,3,2,1,0:T(8,128)(2,1)} %inverse_ref.25) | copy-start | bytes 9633796
  0.0 1.3 %copy-start.2 = (f32[2,7,16,1024]{3,2,1,0:T(8,128)S(1)}, f32[2,7,16,1024]{3,2,1,0:T(8,128)}, u32[]{:S(2)}) copy-start(f32[2,7,16,1024]{3,2,1,0:T(8,128)} %state_ref.7) | copy-start | bytes 2752516
  1.3 14.2 %copy-start.1 = (f32[2,2,16,1024]{3,2,1,0:T(8,128)S(1)}, f32[2,2,16,1024]{3,2,1,0:T(8,128)}, u32[]{:S(2)}) copy-start(f32[2,2,16,1024]{3,2,1,0:T(8,128)} %coupling_ref.25) | copy-start | bytes 786436
  1.5 10.2 %collective-permute-start.11 = (s16[912,128]{1,0:T(8,128)(2,1)S(1)}, s16[912,128]{1,0:T(8,128)(2,1)S(1)}, u32[]{:S(2)}, u32[]{:S(2)}) collective-permute-start(s16[912,128]{1,0:T(8,128)(2,1)S(1)} %encode.3), channel_id=1, source_target_pairs={{0,8},{8,0},{16,24},{24,16},{1,9},{9,1},{17,25},{25,17},{2,10},{10... | collective-permute-start | bytes 700424 | tf_op jit(solution)/shard_map/ppermute | solution.py:418
  4.7 10.5 %collective-permute-start = (s16[912,128]{1,0:T(8,128)(2,1)S(1)}, s16[912,128]{1,0:T(8,128)(2,1)S(1)}, u32[]{:S(2)}, u32[]{:S(2)}) collective-permute-start(s16[912,128]{1,0:T(8,128)(2,1)S(1)} %encode.2.after_ref), channel_id=1, source_target_pairs={{0,8},{8,0},{16,24},{24,16},{1,9},{9,1},{17,25},{25,17},{2,10},{10... | collective-permute-start | bytes 700424 | tf_op jit(solution)/shard_map/ppermute | solution.py:418
  5.0 8.3 %collective-permute-start.1 = (f32[2,7,2,1024]{3,2,1,0:T(2,128)S(1)}, f32[2,7,2,1024]{3,2,1,0:T(2,128)S(1)}, u32[]{:S(2)}, u32[]{:S(2)}) collective-permute-start(f32[2,7,2,1024]{3,2,1,0:T(2,128)S(1)} %get-tuple-element.37), channel_id=1, source_target_pairs={{0,2},{2,0},{4,6},{6,4},{1,3},{3,1},{5,7},{7,5},{8,10},{10,8},{12,... | collective-permute-start | bytes 344072 | tf_op jit(solution)/shard_map/ppermute | solution.py:424
  7.1 7.3 %collective-permute-start.2 = (f32[2,7,2,1024]{3,2,1,0:T(2,128)S(1)}, f32[2,7,2,1024]{3,2,1,0:T(2,128)S(1)}, u32[]{:S(2)}, u32[]{:S(2)}) collective-permute-start(f32[2,7,2,1024]{3,2,1,0:T(2,128)S(1)} %get-tuple-element.38), channel_id=1, source_target_pairs={{0,6},{2,4},{4,2},{6,0},{1,7},{3,5},{5,3},{7,1},{8,14},{10,12},{12... | collective-permute-start | bytes 344072 | tf_op jit(solution)/shard_map/ppermute | solution.py:424
  9.6 4.9 %collective-permute-start.3 = (f32[2,7,16,128]{3,2,1,0:T(8,128)S(1)}, f32[2,7,16,128]{3,2,1,0:T(8,128)S(1)}, u32[]{:S(2)}, u32[]{:S(2)}) collective-permute-start(f32[2,7,16,128]{3,2,1,0:T(8,128)S(1)} %get-tuple-element.39), channel_id=1, source_target_pairs={{0,1},{1,0},{2,3},{3,2},{4,5},{5,4},{6,7},{7,6},{8,9},{9,8},{10,11... | collective-permute-start | bytes 344072 | tf_op jit(solution)/shard_map/ppermute | solution.py:423
  9.6 0.9 %copy-start.3 = (s32[2,16,1024]{2,1,0:T(8,128)S(1)}, s32[2,16,1024]{2,1,0:T(8,128)}, u32[]{:S(2)}) copy-start(s32[2,16,1024]{2,1,0:T(8,128)} %wall_ref.1) | copy-start | bytes 393220
  11.7 11.9 %collective-permute-start.12 = (s16[912,128]{1,0:T(8,128)(2,1)S(1)}, s16[912,128]{1,0:T(8,128)(2,1)S(1)}, u32[]{:S(2)}, u32[]{:S(2)}) collective-permute-start(s16[912,128]{1,0:T(8,128)(2,1)S(1)} %collective-permute-done.11.refs_3_), channel_id=1, source_target_pairs={{0,16},{8,24},{16,0},{24,8},{1,17},{9,25},{17,1},{25,9},{2,18},{10... | collective-permute-start | bytes 700424 | tf_op jit(solution)/shard_map/ppermute | solution.py:445
  16.1 9.6 %collective-permute-start.4 = (s16[912,128]{1,0:T(8,128)(2,1)S(1)}, s16[912,128]{1,0:T(8,128)(2,1)S(1)}, u32[]{:S(2)}, u32[]{:S(2)}) collective-permute-start(s16[912,128]{1,0:T(8,128)(2,1)S(1)} %collective-permute-done.refs_3_), channel_id=1, source_target_pairs={{0,16},{8,24},{16,0},{24,8},{1,17},{9,25},{17,1},{25,9},{2,18},{10... | collective-permute-start | bytes 700424 | tf_op jit(solution)/shard_map/ppermute | solution.py:445
  18.4 5.2 %collective-permute-start.13 = (s16[464,128]{1,0:T(8,128)(2,1)S(1)}, s16[464,128]{1,0:T(8,128)(2,1)S(1)}, u32[]{:S(2)}, u32[]{:S(2)}) collective-permute-start(s16[464,128]{1,0:T(8,128)(2,1)S(1)} %get-tuple-element.54), channel_id=1, source_target_pairs={{0,8},{8,0},{16,24},{24,16},{1,9},{9,1},{17,25},{25,17},{2,10},{10... | collective-permute-start | bytes 356360 | tf_op jit(solution)/shard_map/ppermute | solution.py:439
  19.5 6.2 %collective-permute-start.5 = (s16[464,128]{1,0:T(8,128)(2,1)S(1)}, s16[464,128]{1,0:T(8,128)(2,1)S(1)}, u32[]{:S(2)}, u32[]{:S(2)}) collective-permute-start(s16[464,128]{1,0:T(8,128)(2,1)S(1)} %get-tuple-element.41), channel_id=1, source_target_pairs={{0,8},{8,0},{16,24},{24,16},{1,9},{9,1},{17,25},{25,17},{2,10},{10... | collective-permute-start | bytes 356360 | tf_op jit(solution)/shard_map/ppermute | solution.py:439
  23.6 5.9 %collective-permute-start.14 = (s16[464,128]{1,0:T(8,128)(2,1)S(1)}, s16[464,128]{1,0:T(8,128)(2,1)S(1)}, u32[]{:S(2)}, u32[]{:S(2)}) collective-permute-start(s16[464,128]{1,0:T(8,128)(2,1)S(1)} %get-tuple-element.56), channel_id=1, source_target_pairs={{0,24},{8,16},{16,8},{24,0},{1,25},{9,17},{17,9},{25,1},{2,26},{10... | collective-permute-start | bytes 356360 | tf_op jit(solution)/shard_map/ppermute | solution.py:439
  25.7 7.1 %collective-permute-start.6 = (s16[464,128]{1,0:T(8,128)(2,1)S(1)}, s16[464,128]{1,0:T(8,128)(2,1)S(1)}, u32[]{:S(2)}, u32[]{:S(2)}) collective-permute-start(s16[464,128]{1,0:T(8,128)(2,1)S(1)} %get-tuple-element.44), channel_id=1, source_target_pairs={{0,24},{8,16},{16,8},{24,0},{1,25},{9,17},{17,9},{25,1},{2,26},{10... | collective-permute-start | bytes 356360 | tf_op jit(solution)/shard_map/ppermute | solution.py:439
  29.6 6.2 %collective-permute-start.15 = (s16[464,128]{1,0:T(8,128)(2,1)S(1)}, s16[464,128]{1,0:T(8,128)(2,1)S(1)}, u32[]{:S(2)}, u32[]{:S(2)}) collective-permute-start(s16[464,128]{1,0:T(8,128)(2,1)S(1)} %get-tuple-element.58), channel_id=1, source_target_pairs={{0,8},{8,0},{16,24},{24,16},{1,9},{9,1},{17,25},{25,17},{2,10},{10... | collective-permute-start | bytes 356360 | tf_op jit(solution)/shard_map/ppermute | solution.py:439
  32.9 5.7 %collective-permute-start.7 = (s16[464,128]{1,0:T(8,128)(2,1)S(1)}, s16[464,128]{1,0:T(8,128)(2,1)S(1)}, u32[]{:S(2)}, u32[]{:S(2)}) collective-permute-start(s16[464,128]{1,0:T(8,128)(2,1)S(1)} %get-tuple-element.46), channel_id=1, source_target_pairs={{0,8},{8,0},{16,24},{24,16},{1,9},{9,1},{17,25},{25,17},{2,10},{10... | collective-permute-start | bytes 356360 | tf_op jit(solution)/shard_map/ppermute | solution.py:439
  35.8 5.6 %collective-permute-start.16 = (s16[464,128]{1,0:T(8,128)(2,1)S(1)}, s16[464,128]{1,0:T(8,128)(2,1)S(1)}, u32[]{:S(2)}, u32[]{:S(2)}) collective-permute-start(s16[464,128]{1,0:T(8,128)(2,1)S(1)} %get-tuple-element.60), channel_id=1, source_target_pairs={{0,8},{8,0},{16,24},{24,16},{1,9},{9,1},{17,25},{25,17},{2,10},{10... | collective-permute-start | bytes 356360 | tf_op jit(solution)/shard_map/ppermute | solution.py:439
  38.7 4.9 %collective-permute-start.8 = (s16[464,128]{1,0:T(8,128)(2,1)S(1)}, s16[464,128]{1,0:T(8,128)(2,1)S(1)}, u32[]{:S(2)}, u32[]{:S(2)}) collective-permute-start(s16[464,128]{1,0:T(8,128)(2,1)S(1)} %get-tuple-element.48), channel_id=1, source_target_pairs={{0,8},{8,0},{16,24},{24,16},{1,9},{9,1},{17,25},{25,17},{2,10},{10... | collective-permute-start | bytes 356360 | tf_op jit(solution)/shard_map/ppermute | solution.py:439
  41.5 2.8 %collective-permute-start.17 = (s16[464,128]{1,0:T(8,128)(2,1)S(1)}, s16[464,128]{1,0:T(8,128)(2,1)S(1)}, u32[]{:S(2)}, u32[]{:S(2)}) collective-permute-start(s16[464,128]{1,0:T(8,128)(2,1)S(1)} %get-tuple-element.62), channel_id=1, source_target_pairs={{16,8},{17,9},{18,10},{19,11},{20,12},{21,13},{22,14},{23,15}} | collective-permute-start | bytes 356360 | tf_op jit(solution)/shard_map/ppermute | solution.py:439
  43.6 9.2 %collective-permute-start.9 = (s16[464,128]{1,0:T(8,128)(2,1)S(1)}, s16[464,128]{1,0:T(8,128)(2,1)S(1)}, u32[]{:S(2)}, u32[]{:S(2)}) collective-permute-start(s16[464,128]{1,0:T(8,128)(2,1)S(1)} %get-tuple-element.50), channel_id=1, source_target_pairs={{16,8},{17,9},{18,10},{19,11},{20,12},{21,13},{22,14},{23,15}} | collective-permute-start | bytes 356360 | tf_op jit(solution)/shard_map/ppermute | solution.py:439
  44.6 11.0 %collective-permute-start.18 = (s16[464,128]{1,0:T(8,128)(2,1)S(1)}, s16[464,128]{1,0:T(8,128)(2,1)S(1)}, u32[]{:S(2)}, u32[]{:S(2)}) collective-permute-start(s16[464,128]{1,0:T(8,128)(2,1)S(1)} %get-tuple-element.64), channel_id=1, source_target_pairs={{0,8},{8,0},{16,24},{24,16},{1,9},{9,1},{17,25},{25,17},{2,10},{10... | collective-permute-start | bytes 356360 | tf_op jit(solution)/shard_map/ppermute | solution.py:439
  52.9 5.1 %collective-permute-start.10 = (s16[464,128]{1,0:T(8,128)(2,1)S(1)}, s16[464,128]{1,0:T(8,128)(2,1)S(1)}, u32[]{:S(2)}, u32[]{:S(2)}) collective-permute-start(s16[464,128]{1,0:T(8,128)(2,1)S(1)} %get-tuple-element.52), channel_id=1, source_target_pairs={{0,8},{8,0},{16,24},{24,16},{1,9},{9,1},{17,25},{25,17},{2,10},{10... | collective-permute-start | bytes 356360 | tf_op jit(solution)/shard_map/ppermute | solution.py:439
